TPU v7x, 32 devices: a whole 2x2x4 slice. The times are simulated.
32 devices in a mesh: groups: 2 (over y), gz: 4 (over z), gy: 2 (over x), af: 2 (over core).
Axes of the slice: x: 2, y: 2, z: 4, core: 2. Of those that a mesh axis runs over, the one named last changes fastest.
Arguments:
- atlas_features: bfloat16 [64, 256, 12, 128], P(('groups', 'gz'), ('gy', 'af')), parts along dimension 0, may hold values from -6 to 6
- velocity: bfloat16 [3, 64, 12, 128], P(None, ('groups', 'gz')), parts along dimension 1, may hold values from -0.25 to 0.25
- section_density: bfloat16 [64, 256, 1536], P(('groups', 'gz', 'gy', 'af')), parts along dimension 0, may hold values from -6 to 6
- pixel_mask: int32 [64, 1536], P(('groups', 'gz', 'gy', 'af')), parts along dimension 0, may hold values 0 or 1
- section_slice: int32 [64], P(('groups', 'gz')), parts along dimension 0, may hold values from 0 to 31, as said below
Outputs:
- feature_gradient: bfloat16 [64, 256, 12, 128], P(('groups', 'gz'), ('gy', 'af')), parts along dimension 0
There are 2 independent parts, one for each index of `groups`. A program takes and returns all parts, laid end to end along the dimension named above; each array names one. Nothing has to cross between parts.
Inputs may be any that keep to these rules, and one draw needn't show every extreme that they name: `section_slice`: sections 8 * g to 8 * g + 7 match the slices 8 * g to 8 * g + 7, each once, in some order.
All inputs are finite; a program needn't handle non-finite values. No bound on the sum of `pixel_mask` on one device may be relied on, other than what follows from the above.
Results may differ from a plain program's by a relative error of at most 0.0096.
Values may be sent and summed in bfloat16 or wider, within the bound.
No kernel may reach another device: no remote copies, remote signals or barrier semaphores. Data moves between devices by JAX's collectives and lax.ppermute only.
A program may use at most 64 MiB of HBM per device.

v0:
```python
import jax
import jax.numpy as jnp
from jax import lax
from jax.sharding import PartitionSpec as P

TSTEPS = 4


rate_diffuse = 0.04
ridge_weight = 0.25


def padded_2(cells, sides, width):
    for axis, dim in sides:
        count = lax.axis_size(axis)
        ends = count - 1
        head = lax.slice_in_dim(cells, 0, width, axis=dim)
        tail = lax.slice_in_dim(cells, cells.shape[dim] - width, cells.shape[dim], axis=dim)
        cells = jnp.concatenate(
            [
                lax.ppermute(tail, axis, [(i, (i + 1) % count) for i in range(ends)]),
                cells,
                lax.ppermute(head, axis, [((i + 1) % count, i) for i in range(ends)]),
            ],
            axis=dim,
        )
    return cells


def advance(padded, velocity_field):
    center = padded[1:-1]
    below_cell = padded[:-2]
    above_cell = padded[2:]
    sideways = jnp.pad(center, ((0, 0), (0, 0), (1, 1), (1, 1)))
    row_below = sideways[:, :, :-2, 1:-1]
    row_above = sideways[:, :, 2:, 1:-1]
    col_below = sideways[:, :, 1:-1, :-2]
    col_above = sideways[:, :, 1:-1, 2:]
    along_z = velocity_field[0][:, None]
    along_y = velocity_field[1][:, None]
    along_x = velocity_field[2][:, None]
    transport_term = (
        jnp.maximum(along_z, 0.0) * (center - below_cell)
        + jnp.minimum(along_z, 0.0) * (above_cell - center)
        + jnp.maximum(along_y, 0.0) * (center - row_below)
        + jnp.minimum(along_y, 0.0) * (row_above - center)
        + jnp.maximum(along_x, 0.0) * (center - col_below)
        + jnp.minimum(along_x, 0.0) * (col_above - center)
    )
    diffusion_term = (
        below_cell + above_cell + row_below + row_above + col_below + col_above - 6.0 * center
    )
    return center - transport_term + rate_diffuse * diffusion_term


def fit_section(slice_panel, density, pixel_valid):
    pixels = slice_panel.shape[-1]
    valid_pixel = pixel_valid[None, :] > 0
    masked = jnp.where(valid_pixel, slice_panel, jnp.zeros_like(slice_panel))
    gram_matrix = (
        lax.dot_general(
            masked, slice_panel, (((1,), (1,)), ((), ())), preferred_element_type=jnp.float32
        )
        / pixels
    )
    gram_matrix = gram_matrix + ridge_weight * jnp.eye(slice_panel.shape[0], dtype=jnp.float32)
    right_side = (
        lax.dot_general(
            masked, density, (((1,), (1,)), ((), ())), preferred_element_type=jnp.float32
        )
        / pixels
    )
    lower_factor = lax.linalg.cholesky(gram_matrix)
    halfway = lax.linalg.triangular_solve(lower_factor, right_side, left_side=True, lower=True)
    coefficient = lax.linalg.triangular_solve(
        lower_factor, halfway, left_side=True, lower=True, transpose_a=True
    )
    coefficient_low = coefficient.astype(jnp.bfloat16)
    fitted = lax.dot_general(
        coefficient_low, slice_panel, (((0,), (0,)), ((), ())), preferred_element_type=jnp.float32
    )
    residual = (fitted - density.astype(jnp.float32)).astype(jnp.bfloat16)
    pushed = jnp.dot(coefficient_low, residual, preferred_element_type=jnp.float32)
    return jnp.where(valid_pixel, 2.0 * pushed, 0.0).astype(jnp.bfloat16)


def body(atlas_features, velocity, section_density, pixel_mask, section_slice):
    state_field = atlas_features.astype(jnp.float32)
    velocity_field = velocity.astype(jnp.float32)
    slab_rows = state_field.shape[0]
    for repeat in range(TSTEPS):
        padded = padded_2(state_field, (("gz", 0),), 1)
        state_field = advance(padded, velocity_field)
    moved_panel = state_field.astype(jnp.bfloat16)
    local_slot = section_slice - lax.axis_index("gz") * slab_rows
    ordered = jnp.take(moved_panel, local_slot, axis=0)
    channels = moved_panel.shape[1]
    pixels = moved_panel.shape[2] * moved_panel.shape[3]
    width_gy = lax.axis_size("gy")
    width_af = lax.axis_size("af")
    groups_count = width_gy * width_af
    per_device = slab_rows // groups_count
    outgoing = ordered.reshape(groups_count, per_device, channels, pixels)
    arrived = lax.all_to_all(outgoing, ("gy", "af"), split_axis=0, concat_axis=2, tiled=True)
    gradients = jax.vmap(fit_section)(arrived[0], section_density, pixel_mask)
    returned_blocks = lax.all_to_all(
        gradients[None], ("gy", "af"), split_axis=2, concat_axis=0, tiled=True
    )
    restored = returned_blocks.reshape(
        slab_rows, channels, moved_panel.shape[2], moved_panel.shape[3]
    )
    return jnp.zeros_like(moved_panel).at[local_slot].set(restored)


def solution(mesh):
    return jax.shard_map(
        body,
        mesh=mesh,
        in_specs=(
            P(("groups", "gz"), ("gy", "af"), None, None),
            P(None, ("groups", "gz"), None, None),
            P(("groups", "gz", "gy", "af"), None, None),
            P(("groups", "gz", "gy", "af"), None),
            P(("groups", "gz")),
        ),
        out_specs=P(("groups", "gz"), ("gy", "af"), None, None),
        check_vma=False,
    )
```

profile of v0, /device:TPU:0, one launch (start us, length us, event | category | flops | bytes accessed | tf_op | source)
XLA Modules:
  0.0 267.7 jit_solution(9639371441279526746)
XLA Ops:
  0.0 1.1 fusion.114
  1.1 5.1 %collective-permute-start = (f32[1,64,12,128]{3,1,2,0:T(8,128)S(1)}, f32[1,64,12,128]{3,1,2,0:T(8,128)S(1)}, u32[]{:S(2)}, u32[]{:S(2)}) collective-permute-start(f32[1,64,12,128]{3,1,2,0:T(8,128)S(1)} %get-tuple-element.34), channel_id=1, source_target_pairs={{0,4},{4,8},{8,12},{1,5},{5,9},{9,13},{2,6},{6,10},{10,14},{3,7},{... | collective-permute-start | bytes 1179656 | tf_op jit(solution)/shard_map/ppermute | solution.py:21
  6.2 1.3 collective-permute-start.1
  7.5 1.8 convert_element_type.25
  9.5 5.1 %collective-permute-done = f32[1,64,12,128]{3,1,2,0:T(8,128)S(1)} collective-permute-done((f32[1,64,12,128]{3,1,2,0:T(8,128)S(1)}, f32[1,64,12,128]{3,1,2,0:T(8,128)S(1)}, u32[]{:S(2)}, u32[]{:S(2)}) %collective-permute-start) | collective-permute-done | bytes 393248 | tf_op jit(solution)/shard_map/ppermute | solution.py:21
  14.6 4.1 %collective-permute-done.1 = f32[1,64,12,128]{3,1,2,0:T(8,128)S(1)} collective-permute-done((f32[1,64,12,128]{3,1,2,0:T(8,128)S(1)}, f32[1,64,12,128]{3,1,2,0:T(8,128)S(1)}, u32[]{:S(2)}, u32[]{:S(2)}) %collective-permute-start.1) | collective-permute-done | bytes 393248 | tf_op jit(solution)/shard_map/ppermute | solution.py:23
  18.7 3.7 %fusion.12 = f32[8,64,12,128]{3,1,2,0:T(8,128)S(1)} fusion(bf16[8,64,12,128]{3,1,2,0:T(8,128)(2,1)S(1)} %copy-done, f32[8,64,12,128]{3,1,2,0:T(8,128)S(1)} %convert_element_type.25, f32[1,64,12,128]{3,1,2,0:T(8,128)S(1)} %collective-permute-done, f32[1,64,12,128]{3,1,2,0:T(8,128)S(1)} %collective-permute-done.1, f32[8,12,128]{2,1,0:T(8,128)S(1)} %copy.71, ...), kind=kLoop, calls=%fused_computation.42 | loop fusion | flops 23592960 | bytes 8945664 | tf_op jit(solution)/shard_map/add | solution.py:53
  22.5 3.5 %collective-permute-start.2 = (f32[1,64,12,128]{3,1,2,0:T(8,128)S(1)}, f32[1,64,12,128]{3,1,2,0:T(8,128)S(1)}, u32[]{:S(2)}, u32[]{:S(2)}) collective-permute-start(f32[1,64,12,128]{3,1,2,0:T(8,128)S(1)} %get-tuple-element.31), channel_id=1, source_target_pairs={{0,4},{4,8},{8,12},{1,5},{5,9},{9,13},{2,6},{6,10},{10,14},{3,7},{... | collective-permute-start | bytes 1179656 | tf_op jit(solution)/shard_map/ppermute | solution.py:21
  26.0 1.3 collective-permute-start.3
  27.3 5.8 %collective-permute-done.2 = f32[1,64,12,128]{3,1,2,0:T(8,128)S(1)} collective-permute-done((f32[1,64,12,128]{3,1,2,0:T(8,128)S(1)}, f32[1,64,12,128]{3,1,2,0:T(8,128)S(1)}, u32[]{:S(2)}, u32[]{:S(2)}) %collective-permute-start.2) | collective-permute-done | bytes 393248 | tf_op jit(solution)/shard_map/ppermute | solution.py:21
  33.1 4.1 %collective-permute-done.3 = f32[1,64,12,128]{3,1,2,0:T(8,128)S(1)} collective-permute-done((f32[1,64,12,128]{3,1,2,0:T(8,128)S(1)}, f32[1,64,12,128]{3,1,2,0:T(8,128)S(1)}, u32[]{:S(2)}, u32[]{:S(2)}) %collective-permute-start.3) | collective-permute-done | bytes 393248 | tf_op jit(solution)/shard_map/ppermute | solution.py:23
  37.3 3.8 %fusion.60 = f32[8,64,12,128]{3,1,2,0:T(8,128)S(1)} fusion(f32[1,64,12,128]{3,1,2,0:T(8,128)S(1)} %collective-permute-done.3, f32[8,64,12,128]{3,1,2,0:T(8,128)S(1)} %fusion.12, f32[1,64,12,128]{3,1,2,0:T(8,128)S(1)} %collective-permute-done.2, f32[8,12,128]{2,1,0:T(8,128)S(1)} %copy.71, f32[8,12,128]{2,1,0:T(8,128)S(1)} %copy.70, ...), kind=kLoop, calls=%fused_computation.95 | loop fusion | flops 22806528 | bytes 7372800 | tf_op jit(solution)/shard_map/add | solution.py:53
  41.1 3.5 %collective-permute-start.4 = (f32[1,64,12,128]{3,1,2,0:T(8,128)S(1)}, f32[1,64,12,128]{3,1,2,0:T(8,128)S(1)}, u32[]{:S(2)}, u32[]{:S(2)}) collective-permute-start(f32[1,64,12,128]{3,1,2,0:T(8,128)S(1)} %get-tuple-element.29), channel_id=1, source_target_pairs={{0,4},{4,8},{8,12},{1,5},{5,9},{9,13},{2,6},{6,10},{10,14},{3,7},{... | collective-permute-start | bytes 1179656 | tf_op jit(solution)/shard_map/ppermute | solution.py:21
  44.6 1.3 collective-permute-start.5
  45.9 4.6 %collective-permute-done.4 = f32[1,64,12,128]{3,1,2,0:T(8,128)S(1)} collective-permute-done((f32[1,64,12,128]{3,1,2,0:T(8,128)S(1)}, f32[1,64,12,128]{3,1,2,0:T(8,128)S(1)}, u32[]{:S(2)}, u32[]{:S(2)}) %collective-permute-start.4) | collective-permute-done | bytes 393248 | tf_op jit(solution)/shard_map/ppermute | solution.py:21
  50.6 4.1 %collective-permute-done.5 = f32[1,64,12,128]{3,1,2,0:T(8,128)S(1)} collective-permute-done((f32[1,64,12,128]{3,1,2,0:T(8,128)S(1)}, f32[1,64,12,128]{3,1,2,0:T(8,128)S(1)}, u32[]{:S(2)}, u32[]{:S(2)}) %collective-permute-start.5) | collective-permute-done | bytes 393248 | tf_op jit(solution)/shard_map/ppermute | solution.py:23
  54.7 3.8 %fusion.42 = f32[8,64,12,128]{3,1,2,0:T(8,128)S(1)} fusion(f32[1,64,12,128]{3,1,2,0:T(8,128)S(1)} %collective-permute-done.5, f32[8,64,12,128]{3,1,2,0:T(8,128)S(1)} %fusion.60, f32[1,64,12,128]{3,1,2,0:T(8,128)S(1)} %collective-permute-done.4, f32[8,12,128]{2,1,0:T(8,128)S(1)} %copy.71, f32[8,12,128]{2,1,0:T(8,128)S(1)} %copy.70, ...), kind=kLoop, calls=%fused_computation.75 | loop fusion | flops 22806528 | bytes 7372800 | tf_op jit(solution)/shard_map/add | solution.py:53
  58.5 0.9 fusion.111
  59.4 3.2 %collective-permute-start.6 = (f32[1,64,12,128]{3,1,2,0:T(8,128)}, f32[1,64,12,128]{3,1,2,0:T(8,128)}, u32[]{:S(2)}, u32[]{:S(2)}) collective-permute-start(f32[1,64,12,128]{3,1,2,0:T(8,128)} %get-tuple-element.27), channel_id=1, source_target_pairs={{0,4},{4,8},{8,12},{1,5},{5,9},{9,13},{2,6},{6,10},{10,14},{3,7},{... | collective-permute-start | bytes 1179656 | tf_op jit(solution)/shard_map/ppermute | solution.py:21
  62.6 1.3 collective-permute-start.7
  63.9 0.1 broadcast_in_dim.51
  64.0 3.4 %collective-permute-done.6 = f32[1,64,12,128]{3,1,2,0:T(8,128)} collective-permute-done((f32[1,64,12,128]{3,1,2,0:T(8,128)}, f32[1,64,12,128]{3,1,2,0:T(8,128)}, u32[]{:S(2)}, u32[]{:S(2)}) %collective-permute-start.6) | collective-permute-done | bytes 393248 | tf_op jit(solution)/shard_map/ppermute | solution.py:21
  67.5 5.1 %collective-permute-done.7 = f32[1,64,12,128]{3,1,2,0:T(8,128)} collective-permute-done((f32[1,64,12,128]{3,1,2,0:T(8,128)}, f32[1,64,12,128]{3,1,2,0:T(8,128)}, u32[]{:S(2)}, u32[]{:S(2)}) %collective-permute-start.7) | collective-permute-done | bytes 393248 | tf_op jit(solution)/shard_map/ppermute | solution.py:23
  72.6 5.4 %fusion.24 = bf16[8,64,12,128]{3,1,2,0:T(8,128)(2,1)} fusion(f32[1,64,12,128]{3,1,2,0:T(8,128)} %collective-permute-done.7, f32[8,64,12,128]{3,1,2,0:T(8,128)S(1)} %fusion.42, f32[1,64,12,128]{3,1,2,0:T(8,128)} %collective-permute-done.6, f32[8,12,128]{2,1,0:T(8,128)S(1)} %copy.71, f32[8,12,128]{2,1,0:T(8,128)S(1)} %copy.70, f32[8,12,128]{2,1,0:T(8,128)S(1)} %copy.69, ...), kind=kLoop, calls=%fused_computation.55 | loop fusion | flops 23592960 | bytes 5799936 | tf_op jit(solution)/shard_map/convert_element_type | solution.py:94
  78.0 2.3 gather_fusion
  80.3 2.5 copy.72
  82.8 3.0 %gather.11 = bf16[4,2,64,1536]{3,2,1,0:T(8,128)(2,1)S(1)} reshape(bf16[8,64,12,128]{3,2,1,0:T(8,128)(2,1)} %copy.72) | data formatting | bytes 3145728 | tf_op jit(solution)/shard_map/jit(_take)/gather | solution.py:96
  85.7 1.4 broadcast_select_fusion
  87.1 3.7 %all-to-all-start = ((bf16[4,2,64,1536]{3,2,1,0:T(8,128)(2,1)}), bf16[4,2,64,1536]{3,2,1,0:T(8,128)(2,1)S(1)}, u32[]{:S(2)}, u32[]{:S(2)}) async-start(bf16[4,2,64,1536]{3,2,1,0:T(8,128)(2,1)} %broadcast_select_fusion), calls=%async_computation | async-start | bytes 3145728 | tf_op jit(solution)/shard_map/all_to_all | solution.py:104
  90.9 0.8 copy.75
  91.9 18.9 %all-to-all-done = bf16[4,2,64,1536]{3,2,1,0:T(8,128)(2,1)S(1)} async-done(((bf16[4,2,64,1536]{3,2,1,0:T(8,128)(2,1)}), bf16[4,2,64,1536]{3,2,1,0:T(8,128)(2,1)S(1)}, u32[]{:S(2)}, u32[]{:S(2)}) %all-to-all-start) | async-done | bytes 1572896 | tf_op jit(solution)/shard_map/all_to_all | solution.py:104
  110.7 0.1 copy.73
  110.8 0.8 copy-done.1
  111.7 0.6 broadcast_add_fusion
  112.3 0.2 copy.76
  112.5 0.1 fusion.88
  112.6 23.5 %custom-call.15 = f32[2,128,128]{2,1,0:T(8,128)S(1)} custom-call(f32[2,128,128]{2,1,0:T(8,128)S(1)} %cholesky.122), custom_call_target="Cholesky" | custom-call | tf_op jit(solution)/shard_map/vmap()/cholesky | solution.py:73
  136.1 19.7 %custom-call.16 = f32[2,1,128,128]{2,3,1,0:T(8,128)S(1)} custom-call(f32[2,1,128,128]{3,2,1,0:T(8,128)S(1)} %select_bitcast_fusion), custom_call_target="InvertDiagBlocksLowerTriangular" | custom-call | tf_op jit(solution)/shard_map/vmap()/cholesky | solution.py:73
  155.8 0.3 constant_dynamic-update-slice_fusion.1
  156.1 0.4 convolution_subtract_fusion.3
  156.5 23.5 %custom-call.17 = f32[2,128,128]{2,1,0:T(8,128)S(1)} custom-call(f32[2,128,128]{2,1,0:T(8,128)S(1)} %convolution_subtract_fusion.3), custom_call_target="Cholesky" | custom-call | tf_op jit(solution)/shard_map/vmap()/cholesky | solution.py:73
  180.0 0.2 compare_reduce_fusion
  180.1 0.1 select_select_fusion
  180.4 5.2 %while.1 = (s32[]{:T(128)}, f32[2,256,256]{2,1,0:T(8,128)S(1)}, s32[2,2]{1,0:T(2,128)S(1)}, f32[2,2,128,128]{3,2,0,1:T(8,128)}, s32[]{:T(128)}) while((s32[]{:T(128)}, f32[2,256,256]{2,1,0:T(8,128)S(1)}, s32[2,2]{1,0:T(2,128)S(1)}, f32[2,2,128,128]{3,2,0,1:T(8,128)}, s32[]{:T(128)}) %tuple.35), condition=%wide.while_cond, body=%wide.while_body.sunk | while | flops 2 | bytes 263777 | solution.py:75
  180.4 0.6 fusion.127
  181.0 2.0 bitcast_dynamic-update-slice_fusion.2
  183.0 0.6 fusion.127
  183.6 2.0 bitcast_dynamic-update-slice_fusion.2
  185.6 40.1 %custom-call.18 = f32[2,2,128,128]{2,3,1,0:T(8,128)S(1)} custom-call(f32[2,2,128,128]{3,2,1,0:T(8,128)} %bitcast.80), custom_call_target="InvertDiagBlocksLowerTriangular" | custom-call | tf_op jit(solution)/shard_map/vmap()/triangular_solve | solution.py:75
  225.8 2.0 fusion.82
  227.8 0.4 fusion.89
  228.2 0.6 convolution_subtract_fusion.2
  228.8 0.4 fusion.103
  229.2 0.4 fusion.115
  229.6 0.4 convolution_subtract_fusion.1
  230.0 0.4 convolution_convert_fusion
  230.4 2.5 fusion.72
  232.9 1.6 copy.88
  234.5 22.5 %all_to_all.30 = bf16[1,2,256,1536]{3,1,0,2:T(2,128)(2,1)S(1)} all-to-all(bf16[1,2,256,1536]{3,1,0,2:T(2,128)(2,1)S(1)} %copy.88), channel_id=1, replica_groups=mesh['groups'=2,'gz'=4,'gy'=2,'af'=2] {'gy','af'}, dimensions={2} | all-to-all | bytes 3145728 | tf_op jit(solution)/shard_map/all_to_all | solution.py:106
  257.0 0.2 copy.111
  257.2 2.1 reshape.136
  259.3 2.0 copy.90
  261.3 1.5 broadcast_in_dim.48
  262.9 4.8 %scatter_fusion = bf16[8,64,12,128]{3,1,2,0:T(8,128)(2,1)} fusion(bf16[8,64,12,128]{3,1,2,0:T(8,128)(2,1)} %broadcast_in_dim.48, s32[8]{0:T(128)S(1)} %get-tuple-element.24, bf16[8,64,12,128]{3,1,2,0:T(8,128)(2,1)S(1)} %copy.90), kind=kCustom, calls=%fused_computation.1 | custom fusion | bytes 4718624 | tf_op jit(solution)/shard_map/scatter | solution.py:112
  (37 shorter events, 0.6 us)
Async XLA Ops:
  0.0 9.3 %copy-start.2 = (bf16[3,8,12,128]{3,1,2,0:T(8,128)(2,1)S(1)}, bf16[3,8,12,128]{3,1,2,0:T(8,128)(2,1)}, u32[]{:S(2)}) copy-start(bf16[3,8,12,128]{3,1,2,0:T(8,128)(2,1)} %param.6) | copy-start | bytes 221188
  1.1 17.6 %copy-start = (bf16[8,64,12,128]{3,1,2,0:T(8,128)(2,1)S(1)}, bf16[8,64,12,128]{3,1,2,0:T(8,128)(2,1)}, u32[]{:S(2)}) copy-start(bf16[8,64,12,128]{3,1,2,0:T(8,128)(2,1)} %param.5) | copy-start | bytes 4718596
  1.1 13.4 %collective-permute-start = (f32[1,64,12,128]{3,1,2,0:T(8,128)S(1)}, f32[1,64,12,128]{3,1,2,0:T(8,128)S(1)}, u32[]{:S(2)}, u32[]{:S(2)}) collective-permute-start(f32[1,64,12,128]{3,1,2,0:T(8,128)S(1)} %get-tuple-element.34), channel_id=1, source_target_pairs={{0,4},{4,8},{8,12},{1,5},{5,9},{9,13},{2,6},{6,10},{10,14},{3,7},{... | collective-permute-start | bytes 1179656 | tf_op jit(solution)/shard_map/ppermute | solution.py:21
  6.2 12.5 %collective-permute-start.1 = (f32[1,64,12,128]{3,1,2,0:T(8,128)S(1)}, f32[1,64,12,128]{3,1,2,0:T(8,128)S(1)}, u32[]{:S(2)}, u32[]{:S(2)}) collective-permute-start(f32[1,64,12,128]{3,1,2,0:T(8,128)S(1)} %get-tuple-element.33), channel_id=1, source_target_pairs={{4,0},{8,4},{12,8},{5,1},{9,5},{13,9},{6,2},{10,6},{14,10},{7,3},{... | collective-permute-start | bytes 1179656 | tf_op jit(solution)/shard_map/ppermute | solution.py:23
  22.5 10.6 %collective-permute-start.2 = (f32[1,64,12,128]{3,1,2,0:T(8,128)S(1)}, f32[1,64,12,128]{3,1,2,0:T(8,128)S(1)}, u32[]{:S(2)}, u32[]{:S(2)}) collective-permute-start(f32[1,64,12,128]{3,1,2,0:T(8,128)S(1)} %get-tuple-element.31), channel_id=1, source_target_pairs={{0,4},{4,8},{8,12},{1,5},{5,9},{9,13},{2,6},{6,10},{10,14},{3,7},{... | collective-permute-start | bytes 1179656 | tf_op jit(solution)/shard_map/ppermute | solution.py:21
  26.0 11.3 %collective-permute-start.3 = (f32[1,64,12,128]{3,1,2,0:T(8,128)S(1)}, f32[1,64,12,128]{3,1,2,0:T(8,128)S(1)}, u32[]{:S(2)}, u32[]{:S(2)}) collective-permute-start(f32[1,64,12,128]{3,1,2,0:T(8,128)S(1)} %get-tuple-element.32), channel_id=1, source_target_pairs={{4,0},{8,4},{12,8},{5,1},{9,5},{13,9},{6,2},{10,6},{14,10},{7,3},{... | collective-permute-start | bytes 1179656 | tf_op jit(solution)/shard_map/ppermute | solution.py:23
  41.1 9.4 %collective-permute-start.4 = (f32[1,64,12,128]{3,1,2,0:T(8,128)S(1)}, f32[1,64,12,128]{3,1,2,0:T(8,128)S(1)}, u32[]{:S(2)}, u32[]{:S(2)}) collective-permute-start(f32[1,64,12,128]{3,1,2,0:T(8,128)S(1)} %get-tuple-element.29), channel_id=1, source_target_pairs={{0,4},{4,8},{8,12},{1,5},{5,9},{9,13},{2,6},{6,10},{10,14},{3,7},{... | collective-permute-start | bytes 1179656 | tf_op jit(solution)/shard_map/ppermute | solution.py:21
  44.6 19.3 %copy-start.4 = (s32[8]{0:T(128)S(1)}, s32[8]{0:T(128)}, u32[]{:S(2)}) copy-start(s32[8]{0:T(128)} %param.9) | copy-start | bytes 100
  44.6 10.1 %collective-permute-start.5 = (f32[1,64,12,128]{3,1,2,0:T(8,128)S(1)}, f32[1,64,12,128]{3,1,2,0:T(8,128)S(1)}, u32[]{:S(2)}, u32[]{:S(2)}) collective-permute-start(f32[1,64,12,128]{3,1,2,0:T(8,128)S(1)} %get-tuple-element.30), channel_id=1, source_target_pairs={{4,0},{8,4},{12,8},{5,1},{9,5},{13,9},{6,2},{10,6},{14,10},{7,3},{... | collective-permute-start | bytes 1179656 | tf_op jit(solution)/shard_map/ppermute | solution.py:23
  59.4 8.0 %collective-permute-start.6 = (f32[1,64,12,128]{3,1,2,0:T(8,128)}, f32[1,64,12,128]{3,1,2,0:T(8,128)}, u32[]{:S(2)}, u32[]{:S(2)}) collective-permute-start(f32[1,64,12,128]{3,1,2,0:T(8,128)} %get-tuple-element.27), channel_id=1, source_target_pairs={{0,4},{4,8},{8,12},{1,5},{5,9},{9,13},{2,6},{6,10},{10,14},{3,7},{... | collective-permute-start | bytes 1179656 | tf_op jit(solution)/shard_map/ppermute | solution.py:21
  62.6 10.0 %collective-permute-start.7 = (f32[1,64,12,128]{3,1,2,0:T(8,128)}, f32[1,64,12,128]{3,1,2,0:T(8,128)}, u32[]{:S(2)}, u32[]{:S(2)}) collective-permute-start(f32[1,64,12,128]{3,1,2,0:T(8,128)} %get-tuple-element.28), channel_id=1, source_target_pairs={{4,0},{8,4},{12,8},{5,1},{9,5},{13,9},{6,2},{10,6},{14,10},{7,3},{... | collective-permute-start | bytes 1179656 | tf_op jit(solution)/shard_map/ppermute | solution.py:23
  85.7 6.1 %copy-start.3 = (s32[2,1536]{1,0:T(2,128)S(1)}, s32[2,1536]{1,0:T(2,128)}, u32[]{:S(2)}) copy-start(s32[2,1536]{1,0:T(2,128)} %param.8) | copy-start | bytes 36868
  87.1 23.6 %all-to-all-start = ((bf16[4,2,64,1536]{3,2,1,0:T(8,128)(2,1)}), bf16[4,2,64,1536]{3,2,1,0:T(8,128)(2,1)S(1)}, u32[]{:S(2)}, u32[]{:S(2)}) async-start(bf16[4,2,64,1536]{3,2,1,0:T(8,128)(2,1)} %broadcast_select_fusion), calls=%async_computation | async-start | bytes 3145728 | tf_op jit(solution)/shard_map/all_to_all | solution.py:104
  110.7 1.0 copy-start.1
where the time goes:
time: 268 us
  other arithmetic  127 us (47%)
  waiting for transfers between devices  55.4 us (21%)
  local copies, waits for them, and re-layouts  29.6 us (11%)
  starting transfers between devices  24.2 us (9%)
  blocking collectives  22.5 us (8%)
  matrix products  8.33 us (3%)
    another operation x9, other arithmetic, fit_section(): lower_factor = lax.linalg.cholesky(gram_matrix)  66.8 us
    another operation x4, other arithmetic, fit_section(): lax.linalg.triangular_solve(lower_factor, halfway, left_side=True, lower=...  40.3 us
    all_to_all x1, blocking collectives, body(): lax.all_to_all(gradients[None], ('gy', 'af'), split_axis=2, concat_axis=0...  22.5 us
    ppermute x4, waiting for transfers between devices, padded_2(): lax.ppermute(tail, axis, [(i, (i + 1) % count) for i in range(ends)])  19 us
    all_to_all x1, waiting for transfers between devices, body(): lax.all_to_all(outgoing, ('gy', 'af'), split_axis=0, concat_axis=2, tiled...  18.9 us
    ppermute x4, waiting for transfers between devices, padded_2(): lax.ppermute(head, axis, [((i + 1) % count, i) for i in range(ends)])  17.6 us
    ppermute x4, starting transfers between devices, padded_2(): lax.ppermute(tail, axis, [(i, (i + 1) % count) for i in range(ends)])  15.3 us
    add x3, other arithmetic, advance(): return center - transport_term + rate_diffuse * diffusion_term  11.3 us
  transfers between devices with their start and end apart: 9, of which 9 were waited for; matrix products, arithmetic and copies ran while one was open for 1% of the time, Pallas kernels for 0%

commit v1 on v0

v1 whole, which is shorter than its diff:
```python
import functools

import jax
import jax.numpy as jnp
from jax import lax
from jax.experimental import pallas as pl
from jax.experimental.pallas import tpu as pltpu
from jax.sharding import PartitionSpec as P

TSTEPS = 4
RATE = 0.04
RIDGE = 0.25
LANES = 128
F32 = jnp.float32
BF16 = jnp.bfloat16
VEL_ROWS = 16
EASY = 1.08
FAIR = 3.8


def spec(memory_space):
    return pl.BlockSpec(memory_space=memory_space)


def params(mib):
    return pltpu.CompilerParams(vmem_limit_bytes=mib << 20)


def pack_kernel(width, chunks, atlas, vel, *refs):
    outs, (low_vel, high_vel, sems) = refs[: 2 * chunks], refs[2 * chunks :]
    rows = atlas.shape[0]
    copies = []
    for part in range(chunks):
        for side, first in ((0, 0), (1, rows - TSTEPS)):
            out = outs[2 * part + side]
            for step in range(TSTEPS):
                copies.append(
                    pltpu.make_async_copy(
                        atlas.at[first + step, :, pl.ds(part * width, width), :],
                        out.at[:, pl.ds(step * width, width), :],
                        sems.at[len(copies)],
                    )
                )
                copies[-1].start()
    ny = atlas.shape[1]
    slots = TSTEPS - 1
    for side, first, box in ((0, 0, low_vel), (1, rows - slots, high_vel)):
        parts = [vel[k, :, first : first + slots, :].astype(F32) for k in range(3)]
        parts.append(jnp.zeros((ny, VEL_ROWS - 3 * slots, LANES), F32))
        box[...] = jnp.concatenate(parts, axis=1).astype(BF16)
        copies.append(
            pltpu.make_async_copy(
                box, outs[side].at[:, pl.ds(TSTEPS * width, VEL_ROWS), :], sems.at[len(copies)]
            )
        )
        copies[-1].start()
    for copy in copies:
        copy.wait()


def pack(atlas, vel, width, chunks):
    ny = atlas.shape[1]
    shapes = []
    for part in range(chunks):
        rows = TSTEPS * width + (VEL_ROWS if part == 0 else 0)
        shapes += [jax.ShapeDtypeStruct((ny, rows, LANES), BF16)] * 2
    return pl.pallas_call(
        functools.partial(pack_kernel, width, chunks),
        out_shape=shapes,
        in_specs=[spec(pl.ANY), spec(pltpu.VMEM)],
        out_specs=[spec(pl.ANY)] * len(shapes),
        scratch_shapes=[
            pltpu.VMEM((ny, VEL_ROWS, LANES), BF16),
            pltpu.VMEM((ny, VEL_ROWS, LANES), BF16),
            pltpu.SemaphoreType.DMA((2 * chunks * TSTEPS + 2,)),
        ],
        compiler_params=params(8),
        name="pack_edges",
    )(atlas, vel)


def transport_kernel(peers, per, scalars, slots, atlas, vel, low, high, low_vel, high_vel, *refs):
    outs, (state, speed, coef) = refs[: peers * per], refs[peers * per :]
    rows, ny, width = atlas.shape[:3]
    deep = rows + 2 * TSTEPS
    edge = TSTEPS - 1
    has_low, has_high, me = scalars[0], scalars[1], scalars[2]

    for k in range(3):
        speed[k, :, TSTEPS : TSTEPS + rows, :] = vel[k].astype(F32)
        below = low_vel[...].astype(F32)[:, edge * k : edge * (k + 1), :]
        above = high_vel[...].astype(F32)[:, edge * k : edge * (k + 1), :]
        speed[k, :, 1:TSTEPS, :] = below
        speed[k, :, TSTEPS + rows : TSTEPS + rows + edge, :] = above
    place = lax.broadcasted_iota(jnp.int32, (1, deep, LANES), 1)
    lane = lax.broadcasted_iota(jnp.int32, (1, deep, LANES), 2)
    inside = ((place >= TSTEPS) | (has_low > 0)) & ((place < TSTEPS + rows) | (has_high > 0))
    inside = inside & (place > 0) & (place < deep - 1)
    for y in range(ny):
        total = jnp.zeros((1, deep, LANES), F32)
        for k in range(3):
            v = speed[k, y : y + 1]
            from_low = jnp.maximum(v, 0.0) + RATE
            from_high = RATE - jnp.minimum(v, 0.0)
            total = total + (from_low + from_high)
            if k == 2:
                from_low = jnp.where(lane == 0, 0.0, from_low)
                from_high = jnp.where(lane == LANES - 1, 0.0, from_high)
            coef[2 * k + 1, y : y + 1] = jnp.where(inside, from_low, 0.0)
            coef[2 * k + 2, y : y + 1] = jnp.where(inside, from_high, 0.0)
        coef[0, y : y + 1] = jnp.where(inside, 1.0 - total, 0.0)

    def load(z, carry):
        state[0, z + TSTEPS] = atlas[z].astype(F32)
        return carry

    lax.fori_loop(0, rows, load, 0)
    for step in range(TSTEPS):
        part = slice(step * width, (step + 1) * width)
        state[0, step] = low[:, part, :].astype(F32)
        state[0, step + TSTEPS + rows] = high[:, part, :].astype(F32)

    def advance(source, z, carry):
        target = 1 - source
        for y in range(ny):
            weight = [coef[i, y, pl.ds(z, 1), :] for i in range(7)]
            center = state[source, z, y]
            total = weight[0] * center
            total = total + weight[1] * state[source, z - 1, y]
            total = total + weight[2] * state[source, z + 1, y]
            if y > 0:
                total = total + weight[3] * state[source, z, y - 1]
            if y < ny - 1:
                total = total + weight[4] * state[source, z, y + 1]
            total = total + weight[5] * pltpu.roll(center, 1, axis=1)
            total = total + weight[6] * pltpu.roll(center, LANES - 1, axis=1)
            state[target, z, y] = total
        return carry

    for step in range(TSTEPS):
        lax.fori_loop(step + 1, deep - 1 - step, functools.partial(advance, step % 2), 0)

    for k in range(peers):
        for s in range(per):
            z = slots[(me ^ k) * per + s] + TSTEPS
            for y in range(ny):
                value = state[TSTEPS % 2, z, y].astype(BF16)
                outs[k * per + s][:, y * LANES : (y + 1) * LANES] = value


def transport(scalars, slots, atlas, vel, low, high, low0, high0, width, part, peers, per):
    rows, ny = atlas.shape[:2]
    deep = rows + 2 * TSTEPS
    pixels = ny * LANES
    halo = pl.BlockSpec((ny, TSTEPS * width, LANES), lambda i: (0, 0, 0))
    tail = pl.BlockSpec((ny, VEL_ROWS, LANES), lambda i: (0, TSTEPS * width // VEL_ROWS, 0))
    return pl.pallas_call(
        functools.partial(transport_kernel, peers, per),
        grid=(1,),
        out_shape=[jax.ShapeDtypeStruct((width, pixels), BF16)] * (peers * per),
        in_specs=[
            spec(pltpu.SMEM),
            spec(pltpu.SMEM),
            pl.BlockSpec((rows, ny, width, LANES), lambda i: (0, 0, part, 0)),
            pl.BlockSpec(vel.shape, lambda i: (0, 0, 0, 0)),
            halo,
            halo,
            tail,
            tail,
        ],
        out_specs=[pl.BlockSpec((width, pixels), lambda i: (0, 0))] * (peers * per),
        scratch_shapes=[
            pltpu.VMEM((2, deep, ny, width, LANES), F32),
            pltpu.VMEM((3, ny, deep, LANES), F32),
            pltpu.VMEM((7, ny, deep, LANES), F32),
        ],
        compiler_params=params(56),
        name="transport",
    )(scalars, slots, atlas, vel, low, high, low0, high0)


def dot(a, b):
    return jnp.dot(a, b, preferred_element_type=F32)


def dot_full(a, b):
    return jnp.dot(a, b, preferred_element_type=F32, precision=lax.Precision.HIGHEST)


def halves(value):
    high = value.astype(BF16)
    return high, (value - high.astype(F32)).astype(BF16)


def fit_kernel(parts, peers, mask, density, *refs):
    blocks = refs[: parts * peers]
    outs = refs[parts * peers : parts * peers + peers]
    panel, gram, right, inverse, answer = refs[parts * peers + peers :]
    width, pixels = blocks[0].shape
    channels = panel.shape[0]
    share = channels // peers
    ny = pixels // LANES
    for k in range(peers):
        for part in range(parts):
            first = k * share + part * width
            panel[first : first + width, :] = blocks[k * parts + part][...]
    valid = mask[0] > 0
    every = panel[...]
    maps = density[0]
    masked = jnp.where(valid, every, jnp.zeros_like(every))
    contract = (((1,), (1,)), ((), ()))
    row = lax.broadcasted_iota(jnp.int32, (channels, channels), 0)
    column = lax.broadcasted_iota(jnp.int32, (channels, channels), 1)
    same = row == column
    gram[...] = lax.dot_general(every, masked, contract, preferred_element_type=F32) * (
        1.0 / pixels
    ) + jnp.where(same, RIDGE, 0.0)
    right[...] = lax.dot_general(maps, masked, contract, preferred_element_type=F32) * (
        1.0 / pixels
    )
    sums = jnp.sum(jnp.abs(gram[...]), axis=0, keepdims=True)
    bound_row = jnp.max(sums, axis=1, keepdims=True)
    bound = jnp.max(sums)
    start = 2.0 / (RIDGE + bound_row)
    spread = (bound_row - RIDGE) / (bound_row + RIDGE)

    def narrowed(spread):
        square = spread * spread
        return square / (2.0 - square), 2.0 / (2.0 - square)

    def doubled(scale):
        low = inverse[...].astype(BF16)
        left = jnp.where(same, 1.0, 0.0) - dot(gram[...].astype(BF16), low)
        inverse[...] = scale * (inverse[...] + dot(low, left.astype(BF16)))

    def refined():
        high, rest = halves(answer[...])
        gram_high, gram_rest = halves(gram[...])
        product = dot(high, gram_high) + (dot(rest, gram_high) + dot(high, gram_rest))
        left = (right[...] - product).astype(BF16)
        answer[...] = answer[...] + dot(left, inverse[...].astype(BF16))

    @pl.when(bound <= FAIR)
    def _():
        spread1, scale1 = narrowed(spread)
        spread2, scale2 = narrowed(spread1)
        _, scale3 = narrowed(spread2)
        inverse[...] = scale1 * (
            jnp.where(same, 2.0 * start, 0.0) - (start * start) * gram[...]
        )
        doubled(scale2)

        @pl.when(bound > EASY)
        def _():
            doubled(scale3)

        answer[...] = dot(right[...].astype(BF16), inverse[...].astype(BF16))
        refined()
        refined()

        @pl.when(bound > EASY)
        def _():
            refined()

    @pl.when(bound > FAIR)
    def _():
        inverse[...] = jnp.where(same, start, 0.0)

        def step(spread):
            left = jnp.where(same, 2.0, 0.0) - dot_full(gram[...], inverse[...])
            inverse[...] = dot_full(inverse[...], left)
            return spread * spread

        lax.while_loop(lambda spread: spread > 1e-4, step, jnp.max(spread))
        answer[...] = dot_full(right[...], inverse[...])
        for _ in range(3):
            left = right[...] - dot_full(answer[...], gram[...])
            answer[...] = answer[...] + dot_full(left, inverse[...])

    coefficient_t = answer[...].astype(BF16)
    coefficient = answer[...].T.astype(BF16)
    fitted = dot(coefficient_t, panel[...])
    residual = (fitted - maps.astype(F32)).astype(BF16)
    pushed = dot(coefficient, residual)
    gradient = jnp.where(valid, 2.0 * pushed, 0.0).astype(BF16)
    for k in range(peers):
        for y in range(ny):
            outs[k][y] = gradient[k * share : (k + 1) * share, y * LANES : (y + 1) * LANES]


def fit(mask, density, section, blocks, parts, peers):
    width, pixels = blocks[0].shape
    channels = width * parts * peers
    classes = density.shape[1]
    ny = pixels // LANES
    whole = pl.BlockSpec((width, pixels), lambda i: (0, 0))
    out = (ny, channels // peers, LANES)
    return pl.pallas_call(
        functools.partial(fit_kernel, parts, peers),
        grid=(1,),
        out_shape=[jax.ShapeDtypeStruct(out, BF16)] * peers,
        in_specs=[
            pl.BlockSpec((1, 1, pixels), lambda i: (section, 0, 0)),
            pl.BlockSpec((1, classes, pixels), lambda i: (section, 0, 0)),
        ]
        + [whole] * len(blocks),
        out_specs=[pl.BlockSpec(out, lambda i: (0, 0, 0))] * peers,
        scratch_shapes=[
            pltpu.VMEM((channels, pixels), BF16),
            pltpu.VMEM((channels, channels), F32),
            pltpu.VMEM((classes, channels), F32),
            pltpu.VMEM((channels, channels), F32),
            pltpu.VMEM((classes, channels), F32),
        ],
        compiler_params=params(48),
        name="fit",
    )(mask, density, *blocks)


def place_kernel(peers, per, section, scalars, slots, *refs):
    blocks = refs[:peers]
    out, sems = refs[-2], refs[-1]
    me = scalars[2]
    copies = [
        pltpu.make_async_copy(
            blocks[k], out.at[slots[(me ^ k) * per + section]], sems.at[k]
        )
        for k in range(peers)
    ]
    for copy in copies:
        copy.start()
    for copy in copies:
        copy.wait()


def place(scalars, slots, blocks, earlier, rows, section, per):
    peers = len(blocks)
    extra = [] if earlier is None else [earlier]
    return pl.pallas_call(
        functools.partial(place_kernel, peers, per, section),
        out_shape=jax.ShapeDtypeStruct((rows,) + blocks[0].shape, BF16),
        in_specs=[spec(pltpu.SMEM)] * 2 + [spec(pl.ANY)] * (peers + len(extra)),
        out_specs=spec(pl.ANY),
        scratch_shapes=[pltpu.SemaphoreType.DMA((peers,))],
        input_output_aliases={2 + peers: 0} if extra else {},
        name="place",
    )(scalars, slots, *blocks, *extra)


def body(atlas_features, velocity, section_density, pixel_mask, section_slice):
    rows, channels = atlas_features.shape[:2]
    slabs = lax.axis_size("gz")
    slab = lax.axis_index("gz")
    peers = lax.axis_size(("gy", "af"))
    me = lax.axis_index(("gy", "af"))
    per = section_density.shape[0]
    chunks = 1
    width = channels // chunks

    atlas = jnp.transpose(atlas_features, (0, 2, 1, 3))
    vel = jnp.transpose(velocity, (0, 2, 1, 3))
    mask = pixel_mask.reshape(per, 1, -1)
    slots = section_slice - slab * rows
    scalars = jnp.stack([slab > 0, slab < slabs - 1, me]).astype(jnp.int32)

    edges = pack(atlas, vel, width, chunks)
    upward = [(i, i + 1) for i in range(slabs - 1)]
    downward = [(i + 1, i) for i in range(slabs - 1)]
    halos = []
    for part in range(chunks):
        low = lax.ppermute(edges[2 * part + 1], "gz", upward)
        high = lax.ppermute(edges[2 * part], "gz", downward)
        halos.append((low, high))

    def swap(block, k):
        if k == 0:
            return block
        return lax.ppermute(block, ("gy", "af"), [(i, i ^ k) for i in range(peers)])

    arrived = {}
    for part in range(chunks):
        moved = transport(
            scalars, slots, atlas, vel, *halos[part], *halos[0], width, part, peers, per
        )
        for s in range(per):
            for k in range(peers):
                arrived[s, k, part] = swap(moved[k * per + s], k)

    result = None
    for s in range(per):
        blocks = [arrived[s, k, part] for k in range(peers) for part in range(chunks)]
        gradients = fit(mask, section_density, s, blocks, chunks, peers)
        returned = [swap(gradients[k], k) for k in range(peers)]
        result = place(scalars, slots, returned, result, rows, s, per)
    return jnp.transpose(result, (0, 2, 1, 3))


def solution(mesh):
    return jax.shard_map(
        body,
        mesh=mesh,
        in_specs=(
            P(("groups", "gz"), ("gy", "af"), None, None),
            P(None, ("groups", "gz"), None, None),
            P(("groups", "gz", "gy", "af"), None, None),
            P(("groups", "gz", "gy", "af"), None),
            P(("groups", "gz")),
        ),
        out_specs=P(("groups", "gz"), ("gy", "af"), None, None),
        check_vma=False,
    )
```

time: 268 us -> 165 us (0.62)
  the two profiles are of different devices: /device:TPU:0 before, /device:TPU:23 now
where the time goes in v1:
time: 165 us; the launch traced here: 164 us
  Pallas kernels  108 us (65%)
  waiting for transfers between devices  33.2 us (20%)
  starting transfers between devices  15 us (9%)
  local copies, waits for them, and re-layouts  6.97 us (4%)
    pallas_call x2, Pallas kernels, place(): pl.pallas_call(functools.partial(place_kernel, peers, per, section), out_...  51.3 us
    pallas_call x2, Pallas kernels, fit(): pl.pallas_call(functools.partial(fit_kernel, parts, peers), grid=(1,), ou...  39.9 us
    pallas_call x1, Pallas kernels, transport(): pl.pallas_call(functools.partial(transport_kernel, peers, per), grid=(1,)...  16.1 us
    ppermute x12, waiting for transfers between devices, swap(): return lax.ppermute(block, ('gy', 'af'), [(i, i ^ k) for i in range(peers)])  15.4 us
    ppermute x1, waiting for transfers between devices, body(): low = lax.ppermute(edges[2 * part + 1], 'gz', upward)  15 us
    ppermute x12, starting transfers between devices, swap(): return lax.ppermute(block, ('gy', 'af'), [(i, i ^ k) for i in range(peers)])  9.76 us
    unnamed x34, local copies, waits for them, and re-layouts  6.96 us
  transfers between devices with their start and end apart: 14, of which 6 were waited for; matrix products, arithmetic and copies ran while one was open for 1% of the time, Pallas kernels for 40%

profile of v1, /device:TPU:23, one launch (start us, length us, event | category | flops | bytes accessed | tf_op | source)
XLA Modules:
  0.0 164.3 jit_solution(9754519399314023184)
XLA Ops:
  0.0 0.0 copy-start.16
  0.0 0.0 copy-start.1
  0.0 1.4 copy-done.1
  1.4 0.0 copy-start.2
  1.4 0.9 copy-done.2
  2.3 0.4 pack_edges.1
  2.7 3.2 %collective-permute-start = (bf16[12,272,128]{2,1,0:T(8,128)(2,1)S(1)}, bf16[12,272,128]{2,1,0:T(8,128)(2,1)S(1)}, u32[]{:S(2)}, u32[]{:S(2)}) collective-permute-start(bf16[12,272,128]{2,1,0:T(8,128)(2,1)S(1)} %get-tuple-element.23), channel_id=1, source_target_pairs={{0,4},{4,8},{8,12},{1,5},{5,9},{9,13},{2,6},{6,10},{10,14},{3,7},{... | collective-permute-start | bytes 2506760 | tf_op jit(solution)/shard_map/ppermute | solution.py:371
  5.9 2.1 %collective-permute-start.1 = (bf16[12,272,128]{2,1,0:T(8,128)(2,1)S(1)}, bf16[12,272,128]{2,1,0:T(8,128)(2,1)S(1)}, u32[]{:S(2)}, u32[]{:S(2)}) collective-permute-start(bf16[12,272,128]{2,1,0:T(8,128)(2,1)S(1)} %get-tuple-element.24), channel_id=1, source_target_pairs={{4,0},{8,4},{12,8},{5,1},{9,5},{13,9},{6,2},{10,6},{14,10},{7,3},{... | collective-permute-start | bytes 2506760 | tf_op jit(solution)/shard_map/ppermute | solution.py:372
  8.0 0.6 pad_add_fusion.scalars
  8.6 0.0 copy-done.16
  8.6 0.5 broadcast_subtract_fusion.slots
  9.1 0.0 copy-start.15
  9.1 0.0 copy-start
  9.1 15.0 %collective-permute-done.low.low_vel = bf16[12,272,128]{2,1,0:T(8,128)(2,1)S(1)} collective-permute-done((bf16[12,272,128]{2,1,0:T(8,128)(2,1)S(1)}, bf16[12,272,128]{2,1,0:T(8,128)(2,1)S(1)}, u32[]{:S(2)}, u32[]{:S(2)}) %collective-permute-start) | collective-permute-done | bytes 835616 | tf_op jit(solution)/shard_map/ppermute | solution.py:371
  24.1 0.0 copy-start.7
  24.1 2.9 %collective-permute-done.1.high.high_vel = bf16[12,272,128]{2,1,0:T(8,128)(2,1)S(1)} collective-permute-done((bf16[12,272,128]{2,1,0:T(8,128)(2,1)S(1)}, bf16[12,272,128]{2,1,0:T(8,128)(2,1)S(1)}, u32[]{:S(2)}, u32[]{:S(2)}) %collective-permute-start.1) | collective-permute-done | bytes 835616 | tf_op jit(solution)/shard_map/ppermute | solution.py:372
  26.9 0.0 copy-done.7
  27.0 0.9 copy-done.8
  27.9 16.1 %transport.1 = (bf16[64,1536]{1,0:T(8,128)(2,1)}, bf16[64,1536]{1,0:T(8,128)(2,1)}, bf16[64,1536]{1,0:T(8,128)(2,1)}, bf16[64,1536]{1,0:T(8,128)(2,1)}, bf16[64,...) custom-call(s32[3]{0:T(128)} %pad_add_fusion.scalars, ...), custom_call_target="tpu_custom_call" | custom-call | tf_op jit(solution)/shard_map/transport/pallas_call | solution.py:157
  43.9 1.9 %collective-permute-start.8 = (bf16[64,1536]{1,0:T(8,128)(2,1)}, bf16[64,1536]{1,0:T(8,128)(2,1)S(1)}, u32[]{:S(2)}, u32[]{:S(2)}) collective-permute-start(bf16[64,1536]{1,0:T(8,128)(2,1)} %get-tuple-element.34), channel_id=1, source_target_pairs={{0,1},{1,0},{2,3},{3,2},{4,5},{5,4},{6,7},{7,6},{8,9},{9,8},{10,11... | collective-permute-start | bytes 589832 | tf_op jit(solution)/shard_map/ppermute | solution.py:378
  45.8 0.3 collective-permute-start.9
  46.1 1.4 collective-permute-start.10
  47.5 0.2 collective-permute-start.2
  47.7 0.3 collective-permute-start.3
  48.0 0.0 collective-permute-done.8.refs_1_
  48.0 1.7 %collective-permute-start.4 = (bf16[64,1536]{1,0:T(8,128)(2,1)}, bf16[64,1536]{1,0:T(8,128)(2,1)S(1)}, u32[]{:S(2)}, u32[]{:S(2)}) collective-permute-start(bf16[64,1536]{1,0:T(8,128)(2,1)} %get-tuple-element.28), channel_id=1, source_target_pairs={{0,3},{1,2},{2,1},{3,0},{4,7},{5,6},{6,5},{7,4},{8,11},{9,10},{10,... | collective-permute-start | bytes 589832 | tf_op jit(solution)/shard_map/ppermute | solution.py:378
  49.7 0.0 copy-done.15
  49.7 2.8 %collective-permute-done.9.refs_2_ = bf16[64,1536]{1,0:T(8,128)(2,1)S(1)} collective-permute-done((bf16[64,1536]{1,0:T(8,128)(2,1)}, bf16[64,1536]{1,0:T(8,128)(2,1)S(1)}, u32[]{:S(2)}, u32[]{:S(2)}) %collective-permute-start.9) | collective-permute-done | bytes 196640 | tf_op jit(solution)/shard_map/ppermute | solution.py:378
  52.5 4.8 %collective-permute-done.10.refs_3_ = bf16[64,1536]{1,0:T(8,128)(2,1)S(1)} collective-permute-done((bf16[64,1536]{1,0:T(8,128)(2,1)}, bf16[64,1536]{1,0:T(8,128)(2,1)S(1)}, u32[]{:S(2)}, u32[]{:S(2)}) %collective-permute-start.10) | collective-permute-done | bytes 196640 | tf_op jit(solution)/shard_map/ppermute | solution.py:378
  57.3 0.0 copy-done
  57.3 0.9 copy-done.6
  58.3 19.8 %fit.3 = (bf16[12,64,128]{2,1,0:T(8,128)(2,1)S(1)}, bf16[12,64,128]{2,1,0:T(8,128)(2,1)S(1)}, bf16[12,64,128]{2,1,0:T(8,128)(2,1)S(1)}, bf16[12,64,128]{2,1,0:T(8,128)(2,1)S(1)}) custom-call(s32[2,1,1536]{2,1,0:T(1,128)S(1)} %reshape.3.mask, bf16[2,256,1536]{2,1,0:T(8,128)(2,1)S(1)} %copy-done, bf16[64,1536]{1,0:T(8,128)(2,1)S(1)} %copy-done.6, ...), custom_call_target="tpu_custom_call" | custom-call | tf_op jit(solution)/shard_map/fit/pallas_call | solution.py:298
  78.0 0.0 copy-start.5
  78.0 0.7 copy-done.5
  78.7 0.0 collective-permute-start.11
  78.7 0.0 collective-permute-done.2.refs_1_
  78.7 0.0 collective-permute-done.3.refs_2_
  78.7 0.0 collective-permute-done.4.refs_3_
  78.7 0.0 copy-done.4
  78.7 20.1 %fit.2 = (bf16[12,64,128]{2,1,0:T(8,128)(2,1)S(1)}, bf16[12,64,128]{2,1,0:T(8,128)(2,1)S(1)}, bf16[12,64,128]{2,1,0:T(8,128)(2,1)S(1)}, bf16[12,64,128]{2,1,0:T(8,128)(2,1)S(1)}) custom-call(s32[2,1,1536]{2,1,0:T(1,128)S(1)} %reshape.3.mask, bf16[2,256,1536]{2,1,0:T(8,128)(2,1)S(1)} %copy-done, bf16[64,1536]{1,0:T(8,128)(2,1)S(1)} %copy-done.4, ...), custom_call_target="tpu_custom_call" | custom-call | tf_op jit(solution)/shard_map/fit/pallas_call | solution.py:298
  98.9 0.0 copy-start.3
  98.9 0.7 copy-done.3
  99.6 0.5 collective-permute-start.5
  100.1 0.2 collective-permute-start.12
  100.3 1.4 collective-permute-start.13
  101.7 0.2 collective-permute-start.6
  102.0 0.0 collective-permute-done.11.refs_1_
  102.0 1.6 collective-permute-start.7
  103.6 3.0 %collective-permute-done.12.refs_2_ = bf16[12,64,128]{2,1,0:T(8,128)(2,1)S(1)} collective-permute-done((bf16[12,64,128]{2,1,0:T(8,128)(2,1)S(1)}, bf16[12,64,128]{2,1,0:T(8,128)(2,1)S(1)}, u32[]{:S(2)}, u32[]{:S(2)}) %collective-permute-start.12) | collective-permute-done | bytes 196640 | tf_op jit(solution)/shard_map/ppermute | solution.py:378
  106.6 4.7 %collective-permute-done.13.refs_3_ = bf16[12,64,128]{2,1,0:T(8,128)(2,1)S(1)} collective-permute-done((bf16[12,64,128]{2,1,0:T(8,128)(2,1)S(1)}, bf16[12,64,128]{2,1,0:T(8,128)(2,1)S(1)}, u32[]{:S(2)}, u32[]{:S(2)}) %collective-permute-start.13) | collective-permute-done | bytes 196640 | tf_op jit(solution)/shard_map/ppermute | solution.py:378
  111.3 0.0 copy-done.12
  111.3 0.0 copy-done.13
  111.3 0.7 copy-done.14
  112.0 25.6 %place.2.refs_4_ = bf16[8,12,64,128]{3,2,1,0:T(8,128)(2,1)} custom-call(s32[3]{0:T(128)} %pad_add_fusion.scalars, s32[8]{0:T(128)} %broadcast_subtract_fusion.slots, bf16[12,64,128]{2,1,0:T(8,128)(2,1)} %copy-done.5, bf16[12,64,128]{2,1,0:T(8,128)(2,1)} %copy-done.12, bf16[12,64,128]{2,1,0:T(8,128)(2,1)} %copy-done.13, bf16[12,64,128]{2,1,0:T(8,128)(2,1)} %copy-done.14), custom_call_target="tpu_custom_call" | custom-call | tf_op jit(solution)/shard_map/place/pallas_call | solution.py:339
  137.6 0.0 collective-permute-done.5.refs_1_
  137.7 0.0 copy-start.9
  137.7 0.0 collective-permute-done.6.refs_2_
  137.7 0.0 copy-start.10
  137.7 0.0 collective-permute-done.7.refs_3_
  137.7 0.0 copy-start.11
  137.7 0.6 copy-done.9
  138.3 0.1 copy-done.10
  138.4 0.1 copy-done.11
  138.5 25.6 %place.3 = bf16[8,12,64,128]{3,2,1,0:T(8,128)(2,1)} custom-call(s32[3]{0:T(128)} %pad_add_fusion.scalars, s32[8]{0:T(128)} %broadcast_subtract_fusion.slots, bf16[12,64,128]{2,1,0:T(8,128)(2,1)} %copy-done.3, bf16[12,64,128]{2,1,0:T(8,128)(2,1)} %copy-done.9, bf16[12,64,128]{2,1,0:T(8,128)(2,1)} %copy-done.10, ...), custom_call_target="tpu_custom_call", output_to_operand_aliasing={{}: (6, {})} | custom-call | tf_op jit(solution)/shard_map/place/pallas_call | solution.py:339
  (7 shorter events, 0.0 us)
Async XLA Ops:
  0.0 8.6 %copy-start.16 = (s32[8]{0:T(128)S(1)}, s32[8]{0:T(128)}, u32[]{:S(2)}) copy-start(s32[8]{0:T(128)} %param.9) | copy-start | bytes 100
  0.0 1.4 copy-start.1
  1.4 0.9 copy-start.2
  2.7 21.4 %collective-permute-start = (bf16[12,272,128]{2,1,0:T(8,128)(2,1)S(1)}, bf16[12,272,128]{2,1,0:T(8,128)(2,1)S(1)}, u32[]{:S(2)}, u32[]{:S(2)}) collective-permute-start(bf16[12,272,128]{2,1,0:T(8,128)(2,1)S(1)} %get-tuple-element.23), channel_id=1, source_target_pairs={{0,4},{4,8},{8,12},{1,5},{5,9},{9,13},{2,6},{6,10},{10,14},{3,7},{... | collective-permute-start | bytes 2506760 | tf_op jit(solution)/shard_map/ppermute | solution.py:371
  5.9 21.0 %collective-permute-start.1 = (bf16[12,272,128]{2,1,0:T(8,128)(2,1)S(1)}, bf16[12,272,128]{2,1,0:T(8,128)(2,1)S(1)}, u32[]{:S(2)}, u32[]{:S(2)}) collective-permute-start(bf16[12,272,128]{2,1,0:T(8,128)(2,1)S(1)} %get-tuple-element.24), channel_id=1, source_target_pairs={{4,0},{8,4},{12,8},{5,1},{9,5},{13,9},{6,2},{10,6},{14,10},{7,3},{... | collective-permute-start | bytes 2506760 | tf_op jit(solution)/shard_map/ppermute | solution.py:372
  9.1 40.6 %copy-start.15 = (s32[2,1536]{1,0:T(2,128)S(1)}, s32[2,1536]{1,0:T(2,128)}, u32[]{:S(2)}) copy-start(s32[2,1536]{1,0:T(2,128)} %param.8) | copy-start | bytes 36868
  9.1 48.2 %copy-start = (bf16[2,256,1536]{2,1,0:T(8,128)(2,1)S(1)}, bf16[2,256,1536]{2,1,0:T(8,128)(2,1)}, u32[]{:S(2)}) copy-start(bf16[2,256,1536]{2,1,0:T(8,128)(2,1)} %density.3) | copy-start | bytes 4718596
  24.1 2.9 %copy-start.7 = (bf16[12,272,128]{2,1,0:T(8,128)(2,1)}, bf16[12,272,128]{2,1,0:T(8,128)(2,1)S(1)}, u32[]{:S(2)}) copy-start(bf16[12,272,128]{2,1,0:T(8,128)(2,1)S(1)} %collective-permute-done.low.low_vel) | copy-start | bytes 2506756
  26.9 0.9 copy-start.8
  43.9 34.8 %copy-start.4 = (bf16[64,1536]{1,0:T(8,128)(2,1)S(1)}, bf16[64,1536]{1,0:T(8,128)(2,1)}, u32[]{:S(2)}) copy-start(bf16[64,1536]{1,0:T(8,128)(2,1)} %get-tuple-element.25.refs_0_) | copy-start | bytes 589828
  43.9 4.0 %collective-permute-start.8 = (bf16[64,1536]{1,0:T(8,128)(2,1)}, bf16[64,1536]{1,0:T(8,128)(2,1)S(1)}, u32[]{:S(2)}, u32[]{:S(2)}) collective-permute-start(bf16[64,1536]{1,0:T(8,128)(2,1)} %get-tuple-element.34), channel_id=1, source_target_pairs={{0,1},{1,0},{2,3},{3,2},{4,5},{5,4},{6,7},{7,6},{8,9},{9,8},{10,11... | collective-permute-start | bytes 589832 | tf_op jit(solution)/shard_map/ppermute | solution.py:378
  45.8 6.7 %collective-permute-start.9 = (bf16[64,1536]{1,0:T(8,128)(2,1)}, bf16[64,1536]{1,0:T(8,128)(2,1)S(1)}, u32[]{:S(2)}, u32[]{:S(2)}) collective-permute-start(bf16[64,1536]{1,0:T(8,128)(2,1)} %get-tuple-element.35), channel_id=1, source_target_pairs={{0,2},{1,3},{2,0},{3,1},{4,6},{5,7},{6,4},{7,5},{8,10},{9,11},{10,... | collective-permute-start | bytes 589832 | tf_op jit(solution)/shard_map/ppermute | solution.py:378
  46.1 11.2 %collective-permute-start.10 = (bf16[64,1536]{1,0:T(8,128)(2,1)}, bf16[64,1536]{1,0:T(8,128)(2,1)S(1)}, u32[]{:S(2)}, u32[]{:S(2)}) collective-permute-start(bf16[64,1536]{1,0:T(8,128)(2,1)} %get-tuple-element.36), channel_id=1, source_target_pairs={{0,3},{1,2},{2,1},{3,0},{4,7},{5,6},{6,5},{7,4},{8,11},{9,10},{10,... | collective-permute-start | bytes 589832 | tf_op jit(solution)/shard_map/ppermute | solution.py:378
  47.5 31.2 %collective-permute-start.2 = (bf16[64,1536]{1,0:T(8,128)(2,1)}, bf16[64,1536]{1,0:T(8,128)(2,1)S(1)}, u32[]{:S(2)}, u32[]{:S(2)}) collective-permute-start(bf16[64,1536]{1,0:T(8,128)(2,1)} %get-tuple-element.26), channel_id=1, source_target_pairs={{0,1},{1,0},{2,3},{3,2},{4,5},{5,4},{6,7},{7,6},{8,9},{9,8},{10,11... | collective-permute-start | bytes 589832 | tf_op jit(solution)/shard_map/ppermute | solution.py:378
  47.7 31.0 %collective-permute-start.3 = (bf16[64,1536]{1,0:T(8,128)(2,1)}, bf16[64,1536]{1,0:T(8,128)(2,1)S(1)}, u32[]{:S(2)}, u32[]{:S(2)}) collective-permute-start(bf16[64,1536]{1,0:T(8,128)(2,1)} %get-tuple-element.27), channel_id=1, source_target_pairs={{0,2},{1,3},{2,0},{3,1},{4,6},{5,7},{6,4},{7,5},{8,10},{9,11},{10,... | collective-permute-start | bytes 589832 | tf_op jit(solution)/shard_map/ppermute | solution.py:378
  48.0 30.8 %collective-permute-start.4 = (bf16[64,1536]{1,0:T(8,128)(2,1)}, bf16[64,1536]{1,0:T(8,128)(2,1)S(1)}, u32[]{:S(2)}, u32[]{:S(2)}) collective-permute-start(bf16[64,1536]{1,0:T(8,128)(2,1)} %get-tuple-element.28), channel_id=1, source_target_pairs={{0,3},{1,2},{2,1},{3,0},{4,7},{5,6},{6,5},{7,4},{8,11},{9,10},{10,... | collective-permute-start | bytes 589832 | tf_op jit(solution)/shard_map/ppermute | solution.py:378
  57.3 0.9 copy-start.6
  78.0 0.7 copy-start.5
  78.7 23.3 %collective-permute-start.11 = (bf16[12,64,128]{2,1,0:T(8,128)(2,1)S(1)}, bf16[12,64,128]{2,1,0:T(8,128)(2,1)S(1)}, u32[]{:S(2)}, u32[]{:S(2)}) collective-permute-start(bf16[12,64,128]{2,1,0:T(8,128)(2,1)S(1)} %get-tuple-element.38), channel_id=1, source_target_pairs={{0,1},{1,0},{2,3},{3,2},{4,5},{5,4},{6,7},{7,6},{8,9},{9,8},{10,11... | collective-permute-start | bytes 589832 | tf_op jit(solution)/shard_map/ppermute | solution.py:378
  98.9 0.7 copy-start.3
  99.6 38.1 %collective-permute-start.5 = (bf16[12,64,128]{2,1,0:T(8,128)(2,1)S(1)}, bf16[12,64,128]{2,1,0:T(8,128)(2,1)S(1)}, u32[]{:S(2)}, u32[]{:S(2)}) collective-permute-start(bf16[12,64,128]{2,1,0:T(8,128)(2,1)S(1)} %get-tuple-element.30), channel_id=1, source_target_pairs={{0,1},{1,0},{2,3},{3,2},{4,5},{5,4},{6,7},{7,6},{8,9},{9,8},{10,11... | collective-permute-start | bytes 589832 | tf_op jit(solution)/shard_map/ppermute | solution.py:378
  100.1 6.5 %collective-permute-start.12 = (bf16[12,64,128]{2,1,0:T(8,128)(2,1)S(1)}, bf16[12,64,128]{2,1,0:T(8,128)(2,1)S(1)}, u32[]{:S(2)}, u32[]{:S(2)}) collective-permute-start(bf16[12,64,128]{2,1,0:T(8,128)(2,1)S(1)} %get-tuple-element.39), channel_id=1, source_target_pairs={{0,2},{1,3},{2,0},{3,1},{4,6},{5,7},{6,4},{7,5},{8,10},{9,11},{10,... | collective-permute-start | bytes 589832 | tf_op jit(solution)/shard_map/ppermute | solution.py:378
  100.3 11.0 %collective-permute-start.13 = (bf16[12,64,128]{2,1,0:T(8,128)(2,1)S(1)}, bf16[12,64,128]{2,1,0:T(8,128)(2,1)S(1)}, u32[]{:S(2)}, u32[]{:S(2)}) collective-permute-start(bf16[12,64,128]{2,1,0:T(8,128)(2,1)S(1)} %get-tuple-element.40), channel_id=1, source_target_pairs={{0,3},{1,2},{2,1},{3,0},{4,7},{5,6},{6,5},{7,4},{8,11},{9,10},{10,... | collective-permute-start | bytes 589832 | tf_op jit(solution)/shard_map/ppermute | solution.py:378
  101.7 35.9 %collective-permute-start.6 = (bf16[12,64,128]{2,1,0:T(8,128)(2,1)S(1)}, bf16[12,64,128]{2,1,0:T(8,128)(2,1)S(1)}, u32[]{:S(2)}, u32[]{:S(2)}) collective-permute-start(bf16[12,64,128]{2,1,0:T(8,128)(2,1)S(1)} %get-tuple-element.31), channel_id=1, source_target_pairs={{0,2},{1,3},{2,0},{3,1},{4,6},{5,7},{6,4},{7,5},{8,10},{9,11},{10,... | collective-permute-start | bytes 589832 | tf_op jit(solution)/shard_map/ppermute | solution.py:378
  102.0 9.3 %copy-start.12 = (bf16[12,64,128]{2,1,0:T(8,128)(2,1)}, bf16[12,64,128]{2,1,0:T(8,128)(2,1)S(1)}, u32[]{:S(2)}) copy-start(bf16[12,64,128]{2,1,0:T(8,128)(2,1)S(1)} %collective-permute-done.11.refs_1_) | copy-start | bytes 589828
  102.0 35.7 %collective-permute-start.7 = (bf16[12,64,128]{2,1,0:T(8,128)(2,1)S(1)}, bf16[12,64,128]{2,1,0:T(8,128)(2,1)S(1)}, u32[]{:S(2)}, u32[]{:S(2)}) collective-permute-start(bf16[12,64,128]{2,1,0:T(8,128)(2,1)S(1)} %get-tuple-element.32), channel_id=1, source_target_pairs={{0,3},{1,2},{2,1},{3,0},{4,7},{5,6},{6,5},{7,4},{8,11},{9,10},{10,... | collective-permute-start | bytes 589832 | tf_op jit(solution)/shard_map/ppermute | solution.py:378
  106.6 4.7 %copy-start.13 = (bf16[12,64,128]{2,1,0:T(8,128)(2,1)}, bf16[12,64,128]{2,1,0:T(8,128)(2,1)S(1)}, u32[]{:S(2)}) copy-start(bf16[12,64,128]{2,1,0:T(8,128)(2,1)S(1)} %collective-permute-done.12.refs_2_) | copy-start | bytes 589828
  111.3 0.7 copy-start.14
  137.7 0.7 copy-start.9
  137.7 0.7 copy-start.10
  137.7 0.8 copy-start.11

commit v2 on v1

--- a/solution.py
+++ b/solution.py
@@ -67,7 +67,7 @@
     return pl.pallas_call(
         functools.partial(pack_kernel, width, chunks),
         out_shape=shapes,
-        in_specs=[spec(pl.ANY), spec(pltpu.VMEM)],
+        in_specs=[spec(pltpu.HBM), spec(pltpu.VMEM)],
         out_specs=[spec(pl.ANY)] * len(shapes),
         scratch_shapes=[
             pltpu.VMEM((ny, VEL_ROWS, LANES), BF16),
@@ -339,10 +339,13 @@
     return pl.pallas_call(
         functools.partial(place_kernel, peers, per, section),
         out_shape=jax.ShapeDtypeStruct((rows,) + blocks[0].shape, BF16),
-        in_specs=[spec(pltpu.SMEM)] * 2 + [spec(pl.ANY)] * (peers + len(extra)),
+        in_specs=[spec(pltpu.SMEM)] * 2
+        + [spec(pltpu.VMEM)] * peers
+        + [spec(pl.ANY)] * len(extra),
         out_specs=spec(pl.ANY),
         scratch_shapes=[pltpu.SemaphoreType.DMA((peers,))],
         input_output_aliases={2 + peers: 0} if extra else {},
+        compiler_params=params(16),
         name="place",
     )(scalars, slots, *blocks, *extra)
 

time: 165 us -> 121 us (0.73)
  Pallas kernels: 108 us -> 58.2 us
  waiting for transfers between devices: 33.2 us -> 39.7 us
  local copies, waits for them, and re-layouts: 6.97 us -> 4.19 us
    pallas_call x2, Pallas kernels: 51.3 us -> 2.91 us  [place(): pl.pallas_call(functools.partial(place_kernel, peers, per, section), out_...]
    ppermute x12, waiting for transfers between devices: 15.4 us -> 21.9 us  [swap(): return lax.ppermute(block, ('gy', 'af'), [(i, i ^ k) for i in range(peers)])]
    unnamed x34 -> x22, local copies, waits for them, and re-layouts: 6.96 us -> 4.18 us
  transfers between devices with their start and end apart: 14 -> 14, of which waited for: 6 -> 8; matrix products, arithmetic and copies ran while one was open for 1% -> 1% of each run, Pallas kernels for 40% -> 34%
where the time goes in v2:
time: 121 us; the launch traced here: 119 us
  Pallas kernels  58.2 us (48%)
  waiting for transfers between devices  39.7 us (33%)
  starting transfers between devices  15.6 us (13%)
  local copies, waits for them, and re-layouts  4.19 us (3%)
    pallas_call x2, Pallas kernels, fit(): pl.pallas_call(functools.partial(fit_kernel, parts, peers), grid=(1,), ou...  38.8 us
    ppermute x12, waiting for transfers between devices, swap(): return lax.ppermute(block, ('gy', 'af'), [(i, i ^ k) for i in range(peers)])  21.9 us
    pallas_call x1, Pallas kernels, transport(): pl.pallas_call(functools.partial(transport_kernel, peers, per), grid=(1,)...  16.1 us
    ppermute x1, waiting for transfers between devices, body(): low = lax.ppermute(edges[2 * part + 1], 'gz', upward)  14.9 us
    ppermute x12, starting transfers between devices, swap(): return lax.ppermute(block, ('gy', 'af'), [(i, i ^ k) for i in range(peers)])  10.3 us
    unnamed x22, local copies, waits for them, and re-layouts  4.18 us
    ppermute x1, starting transfers between devices, body(): low = lax.ppermute(edges[2 * part + 1], 'gz', upward)  3.2 us
    pallas_call x2, Pallas kernels, place(): pl.pallas_call(functools.partial(place_kernel, peers, per, section), out_...  2.91 us
  transfers between devices with their start and end apart: 14, of which 8 were waited for; matrix products, arithmetic and copies ran while one was open for 1% of the time, Pallas kernels for 34%

profile of v2, /device:TPU:23, one launch (start us, length us, event | category | flops | bytes accessed | tf_op | source)
XLA Modules:
  0.0 119.2 jit_solution(11454199968608765764)
XLA Ops:
  0.0 0.0 copy-start.10
  0.0 0.0 copy-start.1
  0.0 1.4 %copy-done.1 = bf16[8,64,12,128]{3,1,2,0:T(8,128)(2,1)S(1)} copy-done((bf16[8,64,12,128]{3,1,2,0:T(8,128)(2,1)S(1)}, bf16[8,64,12,128]{3,1,2,0:T(8,128)(2,1)}, u32[]{:S(2)}) %copy-start.1) | copy-done | bytes 1572888
  1.4 0.0 copy-start.2
  1.4 0.9 copy-done.2
  2.3 0.4 pack_edges.1
  2.7 3.2 %collective-permute-start = (bf16[12,272,128]{2,1,0:T(8,128)(2,1)S(1)}, bf16[12,272,128]{2,1,0:T(8,128)(2,1)S(1)}, u32[]{:S(2)}, u32[]{:S(2)}) collective-permute-start(bf16[12,272,128]{2,1,0:T(8,128)(2,1)S(1)} %get-tuple-element.23), channel_id=1, source_target_pairs={{0,4},{4,8},{8,12},{1,5},{5,9},{9,13},{2,6},{6,10},{10,14},{3,7},{... | collective-permute-start | bytes 2506760 | tf_op jit(solution)/shard_map/ppermute | solution.py:374
  5.9 2.1 %collective-permute-start.1 = (bf16[12,272,128]{2,1,0:T(8,128)(2,1)S(1)}, bf16[12,272,128]{2,1,0:T(8,128)(2,1)S(1)}, u32[]{:S(2)}, u32[]{:S(2)}) collective-permute-start(bf16[12,272,128]{2,1,0:T(8,128)(2,1)S(1)} %get-tuple-element.24), channel_id=1, source_target_pairs={{4,0},{8,4},{12,8},{5,1},{9,5},{13,9},{6,2},{10,6},{14,10},{7,3},{... | collective-permute-start | bytes 2506760 | tf_op jit(solution)/shard_map/ppermute | solution.py:375
  8.0 0.7 pad_add_fusion.scalars
  8.7 0.0 copy-done.10
  8.7 0.5 broadcast_subtract_fusion.slots
  9.2 0.0 copy-start.9
  9.2 0.0 copy-start
  9.2 14.9 %collective-permute-done.low.low_vel = bf16[12,272,128]{2,1,0:T(8,128)(2,1)S(1)} collective-permute-done((bf16[12,272,128]{2,1,0:T(8,128)(2,1)S(1)}, bf16[12,272,128]{2,1,0:T(8,128)(2,1)S(1)}, u32[]{:S(2)}, u32[]{:S(2)}) %collective-permute-start) | collective-permute-done | bytes 835616 | tf_op jit(solution)/shard_map/ppermute | solution.py:374
  24.1 0.0 copy-start.7
  24.1 2.9 %collective-permute-done.1.high.high_vel = bf16[12,272,128]{2,1,0:T(8,128)(2,1)S(1)} collective-permute-done((bf16[12,272,128]{2,1,0:T(8,128)(2,1)S(1)}, bf16[12,272,128]{2,1,0:T(8,128)(2,1)S(1)}, u32[]{:S(2)}, u32[]{:S(2)}) %collective-permute-start.1) | collective-permute-done | bytes 835616 | tf_op jit(solution)/shard_map/ppermute | solution.py:375
  26.9 0.0 copy-done.7
  26.9 0.0 copy-start.8
  27.0 0.9 copy-done.8
  27.9 16.1 %transport.1 = (bf16[64,1536]{1,0:T(8,128)(2,1)}, bf16[64,1536]{1,0:T(8,128)(2,1)}, bf16[64,1536]{1,0:T(8,128)(2,1)}, bf16[64,1536]{1,0:T(8,128)(2,1)}, bf16[64,...) custom-call(s32[3]{0:T(128)} %pad_add_fusion.scalars, ...), custom_call_target="tpu_custom_call" | custom-call | tf_op jit(solution)/shard_map/transport/pallas_call | solution.py:157
  43.9 0.0 copy-start.3
  43.9 1.9 %collective-permute-start.8 = (bf16[64,1536]{1,0:T(8,128)(2,1)}, bf16[64,1536]{1,0:T(8,128)(2,1)S(1)}, u32[]{:S(2)}, u32[]{:S(2)}) collective-permute-start(bf16[64,1536]{1,0:T(8,128)(2,1)} %get-tuple-element.34), channel_id=1, source_target_pairs={{0,1},{1,0},{2,3},{3,2},{4,5},{5,4},{6,7},{7,6},{8,9},{9,8},{10,11... | collective-permute-start | bytes 589832 | tf_op jit(solution)/shard_map/ppermute | solution.py:381
  45.9 0.3 collective-permute-start.9
  46.1 1.4 %collective-permute-start.10 = (bf16[64,1536]{1,0:T(8,128)(2,1)}, bf16[64,1536]{1,0:T(8,128)(2,1)S(1)}, u32[]{:S(2)}, u32[]{:S(2)}) collective-permute-start(bf16[64,1536]{1,0:T(8,128)(2,1)} %get-tuple-element.36), channel_id=1, source_target_pairs={{0,3},{1,2},{2,1},{3,0},{4,7},{5,6},{6,5},{7,4},{8,11},{9,10},{10,... | collective-permute-start | bytes 589832 | tf_op jit(solution)/shard_map/ppermute | solution.py:381
  47.6 0.2 collective-permute-start.2
  47.7 0.3 collective-permute-start.3
  48.0 0.0 collective-permute-done.8.refs_1_
  48.0 1.7 %collective-permute-start.4 = (bf16[64,1536]{1,0:T(8,128)(2,1)}, bf16[64,1536]{1,0:T(8,128)(2,1)S(1)}, u32[]{:S(2)}, u32[]{:S(2)}) collective-permute-start(bf16[64,1536]{1,0:T(8,128)(2,1)} %get-tuple-element.28), channel_id=1, source_target_pairs={{0,3},{1,2},{2,1},{3,0},{4,7},{5,6},{6,5},{7,4},{8,11},{9,10},{10,... | collective-permute-start | bytes 589832 | tf_op jit(solution)/shard_map/ppermute | solution.py:381
  49.7 0.0 copy-done.9
  49.7 2.8 %collective-permute-done.9.refs_2_ = bf16[64,1536]{1,0:T(8,128)(2,1)S(1)} collective-permute-done((bf16[64,1536]{1,0:T(8,128)(2,1)}, bf16[64,1536]{1,0:T(8,128)(2,1)S(1)}, u32[]{:S(2)}, u32[]{:S(2)}) %collective-permute-start.9) | collective-permute-done | bytes 196640 | tf_op jit(solution)/shard_map/ppermute | solution.py:381
  52.6 4.8 %collective-permute-done.10.refs_3_ = bf16[64,1536]{1,0:T(8,128)(2,1)S(1)} collective-permute-done((bf16[64,1536]{1,0:T(8,128)(2,1)}, bf16[64,1536]{1,0:T(8,128)(2,1)S(1)}, u32[]{:S(2)}, u32[]{:S(2)}) %collective-permute-start.10) | collective-permute-done | bytes 196640 | tf_op jit(solution)/shard_map/ppermute | solution.py:381
  57.4 0.0 copy-done
  57.4 0.0 copy-start.4
  57.4 0.9 copy-done.4
  58.3 18.7 %fit.3 = (bf16[12,64,128]{2,1,0:T(8,128)(2,1)S(1)}, bf16[12,64,128]{2,1,0:T(8,128)(2,1)S(1)}, bf16[12,64,128]{2,1,0:T(8,128)(2,1)S(1)}, bf16[12,64,128]{2,1,0:T(8,128)(2,1)S(1)}) custom-call(s32[2,1,1536]{2,1,0:T(1,128)S(1)} %reshape.3.mask, bf16[2,256,1536]{2,1,0:T(8,128)(2,1)S(1)} %copy-done, bf16[64,1536]{1,0:T(8,128)(2,1)S(1)} %copy-done.4, ...), custom_call_target="tpu_custom_call" | custom-call | tf_op jit(solution)/shard_map/fit/pallas_call | solution.py:298
  77.0 0.0 copy-start.5
  77.0 0.0 copy-start.6
  77.0 0.9 collective-permute-start.11
  77.9 0.0 collective-permute-done.2.refs_1_
  77.9 0.0 collective-permute-done.3.refs_2_
  77.9 0.0 collective-permute-done.4.refs_3_
  78.0 0.0 copy-done.3
  78.0 20.2 %fit.2 = (bf16[12,64,128]{2,1,0:T(8,128)(2,1)S(1)}, bf16[12,64,128]{2,1,0:T(8,128)(2,1)S(1)}, bf16[12,64,128]{2,1,0:T(8,128)(2,1)S(1)}, bf16[12,64,128]{2,1,0:T(8,128)(2,1)S(1)}) custom-call(s32[2,1,1536]{2,1,0:T(1,128)S(1)} %reshape.3.mask, bf16[2,256,1536]{2,1,0:T(8,128)(2,1)S(1)} %copy-done, bf16[64,1536]{1,0:T(8,128)(2,1)S(1)} %copy-done.3, ...), custom_call_target="tpu_custom_call" | custom-call | tf_op jit(solution)/shard_map/fit/pallas_call | solution.py:298
  98.1 0.1 collective-permute-start.5
  98.2 0.1 collective-permute-start.12
  98.3 2.0 %collective-permute-start.13 = (bf16[12,64,128]{2,1,0:T(8,128)(2,1)S(1)}, bf16[12,64,128]{2,1,0:T(8,128)(2,1)S(1)}, u32[]{:S(2)}, u32[]{:S(2)}) collective-permute-start(bf16[12,64,128]{2,1,0:T(8,128)(2,1)S(1)} %get-tuple-element.40), channel_id=1, source_target_pairs={{0,3},{1,2},{2,1},{3,0},{4,7},{5,6},{6,5},{7,4},{8,11},{9,10},{10,... | collective-permute-start | bytes 589832 | tf_op jit(solution)/shard_map/ppermute | solution.py:381
  100.3 0.0 collective-permute-start.6
  100.3 0.0 collective-permute-done.11.refs_1_
  100.3 1.4 %collective-permute-start.7 = (bf16[12,64,128]{2,1,0:T(8,128)(2,1)S(1)}, bf16[12,64,128]{2,1,0:T(8,128)(2,1)S(1)}, u32[]{:S(2)}, u32[]{:S(2)}) collective-permute-start(bf16[12,64,128]{2,1,0:T(8,128)(2,1)S(1)} %get-tuple-element.32), channel_id=1, source_target_pairs={{0,3},{1,2},{2,1},{3,0},{4,7},{5,6},{6,5},{7,4},{8,11},{9,10},{10,... | collective-permute-start | bytes 589832 | tf_op jit(solution)/shard_map/ppermute | solution.py:381
  101.8 2.5 %collective-permute-done.12.refs_2_ = bf16[12,64,128]{2,1,0:T(8,128)(2,1)S(1)} collective-permute-done((bf16[12,64,128]{2,1,0:T(8,128)(2,1)S(1)}, bf16[12,64,128]{2,1,0:T(8,128)(2,1)S(1)}, u32[]{:S(2)}, u32[]{:S(2)}) %collective-permute-start.12) | collective-permute-done | bytes 196640 | tf_op jit(solution)/shard_map/ppermute | solution.py:381
  104.3 5.7 %collective-permute-done.13.refs_3_ = bf16[12,64,128]{2,1,0:T(8,128)(2,1)S(1)} collective-permute-done((bf16[12,64,128]{2,1,0:T(8,128)(2,1)S(1)}, bf16[12,64,128]{2,1,0:T(8,128)(2,1)S(1)}, u32[]{:S(2)}, u32[]{:S(2)}) %collective-permute-start.13) | collective-permute-done | bytes 196640 | tf_op jit(solution)/shard_map/ppermute | solution.py:381
  110.0 0.0 copy-done.5
  110.0 0.0 copy-done.6
  110.0 1.5 %place.2.refs_4_ = bf16[8,12,64,128]{3,2,1,0:T(8,128)(2,1)} custom-call(s32[3]{0:T(128)S(1)} %copy-done.5, s32[8]{0:T(128)S(1)} %copy-done.6, bf16[12,64,128]{2,1,0:T(8,128)(2,1)S(1)} %get-tuple-element.37.refs_0_, bf16[12,64,128]{2,1,0:T(8,128)(2,1)S(1)} %collective-permute-done.11.refs_1_, bf16[12,64,128]{2,1,0:T(8,128)(2,1)S(1)} %collective-permute-done.12.refs_2_, ...), custom_call_target="tpu_custom_call" | custom-call | tf_op jit(solution)/shard_map/place/pallas_call | solution.py:339
  111.5 0.0 collective-permute-done.5.refs_1_
  111.5 1.3 %collective-permute-done.6.refs_2_ = bf16[12,64,128]{2,1,0:T(8,128)(2,1)S(1)} collective-permute-done((bf16[12,64,128]{2,1,0:T(8,128)(2,1)S(1)}, bf16[12,64,128]{2,1,0:T(8,128)(2,1)S(1)}, u32[]{:S(2)}, u32[]{:S(2)}) %collective-permute-start.6) | collective-permute-done | bytes 196640 | tf_op jit(solution)/shard_map/ppermute | solution.py:381
  112.7 4.8 %collective-permute-done.7.refs_3_ = bf16[12,64,128]{2,1,0:T(8,128)(2,1)S(1)} collective-permute-done((bf16[12,64,128]{2,1,0:T(8,128)(2,1)S(1)}, bf16[12,64,128]{2,1,0:T(8,128)(2,1)S(1)}, u32[]{:S(2)}, u32[]{:S(2)}) %collective-permute-start.7) | collective-permute-done | bytes 196640 | tf_op jit(solution)/shard_map/ppermute | solution.py:381
  117.5 1.5 %place.3 = bf16[8,12,64,128]{3,2,1,0:T(8,128)(2,1)} custom-call(s32[3]{0:T(128)S(1)} %copy-done.5, s32[8]{0:T(128)S(1)} %copy-done.6, bf16[12,64,128]{2,1,0:T(8,128)(2,1)S(1)} %get-tuple-element.29.refs_0_, bf16[12,64,128]{2,1,0:T(8,128)(2,1)S(1)} %collective-permute-done.5.refs_1_, ...), custom_call_target="tpu_custom_call", output_to_operand_aliasing={{}: (6, {})} | custom-call | tf_op jit(solution)/shard_map/place/pallas_call | solution.py:339
  (1 shorter events, 0.0 us)
Async XLA Ops:
  0.0 8.7 %copy-start.10 = (s32[8]{0:T(128)S(1)}, s32[8]{0:T(128)}, u32[]{:S(2)}) copy-start(s32[8]{0:T(128)} %param.9) | copy-start | bytes 100
  0.0 1.4 %copy-start.1 = (bf16[8,64,12,128]{3,1,2,0:T(8,128)(2,1)S(1)}, bf16[8,64,12,128]{3,1,2,0:T(8,128)(2,1)}, u32[]{:S(2)}) copy-start(bf16[8,64,12,128]{3,1,2,0:T(8,128)(2,1)} %param.5) | copy-start | bytes 4718596
  1.4 0.9 copy-start.2
  2.7 21.4 %collective-permute-start = (bf16[12,272,128]{2,1,0:T(8,128)(2,1)S(1)}, bf16[12,272,128]{2,1,0:T(8,128)(2,1)S(1)}, u32[]{:S(2)}, u32[]{:S(2)}) collective-permute-start(bf16[12,272,128]{2,1,0:T(8,128)(2,1)S(1)} %get-tuple-element.23), channel_id=1, source_target_pairs={{0,4},{4,8},{8,12},{1,5},{5,9},{9,13},{2,6},{6,10},{10,14},{3,7},{... | collective-permute-start | bytes 2506760 | tf_op jit(solution)/shard_map/ppermute | solution.py:374
  5.9 21.0 %collective-permute-start.1 = (bf16[12,272,128]{2,1,0:T(8,128)(2,1)S(1)}, bf16[12,272,128]{2,1,0:T(8,128)(2,1)S(1)}, u32[]{:S(2)}, u32[]{:S(2)}) collective-permute-start(bf16[12,272,128]{2,1,0:T(8,128)(2,1)S(1)} %get-tuple-element.24), channel_id=1, source_target_pairs={{4,0},{8,4},{12,8},{5,1},{9,5},{13,9},{6,2},{10,6},{14,10},{7,3},{... | collective-permute-start | bytes 2506760 | tf_op jit(solution)/shard_map/ppermute | solution.py:375
  9.2 40.5 %copy-start.9 = (s32[2,1536]{1,0:T(2,128)S(1)}, s32[2,1536]{1,0:T(2,128)}, u32[]{:S(2)}) copy-start(s32[2,1536]{1,0:T(2,128)} %param.8) | copy-start | bytes 36868
  9.2 48.2 %copy-start = (bf16[2,256,1536]{2,1,0:T(8,128)(2,1)S(1)}, bf16[2,256,1536]{2,1,0:T(8,128)(2,1)}, u32[]{:S(2)}) copy-start(bf16[2,256,1536]{2,1,0:T(8,128)(2,1)} %density.3) | copy-start | bytes 4718596
  24.1 2.9 %copy-start.7 = (bf16[12,272,128]{2,1,0:T(8,128)(2,1)}, bf16[12,272,128]{2,1,0:T(8,128)(2,1)S(1)}, u32[]{:S(2)}) copy-start(bf16[12,272,128]{2,1,0:T(8,128)(2,1)S(1)} %collective-permute-done.low.low_vel) | copy-start | bytes 2506756
  26.9 0.9 copy-start.8
  43.9 34.0 %copy-start.3 = (bf16[64,1536]{1,0:T(8,128)(2,1)S(1)}, bf16[64,1536]{1,0:T(8,128)(2,1)}, u32[]{:S(2)}) copy-start(bf16[64,1536]{1,0:T(8,128)(2,1)} %get-tuple-element.25.refs_0_) | copy-start | bytes 589828
  43.9 4.0 %collective-permute-start.8 = (bf16[64,1536]{1,0:T(8,128)(2,1)}, bf16[64,1536]{1,0:T(8,128)(2,1)S(1)}, u32[]{:S(2)}, u32[]{:S(2)}) collective-permute-start(bf16[64,1536]{1,0:T(8,128)(2,1)} %get-tuple-element.34), channel_id=1, source_target_pairs={{0,1},{1,0},{2,3},{3,2},{4,5},{5,4},{6,7},{7,6},{8,9},{9,8},{10,11... | collective-permute-start | bytes 589832 | tf_op jit(solution)/shard_map/ppermute | solution.py:381
  45.9 6.7 %collective-permute-start.9 = (bf16[64,1536]{1,0:T(8,128)(2,1)}, bf16[64,1536]{1,0:T(8,128)(2,1)S(1)}, u32[]{:S(2)}, u32[]{:S(2)}) collective-permute-start(bf16[64,1536]{1,0:T(8,128)(2,1)} %get-tuple-element.35), channel_id=1, source_target_pairs={{0,2},{1,3},{2,0},{3,1},{4,6},{5,7},{6,4},{7,5},{8,10},{9,11},{10,... | collective-permute-start | bytes 589832 | tf_op jit(solution)/shard_map/ppermute | solution.py:381
  46.1 11.2 %collective-permute-start.10 = (bf16[64,1536]{1,0:T(8,128)(2,1)}, bf16[64,1536]{1,0:T(8,128)(2,1)S(1)}, u32[]{:S(2)}, u32[]{:S(2)}) collective-permute-start(bf16[64,1536]{1,0:T(8,128)(2,1)} %get-tuple-element.36), channel_id=1, source_target_pairs={{0,3},{1,2},{2,1},{3,0},{4,7},{5,6},{6,5},{7,4},{8,11},{9,10},{10,... | collective-permute-start | bytes 589832 | tf_op jit(solution)/shard_map/ppermute | solution.py:381
  47.6 30.4 %collective-permute-start.2 = (bf16[64,1536]{1,0:T(8,128)(2,1)}, bf16[64,1536]{1,0:T(8,128)(2,1)S(1)}, u32[]{:S(2)}, u32[]{:S(2)}) collective-permute-start(bf16[64,1536]{1,0:T(8,128)(2,1)} %get-tuple-element.26), channel_id=1, source_target_pairs={{0,1},{1,0},{2,3},{3,2},{4,5},{5,4},{6,7},{7,6},{8,9},{9,8},{10,11... | collective-permute-start | bytes 589832 | tf_op jit(solution)/shard_map/ppermute | solution.py:381
  47.7 30.2 %collective-permute-start.3 = (bf16[64,1536]{1,0:T(8,128)(2,1)}, bf16[64,1536]{1,0:T(8,128)(2,1)S(1)}, u32[]{:S(2)}, u32[]{:S(2)}) collective-permute-start(bf16[64,1536]{1,0:T(8,128)(2,1)} %get-tuple-element.27), channel_id=1, source_target_pairs={{0,2},{1,3},{2,0},{3,1},{4,6},{5,7},{6,4},{7,5},{8,10},{9,11},{10,... | collective-permute-start | bytes 589832 | tf_op jit(solution)/shard_map/ppermute | solution.py:381
  48.0 30.0 %collective-permute-start.4 = (bf16[64,1536]{1,0:T(8,128)(2,1)}, bf16[64,1536]{1,0:T(8,128)(2,1)S(1)}, u32[]{:S(2)}, u32[]{:S(2)}) collective-permute-start(bf16[64,1536]{1,0:T(8,128)(2,1)} %get-tuple-element.28), channel_id=1, source_target_pairs={{0,3},{1,2},{2,1},{3,0},{4,7},{5,6},{6,5},{7,4},{8,11},{9,10},{10,... | collective-permute-start | bytes 589832 | tf_op jit(solution)/shard_map/ppermute | solution.py:381
  57.4 0.9 copy-start.4
  77.0 33.0 %copy-start.5 = (s32[3]{0:T(128)S(1)}, s32[3]{0:T(128)}, u32[]{:S(2)}) copy-start(s32[3]{0:T(128)} %pad_add_fusion.scalars) | copy-start | bytes 40
  77.0 33.0 %copy-start.6 = (s32[8]{0:T(128)S(1)}, s32[8]{0:T(128)}, u32[]{:S(2)}) copy-start(s32[8]{0:T(128)} %broadcast_subtract_fusion.slots) | copy-start | bytes 100
  77.0 23.3 %collective-permute-start.11 = (bf16[12,64,128]{2,1,0:T(8,128)(2,1)S(1)}, bf16[12,64,128]{2,1,0:T(8,128)(2,1)S(1)}, u32[]{:S(2)}, u32[]{:S(2)}) collective-permute-start(bf16[12,64,128]{2,1,0:T(8,128)(2,1)S(1)} %get-tuple-element.38), channel_id=1, source_target_pairs={{0,1},{1,0},{2,3},{3,2},{4,5},{5,4},{6,7},{7,6},{8,9},{9,8},{10,11... | collective-permute-start | bytes 589832 | tf_op jit(solution)/shard_map/ppermute | solution.py:381
  98.1 13.3 %collective-permute-start.5 = (bf16[12,64,128]{2,1,0:T(8,128)(2,1)S(1)}, bf16[12,64,128]{2,1,0:T(8,128)(2,1)S(1)}, u32[]{:S(2)}, u32[]{:S(2)}) collective-permute-start(bf16[12,64,128]{2,1,0:T(8,128)(2,1)S(1)} %get-tuple-element.30), channel_id=1, source_target_pairs={{0,1},{1,0},{2,3},{3,2},{4,5},{5,4},{6,7},{7,6},{8,9},{9,8},{10,11... | collective-permute-start | bytes 589832 | tf_op jit(solution)/shard_map/ppermute | solution.py:381
  98.2 6.1 %collective-permute-start.12 = (bf16[12,64,128]{2,1,0:T(8,128)(2,1)S(1)}, bf16[12,64,128]{2,1,0:T(8,128)(2,1)S(1)}, u32[]{:S(2)}, u32[]{:S(2)}) collective-permute-start(bf16[12,64,128]{2,1,0:T(8,128)(2,1)S(1)} %get-tuple-element.39), channel_id=1, source_target_pairs={{0,2},{1,3},{2,0},{3,1},{4,6},{5,7},{6,4},{7,5},{8,10},{9,11},{10,... | collective-permute-start | bytes 589832 | tf_op jit(solution)/shard_map/ppermute | solution.py:381
  98.3 11.7 %collective-permute-start.13 = (bf16[12,64,128]{2,1,0:T(8,128)(2,1)S(1)}, bf16[12,64,128]{2,1,0:T(8,128)(2,1)S(1)}, u32[]{:S(2)}, u32[]{:S(2)}) collective-permute-start(bf16[12,64,128]{2,1,0:T(8,128)(2,1)S(1)} %get-tuple-element.40), channel_id=1, source_target_pairs={{0,3},{1,2},{2,1},{3,0},{4,7},{5,6},{6,5},{7,4},{8,11},{9,10},{10,... | collective-permute-start | bytes 589832 | tf_op jit(solution)/shard_map/ppermute | solution.py:381
  100.3 12.4 %collective-permute-start.6 = (bf16[12,64,128]{2,1,0:T(8,128)(2,1)S(1)}, bf16[12,64,128]{2,1,0:T(8,128)(2,1)S(1)}, u32[]{:S(2)}, u32[]{:S(2)}) collective-permute-start(bf16[12,64,128]{2,1,0:T(8,128)(2,1)S(1)} %get-tuple-element.31), channel_id=1, source_target_pairs={{0,2},{1,3},{2,0},{3,1},{4,6},{5,7},{6,4},{7,5},{8,10},{9,11},{10,... | collective-permute-start | bytes 589832 | tf_op jit(solution)/shard_map/ppermute | solution.py:381
  100.3 17.2 %collective-permute-start.7 = (bf16[12,64,128]{2,1,0:T(8,128)(2,1)S(1)}, bf16[12,64,128]{2,1,0:T(8,128)(2,1)S(1)}, u32[]{:S(2)}, u32[]{:S(2)}) collective-permute-start(bf16[12,64,128]{2,1,0:T(8,128)(2,1)S(1)} %get-tuple-element.32), channel_id=1, source_target_pairs={{0,3},{1,2},{2,1},{3,0},{4,7},{5,6},{6,5},{7,4},{8,11},{9,10},{10,... | collective-permute-start | bytes 589832 | tf_op jit(solution)/shard_map/ppermute | solution.py:381

commit v3 on v2

--- a/solution.py
+++ b/solution.py
@@ -14,12 +14,18 @@
 F32 = jnp.float32
 BF16 = jnp.bfloat16
 VEL_ROWS = 16
+CHUNK = 32
+COST_T, COST_F, COST_P = 10 * 10**9, 3 * 10**9, 15 * 10**8
 EASY = 1.08
 FAIR = 3.8
 
 
 def spec(memory_space):
     return pl.BlockSpec(memory_space=memory_space)
+
+
+def cost(count):
+    return pl.CostEstimate(flops=count, bytes_accessed=0, transcendentals=0)
 
 
 def params(mib):
@@ -79,17 +85,20 @@
     )(atlas, vel)
 
 
-def transport_kernel(peers, per, scalars, slots, atlas, vel, low, high, low_vel, high_vel, *refs):
-    outs, (state, speed, coef) = refs[: peers * per], refs[peers * per :]
-    rows, ny, width = atlas.shape[:3]
+def transport_kernel(
+    peers, per, joined, width, part, scalars, slots, atlas, vel, low, high, low0, high0, *refs
+):
+    outs, (state, speed, coef) = refs[:-3], refs[-3:]
+    rows, ny = atlas.shape[:2]
+    tail = slice(TSTEPS * width, TSTEPS * width + VEL_ROWS)
     deep = rows + 2 * TSTEPS
     edge = TSTEPS - 1
     has_low, has_high, me = scalars[0], scalars[1], scalars[2]
 
     for k in range(3):
         speed[k, :, TSTEPS : TSTEPS + rows, :] = vel[k].astype(F32)
-        below = low_vel[...].astype(F32)[:, edge * k : edge * (k + 1), :]
-        above = high_vel[...].astype(F32)[:, edge * k : edge * (k + 1), :]
+        below = low0[:, tail, :].astype(F32)[:, edge * k : edge * (k + 1), :]
+        above = high0[:, tail, :].astype(F32)[:, edge * k : edge * (k + 1), :]
         speed[k, :, 1:TSTEPS, :] = below
         speed[k, :, TSTEPS + rows : TSTEPS + rows + edge, :] = above
     place = lax.broadcasted_iota(jnp.int32, (1, deep, LANES), 1)
@@ -111,16 +120,16 @@
         coef[0, y : y + 1] = jnp.where(inside, 1.0 - total, 0.0)
 
     def load(z, carry):
-        state[0, z + TSTEPS] = atlas[z].astype(F32)
+        state[0, z + TSTEPS] = atlas[z, :, part * width : (part + 1) * width, :].astype(F32)
         return carry
 
     lax.fori_loop(0, rows, load, 0)
     for step in range(TSTEPS):
-        part = slice(step * width, (step + 1) * width)
-        state[0, step] = low[:, part, :].astype(F32)
-        state[0, step + TSTEPS + rows] = high[:, part, :].astype(F32)
-
-    def advance(source, z, carry):
+        span = slice(step * width, (step + 1) * width)
+        state[0, step] = low[:, span, :].astype(F32)
+        state[0, step + TSTEPS + rows] = high[:, span, :].astype(F32)
+
+    def advance(source, z):
         target = 1 - source
         for y in range(ny):
             weight = [coef[i, y, pl.ds(z, 1), :] for i in range(7)]
@@ -135,46 +144,43 @@
             total = total + weight[5] * pltpu.roll(center, 1, axis=1)
             total = total + weight[6] * pltpu.roll(center, LANES - 1, axis=1)
             state[target, z, y] = total
+
+    def two(source, first, i, carry):
+        advance(source, first + 2 * i)
+        advance(source, first + 2 * i + 1)
         return carry
 
     for step in range(TSTEPS):
-        lax.fori_loop(step + 1, deep - 1 - step, functools.partial(advance, step % 2), 0)
+        pairs = (deep - 2 * (step + 1)) // 2
+        lax.fori_loop(0, pairs, functools.partial(two, step % 2, step + 1), 0)
 
     for k in range(peers):
         for s in range(per):
             z = slots[(me ^ k) * per + s] + TSTEPS
+            out = outs[k].at[s] if joined else outs[k * per + s].at[0]
             for y in range(ny):
                 value = state[TSTEPS % 2, z, y].astype(BF16)
-                outs[k * per + s][:, y * LANES : (y + 1) * LANES] = value
-
-
-def transport(scalars, slots, atlas, vel, low, high, low0, high0, width, part, peers, per):
+                out[:, y * LANES : (y + 1) * LANES] = value
+
+
+def transport(scalars, slots, atlas, vel, low, high, low0, high0, width, part, peers, per, joined):
     rows, ny = atlas.shape[:2]
     deep = rows + 2 * TSTEPS
     pixels = ny * LANES
-    halo = pl.BlockSpec((ny, TSTEPS * width, LANES), lambda i: (0, 0, 0))
-    tail = pl.BlockSpec((ny, VEL_ROWS, LANES), lambda i: (0, TSTEPS * width // VEL_ROWS, 0))
+    out = (per if joined else 1, width, pixels)
+    count = peers if joined else peers * per
     return pl.pallas_call(
-        functools.partial(transport_kernel, peers, per),
-        grid=(1,),
-        out_shape=[jax.ShapeDtypeStruct((width, pixels), BF16)] * (peers * per),
-        in_specs=[
-            spec(pltpu.SMEM),
-            spec(pltpu.SMEM),
-            pl.BlockSpec((rows, ny, width, LANES), lambda i: (0, 0, part, 0)),
-            pl.BlockSpec(vel.shape, lambda i: (0, 0, 0, 0)),
-            halo,
-            halo,
-            tail,
-            tail,
-        ],
-        out_specs=[pl.BlockSpec((width, pixels), lambda i: (0, 0))] * (peers * per),
+        functools.partial(transport_kernel, peers, per, joined, width, part),
+        out_shape=[jax.ShapeDtypeStruct(out, BF16)] * count,
+        in_specs=[spec(pltpu.SMEM)] * 2 + [spec(pltpu.VMEM)] * 6,
+        out_specs=[spec(pltpu.VMEM)] * count,
         scratch_shapes=[
             pltpu.VMEM((2, deep, ny, width, LANES), F32),
             pltpu.VMEM((3, ny, deep, LANES), F32),
             pltpu.VMEM((7, ny, deep, LANES), F32),
         ],
-        compiler_params=params(56),
+        compiler_params=params(28),
+        cost_estimate=cost(COST_T),
         name="transport",
     )(scalars, slots, atlas, vel, low, high, low0, high0)
 
@@ -196,14 +202,14 @@
     blocks = refs[: parts * peers]
     outs = refs[parts * peers : parts * peers + peers]
     panel, gram, right, inverse, answer = refs[parts * peers + peers :]
-    width, pixels = blocks[0].shape
+    width, pixels = blocks[0].shape[1:]
     channels = panel.shape[0]
     share = channels // peers
     ny = pixels // LANES
     for k in range(peers):
         for part in range(parts):
             first = k * share + part * width
-            panel[first : first + width, :] = blocks[k * parts + part][...]
+            panel[first : first + width, :] = blocks[k * parts + part][0]
     valid = mask[0] > 0
     every = panel[...]
     maps = density[0]
@@ -289,11 +295,15 @@
 
 
 def fit(mask, density, section, blocks, parts, peers):
-    width, pixels = blocks[0].shape
+    width, pixels = blocks[0].shape[1:]
     channels = width * parts * peers
     classes = density.shape[1]
     ny = pixels // LANES
-    whole = pl.BlockSpec((width, pixels), lambda i: (0, 0))
+
+    def one(block):
+        at = section if block.shape[0] > 1 else 0
+        return pl.BlockSpec((1, width, pixels), lambda i: (at, 0, 0))
+
     out = (ny, channels // peers, LANES)
     return pl.pallas_call(
         functools.partial(fit_kernel, parts, peers),
@@ -303,7 +313,7 @@
             pl.BlockSpec((1, 1, pixels), lambda i: (section, 0, 0)),
             pl.BlockSpec((1, classes, pixels), lambda i: (section, 0, 0)),
         ]
-        + [whole] * len(blocks),
+        + [one(block) for block in blocks],
         out_specs=[pl.BlockSpec(out, lambda i: (0, 0, 0))] * peers,
         scratch_shapes=[
             pltpu.VMEM((channels, pixels), BF16),
@@ -312,7 +322,8 @@
             pltpu.VMEM((channels, channels), F32),
             pltpu.VMEM((classes, channels), F32),
         ],
-        compiler_params=params(48),
+        compiler_params=params(24),
+        cost_estimate=cost(COST_F),
         name="fit",
     )(mask, density, *blocks)
 
@@ -345,7 +356,8 @@
         out_specs=spec(pl.ANY),
         scratch_shapes=[pltpu.SemaphoreType.DMA((peers,))],
         input_output_aliases={2 + peers: 0} if extra else {},
-        compiler_params=params(16),
+        compiler_params=params(8),
+        cost_estimate=cost(COST_P),
         name="place",
     )(scalars, slots, *blocks, *extra)
 
@@ -357,7 +369,7 @@
     peers = lax.axis_size(("gy", "af"))
     me = lax.axis_index(("gy", "af"))
     per = section_density.shape[0]
-    chunks = 1
+    chunks = max(1, channels // CHUNK)
     width = channels // chunks
 
     atlas = jnp.transpose(atlas_features, (0, 2, 1, 3))
@@ -382,12 +394,20 @@
 
     arrived = {}
     for part in range(chunks):
+        joined = part < chunks - 1
+        order = slots
+        if part > 0:
+            order, _ = lax.optimization_barrier((slots, moved[0]))
         moved = transport(
-            scalars, slots, atlas, vel, *halos[part], *halos[0], width, part, peers, per
+            scalars, order, atlas, vel, *halos[part], *halos[0], width, part, peers, per, joined
         )
-        for s in range(per):
+        if part > 0:
+            moved, _ = lax.optimization_barrier((moved, arrived[0, peers // 2, part - 1]))
+        for s in range(1 if joined else per):
             for k in range(peers):
-                arrived[s, k, part] = swap(moved[k * per + s], k)
+                block = swap(moved[k if joined else k * per + s], k)
+                for section in range(per) if joined else [s]:
+                    arrived[section, k, part] = block
 
     result = None
     for s in range(per):

time: 121 us -> 104 us (0.86); the launches traced: 119 us -> 104 us
  waiting for transfers between devices: 39.7 us -> 16.1 us
  starting transfers between devices: 15.6 us -> 24.8 us
  Pallas kernels: 58.2 us -> 60.1 us
  local copies, waits for them, and re-layouts: 4.19 us -> 2.33 us
    ppermute x1 -> x2, waiting for transfers between devices: 14.9 us -> 2.24 us  [body(): low = lax.ppermute(edges[2 * part + 1], 'gz', upward)]
    ppermute x12 -> x15, waiting for transfers between devices: 21.9 us -> 10.8 us  [swap(): return lax.ppermute(block, ('gy', 'af'), [(i, i ^ k) for i in range(peers)])]
    ppermute x12 -> x15, starting transfers between devices: 10.3 us -> 14.3 us  [swap(): return lax.ppermute(block, ('gy', 'af'), [(i, i ^ k) for i in range(peers)])]
    ppermute x1 -> x2, starting transfers between devices: 3.2 us -> 6.43 us  [body(): low = lax.ppermute(edges[2 * part + 1], 'gz', upward)]
    pallas_call x2, Pallas kernels: 38.8 us -> 41 us  [fit(): pl.pallas_call(functools.partial(fit_kernel, parts, peers), grid=(1,), ou...]
    ppermute x1 -> x2, starting transfers between devices: 2.08 us -> 4.13 us  [body(): high = lax.ppermute(edges[2 * part], 'gz', downward)]
    unnamed x22 -> x14, local copies, waits for them, and re-layouts: 4.18 us -> 2.32 us
    pallas_call x1 -> x2, Pallas kernels: 16.1 us -> 15 us  [transport(): pl.pallas_call(functools.partial(transport_kernel, peers, per, joined, wi...]
  transfers between devices with their start and end apart: 14 -> 19, of which waited for: 8 -> 6; matrix products, arithmetic and copies ran while one was open for 1% -> 0% of each run, Pallas kernels for 34% -> 55%
where the time goes in v3:
time: 104 us
  Pallas kernels  60.1 us (58%)
  starting transfers between devices  24.8 us (24%)
  waiting for transfers between devices  16.1 us (15%)
  local copies, waits for them, and re-layouts  2.33 us (2%)
    pallas_call x2, Pallas kernels, fit(): pl.pallas_call(functools.partial(fit_kernel, parts, peers), grid=(1,), ou...  41 us
    pallas_call x2, Pallas kernels, transport(): pl.pallas_call(functools.partial(transport_kernel, peers, per, joined, wi...  15 us
    ppermute x15, starting transfers between devices, swap(): return lax.ppermute(block, ('gy', 'af'), [(i, i ^ k) for i in range(peers)])  14.3 us
    ppermute x15, waiting for transfers between devices, swap(): return lax.ppermute(block, ('gy', 'af'), [(i, i ^ k) for i in range(peers)])  10.8 us
    ppermute x2, starting transfers between devices, body(): low = lax.ppermute(edges[2 * part + 1], 'gz', upward)  6.43 us
    ppermute x2, starting transfers between devices, body(): high = lax.ppermute(edges[2 * part], 'gz', downward)  4.13 us
    ppermute x2, waiting for transfers between devices, body(): high = lax.ppermute(edges[2 * part], 'gz', downward)  3 us
    pallas_call x2, Pallas kernels, place(): pl.pallas_call(functools.partial(place_kernel, peers, per, section), out_...  2.91 us
  transfers between devices with their start and end apart: 19, of which 6 were waited for; matrix products, arithmetic and copies ran while one was open for 0% of the time, Pallas kernels for 55%

profile of v3, /device:TPU:23, one launch (start us, length us, event | category | flops | bytes accessed | tf_op | source)
XLA Modules:
  0.0 103.7 jit_solution(1321621212098386541)
XLA Ops:
  0.0 0.0 copy-start.6
  0.0 0.0 copy-start
  0.0 1.4 %copy-done = bf16[8,64,12,128]{3,1,2,0:T(8,128)(2,1)S(1)} copy-done((bf16[8,64,12,128]{3,1,2,0:T(8,128)(2,1)S(1)}, bf16[8,64,12,128]{3,1,2,0:T(8,128)(2,1)}, u32[]{:S(2)}) %copy-start) | copy-done | bytes 1572888
  1.4 0.0 copy-start.2
  1.4 0.9 copy-done.2
  2.3 0.0 copy-start.1
  2.3 0.0 copy-start.3
  2.3 1.2 %pack_edges.1 = (bf16[12,144,128]{2,1,0:T(8,128)(2,1)S(1)}, bf16[12,144,128]{2,1,0:T(8,128)(2,1)S(1)}, bf16[12,128,128]{2,1,0:T(8,128)(2,1)}, bf16[12,128,128]{2,1,0:T(8,128)(2,1)}) custom-call(bf16[8,12,64,128]{3,2,1,0:T(8,128)(2,1)S(1)} %bitcast.6, bf16[3,12,8,128]{3,2,1,0:T(8,128)(2,1)S(1)} %bitcast.9), custom_call_target="tpu_custom_call" | custom-call | tf_op jit(solution)/shard_map/pack_edges/pallas_call | solution.py:73
  3.5 3.2 %collective-permute-start = (bf16[12,144,128]{2,1,0:T(8,128)(2,1)S(1)}, bf16[12,144,128]{2,1,0:T(8,128)(2,1)S(1)}, u32[]{:S(2)}, u32[]{:S(2)}) collective-permute-start(bf16[12,144,128]{2,1,0:T(8,128)(2,1)S(1)} %get-tuple-element.38), channel_id=1, source_target_pairs={{0,4},{4,8},{8,12},{1,5},{5,9},{9,13},{2,6},{6,10},{10,14},{3,7},{... | collective-permute-start | bytes 1327112 | tf_op jit(solution)/shard_map/ppermute | solution.py:386
  6.7 2.1 %collective-permute-start.1 = (bf16[12,144,128]{2,1,0:T(8,128)(2,1)S(1)}, bf16[12,144,128]{2,1,0:T(8,128)(2,1)S(1)}, u32[]{:S(2)}, u32[]{:S(2)}) collective-permute-start(bf16[12,144,128]{2,1,0:T(8,128)(2,1)S(1)} %get-tuple-element.39), channel_id=1, source_target_pairs={{4,0},{8,4},{12,8},{5,1},{9,5},{13,9},{6,2},{10,6},{14,10},{7,3},{... | collective-permute-start | bytes 1327112 | tf_op jit(solution)/shard_map/ppermute | solution.py:387
  8.8 3.2 %collective-permute-start.2 = (bf16[12,128,128]{2,1,0:T(8,128)(2,1)}, bf16[12,128,128]{2,1,0:T(8,128)(2,1)}, u32[]{:S(2)}, u32[]{:S(2)}) collective-permute-start(bf16[12,128,128]{2,1,0:T(8,128)(2,1)} %get-tuple-element.42), channel_id=1, source_target_pairs={{0,4},{4,8},{8,12},{1,5},{5,9},{9,13},{2,6},{6,10},{10,14},{3,7},{... | collective-permute-start | bytes 1179656 | tf_op jit(solution)/shard_map/ppermute | solution.py:386
  12.0 2.1 %collective-permute-start.3 = (bf16[12,128,128]{2,1,0:T(8,128)(2,1)}, bf16[12,128,128]{2,1,0:T(8,128)(2,1)}, u32[]{:S(2)}, u32[]{:S(2)}) collective-permute-start(bf16[12,128,128]{2,1,0:T(8,128)(2,1)} %get-tuple-element.43), channel_id=1, source_target_pairs={{4,0},{8,4},{12,8},{5,1},{9,5},{13,9},{6,2},{10,6},{14,10},{7,3},{... | collective-permute-start | bytes 1179656 | tf_op jit(solution)/shard_map/ppermute | solution.py:387
  14.1 0.1 pad_add_fusion.scalars
  14.2 0.0 copy-done.6
  14.2 2.2 %collective-permute-done.low.low0 = bf16[12,144,128]{2,1,0:T(8,128)(2,1)S(1)} collective-permute-done((bf16[12,144,128]{2,1,0:T(8,128)(2,1)S(1)}, bf16[12,144,128]{2,1,0:T(8,128)(2,1)S(1)}, u32[]{:S(2)}, u32[]{:S(2)}) %collective-permute-start) | collective-permute-done | bytes 442400 | tf_op jit(solution)/shard_map/ppermute | solution.py:386
  16.4 3.0 %collective-permute-done.1.high.high0 = bf16[12,144,128]{2,1,0:T(8,128)(2,1)S(1)} collective-permute-done((bf16[12,144,128]{2,1,0:T(8,128)(2,1)S(1)}, bf16[12,144,128]{2,1,0:T(8,128)(2,1)S(1)}, u32[]{:S(2)}, u32[]{:S(2)}) %collective-permute-start.1) | collective-permute-done | bytes 442400 | tf_op jit(solution)/shard_map/ppermute | solution.py:387
  19.4 0.0 copy-done.1
  19.4 0.0 copy-done.3
  19.4 7.2 %transport.2 = (bf16[2,32,1536]{2,1,0:T(8,128)(2,1)S(1)}, bf16[2,32,1536]{2,1,0:T(8,128)(2,1)S(1)}, bf16[2,32,1536]{2,1,0:T(8,128)(2,1)S(1)}, bf16[2,32,1536]{2,1,0:T(8,128)(2,1)S(1)}) custom-call(s32[3]{0:T(128)S(1)} %pad_add_fusion.scalars, s32[8]{0:T(128)S(1)} %broadcast_subtract_fusion.slots, bf16[8,12,64,128]{3,2,1,0:T(8,128)(2,1)S(1)} %bitcast.7, ...), custom_call_target="tpu_custom_call" | custom-call | flops 10000000000 | tf_op jit(solution)/shard_map/transport/pallas_call | solution.py:172
  26.6 0.3 collective-permute-start.4
  27.0 3.5 %collective-permute-start.5 = (bf16[2,32,1536]{2,1,0:T(8,128)(2,1)S(1)}, bf16[2,32,1536]{2,1,0:T(8,128)(2,1)S(1)}, u32[]{:S(2)}, u32[]{:S(2)}) collective-permute-start(bf16[2,32,1536]{2,1,0:T(8,128)(2,1)S(1)} %get-tuple-element.54), channel_id=1, source_target_pairs={{0,1},{1,0},{2,3},{3,2},{4,5},{5,4},{6,7},{7,6},{8,9},{9,8},{10,11... | collective-permute-start | bytes 589832 | tf_op jit(solution)/shard_map/ppermute | solution.py:393
  30.5 0.0 copy-start.5
  30.5 0.0 copy-start.4
  30.5 1.1 %collective-permute-start.8 = (bf16[2,32,1536]{2,1,0:T(8,128)(2,1)S(1)}, bf16[2,32,1536]{2,1,0:T(8,128)(2,1)S(1)}, u32[]{:S(2)}, u32[]{:S(2)}) collective-permute-start(bf16[2,32,1536]{2,1,0:T(8,128)(2,1)S(1)} %get-tuple-element.57), channel_id=1, source_target_pairs={{0,3},{1,2},{2,1},{3,0},{4,7},{5,6},{6,5},{7,4},{8,11},{9,10},{10,... | collective-permute-start | bytes 589832 | tf_op jit(solution)/shard_map/ppermute | solution.py:393
  31.6 0.0 collective-permute-done.2.low
  31.6 0.0 collective-permute-done.3.high
  31.6 7.8 %transport.3 = (bf16[1,32,1536]{2,1,0:T(8,128)(2,1)S(1)}, bf16[1,32,1536]{2,1,0:T(8,128)(2,1)S(1)}, bf16[1,32,1536]{2,1,0:T(8,128)(2,1)S(1)}, bf16[1,32,1536]{2,...) custom-call(s32[3]{0:T(128)S(1)} %pad_add_fusion.scalars, ...), custom_call_target="tpu_custom_call" | custom-call | flops 10000000000 | tf_op jit(solution)/shard_map/transport/pallas_call | solution.py:172
  39.4 0.0 collective-permute-done.4.refs_4_
  39.4 0.6 collective-permute-start.13
  40.0 0.3 collective-permute-start.14
  40.2 1.4 %collective-permute-start.15 = (bf16[1,32,1536]{2,1,0:T(8,128)(2,1)S(1)}, bf16[1,32,1536]{2,1,0:T(8,128)(2,1)S(1)}, u32[]{:S(2)}, u32[]{:S(2)}) collective-permute-start(bf16[1,32,1536]{2,1,0:T(8,128)(2,1)S(1)} %get-tuple-element.66), channel_id=1, source_target_pairs={{0,3},{1,2},{2,1},{3,0},{4,7},{5,6},{6,5},{7,4},{8,11},{9,10},{10,... | collective-permute-start | bytes 294920 | tf_op jit(solution)/shard_map/ppermute | solution.py:393
  41.7 0.0 copy-done.5
  41.7 0.0 collective-permute-done.5.refs_2_
  41.7 0.2 collective-permute-start.6
  41.9 0.0 collective-permute-done.8.refs_6_
  41.9 0.3 collective-permute-start.7
  42.2 0.0 collective-permute-done.13.refs_3_
  42.2 1.7 %collective-permute-start.9 = (bf16[1,32,1536]{2,1,0:T(8,128)(2,1)S(1)}, bf16[1,32,1536]{2,1,0:T(8,128)(2,1)S(1)}, u32[]{:S(2)}, u32[]{:S(2)}) collective-permute-start(bf16[1,32,1536]{2,1,0:T(8,128)(2,1)S(1)} %get-tuple-element.58), channel_id=1, source_target_pairs={{0,3},{1,2},{2,1},{3,0},{4,7},{5,6},{6,5},{7,4},{8,11},{9,10},{10,... | collective-permute-start | bytes 294920 | tf_op jit(solution)/shard_map/ppermute | solution.py:393
  43.9 0.4 collective-permute-done.14.refs_5_
  44.3 2.7 %collective-permute-done.15.refs_7_ = bf16[1,32,1536]{2,1,0:T(8,128)(2,1)S(1)} collective-permute-done((bf16[1,32,1536]{2,1,0:T(8,128)(2,1)S(1)}, bf16[1,32,1536]{2,1,0:T(8,128)(2,1)S(1)}, u32[]{:S(2)}, u32[]{:S(2)}) %collective-permute-start.15) | collective-permute-done | bytes 98336 | tf_op jit(solution)/shard_map/ppermute | solution.py:393
  47.0 0.0 copy-done.4
  47.0 20.9 %fit.3 = (bf16[12,64,128]{2,1,0:T(8,128)(2,1)S(1)}, bf16[12,64,128]{2,1,0:T(8,128)(2,1)S(1)}, bf16[12,64,128]{2,1,0:T(8,128)(2,1)S(1)}, bf16[12,64,128]{2,1,0:T(8,128)(2,1)S(1)}) custom-call(s32[2,1,1536]{2,1,0:T(1,128)S(1)} %reshape.3.mask, bf16[2,256,1536]{2,1,0:T(8,128)(2,1)S(1)} %copy-done.4, bf16[2,32,1536]{2,1,0:T(8,128)(2,1)S(1)} %get-tuple-element.40.refs_0_, ...), custom_call_target="tpu_custom_call" | custom-call | flops 3000000000 | tf_op jit(solution)/shard_map/fit/pallas_call | solution.py:308
  67.9 0.1 collective-permute-start.16
  68.0 0.1 collective-permute-start.17
  68.1 0.0 collective-permute-done.6.refs_3_
  68.1 2.0 %collective-permute-start.18 = (bf16[12,64,128]{2,1,0:T(8,128)(2,1)S(1)}, bf16[12,64,128]{2,1,0:T(8,128)(2,1)S(1)}, u32[]{:S(2)}, u32[]{:S(2)}) collective-permute-start(bf16[12,64,128]{2,1,0:T(8,128)(2,1)S(1)} %get-tuple-element.70), channel_id=1, source_target_pairs={{0,3},{1,2},{2,1},{3,0},{4,7},{5,6},{6,5},{7,4},{8,11},{9,10},{10,... | collective-permute-start | bytes 589832 | tf_op jit(solution)/shard_map/ppermute | solution.py:393
  70.1 0.0 collective-permute-done.7.refs_5_
  70.1 0.0 collective-permute-done.9.refs_7_
  70.1 20.2 %fit.2 = (bf16[12,64,128]{2,1,0:T(8,128)(2,1)S(1)}, bf16[12,64,128]{2,1,0:T(8,128)(2,1)S(1)}, bf16[12,64,128]{2,1,0:T(8,128)(2,1)S(1)}, bf16[12,64,128]{2,1,0:T(8,128)(2,1)S(1)}) custom-call(s32[2,1,1536]{2,1,0:T(1,128)S(1)} %reshape.3.mask, bf16[2,256,1536]{2,1,0:T(8,128)(2,1)S(1)} %copy-done.4, bf16[2,32,1536]{2,1,0:T(8,128)(2,1)S(1)} %get-tuple-element.40.refs_0_, ...), custom_call_target="tpu_custom_call" | custom-call | flops 3000000000 | tf_op jit(solution)/shard_map/fit/pallas_call | solution.py:308
  90.3 1.0 collective-permute-start.10
  91.3 0.0 collective-permute-start.11
  91.3 0.0 collective-permute-done.16.refs_1_
  91.3 1.7 %collective-permute-start.12 = (bf16[12,64,128]{2,1,0:T(8,128)(2,1)S(1)}, bf16[12,64,128]{2,1,0:T(8,128)(2,1)S(1)}, u32[]{:S(2)}, u32[]{:S(2)}) collective-permute-start(bf16[12,64,128]{2,1,0:T(8,128)(2,1)S(1)} %get-tuple-element.62), channel_id=1, source_target_pairs={{0,3},{1,2},{2,1},{3,0},{4,7},{5,6},{6,5},{7,4},{8,11},{9,10},{10,... | collective-permute-start | bytes 589832 | tf_op jit(solution)/shard_map/ppermute | solution.py:393
  93.0 0.0 collective-permute-done.17.refs_2_
  93.0 0.0 collective-permute-done.18.refs_3_
  93.0 1.5 %place.2.refs_4_ = bf16[8,12,64,128]{3,2,1,0:T(8,128)(2,1)} custom-call(s32[3]{0:T(128)S(1)} %pad_add_fusion.scalars, s32[8]{0:T(128)S(1)} %broadcast_subtract_fusion.slots, bf16[12,64,128]{2,1,0:T(8,128)(2,1)S(1)} %get-tuple-element.67.refs_0_, bf16[12,64,128]{2,1,0:T(8,128)(2,1)S(1)} %collective-permute-done.16.refs_1_, ...), custom_call_target="tpu_custom_call" | custom-call | flops 1500000000 | tf_op jit(solution)/shard_map/place/pallas_call | solution.py:350
  94.4 0.0 collective-permute-done.10.refs_1_
  94.4 3.3 %collective-permute-done.11.refs_2_ = bf16[12,64,128]{2,1,0:T(8,128)(2,1)S(1)} collective-permute-done((bf16[12,64,128]{2,1,0:T(8,128)(2,1)S(1)}, bf16[12,64,128]{2,1,0:T(8,128)(2,1)S(1)}, u32[]{:S(2)}, u32[]{:S(2)}) %collective-permute-start.11) | collective-permute-done | bytes 196640 | tf_op jit(solution)/shard_map/ppermute | solution.py:393
  97.7 4.4 %collective-permute-done.12.refs_3_ = bf16[12,64,128]{2,1,0:T(8,128)(2,1)S(1)} collective-permute-done((bf16[12,64,128]{2,1,0:T(8,128)(2,1)S(1)}, bf16[12,64,128]{2,1,0:T(8,128)(2,1)S(1)}, u32[]{:S(2)}, u32[]{:S(2)}) %collective-permute-start.12) | collective-permute-done | bytes 196640 | tf_op jit(solution)/shard_map/ppermute | solution.py:393
  102.1 1.5 %place.3 = bf16[8,12,64,128]{3,2,1,0:T(8,128)(2,1)} custom-call(s32[3]{0:T(128)S(1)} %pad_add_fusion.scalars, s32[8]{0:T(128)S(1)} %broadcast_subtract_fusion.slots, bf16[12,64,128]{2,1,0:T(8,128)(2,1)S(1)} %get-tuple-element.59.refs_0_, bf16[12,64,128]{2,1,0:T(8,128)(2,1)S(1)} %collective-permute-done.10.refs_1_, ...), custom_call_target="tpu_custom_call", output_to_operand_aliasing={{}: (6, {})} | custom-call | flops 1500000000 | tf_op jit(solution)/shard_map/place/pallas_call | solution.py:350
  (2 shorter events, 0.0 us)
Async XLA Ops:
  0.0 14.2 %copy-start.6 = (s32[8]{0:T(128)S(1)}, s32[8]{0:T(128)}, u32[]{:S(2)}) copy-start(s32[8]{0:T(128)} %param.9) | copy-start | bytes 100
  0.0 1.4 %copy-start = (bf16[8,64,12,128]{3,1,2,0:T(8,128)(2,1)S(1)}, bf16[8,64,12,128]{3,1,2,0:T(8,128)(2,1)}, u32[]{:S(2)}) copy-start(bf16[8,64,12,128]{3,1,2,0:T(8,128)(2,1)} %param.5) | copy-start | bytes 4718596
  1.4 0.9 copy-start.2
  2.3 17.1 %copy-start.1 = (bf16[8,64,12,128]{3,1,2,0:T(8,128)(2,1)S(1)}, bf16[8,64,12,128]{3,1,2,0:T(8,128)(2,1)}, u32[]{:S(2)}) copy-start(bf16[8,64,12,128]{3,1,2,0:T(8,128)(2,1)} %param.5) | copy-start | bytes 4718596
  2.3 17.1 %copy-start.3 = (bf16[3,8,12,128]{3,1,2,0:T(8,128)(2,1)S(1)}, bf16[3,8,12,128]{3,1,2,0:T(8,128)(2,1)}, u32[]{:S(2)}) copy-start(bf16[3,8,12,128]{3,1,2,0:T(8,128)(2,1)} %param.6) | copy-start | bytes 221188
  3.5 12.9 %collective-permute-start = (bf16[12,144,128]{2,1,0:T(8,128)(2,1)S(1)}, bf16[12,144,128]{2,1,0:T(8,128)(2,1)S(1)}, u32[]{:S(2)}, u32[]{:S(2)}) collective-permute-start(bf16[12,144,128]{2,1,0:T(8,128)(2,1)S(1)} %get-tuple-element.38), channel_id=1, source_target_pairs={{0,4},{4,8},{8,12},{1,5},{5,9},{9,13},{2,6},{6,10},{10,14},{3,7},{... | collective-permute-start | bytes 1327112 | tf_op jit(solution)/shard_map/ppermute | solution.py:386
  6.7 12.7 %collective-permute-start.1 = (bf16[12,144,128]{2,1,0:T(8,128)(2,1)S(1)}, bf16[12,144,128]{2,1,0:T(8,128)(2,1)S(1)}, u32[]{:S(2)}, u32[]{:S(2)}) collective-permute-start(bf16[12,144,128]{2,1,0:T(8,128)(2,1)S(1)} %get-tuple-element.39), channel_id=1, source_target_pairs={{4,0},{8,4},{12,8},{5,1},{9,5},{13,9},{6,2},{10,6},{14,10},{7,3},{... | collective-permute-start | bytes 1327112 | tf_op jit(solution)/shard_map/ppermute | solution.py:387
  8.8 22.8 %collective-permute-start.2 = (bf16[12,128,128]{2,1,0:T(8,128)(2,1)}, bf16[12,128,128]{2,1,0:T(8,128)(2,1)}, u32[]{:S(2)}, u32[]{:S(2)}) collective-permute-start(bf16[12,128,128]{2,1,0:T(8,128)(2,1)} %get-tuple-element.42), channel_id=1, source_target_pairs={{0,4},{4,8},{8,12},{1,5},{5,9},{9,13},{2,6},{6,10},{10,14},{3,7},{... | collective-permute-start | bytes 1179656 | tf_op jit(solution)/shard_map/ppermute | solution.py:386
  12.0 19.5 %collective-permute-start.3 = (bf16[12,128,128]{2,1,0:T(8,128)(2,1)}, bf16[12,128,128]{2,1,0:T(8,128)(2,1)}, u32[]{:S(2)}, u32[]{:S(2)}) collective-permute-start(bf16[12,128,128]{2,1,0:T(8,128)(2,1)} %get-tuple-element.43), channel_id=1, source_target_pairs={{4,0},{8,4},{12,8},{5,1},{9,5},{13,9},{6,2},{10,6},{14,10},{7,3},{... | collective-permute-start | bytes 1179656 | tf_op jit(solution)/shard_map/ppermute | solution.py:387
  26.6 12.7 %collective-permute-start.4 = (bf16[2,32,1536]{2,1,0:T(8,128)(2,1)S(1)}, bf16[2,32,1536]{2,1,0:T(8,128)(2,1)S(1)}, u32[]{:S(2)}, u32[]{:S(2)}) collective-permute-start(bf16[2,32,1536]{2,1,0:T(8,128)(2,1)S(1)} %get-tuple-element.52), channel_id=1, source_target_pairs={{0,2},{1,3},{2,0},{3,1},{4,6},{5,7},{6,4},{7,5},{8,10},{9,11},{10,... | collective-permute-start | bytes 589832 | tf_op jit(solution)/shard_map/ppermute | solution.py:393
  27.0 14.7 %collective-permute-start.5 = (bf16[2,32,1536]{2,1,0:T(8,128)(2,1)S(1)}, bf16[2,32,1536]{2,1,0:T(8,128)(2,1)S(1)}, u32[]{:S(2)}, u32[]{:S(2)}) collective-permute-start(bf16[2,32,1536]{2,1,0:T(8,128)(2,1)S(1)} %get-tuple-element.54), channel_id=1, source_target_pairs={{0,1},{1,0},{2,3},{3,2},{4,5},{5,4},{6,7},{7,6},{8,9},{9,8},{10,11... | collective-permute-start | bytes 589832 | tf_op jit(solution)/shard_map/ppermute | solution.py:393
  30.5 11.2 %copy-start.5 = (s32[2,1536]{1,0:T(2,128)S(1)}, s32[2,1536]{1,0:T(2,128)}, u32[]{:S(2)}) copy-start(s32[2,1536]{1,0:T(2,128)} %param.8) | copy-start | bytes 36868
  30.5 16.6 %copy-start.4 = (bf16[2,256,1536]{2,1,0:T(8,128)(2,1)S(1)}, bf16[2,256,1536]{2,1,0:T(8,128)(2,1)}, u32[]{:S(2)}) copy-start(bf16[2,256,1536]{2,1,0:T(8,128)(2,1)} %density.3) | copy-start | bytes 4718596
  30.5 11.5 %collective-permute-start.8 = (bf16[2,32,1536]{2,1,0:T(8,128)(2,1)S(1)}, bf16[2,32,1536]{2,1,0:T(8,128)(2,1)S(1)}, u32[]{:S(2)}, u32[]{:S(2)}) collective-permute-start(bf16[2,32,1536]{2,1,0:T(8,128)(2,1)S(1)} %get-tuple-element.57), channel_id=1, source_target_pairs={{0,3},{1,2},{2,1},{3,0},{4,7},{5,6},{6,5},{7,4},{8,11},{9,10},{10,... | collective-permute-start | bytes 589832 | tf_op jit(solution)/shard_map/ppermute | solution.py:393
  39.4 2.8 %collective-permute-start.13 = (bf16[1,32,1536]{2,1,0:T(8,128)(2,1)S(1)}, bf16[1,32,1536]{2,1,0:T(8,128)(2,1)S(1)}, u32[]{:S(2)}, u32[]{:S(2)}) collective-permute-start(bf16[1,32,1536]{2,1,0:T(8,128)(2,1)S(1)} %get-tuple-element.64), channel_id=1, source_target_pairs={{0,1},{1,0},{2,3},{3,2},{4,5},{5,4},{6,7},{7,6},{8,9},{9,8},{10,11... | collective-permute-start | bytes 294920 | tf_op jit(solution)/shard_map/ppermute | solution.py:393
  40.0 4.4 %collective-permute-start.14 = (bf16[1,32,1536]{2,1,0:T(8,128)(2,1)S(1)}, bf16[1,32,1536]{2,1,0:T(8,128)(2,1)S(1)}, u32[]{:S(2)}, u32[]{:S(2)}) collective-permute-start(bf16[1,32,1536]{2,1,0:T(8,128)(2,1)S(1)} %get-tuple-element.65), channel_id=1, source_target_pairs={{0,2},{1,3},{2,0},{3,1},{4,6},{5,7},{6,4},{7,5},{8,10},{9,11},{10,... | collective-permute-start | bytes 294920 | tf_op jit(solution)/shard_map/ppermute | solution.py:393
  40.2 6.8 %collective-permute-start.15 = (bf16[1,32,1536]{2,1,0:T(8,128)(2,1)S(1)}, bf16[1,32,1536]{2,1,0:T(8,128)(2,1)S(1)}, u32[]{:S(2)}, u32[]{:S(2)}) collective-permute-start(bf16[1,32,1536]{2,1,0:T(8,128)(2,1)S(1)} %get-tuple-element.66), channel_id=1, source_target_pairs={{0,3},{1,2},{2,1},{3,0},{4,7},{5,6},{6,5},{7,4},{8,11},{9,10},{10,... | collective-permute-start | bytes 294920 | tf_op jit(solution)/shard_map/ppermute | solution.py:393
  41.7 26.4 %collective-permute-start.6 = (bf16[1,32,1536]{2,1,0:T(8,128)(2,1)S(1)}, bf16[1,32,1536]{2,1,0:T(8,128)(2,1)S(1)}, u32[]{:S(2)}, u32[]{:S(2)}) collective-permute-start(bf16[1,32,1536]{2,1,0:T(8,128)(2,1)S(1)} %get-tuple-element.55), channel_id=1, source_target_pairs={{0,1},{1,0},{2,3},{3,2},{4,5},{5,4},{6,7},{7,6},{8,9},{9,8},{10,11... | collective-permute-start | bytes 294920 | tf_op jit(solution)/shard_map/ppermute | solution.py:393
  41.9 28.2 %collective-permute-start.7 = (bf16[1,32,1536]{2,1,0:T(8,128)(2,1)S(1)}, bf16[1,32,1536]{2,1,0:T(8,128)(2,1)S(1)}, u32[]{:S(2)}, u32[]{:S(2)}) collective-permute-start(bf16[1,32,1536]{2,1,0:T(8,128)(2,1)S(1)} %get-tuple-element.56), channel_id=1, source_target_pairs={{0,2},{1,3},{2,0},{3,1},{4,6},{5,7},{6,4},{7,5},{8,10},{9,11},{10,... | collective-permute-start | bytes 294920 | tf_op jit(solution)/shard_map/ppermute | solution.py:393
  42.2 27.9 %collective-permute-start.9 = (bf16[1,32,1536]{2,1,0:T(8,128)(2,1)S(1)}, bf16[1,32,1536]{2,1,0:T(8,128)(2,1)S(1)}, u32[]{:S(2)}, u32[]{:S(2)}) collective-permute-start(bf16[1,32,1536]{2,1,0:T(8,128)(2,1)S(1)} %get-tuple-element.58), channel_id=1, source_target_pairs={{0,3},{1,2},{2,1},{3,0},{4,7},{5,6},{6,5},{7,4},{8,11},{9,10},{10,... | collective-permute-start | bytes 294920 | tf_op jit(solution)/shard_map/ppermute | solution.py:393
  67.9 23.3 %collective-permute-start.16 = (bf16[12,64,128]{2,1,0:T(8,128)(2,1)S(1)}, bf16[12,64,128]{2,1,0:T(8,128)(2,1)S(1)}, u32[]{:S(2)}, u32[]{:S(2)}) collective-permute-start(bf16[12,64,128]{2,1,0:T(8,128)(2,1)S(1)} %get-tuple-element.68), channel_id=1, source_target_pairs={{0,1},{1,0},{2,3},{3,2},{4,5},{5,4},{6,7},{7,6},{8,9},{9,8},{10,11... | collective-permute-start | bytes 589832 | tf_op jit(solution)/shard_map/ppermute | solution.py:393
  68.0 25.0 %collective-permute-start.17 = (bf16[12,64,128]{2,1,0:T(8,128)(2,1)S(1)}, bf16[12,64,128]{2,1,0:T(8,128)(2,1)S(1)}, u32[]{:S(2)}, u32[]{:S(2)}) collective-permute-start(bf16[12,64,128]{2,1,0:T(8,128)(2,1)S(1)} %get-tuple-element.69), channel_id=1, source_target_pairs={{0,2},{1,3},{2,0},{3,1},{4,6},{5,7},{6,4},{7,5},{8,10},{9,11},{10,... | collective-permute-start | bytes 589832 | tf_op jit(solution)/shard_map/ppermute | solution.py:393
  68.1 24.9 %collective-permute-start.18 = (bf16[12,64,128]{2,1,0:T(8,128)(2,1)S(1)}, bf16[12,64,128]{2,1,0:T(8,128)(2,1)S(1)}, u32[]{:S(2)}, u32[]{:S(2)}) collective-permute-start(bf16[12,64,128]{2,1,0:T(8,128)(2,1)S(1)} %get-tuple-element.70), channel_id=1, source_target_pairs={{0,3},{1,2},{2,1},{3,0},{4,7},{5,6},{6,5},{7,4},{8,11},{9,10},{10,... | collective-permute-start | bytes 589832 | tf_op jit(solution)/shard_map/ppermute | solution.py:393
  90.3 4.1 %collective-permute-start.10 = (bf16[12,64,128]{2,1,0:T(8,128)(2,1)S(1)}, bf16[12,64,128]{2,1,0:T(8,128)(2,1)S(1)}, u32[]{:S(2)}, u32[]{:S(2)}) collective-permute-start(bf16[12,64,128]{2,1,0:T(8,128)(2,1)S(1)} %get-tuple-element.60), channel_id=1, source_target_pairs={{0,1},{1,0},{2,3},{3,2},{4,5},{5,4},{6,7},{7,6},{8,9},{9,8},{10,11... | collective-permute-start | bytes 589832 | tf_op jit(solution)/shard_map/ppermute | solution.py:393
  91.3 6.5 %collective-permute-start.11 = (bf16[12,64,128]{2,1,0:T(8,128)(2,1)S(1)}, bf16[12,64,128]{2,1,0:T(8,128)(2,1)S(1)}, u32[]{:S(2)}, u32[]{:S(2)}) collective-permute-start(bf16[12,64,128]{2,1,0:T(8,128)(2,1)S(1)} %get-tuple-element.61), channel_id=1, source_target_pairs={{0,2},{1,3},{2,0},{3,1},{4,6},{5,7},{6,4},{7,5},{8,10},{9,11},{10,... | collective-permute-start | bytes 589832 | tf_op jit(solution)/shard_map/ppermute | solution.py:393
  91.3 10.8 %collective-permute-start.12 = (bf16[12,64,128]{2,1,0:T(8,128)(2,1)S(1)}, bf16[12,64,128]{2,1,0:T(8,128)(2,1)S(1)}, u32[]{:S(2)}, u32[]{:S(2)}) collective-permute-start(bf16[12,64,128]{2,1,0:T(8,128)(2,1)S(1)} %get-tuple-element.62), channel_id=1, source_target_pairs={{0,3},{1,2},{2,1},{3,0},{4,7},{5,6},{6,5},{7,4},{8,11},{9,10},{10,... | collective-permute-start | bytes 589832 | tf_op jit(solution)/shard_map/ppermute | solution.py:393

commit v4 on v3

v4 whole, which is shorter than its diff:
```python
import functools
import itertools

import jax
import jax.numpy as jnp
from jax import lax
from jax.experimental import pallas as pl
from jax.experimental.pallas import tpu as pltpu
from jax.sharding import PartitionSpec as P

TSTEPS = 4
RATE = 0.04
RIDGE = 0.25
LANES = 128
F32 = jnp.float32
BF16 = jnp.bfloat16
VEL_ROWS = 16
WIDTHS = (32, 32)
COST_I, COST_T, COST_F, COST_P = 4 * 10**9, 6 * 10**9, 3 * 10**9, 15 * 10**8
EASY = 1.08
FAIR = 3.8


def spec(memory_space):
    return pl.BlockSpec(memory_space=memory_space)


def cost(count):
    return pl.CostEstimate(flops=count, bytes_accessed=0, transcendentals=0)


def params(mib):
    return pltpu.CompilerParams(vmem_limit_bytes=mib << 20)


def odd_slab():
    return lax.rem(lax.axis_index("gz"), 2)


def pack_kernel(widths, atlas, vel, *refs):
    outs, (held, boxes, sems) = refs[:-3], refs[-3:]
    rows, ny = atlas.shape[:2]
    odd = odd_slab()
    slots = TSTEPS - 1
    copies = []
    count = itertools.count()

    def move(source, target):
        copies.append(pltpu.make_async_copy(source, target, sems.at[next(count)]))
        copies[-1].start()

    move(vel, held)
    start = 0
    for part, width in enumerate(widths):
        for side in range(2):
            first = jnp.where(odd == side, rows - TSTEPS, 0)
            for step in range(TSTEPS):
                move(
                    atlas.at[first + step, :, pl.ds(start, width), :],
                    outs[2 * part + side].at[:, pl.ds(step * width, width), :],
                )
        start += width
    copies.pop(0).wait()
    speed = held[...].astype(F32)
    filler = jnp.zeros((ny, VEL_ROWS - 3 * slots, LANES), F32)
    edges = []
    for first in (0, rows - slots):
        lines = [speed[k, :, first : first + slots, :] for k in range(3)]
        edges.append(jnp.concatenate(lines + [filler], axis=1))
    for side in range(2):
        boxes[side] = jnp.where(odd == side, edges[1], edges[0]).astype(BF16)
        move(boxes.at[side], outs[side].at[:, pl.ds(TSTEPS * widths[0], VEL_ROWS), :])
    for copy in copies:
        copy.wait()


def pack(atlas, vel, widths):
    ny = atlas.shape[1]
    shapes = []
    for part, width in enumerate(widths):
        rows = TSTEPS * width + (VEL_ROWS if part == 0 else 0)
        shapes += [jax.ShapeDtypeStruct((ny, rows, LANES), BF16)] * 2
    return pl.pallas_call(
        functools.partial(pack_kernel, widths),
        out_shape=shapes,
        in_specs=[spec(pl.ANY)] * 2,
        out_specs=[spec(pl.ANY)] * len(shapes),
        scratch_shapes=[
            pltpu.VMEM(vel.shape, BF16),
            pltpu.VMEM((2, ny, VEL_ROWS, LANES), BF16),
            pltpu.SemaphoreType.DMA((2 * len(widths) * TSTEPS + 3,)),
        ],
        compiler_params=params(8),
        name="pack_edges",
    )(*(pltpu.with_memory_space_constraint(x, pltpu.HBM) for x in (atlas, vel)))


def set_weights(speed, coef, inside):
    lane = lax.broadcasted_iota(jnp.int32, (1,) + speed.shape[2:], 2)
    for y in range(speed.shape[1]):
        total = jnp.zeros(lane.shape, F32)
        for k in range(3):
            v = speed[k, y : y + 1]
            from_low = jnp.maximum(v, 0.0) + RATE
            from_high = RATE - jnp.minimum(v, 0.0)
            total = total + (from_low + from_high)
            if k == 2:
                from_low = jnp.where(lane == 0, 0.0, from_low)
                from_high = jnp.where(lane == LANES - 1, 0.0, from_high)
            coef[2 * k + 1, y : y + 1] = jnp.where(inside, from_low, 0.0)
            coef[2 * k + 2, y : y + 1] = jnp.where(inside, from_high, 0.0)
        coef[0, y : y + 1] = jnp.where(inside, 1.0 - total, 0.0)


def advance(coef, source, target, z, shift=0):
    at = z - shift
    ny = source.shape[1]
    for y in range(ny):
        weight = [coef[i, y, pl.ds(z, 1), :] for i in range(7)]
        center = source[at, y]
        total = weight[0] * center
        total = total + weight[1] * source[at - 1, y]
        total = total + weight[2] * source[at + 1, y]
        if y > 0:
            total = total + weight[3] * source[at, y - 1]
        if y < ny - 1:
            total = total + weight[4] * source[at, y + 1]
        total = total + weight[5] * pltpu.roll(center, 1, axis=1)
        total = total + weight[6] * pltpu.roll(center, LANES - 1, axis=1)
        target[z, y] = total


def advance_pairs(coef, source, target, pairs, first, shift=0):
    def step(i, carry):
        z = first(i)
        advance(coef, source, target, z, shift)
        advance(coef, source, target, z + 1, shift)
        return carry

    lax.fori_loop(0, pairs, step, 0)


def inner_kernel(atlas, vel, one, two, three, state, speed, coef):
    rows = atlas.shape[0]
    speed[...] = vel[...].astype(F32)
    set_weights(speed, coef, True)

    def load(z, carry):
        state[z] = atlas[z].astype(F32)
        return carry

    lax.fori_loop(0, rows, load, 0)
    levels = (state, one, two, three)
    for step in range(TSTEPS - 1):
        pairs = (rows - 2 * (step + 1)) // 2
        first = step + 1
        advance_pairs(coef, levels[step], levels[step + 1], pairs, lambda i: first + 2 * i)


def inner(atlas, vel):
    level = jax.ShapeDtypeStruct(atlas.shape, F32)
    return pl.pallas_call(
        inner_kernel,
        out_shape=[level] * (TSTEPS - 1),
        in_specs=[spec(pltpu.VMEM)] * 2,
        out_specs=[spec(pltpu.VMEM)] * (TSTEPS - 1),
        scratch_shapes=[
            pltpu.VMEM(atlas.shape, F32),
            pltpu.VMEM(vel.shape, F32),
            pltpu.VMEM((7,) + vel.shape[1:], F32),
        ],
        compiler_params=params(24),
        cost_estimate=cost(COST_I),
        name="inner_steps",
    )(atlas, vel)


def transport_kernel(
    peers, per, joined, width, start, slots, atlas, vel, one, two, one0, two0, *refs
):
    inner_levels, refs = refs[: TSTEPS - 1], refs[TSTEPS - 1 :]
    outs, (state, speed, coef) = refs[:-3], refs[-3:]
    rows, ny = atlas.shape[:2]
    tail = slice(one0.shape[1] - VEL_ROWS, one0.shape[1])
    deep = rows + 2 * TSTEPS
    edge = TSTEPS - 1
    slab, slabs = lax.axis_index("gz"), lax.axis_size("gz")
    me = lax.axis_index(("gy", "af"))
    odd = odd_slab() > 0
    has_low, has_high = slab > 0, slab < slabs - 1

    def sides(one, two):
        one, two = one.astype(F32), two.astype(F32)
        return jnp.where(odd, one, two), jnp.where(odd, two, one)

    below, above = sides(one0[:, tail, :], two0[:, tail, :])
    for k in range(3):
        speed[k, :, TSTEPS : TSTEPS + rows, :] = vel[k].astype(F32)
        speed[k, :, 1:TSTEPS, :] = below[:, edge * k : edge * (k + 1), :]
        speed[k, :, TSTEPS + rows : TSTEPS + rows + edge, :] = above[:, edge * k : edge * (k + 1), :]
    place = lax.broadcasted_iota(jnp.int32, (1, deep, LANES), 1)
    inside = ((place >= TSTEPS) | has_low) & ((place < TSTEPS + rows) | has_high)
    set_weights(speed, coef, inside & (place > 0) & (place < deep - 1))

    channels = slice(start, start + width)
    for z in (0, 1, rows - 2, rows - 1):
        state[0, z + TSTEPS] = atlas[z, :, channels, :].astype(F32)
    for step in range(TSTEPS):
        span = slice(step * width, (step + 1) * width)
        low, high = sides(one[:, span, :], two[:, span, :])
        state[0, step] = low
        state[0, step + TSTEPS + rows] = high
    for level in range(1, TSTEPS):
        for z in sorted({level, level + 1, rows - 2 - level, rows - 1 - level}):
            state[level, z + TSTEPS] = inner_levels[level - 1][z, :, channels, :]
    for step in range(TSTEPS):

        def first(i):
            return jnp.where(i < 2, step + 1 + 2 * i, deep - 9 - step + 2 * i)

        target = state.at[(step + 1) % TSTEPS]
        advance_pairs(coef, state.at[step], target, TSTEPS, first)
    if rows > 2 * TSTEPS:
        source = inner_levels[-1].at[:, :, channels, :]
        pairs = (rows - 2 * TSTEPS) // 2
        advance_pairs(coef, source, state.at[0], pairs, lambda i: 2 * TSTEPS + 2 * i, TSTEPS)

    for k in range(peers):
        for s in range(per):
            z = slots[(me ^ k) * per + s] - slab * rows + TSTEPS
            out = outs[k].at[s] if joined else outs[k * per + s].at[0]
            for y in range(ny):
                value = state[0, z, y].astype(BF16)
                out[:, y * LANES : (y + 1) * LANES] = value


def transport(slots, atlas, vel, one, two, one0, two0, levels, width, start, peers, per, joined):
    rows, ny = atlas.shape[:2]
    deep = rows + 2 * TSTEPS
    pixels = ny * LANES
    out = (per if joined else 1, width, pixels)
    count = peers if joined else peers * per
    return pl.pallas_call(
        functools.partial(transport_kernel, peers, per, joined, width, start),
        out_shape=[jax.ShapeDtypeStruct(out, BF16)] * count,
        in_specs=[spec(pltpu.SMEM)] + [spec(pltpu.VMEM)] * (6 + len(levels)),
        out_specs=[spec(pltpu.VMEM)] * count,
        scratch_shapes=[
            pltpu.VMEM((TSTEPS, deep, ny, width, LANES), F32),
            pltpu.VMEM((3, ny, deep, LANES), F32),
            pltpu.VMEM((7, ny, deep, LANES), F32),
        ],
        compiler_params=params(28),
        cost_estimate=cost(COST_T),
        name="transport",
    )(slots, atlas, vel, one, two, one0, two0, *levels)


def dot(a, b):
    return jnp.dot(a, b, preferred_element_type=F32)


def dot_full(a, b):
    return jnp.dot(a, b, preferred_element_type=F32, precision=lax.Precision.HIGHEST)


def halves(value):
    high = value.astype(BF16)
    return high, (value - high.astype(F32)).astype(BF16)


def fit_kernel(parts, peers, mask, density, *refs):
    blocks = refs[: parts * peers]
    outs = refs[parts * peers : parts * peers + peers]
    panel, gram, right, inverse, answer = refs[parts * peers + peers :]
    pixels = panel.shape[1]
    channels = panel.shape[0]
    share = channels // peers
    ny = pixels // LANES
    for k in range(peers):
        first = k * share
        for block in blocks[k * parts : (k + 1) * parts]:
            panel[first : first + block.shape[1], :] = block[0]
            first += block.shape[1]
    valid = mask[0] > 0
    every = panel[...]
    maps = density[0]
    masked = jnp.where(valid, every, jnp.zeros_like(every))
    contract = (((1,), (1,)), ((), ()))
    row = lax.broadcasted_iota(jnp.int32, (channels, channels), 0)
    column = lax.broadcasted_iota(jnp.int32, (channels, channels), 1)
    same = row == column
    gram[...] = lax.dot_general(every, masked, contract, preferred_element_type=F32) * (
        1.0 / pixels
    ) + jnp.where(same, RIDGE, 0.0)
    right[...] = lax.dot_general(maps, masked, contract, preferred_element_type=F32) * (
        1.0 / pixels
    )
    sums = jnp.sum(jnp.abs(gram[...]), axis=0, keepdims=True)
    bound_row = jnp.max(sums, axis=1, keepdims=True)
    bound = jnp.max(sums)
    start = 2.0 / (RIDGE + bound_row)
    spread = (bound_row - RIDGE) / (bound_row + RIDGE)

    def narrowed(spread):
        square = spread * spread
        return square / (2.0 - square), 2.0 / (2.0 - square)

    def doubled(scale):
        low = inverse[...].astype(BF16)
        left = jnp.where(same, 1.0, 0.0) - dot(gram[...].astype(BF16), low)
        inverse[...] = scale * (inverse[...] + dot(low, left.astype(BF16)))

    def refined():
        high, rest = halves(answer[...])
        gram_high, gram_rest = halves(gram[...])
        product = dot(high, gram_high) + (dot(rest, gram_high) + dot(high, gram_rest))
        left = (right[...] - product).astype(BF16)
        answer[...] = answer[...] + dot(left, inverse[...].astype(BF16))

    @pl.when(bound <= FAIR)
    def _():
        spread1, scale1 = narrowed(spread)
        spread2, scale2 = narrowed(spread1)
        _, scale3 = narrowed(spread2)
        inverse[...] = scale1 * (
            jnp.where(same, 2.0 * start, 0.0) - (start * start) * gram[...]
        )
        doubled(scale2)

        @pl.when(bound > EASY)
        def _():
            doubled(scale3)

        answer[...] = dot(right[...].astype(BF16), inverse[...].astype(BF16))
        refined()
        refined()

        @pl.when(bound > EASY)
        def _():
            refined()

    @pl.when(bound > FAIR)
    def _():
        inverse[...] = jnp.where(same, start, 0.0)

        def step(spread):
            left = jnp.where(same, 2.0, 0.0) - dot_full(gram[...], inverse[...])
            inverse[...] = dot_full(inverse[...], left)
            return spread * spread

        lax.while_loop(lambda spread: spread > 1e-4, step, jnp.max(spread))
        answer[...] = dot_full(right[...], inverse[...])
        for _ in range(3):
            left = right[...] - dot_full(answer[...], gram[...])
            answer[...] = answer[...] + dot_full(left, inverse[...])

    coefficient_t = answer[...].astype(BF16)
    coefficient = answer[...].T.astype(BF16)
    fitted = dot(coefficient_t, panel[...])
    residual = (fitted - maps.astype(F32)).astype(BF16)
    pushed = dot(coefficient, residual)
    gradient = jnp.where(valid, 2.0 * pushed, 0.0).astype(BF16)
    for k in range(peers):
        for y in range(ny):
            outs[k][y] = gradient[k * share : (k + 1) * share, y * LANES : (y + 1) * LANES]


def fit(mask, density, section, blocks, parts, peers):
    pixels = blocks[0].shape[2]
    channels = sum(block.shape[1] for block in blocks)
    classes = density.shape[1]
    ny = pixels // LANES

    def one(block):
        at = section if block.shape[0] > 1 else 0
        return pl.BlockSpec((1,) + block.shape[1:], lambda i: (at, 0, 0))

    out = (ny, channels // peers, LANES)
    return pl.pallas_call(
        functools.partial(fit_kernel, parts, peers),
        grid=(1,),
        out_shape=[jax.ShapeDtypeStruct(out, BF16)] * peers,
        in_specs=[
            pl.BlockSpec((1, 1, pixels), lambda i: (section, 0, 0)),
            pl.BlockSpec((1, classes, pixels), lambda i: (section, 0, 0)),
        ]
        + [one(block) for block in blocks],
        out_specs=[pl.BlockSpec(out, lambda i: (0, 0, 0))] * peers,
        scratch_shapes=[
            pltpu.VMEM((channels, pixels), BF16),
            pltpu.VMEM((channels, channels), F32),
            pltpu.VMEM((classes, channels), F32),
            pltpu.VMEM((channels, channels), F32),
            pltpu.VMEM((classes, channels), F32),
        ],
        compiler_params=params(24),
        cost_estimate=cost(COST_F),
        name="fit",
    )(mask, density, *blocks)


def place_kernel(peers, per, section, slots, *refs):
    blocks = refs[:peers]
    out, sems = refs[-2], refs[-1]
    me = lax.axis_index(("gy", "af"))
    first = lax.axis_index("gz") * out.shape[0]
    copies = [
        pltpu.make_async_copy(
            blocks[k], out.at[slots[(me ^ k) * per + section] - first], sems.at[k]
        )
        for k in range(peers)
    ]
    for copy in copies:
        copy.start()
    for copy in copies:
        copy.wait()


def place(slots, blocks, earlier, rows, section, per):
    peers = len(blocks)
    extra = [] if earlier is None else [earlier]
    return pl.pallas_call(
        functools.partial(place_kernel, peers, per, section),
        out_shape=jax.ShapeDtypeStruct((rows,) + blocks[0].shape, BF16),
        in_specs=[spec(pltpu.SMEM)]
        + [spec(pltpu.VMEM)] * peers
        + [spec(pl.ANY)] * len(extra),
        out_specs=spec(pl.ANY),
        scratch_shapes=[pltpu.SemaphoreType.DMA((peers,))],
        input_output_aliases={1 + peers: 0} if extra else {},
        compiler_params=params(8),
        cost_estimate=cost(COST_P),
        name="place",
    )(slots, *blocks, *extra)


def body(atlas_features, velocity, section_density, pixel_mask, section_slice):
    rows, channels = atlas_features.shape[:2]
    slabs = lax.axis_size("gz")
    peers = lax.axis_size(("gy", "af"))
    per = section_density.shape[0]
    widths = WIDTHS if sum(WIDTHS) == channels else (channels,)
    chunks = len(widths)

    atlas = jnp.transpose(atlas_features, (0, 2, 1, 3))
    vel = jnp.transpose(velocity, (0, 2, 1, 3))
    mask = pixel_mask.reshape(per, 1, -1)
    slots = section_slice

    edges = pack(atlas, vel, widths)
    ones = [(i, i ^ 1) for i in range(slabs)]
    twos = [(i, i + 1) for i in range(1, slabs - 1, 2)]
    twos += [(j, i) for i, j in twos]
    halos = []
    for part in range(chunks):
        one = lax.ppermute(edges[2 * part], "gz", ones)
        two = lax.ppermute(edges[2 * part + 1], "gz", twos)
        halos.append((one, two))

    own, _ = lax.optimization_barrier((atlas, edges[0]))
    levels = inner(own, vel)

    def swap(block, k):
        if k == 0:
            return block
        return lax.ppermute(block, ("gy", "af"), [(i, i ^ k) for i in range(peers)])

    arrived = {}
    start = 0
    for part, width in enumerate(widths):
        joined = part < chunks - 1
        order = slots
        if part > 0:
            order, _ = lax.optimization_barrier((slots, moved[0]))
        moved = transport(
            order, atlas, vel, *halos[part], *halos[0], levels, width, start, peers, per, joined
        )
        start += width
        if part > 0:
            moved, _ = lax.optimization_barrier((moved, arrived[0, peers // 2, part - 1]))
        for s in range(1 if joined else per):
            for k in range(peers):
                block = swap(moved[k if joined else k * per + s], k)
                for section in range(per) if joined else [s]:
                    arrived[section, k, part] = block

    result = None
    for s in range(per):
        blocks = [arrived[s, k, part] for k in range(peers) for part in range(chunks)]
        gradients = fit(mask, section_density, s, blocks, chunks, peers)
        returned = [swap(gradients[k], k) for k in range(peers)]
        result = place(slots, returned, result, rows, s, per)
    return jnp.transpose(result, (0, 2, 1, 3))


def solution(mesh):
    return jax.shard_map(
        body,
        mesh=mesh,
        in_specs=(
            P(("groups", "gz"), ("gy", "af"), None, None),
            P(None, ("groups", "gz"), None, None),
            P(("groups", "gz", "gy", "af"), None, None),
            P(("groups", "gz", "gy", "af"), None),
            P(("groups", "gz")),
        ),
        out_specs=P(("groups", "gz"), ("gy", "af"), None, None),
        check_vma=False,
    )
```

time: 104 us -> 94.8 us (0.912)
  starting transfers between devices: 24.8 us -> 20.6 us
  local copies, waits for them, and re-layouts: 2.33 us -> 0.03 us
  waiting for transfers between devices: 16.1 us -> 14.4 us
    ppermute x4, starting transfers between devices: 10.6 us -> 6.7 us  [the longest x2 5.27 us: body(): two = lax.ppermute(edges[2 * part + 1], 'gz', twos)]
    pallas_call x1 -> x2, Pallas kernels: 1.17 us -> 4.96 us  [the longest x1 3.21 us: inner(): pl.pallas_call(inner_kernel, out_shape=[level] * (TSTEPS - 1), in_specs=[...]
    pallas_call x2, Pallas kernels: 15 us -> 11.6 us  [transport(): pl.pallas_call(functools.partial(transport_kernel, peers, per, joined, wi...]
    unnamed x14 -> x10, local copies, waits for them, and re-layouts: 2.32 us -> 0.02 us
    pallas_call x2, Pallas kernels: 41 us -> 39.7 us  [fit(): pl.pallas_call(functools.partial(fit_kernel, parts, peers), grid=(1,), ou...]
    ppermute x4, waiting for transfers between devices: 5.24 us -> 3.99 us  [the longest x2 2.86 us: body(): two = lax.ppermute(edges[2 * part + 1], 'gz', twos)]
  transfers between devices with their start and end apart: 19 -> 19, of which waited for: 6 -> 6; matrix products, arithmetic and copies ran while one was open for 0% -> 0% of each run, Pallas kernels for 55% -> 59%
where the time goes in v4:
time: 94.8 us; the launch traced here: 94.6 us
  Pallas kernels  59.2 us (62%)
  starting transfers between devices  20.6 us (22%)
  waiting for transfers between devices  14.4 us (15%)
    pallas_call x2, Pallas kernels, fit(): pl.pallas_call(functools.partial(fit_kernel, parts, peers), grid=(1,), ou...  39.7 us
    ppermute x15, starting transfers between devices, swap(): return lax.ppermute(block, ('gy', 'af'), [(i, i ^ k) for i in range(peers)])  13.9 us
    pallas_call x2, Pallas kernels, transport(): pl.pallas_call(functools.partial(transport_kernel, peers, per, joined, wi...  11.6 us
    ppermute x15, waiting for transfers between devices, swap(): return lax.ppermute(block, ('gy', 'af'), [(i, i ^ k) for i in range(peers)])  10.5 us
    ppermute x2, starting transfers between devices, body(): two = lax.ppermute(edges[2 * part + 1], 'gz', twos)  5.27 us
    pallas_call x1, Pallas kernels, inner(): pl.pallas_call(inner_kernel, out_shape=[level] * (TSTEPS - 1), in_specs=[...  3.21 us
    pallas_call x2, Pallas kernels, place(): pl.pallas_call(functools.partial(place_kernel, peers, per, section), out_...  2.92 us
    ppermute x2, waiting for transfers between devices, body(): two = lax.ppermute(edges[2 * part + 1], 'gz', twos)  2.86 us
  transfers between devices with their start and end apart: 19, of which 6 were waited for; matrix products, arithmetic and copies ran while one was open for 0% of the time, Pallas kernels for 59%

profile of v4, /device:TPU:23, one launch (start us, length us, event | category | flops | bytes accessed | tf_op | source)
XLA Modules:
  0.0 94.6 jit_solution(9801630756089681234)
XLA Ops:
  0.0 0.0 copy-start
  0.0 0.0 copy-start.1
  0.0 1.8 %pack_edges.1 = (bf16[12,144,128]{2,1,0:T(8,128)(2,1)S(1)}, bf16[12,144,128]{2,1,0:T(8,128)(2,1)S(1)}, bf16[12,128,128]{2,1,0:T(8,128)(2,1)S(1)}, bf16[12,128,128]{2,1,0:T(8,128)(2,1)S(1)}) custom-call(bf16[8,12,64,128]{3,2,1,0:T(8,128)(2,1)} %bitcast.3, bf16[3,12,8,128]{3,2,1,0:T(8,128)(2,1)} %bitcast.7), custom_call_target="tpu_custom_call" | custom-call | tf_op jit(solution)/shard_map/pack_edges/pallas_call | solution.py:83
  1.8 1.4 %collective-permute-start = (bf16[12,144,128]{2,1,0:T(8,128)(2,1)S(1)}, bf16[12,144,128]{2,1,0:T(8,128)(2,1)S(1)}, u32[]{:S(2)}, u32[]{:S(2)}) collective-permute-start(bf16[12,144,128]{2,1,0:T(8,128)(2,1)S(1)} %get-tuple-element.42), channel_id=1, source_target_pairs={{0,4},{4,0},{8,12},{12,8},{1,5},{5,1},{9,13},{13,9},{2,6},{6,2},{1... | collective-permute-start | bytes 1327112 | tf_op jit(solution)/shard_map/ppermute | solution.py:457
  3.1 1.9 %collective-permute-start.1 = (bf16[12,144,128]{2,1,0:T(8,128)(2,1)S(1)}, bf16[12,144,128]{2,1,0:T(8,128)(2,1)S(1)}, u32[]{:S(2)}, u32[]{:S(2)}) collective-permute-start(bf16[12,144,128]{2,1,0:T(8,128)(2,1)S(1)} %get-tuple-element.43), channel_id=1, source_target_pairs={{4,8},{8,4},{5,9},{9,5},{6,10},{10,6},{7,11},{11,7},{20,24},{24,20... | collective-permute-start | bytes 1327112 | tf_op jit(solution)/shard_map/ppermute | solution.py:458
  5.0 0.1 collective-permute-start.2
  5.1 0.0 copy-start.3
  5.1 3.4 %collective-permute-start.3 = (bf16[12,128,128]{2,1,0:T(8,128)(2,1)S(1)}, bf16[12,128,128]{2,1,0:T(8,128)(2,1)S(1)}, u32[]{:S(2)}, u32[]{:S(2)}) collective-permute-start(bf16[12,128,128]{2,1,0:T(8,128)(2,1)S(1)} %get-tuple-element.51), channel_id=1, source_target_pairs={{4,8},{8,4},{5,9},{9,5},{6,10},{10,6},{7,11},{11,7},{20,24},{24,20... | collective-permute-start | bytes 1179656 | tf_op jit(solution)/shard_map/ppermute | solution.py:458
  8.5 0.0 copy-done
  8.5 0.0 copy-done.1
  8.5 3.2 %inner_steps.1 = (f32[8,12,64,128]{3,2,1,0:T(8,128)S(1)}, f32[8,12,64,128]{3,2,1,0:T(8,128)S(1)}, f32[8,12,64,128]{3,2,1,0:T(8,128)S(1)}) custom-call(bf16[8,12,64,128]{3,2,1,0:T(8,128)(2,1)S(1)} %bitcast.4, bf16[3,12,8,128]{3,2,1,0:T(8,128)(2,1)S(1)} %bitcast.8), custom_call_target="tpu_custom_call" | custom-call | flops 4000000000 | tf_op jit(solution)/shard_map/inner_steps/pallas_call | solution.py:162
  11.7 1.1 %collective-permute-done.one.one0 = bf16[12,144,128]{2,1,0:T(8,128)(2,1)S(1)} collective-permute-done((bf16[12,144,128]{2,1,0:T(8,128)(2,1)S(1)}, bf16[12,144,128]{2,1,0:T(8,128)(2,1)S(1)}, u32[]{:S(2)}, u32[]{:S(2)}) %collective-permute-start) | collective-permute-done | bytes 442400 | tf_op jit(solution)/shard_map/ppermute | solution.py:457
  12.9 2.9 %collective-permute-done.1.two.two0 = bf16[12,144,128]{2,1,0:T(8,128)(2,1)S(1)} collective-permute-done((bf16[12,144,128]{2,1,0:T(8,128)(2,1)S(1)}, bf16[12,144,128]{2,1,0:T(8,128)(2,1)S(1)}, u32[]{:S(2)}, u32[]{:S(2)}) %collective-permute-start.1) | collective-permute-done | bytes 442400 | tf_op jit(solution)/shard_map/ppermute | solution.py:458
  15.7 0.0 copy-done.3
  15.7 5.8 %transport.2 = (bf16[2,32,1536]{2,1,0:T(8,128)(2,1)S(1)}, bf16[2,32,1536]{2,1,0:T(8,128)(2,1)S(1)}, bf16[2,32,1536]{2,1,0:T(8,128)(2,1)S(1)}, bf16[2,32,1536]{2,1,0:T(8,128)(2,1)S(1)}) custom-call(s32[8]{0:T(128)S(1)} %copy-done.3, bf16[8,12,64,128]{3,2,1,0:T(8,128)(2,1)S(1)} %bitcast.5, bf16[3,12,8,128]{3,2,1,0:T(8,128)(2,1)S(1)} %bitcast.9, ...), custom_call_target="tpu_custom_call" | custom-call | flops 6000000000 | tf_op jit(solution)/shard_map/transport/pallas_call | solution.py:243
  21.6 0.3 collective-permute-start.4
  21.9 3.6 %collective-permute-start.5 = (bf16[2,32,1536]{2,1,0:T(8,128)(2,1)S(1)}, bf16[2,32,1536]{2,1,0:T(8,128)(2,1)S(1)}, u32[]{:S(2)}, u32[]{:S(2)}) collective-permute-start(bf16[2,32,1536]{2,1,0:T(8,128)(2,1)S(1)} %get-tuple-element.62), channel_id=1, source_target_pairs={{0,1},{1,0},{2,3},{3,2},{4,5},{5,4},{6,7},{7,6},{8,9},{9,8},{10,11... | collective-permute-start | bytes 589832 | tf_op jit(solution)/shard_map/ppermute | solution.py:467
  25.5 0.0 copy-start.4
  25.5 0.0 copy-start.2
  25.5 1.1 %collective-permute-start.8 = (bf16[2,32,1536]{2,1,0:T(8,128)(2,1)S(1)}, bf16[2,32,1536]{2,1,0:T(8,128)(2,1)S(1)}, u32[]{:S(2)}, u32[]{:S(2)}) collective-permute-start(bf16[2,32,1536]{2,1,0:T(8,128)(2,1)S(1)} %get-tuple-element.65), channel_id=1, source_target_pairs={{0,3},{1,2},{2,1},{3,0},{4,7},{5,6},{6,5},{7,4},{8,11},{9,10},{10,... | collective-permute-start | bytes 589832 | tf_op jit(solution)/shard_map/ppermute | solution.py:467
  26.6 0.0 collective-permute-done.2.one
  26.6 0.0 collective-permute-done.3.two
  26.6 5.8 %transport.3 = (bf16[1,32,1536]{2,1,0:T(8,128)(2,1)S(1)}, bf16[1,32,1536]{2,1,0:T(8,128)(2,1)S(1)}, bf16[1,32,1536]{2,1,0:T(8,128)(2,1)S(1)}, bf16[1,32,1536]{2,...) custom-call(s32[8]{0:T(128)S(1)} %copy-done.3, ...), custom_call_target="tpu_custom_call" | custom-call | flops 6000000000 | tf_op jit(solution)/shard_map/transport/pallas_call | solution.py:243
  32.4 0.0 collective-permute-done.4.refs_4_
  32.4 0.6 collective-permute-start.13
  33.0 0.3 collective-permute-start.14
  33.3 1.4 %collective-permute-start.15 = (bf16[1,32,1536]{2,1,0:T(8,128)(2,1)S(1)}, bf16[1,32,1536]{2,1,0:T(8,128)(2,1)S(1)}, u32[]{:S(2)}, u32[]{:S(2)}) collective-permute-start(bf16[1,32,1536]{2,1,0:T(8,128)(2,1)S(1)} %get-tuple-element.74), channel_id=1, source_target_pairs={{0,3},{1,2},{2,1},{3,0},{4,7},{5,6},{6,5},{7,4},{8,11},{9,10},{10,... | collective-permute-start | bytes 294920 | tf_op jit(solution)/shard_map/ppermute | solution.py:467
  34.7 0.0 copy-done.4
  34.7 0.0 collective-permute-done.5.refs_2_
  34.7 0.2 collective-permute-start.6
  35.0 0.0 collective-permute-done.8.refs_6_
  35.0 0.3 collective-permute-start.7
  35.2 0.0 collective-permute-done.13.refs_3_
  35.2 1.7 %collective-permute-start.9 = (bf16[1,32,1536]{2,1,0:T(8,128)(2,1)S(1)}, bf16[1,32,1536]{2,1,0:T(8,128)(2,1)S(1)}, u32[]{:S(2)}, u32[]{:S(2)}) collective-permute-start(bf16[1,32,1536]{2,1,0:T(8,128)(2,1)S(1)} %get-tuple-element.66), channel_id=1, source_target_pairs={{0,3},{1,2},{2,1},{3,0},{4,7},{5,6},{6,5},{7,4},{8,11},{9,10},{10,... | collective-permute-start | bytes 294920 | tf_op jit(solution)/shard_map/ppermute | solution.py:467
  37.0 0.4 collective-permute-done.14.refs_5_
  37.4 2.7 %collective-permute-done.15.refs_7_ = bf16[1,32,1536]{2,1,0:T(8,128)(2,1)S(1)} collective-permute-done((bf16[1,32,1536]{2,1,0:T(8,128)(2,1)S(1)}, bf16[1,32,1536]{2,1,0:T(8,128)(2,1)S(1)}, u32[]{:S(2)}, u32[]{:S(2)}) %collective-permute-start.15) | collective-permute-done | bytes 98336 | tf_op jit(solution)/shard_map/ppermute | solution.py:467
  40.1 0.0 copy-done.2
  40.1 19.9 %fit.3 = (bf16[12,64,128]{2,1,0:T(8,128)(2,1)S(1)}, bf16[12,64,128]{2,1,0:T(8,128)(2,1)S(1)}, bf16[12,64,128]{2,1,0:T(8,128)(2,1)S(1)}, bf16[12,64,128]{2,1,0:T(8,128)(2,1)S(1)}) custom-call(s32[2,1,1536]{2,1,0:T(1,128)S(1)} %reshape.3.mask, bf16[2,256,1536]{2,1,0:T(8,128)(2,1)S(1)} %copy-done.2, bf16[2,32,1536]{2,1,0:T(8,128)(2,1)S(1)} %get-tuple-element.48.refs_0_, ...), custom_call_target="tpu_custom_call" | custom-call | flops 3000000000 | tf_op jit(solution)/shard_map/fit/pallas_call | solution.py:380
  60.0 0.1 collective-permute-start.16
  60.1 0.3 collective-permute-start.17
  60.4 0.0 collective-permute-done.6.refs_3_
  60.5 1.8 %collective-permute-start.18 = (bf16[12,64,128]{2,1,0:T(8,128)(2,1)S(1)}, bf16[12,64,128]{2,1,0:T(8,128)(2,1)S(1)}, u32[]{:S(2)}, u32[]{:S(2)}) collective-permute-start(bf16[12,64,128]{2,1,0:T(8,128)(2,1)S(1)} %get-tuple-element.78), channel_id=1, source_target_pairs={{0,3},{1,2},{2,1},{3,0},{4,7},{5,6},{6,5},{7,4},{8,11},{9,10},{10,... | collective-permute-start | bytes 589832 | tf_op jit(solution)/shard_map/ppermute | solution.py:467
  62.3 0.0 collective-permute-done.7.refs_5_
  62.3 0.0 collective-permute-done.9.refs_7_
  62.3 19.8 %fit.2 = (bf16[12,64,128]{2,1,0:T(8,128)(2,1)S(1)}, bf16[12,64,128]{2,1,0:T(8,128)(2,1)S(1)}, bf16[12,64,128]{2,1,0:T(8,128)(2,1)S(1)}, bf16[12,64,128]{2,1,0:T(8,128)(2,1)S(1)}) custom-call(s32[2,1,1536]{2,1,0:T(1,128)S(1)} %reshape.3.mask, bf16[2,256,1536]{2,1,0:T(8,128)(2,1)S(1)} %copy-done.2, bf16[2,32,1536]{2,1,0:T(8,128)(2,1)S(1)} %get-tuple-element.48.refs_0_, ...), custom_call_target="tpu_custom_call" | custom-call | flops 3000000000 | tf_op jit(solution)/shard_map/fit/pallas_call | solution.py:380
  82.0 0.1 collective-permute-start.10
  82.1 0.3 collective-permute-start.11
  82.4 0.0 collective-permute-done.16.refs_1_
  82.4 1.8 %collective-permute-start.12 = (bf16[12,64,128]{2,1,0:T(8,128)(2,1)S(1)}, bf16[12,64,128]{2,1,0:T(8,128)(2,1)S(1)}, u32[]{:S(2)}, u32[]{:S(2)}) collective-permute-start(bf16[12,64,128]{2,1,0:T(8,128)(2,1)S(1)} %get-tuple-element.70), channel_id=1, source_target_pairs={{0,3},{1,2},{2,1},{3,0},{4,7},{5,6},{6,5},{7,4},{8,11},{9,10},{10,... | collective-permute-start | bytes 589832 | tf_op jit(solution)/shard_map/ppermute | solution.py:467
  84.2 0.0 collective-permute-done.17.refs_2_
  84.2 0.0 collective-permute-done.18.refs_3_
  84.2 1.5 %place.2.refs_4_ = bf16[8,12,64,128]{3,2,1,0:T(8,128)(2,1)} custom-call(s32[8]{0:T(128)S(1)} %copy-done.3, bf16[12,64,128]{2,1,0:T(8,128)(2,1)S(1)} %get-tuple-element.75.refs_0_, bf16[12,64,128]{2,1,0:T(8,128)(2,1)S(1)} %collective-permute-done.16.refs_1_, bf16[12,64,128]{2,1,0:T(8,128)(2,1)S(1)} %collective-permute-done.17.refs_2_, ...), custom_call_target="tpu_custom_call" | custom-call | flops 1500000000 | tf_op jit(solution)/shard_map/place/pallas_call | solution.py:423
  85.7 0.0 collective-permute-done.10.refs_1_
  85.7 2.5 %collective-permute-done.11.refs_2_ = bf16[12,64,128]{2,1,0:T(8,128)(2,1)S(1)} collective-permute-done((bf16[12,64,128]{2,1,0:T(8,128)(2,1)S(1)}, bf16[12,64,128]{2,1,0:T(8,128)(2,1)S(1)}, u32[]{:S(2)}, u32[]{:S(2)}) %collective-permute-start.11) | collective-permute-done | bytes 196640 | tf_op jit(solution)/shard_map/ppermute | solution.py:467
  88.2 4.8 %collective-permute-done.12.refs_3_ = bf16[12,64,128]{2,1,0:T(8,128)(2,1)S(1)} collective-permute-done((bf16[12,64,128]{2,1,0:T(8,128)(2,1)S(1)}, bf16[12,64,128]{2,1,0:T(8,128)(2,1)S(1)}, u32[]{:S(2)}, u32[]{:S(2)}) %collective-permute-start.12) | collective-permute-done | bytes 196640 | tf_op jit(solution)/shard_map/ppermute | solution.py:467
  93.0 1.5 %place.3 = bf16[8,12,64,128]{3,2,1,0:T(8,128)(2,1)} custom-call(s32[8]{0:T(128)S(1)} %copy-done.3, bf16[12,64,128]{2,1,0:T(8,128)(2,1)S(1)} %get-tuple-element.67.refs_0_, bf16[12,64,128]{2,1,0:T(8,128)(2,1)S(1)} %collective-permute-done.10.refs_1_, bf16[12,64,128]{2,1,0:T(8,128)(2,1)S(1)} %collective-permute-done.11.refs_2_, ...), custom_call_target="tpu_custom_call", output_to_operand_aliasing={{}: (5, {})} | custom-call | flops 1500000000 | tf_op jit(solution)/shard_map/place/pallas_call | solution.py:423
  (1 shorter events, 0.0 us)
Async XLA Ops:
  0.0 8.5 %copy-start = (bf16[8,64,12,128]{3,1,2,0:T(8,128)(2,1)S(1)}, bf16[8,64,12,128]{3,1,2,0:T(8,128)(2,1)}, u32[]{:S(2)}) copy-start(bf16[8,64,12,128]{3,1,2,0:T(8,128)(2,1)} %param.5) | copy-start | bytes 4718596
  0.0 8.5 %copy-start.1 = (bf16[3,8,12,128]{3,1,2,0:T(8,128)(2,1)S(1)}, bf16[3,8,12,128]{3,1,2,0:T(8,128)(2,1)}, u32[]{:S(2)}) copy-start(bf16[3,8,12,128]{3,1,2,0:T(8,128)(2,1)} %param.6) | copy-start | bytes 221188
  1.8 11.1 %collective-permute-start = (bf16[12,144,128]{2,1,0:T(8,128)(2,1)S(1)}, bf16[12,144,128]{2,1,0:T(8,128)(2,1)S(1)}, u32[]{:S(2)}, u32[]{:S(2)}) collective-permute-start(bf16[12,144,128]{2,1,0:T(8,128)(2,1)S(1)} %get-tuple-element.42), channel_id=1, source_target_pairs={{0,4},{4,0},{8,12},{12,8},{1,5},{5,1},{9,13},{13,9},{2,6},{6,2},{1... | collective-permute-start | bytes 1327112 | tf_op jit(solution)/shard_map/ppermute | solution.py:457
  3.1 12.6 %collective-permute-start.1 = (bf16[12,144,128]{2,1,0:T(8,128)(2,1)S(1)}, bf16[12,144,128]{2,1,0:T(8,128)(2,1)S(1)}, u32[]{:S(2)}, u32[]{:S(2)}) collective-permute-start(bf16[12,144,128]{2,1,0:T(8,128)(2,1)S(1)} %get-tuple-element.43), channel_id=1, source_target_pairs={{4,8},{8,4},{5,9},{9,5},{6,10},{10,6},{7,11},{11,7},{20,24},{24,20... | collective-permute-start | bytes 1327112 | tf_op jit(solution)/shard_map/ppermute | solution.py:458
  5.0 21.6 %collective-permute-start.2 = (bf16[12,128,128]{2,1,0:T(8,128)(2,1)S(1)}, bf16[12,128,128]{2,1,0:T(8,128)(2,1)S(1)}, u32[]{:S(2)}, u32[]{:S(2)}) collective-permute-start(bf16[12,128,128]{2,1,0:T(8,128)(2,1)S(1)} %get-tuple-element.50), channel_id=1, source_target_pairs={{0,4},{4,0},{8,12},{12,8},{1,5},{5,1},{9,13},{13,9},{2,6},{6,2},{1... | collective-permute-start | bytes 1179656 | tf_op jit(solution)/shard_map/ppermute | solution.py:457
  5.1 10.6 %copy-start.3 = (s32[8]{0:T(128)S(1)}, s32[8]{0:T(128)}, u32[]{:S(2)}) copy-start(s32[8]{0:T(128)} %slots.6) | copy-start | bytes 100
  5.1 21.5 %collective-permute-start.3 = (bf16[12,128,128]{2,1,0:T(8,128)(2,1)S(1)}, bf16[12,128,128]{2,1,0:T(8,128)(2,1)S(1)}, u32[]{:S(2)}, u32[]{:S(2)}) collective-permute-start(bf16[12,128,128]{2,1,0:T(8,128)(2,1)S(1)} %get-tuple-element.51), channel_id=1, source_target_pairs={{4,8},{8,4},{5,9},{9,5},{6,10},{10,6},{7,11},{11,7},{20,24},{24,20... | collective-permute-start | bytes 1179656 | tf_op jit(solution)/shard_map/ppermute | solution.py:458
  21.6 10.9 %collective-permute-start.4 = (bf16[2,32,1536]{2,1,0:T(8,128)(2,1)S(1)}, bf16[2,32,1536]{2,1,0:T(8,128)(2,1)S(1)}, u32[]{:S(2)}, u32[]{:S(2)}) collective-permute-start(bf16[2,32,1536]{2,1,0:T(8,128)(2,1)S(1)} %get-tuple-element.60), channel_id=1, source_target_pairs={{0,2},{1,3},{2,0},{3,1},{4,6},{5,7},{6,4},{7,5},{8,10},{9,11},{10,... | collective-permute-start | bytes 589832 | tf_op jit(solution)/shard_map/ppermute | solution.py:467
  21.9 12.9 %collective-permute-start.5 = (bf16[2,32,1536]{2,1,0:T(8,128)(2,1)S(1)}, bf16[2,32,1536]{2,1,0:T(8,128)(2,1)S(1)}, u32[]{:S(2)}, u32[]{:S(2)}) collective-permute-start(bf16[2,32,1536]{2,1,0:T(8,128)(2,1)S(1)} %get-tuple-element.62), channel_id=1, source_target_pairs={{0,1},{1,0},{2,3},{3,2},{4,5},{5,4},{6,7},{7,6},{8,9},{9,8},{10,11... | collective-permute-start | bytes 589832 | tf_op jit(solution)/shard_map/ppermute | solution.py:467
  25.5 9.2 %copy-start.4 = (s32[2,1536]{1,0:T(2,128)S(1)}, s32[2,1536]{1,0:T(2,128)}, u32[]{:S(2)}) copy-start(s32[2,1536]{1,0:T(2,128)} %param.8) | copy-start | bytes 36868
  25.5 14.6 %copy-start.2 = (bf16[2,256,1536]{2,1,0:T(8,128)(2,1)S(1)}, bf16[2,256,1536]{2,1,0:T(8,128)(2,1)}, u32[]{:S(2)}) copy-start(bf16[2,256,1536]{2,1,0:T(8,128)(2,1)} %density.3) | copy-start | bytes 4718596
  25.5 9.5 %collective-permute-start.8 = (bf16[2,32,1536]{2,1,0:T(8,128)(2,1)S(1)}, bf16[2,32,1536]{2,1,0:T(8,128)(2,1)S(1)}, u32[]{:S(2)}, u32[]{:S(2)}) collective-permute-start(bf16[2,32,1536]{2,1,0:T(8,128)(2,1)S(1)} %get-tuple-element.65), channel_id=1, source_target_pairs={{0,3},{1,2},{2,1},{3,0},{4,7},{5,6},{6,5},{7,4},{8,11},{9,10},{10,... | collective-permute-start | bytes 589832 | tf_op jit(solution)/shard_map/ppermute | solution.py:467
  32.4 2.8 %collective-permute-start.13 = (bf16[1,32,1536]{2,1,0:T(8,128)(2,1)S(1)}, bf16[1,32,1536]{2,1,0:T(8,128)(2,1)S(1)}, u32[]{:S(2)}, u32[]{:S(2)}) collective-permute-start(bf16[1,32,1536]{2,1,0:T(8,128)(2,1)S(1)} %get-tuple-element.72), channel_id=1, source_target_pairs={{0,1},{1,0},{2,3},{3,2},{4,5},{5,4},{6,7},{7,6},{8,9},{9,8},{10,11... | collective-permute-start | bytes 294920 | tf_op jit(solution)/shard_map/ppermute | solution.py:467
  33.0 4.4 %collective-permute-start.14 = (bf16[1,32,1536]{2,1,0:T(8,128)(2,1)S(1)}, bf16[1,32,1536]{2,1,0:T(8,128)(2,1)S(1)}, u32[]{:S(2)}, u32[]{:S(2)}) collective-permute-start(bf16[1,32,1536]{2,1,0:T(8,128)(2,1)S(1)} %get-tuple-element.73), channel_id=1, source_target_pairs={{0,2},{1,3},{2,0},{3,1},{4,6},{5,7},{6,4},{7,5},{8,10},{9,11},{10,... | collective-permute-start | bytes 294920 | tf_op jit(solution)/shard_map/ppermute | solution.py:467
  33.3 6.8 %collective-permute-start.15 = (bf16[1,32,1536]{2,1,0:T(8,128)(2,1)S(1)}, bf16[1,32,1536]{2,1,0:T(8,128)(2,1)S(1)}, u32[]{:S(2)}, u32[]{:S(2)}) collective-permute-start(bf16[1,32,1536]{2,1,0:T(8,128)(2,1)S(1)} %get-tuple-element.74), channel_id=1, source_target_pairs={{0,3},{1,2},{2,1},{3,0},{4,7},{5,6},{6,5},{7,4},{8,11},{9,10},{10,... | collective-permute-start | bytes 294920 | tf_op jit(solution)/shard_map/ppermute | solution.py:467
  34.7 25.7 %collective-permute-start.6 = (bf16[1,32,1536]{2,1,0:T(8,128)(2,1)S(1)}, bf16[1,32,1536]{2,1,0:T(8,128)(2,1)S(1)}, u32[]{:S(2)}, u32[]{:S(2)}) collective-permute-start(bf16[1,32,1536]{2,1,0:T(8,128)(2,1)S(1)} %get-tuple-element.63), channel_id=1, source_target_pairs={{0,1},{1,0},{2,3},{3,2},{4,5},{5,4},{6,7},{7,6},{8,9},{9,8},{10,11... | collective-permute-start | bytes 294920 | tf_op jit(solution)/shard_map/ppermute | solution.py:467
  35.0 27.3 %collective-permute-start.7 = (bf16[1,32,1536]{2,1,0:T(8,128)(2,1)S(1)}, bf16[1,32,1536]{2,1,0:T(8,128)(2,1)S(1)}, u32[]{:S(2)}, u32[]{:S(2)}) collective-permute-start(bf16[1,32,1536]{2,1,0:T(8,128)(2,1)S(1)} %get-tuple-element.64), channel_id=1, source_target_pairs={{0,2},{1,3},{2,0},{3,1},{4,6},{5,7},{6,4},{7,5},{8,10},{9,11},{10,... | collective-permute-start | bytes 294920 | tf_op jit(solution)/shard_map/ppermute | solution.py:467
  35.2 27.0 %collective-permute-start.9 = (bf16[1,32,1536]{2,1,0:T(8,128)(2,1)S(1)}, bf16[1,32,1536]{2,1,0:T(8,128)(2,1)S(1)}, u32[]{:S(2)}, u32[]{:S(2)}) collective-permute-start(bf16[1,32,1536]{2,1,0:T(8,128)(2,1)S(1)} %get-tuple-element.66), channel_id=1, source_target_pairs={{0,3},{1,2},{2,1},{3,0},{4,7},{5,6},{6,5},{7,4},{8,11},{9,10},{10,... | collective-permute-start | bytes 294920 | tf_op jit(solution)/shard_map/ppermute | solution.py:467
  60.0 22.4 %collective-permute-start.16 = (bf16[12,64,128]{2,1,0:T(8,128)(2,1)S(1)}, bf16[12,64,128]{2,1,0:T(8,128)(2,1)S(1)}, u32[]{:S(2)}, u32[]{:S(2)}) collective-permute-start(bf16[12,64,128]{2,1,0:T(8,128)(2,1)S(1)} %get-tuple-element.76), channel_id=1, source_target_pairs={{0,1},{1,0},{2,3},{3,2},{4,5},{5,4},{6,7},{7,6},{8,9},{9,8},{10,11... | collective-permute-start | bytes 589832 | tf_op jit(solution)/shard_map/ppermute | solution.py:467
  60.1 24.1 %collective-permute-start.17 = (bf16[12,64,128]{2,1,0:T(8,128)(2,1)S(1)}, bf16[12,64,128]{2,1,0:T(8,128)(2,1)S(1)}, u32[]{:S(2)}, u32[]{:S(2)}) collective-permute-start(bf16[12,64,128]{2,1,0:T(8,128)(2,1)S(1)} %get-tuple-element.77), channel_id=1, source_target_pairs={{0,2},{1,3},{2,0},{3,1},{4,6},{5,7},{6,4},{7,5},{8,10},{9,11},{10,... | collective-permute-start | bytes 589832 | tf_op jit(solution)/shard_map/ppermute | solution.py:467
  60.5 23.8 %collective-permute-start.18 = (bf16[12,64,128]{2,1,0:T(8,128)(2,1)S(1)}, bf16[12,64,128]{2,1,0:T(8,128)(2,1)S(1)}, u32[]{:S(2)}, u32[]{:S(2)}) collective-permute-start(bf16[12,64,128]{2,1,0:T(8,128)(2,1)S(1)} %get-tuple-element.78), channel_id=1, source_target_pairs={{0,3},{1,2},{2,1},{3,0},{4,7},{5,6},{6,5},{7,4},{8,11},{9,10},{10,... | collective-permute-start | bytes 589832 | tf_op jit(solution)/shard_map/ppermute | solution.py:467
  82.0 3.7 %collective-permute-start.10 = (bf16[12,64,128]{2,1,0:T(8,128)(2,1)S(1)}, bf16[12,64,128]{2,1,0:T(8,128)(2,1)S(1)}, u32[]{:S(2)}, u32[]{:S(2)}) collective-permute-start(bf16[12,64,128]{2,1,0:T(8,128)(2,1)S(1)} %get-tuple-element.68), channel_id=1, source_target_pairs={{0,1},{1,0},{2,3},{3,2},{4,5},{5,4},{6,7},{7,6},{8,9},{9,8},{10,11... | collective-permute-start | bytes 589832 | tf_op jit(solution)/shard_map/ppermute | solution.py:467
  82.1 6.1 %collective-permute-start.11 = (bf16[12,64,128]{2,1,0:T(8,128)(2,1)S(1)}, bf16[12,64,128]{2,1,0:T(8,128)(2,1)S(1)}, u32[]{:S(2)}, u32[]{:S(2)}) collective-permute-start(bf16[12,64,128]{2,1,0:T(8,128)(2,1)S(1)} %get-tuple-element.69), channel_id=1, source_target_pairs={{0,2},{1,3},{2,0},{3,1},{4,6},{5,7},{6,4},{7,5},{8,10},{9,11},{10,... | collective-permute-start | bytes 589832 | tf_op jit(solution)/shard_map/ppermute | solution.py:467
  82.4 10.6 %collective-permute-start.12 = (bf16[12,64,128]{2,1,0:T(8,128)(2,1)S(1)}, bf16[12,64,128]{2,1,0:T(8,128)(2,1)S(1)}, u32[]{:S(2)}, u32[]{:S(2)}) collective-permute-start(bf16[12,64,128]{2,1,0:T(8,128)(2,1)S(1)} %get-tuple-element.70), channel_id=1, source_target_pairs={{0,3},{1,2},{2,1},{3,0},{4,7},{5,6},{6,5},{7,4},{8,11},{9,10},{10,... | collective-permute-start | bytes 589832 | tf_op jit(solution)/shard_map/ppermute | solution.py:467

commit v5 on v4

--- a/solution.py
+++ b/solution.py
@@ -16,7 +16,7 @@
 BF16 = jnp.bfloat16
 VEL_ROWS = 16
 WIDTHS = (32, 32)
-COST_I, COST_T, COST_F, COST_P = 4 * 10**9, 6 * 10**9, 3 * 10**9, 15 * 10**8
+COST_I, COST_T, COST_F, COST_P = 4 * 10**9, 10**9, 3 * 10**9, 15 * 10**8
 EASY = 1.08
 FAIR = 3.8
 
@@ -37,8 +37,8 @@
     return lax.rem(lax.axis_index("gz"), 2)
 
 
-def pack_kernel(widths, atlas, vel, *refs):
-    outs, (held, boxes, sems) = refs[:-3], refs[-3:]
+def pack_kernel(width, start, atlas, vel, low, high, held, boxes, sems):
+    outs = (low, high)
     rows, ny = atlas.shape[:2]
     odd = odd_slab()
     slots = TSTEPS - 1
@@ -49,46 +49,42 @@
         copies.append(pltpu.make_async_copy(source, target, sems.at[next(count)]))
         copies[-1].start()
 
-    move(vel, held)
-    start = 0
-    for part, width in enumerate(widths):
+    if start == 0:
+        move(vel, held)
+    for side in range(2):
+        first = jnp.where(odd == side, rows - TSTEPS, 0)
+        for step in range(TSTEPS):
+            move(
+                atlas.at[first + step, :, pl.ds(start, width), :],
+                outs[side].at[:, pl.ds(step * width, width), :],
+            )
+    if start == 0:
+        copies.pop(0).wait()
+        speed = held[...].astype(F32)
+        filler = jnp.zeros((ny, VEL_ROWS - 3 * slots, LANES), F32)
+        edges = []
+        for first in (0, rows - slots):
+            lines = [speed[k, :, first : first + slots, :] for k in range(3)]
+            edges.append(jnp.concatenate(lines + [filler], axis=1))
         for side in range(2):
-            first = jnp.where(odd == side, rows - TSTEPS, 0)
-            for step in range(TSTEPS):
-                move(
-                    atlas.at[first + step, :, pl.ds(start, width), :],
-                    outs[2 * part + side].at[:, pl.ds(step * width, width), :],
-                )
-        start += width
-    copies.pop(0).wait()
-    speed = held[...].astype(F32)
-    filler = jnp.zeros((ny, VEL_ROWS - 3 * slots, LANES), F32)
-    edges = []
-    for first in (0, rows - slots):
-        lines = [speed[k, :, first : first + slots, :] for k in range(3)]
-        edges.append(jnp.concatenate(lines + [filler], axis=1))
-    for side in range(2):
-        boxes[side] = jnp.where(odd == side, edges[1], edges[0]).astype(BF16)
-        move(boxes.at[side], outs[side].at[:, pl.ds(TSTEPS * widths[0], VEL_ROWS), :])
+            boxes[side] = jnp.where(odd == side, edges[1], edges[0]).astype(BF16)
+            move(boxes.at[side], outs[side].at[:, pl.ds(TSTEPS * width, VEL_ROWS), :])
     for copy in copies:
         copy.wait()
 
 
-def pack(atlas, vel, widths):
+def pack(atlas, vel, width, start):
     ny = atlas.shape[1]
-    shapes = []
-    for part, width in enumerate(widths):
-        rows = TSTEPS * width + (VEL_ROWS if part == 0 else 0)
-        shapes += [jax.ShapeDtypeStruct((ny, rows, LANES), BF16)] * 2
+    rows = TSTEPS * width + (VEL_ROWS if start == 0 else 0)
     return pl.pallas_call(
-        functools.partial(pack_kernel, widths),
-        out_shape=shapes,
+        functools.partial(pack_kernel, width, start),
+        out_shape=[jax.ShapeDtypeStruct((ny, rows, LANES), BF16)] * 2,
         in_specs=[spec(pl.ANY)] * 2,
-        out_specs=[spec(pl.ANY)] * len(shapes),
+        out_specs=[spec(pl.ANY)] * 2,
         scratch_shapes=[
             pltpu.VMEM(vel.shape, BF16),
             pltpu.VMEM((2, ny, VEL_ROWS, LANES), BF16),
-            pltpu.SemaphoreType.DMA((2 * len(widths) * TSTEPS + 3,)),
+            pltpu.SemaphoreType.DMA((2 * TSTEPS + 3,)),
         ],
         compiler_params=params(8),
         name="pack_edges",
@@ -175,85 +171,111 @@
     )(atlas, vel)
 
 
-def transport_kernel(
-    peers, per, joined, width, start, slots, atlas, vel, one, two, one0, two0, *refs
-):
-    inner_levels, refs = refs[: TSTEPS - 1], refs[TSTEPS - 1 :]
-    outs, (state, speed, coef) = refs[:-3], refs[-3:]
+def side_steps(high, width, start, atlas, vel, halo, halo0, levels, state, speed, coef):
     rows, ny = atlas.shape[:2]
-    tail = slice(one0.shape[1] - VEL_ROWS, one0.shape[1])
     deep = rows + 2 * TSTEPS
     edge = TSTEPS - 1
     slab, slabs = lax.axis_index("gz"), lax.axis_size("gz")
-    me = lax.axis_index(("gy", "af"))
-    odd = odd_slab() > 0
-    has_low, has_high = slab > 0, slab < slabs - 1
-
-    def sides(one, two):
-        one, two = one.astype(F32), two.astype(F32)
-        return jnp.where(odd, one, two), jnp.where(odd, two, one)
-
-    below, above = sides(one0[:, tail, :], two0[:, tail, :])
+    has = jnp.where(high, slab < slabs - 1, slab > 0)
+    beyond = halo0[:, halo0.shape[1] - VEL_ROWS :, :].astype(F32)
     for k in range(3):
+        lines = beyond[:, edge * k : edge * (k + 1), :]
         speed[k, :, TSTEPS : TSTEPS + rows, :] = vel[k].astype(F32)
-        speed[k, :, 1:TSTEPS, :] = below[:, edge * k : edge * (k + 1), :]
-        speed[k, :, TSTEPS + rows : TSTEPS + rows + edge, :] = above[:, edge * k : edge * (k + 1), :]
+        speed[k, :, 1:TSTEPS, :] = lines
+        speed[k, :, TSTEPS + rows : TSTEPS + rows + edge, :] = lines
     place = lax.broadcasted_iota(jnp.int32, (1, deep, LANES), 1)
-    inside = ((place >= TSTEPS) | has_low) & ((place < TSTEPS + rows) | has_high)
+    inside = ((place >= TSTEPS) & (place < TSTEPS + rows)) | has
     set_weights(speed, coef, inside & (place > 0) & (place < deep - 1))
 
     channels = slice(start, start + width)
-    for z in (0, 1, rows - 2, rows - 1):
+    base = jnp.where(high, TSTEPS + rows, 0)
+    for step in range(TSTEPS):
+        state[0, base + step] = halo[:, step * width : (step + 1) * width, :].astype(F32)
+    for i in range(2):
+        z = jnp.where(high, rows - 2, 0) + i
         state[0, z + TSTEPS] = atlas[z, :, channels, :].astype(F32)
+        for level in range(1, TSTEPS):
+            z = jnp.where(high, rows - 2 - level, level) + i
+            state[level, z + TSTEPS] = levels[level - 1][z, :, channels, :]
     for step in range(TSTEPS):
-        span = slice(step * width, (step + 1) * width)
-        low, high = sides(one[:, span, :], two[:, span, :])
-        state[0, step] = low
-        state[0, step + TSTEPS + rows] = high
-    for level in range(1, TSTEPS):
-        for z in sorted({level, level + 1, rows - 2 - level, rows - 1 - level}):
-            state[level, z + TSTEPS] = inner_levels[level - 1][z, :, channels, :]
-    for step in range(TSTEPS):
-
-        def first(i):
-            return jnp.where(i < 2, step + 1 + 2 * i, deep - 9 - step + 2 * i)
-
+        first = jnp.where(high, deep - 5 - step, step + 1)
         target = state.at[(step + 1) % TSTEPS]
-        advance_pairs(coef, state.at[step], target, TSTEPS, first)
+        advance_pairs(coef, state.at[step], target, TSTEPS // 2, lambda i: first + 2 * i)
+
+
+def first_kernel(width, start, atlas, vel, halo, halo0, *refs):
+    levels, (done, state, speed, coef) = refs[: TSTEPS - 1], refs[TSTEPS - 1 :]
+    high = odd_slab() == 0
+    side_steps(high, width, start, atlas, vel, halo, halo0, levels, state, speed, coef)
+    first = jnp.where(high, atlas.shape[0] - TSTEPS, 0)
+    for i in range(TSTEPS):
+        done[i] = state[0, first + TSTEPS + i].astype(BF16)
+
+
+def second_kernel(peers, per, joined, width, start, slots, atlas, vel, halo, halo0, *refs):
+    levels, done, refs = refs[: TSTEPS - 1], refs[TSTEPS - 1], refs[TSTEPS:]
+    outs, (moved, state, speed, coef) = refs[:-4], refs[-4:]
+    rows, ny = atlas.shape[:2]
+    high = odd_slab() > 0
+    side_steps(high, width, start, atlas, vel, halo, halo0, levels, state, speed, coef)
     if rows > 2 * TSTEPS:
-        source = inner_levels[-1].at[:, :, channels, :]
+        source = levels[-1].at[:, :, start : start + width, :]
         pairs = (rows - 2 * TSTEPS) // 2
         advance_pairs(coef, source, state.at[0], pairs, lambda i: 2 * TSTEPS + 2 * i, TSTEPS)
-
+        for z in range(TSTEPS, rows - TSTEPS):
+            moved[z] = state[0, z + TSTEPS].astype(BF16)
+    first = jnp.where(high, rows - TSTEPS, 0)
+    other = rows - TSTEPS - first
+    for i in range(TSTEPS):
+        moved[first + i] = state[0, first + TSTEPS + i].astype(BF16)
+        moved[other + i] = done[i]
+    me = lax.axis_index(("gy", "af"))
+    slab = lax.axis_index("gz")
     for k in range(peers):
         for s in range(per):
-            z = slots[(me ^ k) * per + s] - slab * rows + TSTEPS
+            z = slots[(me ^ k) * per + s] - slab * rows
             out = outs[k].at[s] if joined else outs[k * per + s].at[0]
             for y in range(ny):
-                value = state[0, z, y].astype(BF16)
-                out[:, y * LANES : (y + 1) * LANES] = value
-
-
-def transport(slots, atlas, vel, one, two, one0, two0, levels, width, start, peers, per, joined):
+                out[:, y * LANES : (y + 1) * LANES] = moved[z, y]
+
+
+def side_scratch(atlas, width):
     rows, ny = atlas.shape[:2]
     deep = rows + 2 * TSTEPS
-    pixels = ny * LANES
-    out = (per if joined else 1, width, pixels)
+    return [
+        pltpu.VMEM((TSTEPS, deep, ny, width, LANES), F32),
+        pltpu.VMEM((3, ny, deep, LANES), F32),
+        pltpu.VMEM((7, ny, deep, LANES), F32),
+    ]
+
+
+def first_side(atlas, vel, halo, halo0, levels, width, start):
+    return pl.pallas_call(
+        functools.partial(first_kernel, width, start),
+        out_shape=jax.ShapeDtypeStruct((TSTEPS, atlas.shape[1], width, LANES), BF16),
+        in_specs=[spec(pltpu.VMEM)] * (4 + len(levels)),
+        out_specs=spec(pltpu.VMEM),
+        scratch_shapes=side_scratch(atlas, width),
+        compiler_params=params(28),
+        cost_estimate=cost(COST_T),
+        name="first_side",
+    )(atlas, vel, halo, halo0, *levels)
+
+
+def second_side(slots, atlas, vel, halo, halo0, levels, done, width, start, peers, per, joined):
+    rows, ny = atlas.shape[:2]
+    out = (per if joined else 1, width, ny * LANES)
     count = peers if joined else peers * per
     return pl.pallas_call(
-        functools.partial(transport_kernel, peers, per, joined, width, start),
+        functools.partial(second_kernel, peers, per, joined, width, start),
         out_shape=[jax.ShapeDtypeStruct(out, BF16)] * count,
-        in_specs=[spec(pltpu.SMEM)] + [spec(pltpu.VMEM)] * (6 + len(levels)),
+        in_specs=[spec(pltpu.SMEM)] + [spec(pltpu.VMEM)] * (5 + len(levels)),
         out_specs=[spec(pltpu.VMEM)] * count,
-        scratch_shapes=[
-            pltpu.VMEM((TSTEPS, deep, ny, width, LANES), F32),
-            pltpu.VMEM((3, ny, deep, LANES), F32),
-            pltpu.VMEM((7, ny, deep, LANES), F32),
-        ],
+        scratch_shapes=[pltpu.VMEM((rows, ny, width, LANES), BF16)] + side_scratch(atlas, width),
         compiler_params=params(28),
         cost_estimate=cost(COST_T),
-        name="transport",
-    )(slots, atlas, vel, one, two, one0, two0, *levels)
+        name="second_side",
+    )(slots, atlas, vel, halo, halo0, *levels, done)
 
 
 def dot(a, b):
@@ -400,35 +422,32 @@
     )(mask, density, *blocks)
 
 
-def place_kernel(peers, per, section, slots, *refs):
-    blocks = refs[:peers]
-    out, sems = refs[-2], refs[-1]
+def place_kernel(per, which, slots, *refs):
+    blocks, (out, sems) = refs[: len(which)], refs[-2:]
     me = lax.axis_index(("gy", "af"))
     first = lax.axis_index("gz") * out.shape[0]
-    copies = [
-        pltpu.make_async_copy(
-            blocks[k], out.at[slots[(me ^ k) * per + section] - first], sems.at[k]
-        )
-        for k in range(peers)
-    ]
+    copies = []
+    for i, (k, section) in enumerate(which):
+        z = slots[(me ^ k) * per + section] - first
+        copies.append(pltpu.make_async_copy(blocks[i], out.at[z], sems.at[i]))
     for copy in copies:
         copy.start()
     for copy in copies:
         copy.wait()
 
 
-def place(slots, blocks, earlier, rows, section, per):
-    peers = len(blocks)
+def place(slots, returned, which, earlier, rows, per):
+    blocks = [returned[key] for key in which]
     extra = [] if earlier is None else [earlier]
     return pl.pallas_call(
-        functools.partial(place_kernel, peers, per, section),
+        functools.partial(place_kernel, per, which),
         out_shape=jax.ShapeDtypeStruct((rows,) + blocks[0].shape, BF16),
         in_specs=[spec(pltpu.SMEM)]
-        + [spec(pltpu.VMEM)] * peers
+        + [spec(pltpu.VMEM)] * len(blocks)
         + [spec(pl.ANY)] * len(extra),
         out_specs=spec(pl.ANY),
-        scratch_shapes=[pltpu.SemaphoreType.DMA((peers,))],
-        input_output_aliases={1 + peers: 0} if extra else {},
+        scratch_shapes=[pltpu.SemaphoreType.DMA((len(blocks),))],
+        input_output_aliases={1 + len(blocks): 0} if extra else {},
         compiler_params=params(8),
         cost_estimate=cost(COST_P),
         name="place",
@@ -448,18 +467,20 @@
     mask = pixel_mask.reshape(per, 1, -1)
     slots = section_slice
 
-    edges = pack(atlas, vel, widths)
+    edges = pack(atlas, vel, widths[0], 0)
     ones = [(i, i ^ 1) for i in range(slabs)]
     twos = [(i, i + 1) for i in range(1, slabs - 1, 2)]
     twos += [(j, i) for i, j in twos]
+    own, _ = lax.optimization_barrier((atlas, edges[0]))
+    levels = inner(own, vel)
     halos = []
     for part in range(chunks):
-        one = lax.ppermute(edges[2 * part], "gz", ones)
-        two = lax.ppermute(edges[2 * part + 1], "gz", twos)
+        if part > 0:
+            later, _ = lax.optimization_barrier((atlas, edges[0]))
+            edges = pack(later, vel, widths[part], sum(widths[:part]))
+        one = lax.ppermute(edges[0], "gz", ones)
+        two = lax.ppermute(edges[1], "gz", twos)
         halos.append((one, two))
-
-    own, _ = lax.optimization_barrier((atlas, edges[0]))
-    levels = inner(own, vel)
 
     def swap(block, k):
         if k == 0:
@@ -470,27 +491,43 @@
     start = 0
     for part, width in enumerate(widths):
         joined = part < chunks - 1
-        order = slots
+        one, two = halos[part]
         if part > 0:
-            order, _ = lax.optimization_barrier((slots, moved[0]))
-        moved = transport(
-            order, atlas, vel, *halos[part], *halos[0], levels, width, start, peers, per, joined
+            one, _ = lax.optimization_barrier((one, moved[0]))
+        done = first_side(atlas, vel, one, halos[0][0], levels, width, start)
+        moved = second_side(
+            slots, atlas, vel, two, halos[0][1], levels, done, width, start, peers, per, joined
         )
         start += width
         if part > 0:
-            moved, _ = lax.optimization_barrier((moved, arrived[0, peers // 2, part - 1]))
+            moved, waiting, _ = lax.optimization_barrier(
+                (moved, waiting, arrived[0, peers // 2, part - 1])
+            )
+            waiting = swap(waiting, 1)
+            for section in range(per):
+                arrived[section, 1, part - 1] = waiting
         for s in range(1 if joined else per):
-            for k in range(peers):
-                block = swap(moved[k if joined else k * per + s], k)
+            for k in reversed(range(peers)):
+                block = moved[k if joined else k * per + s]
+                if joined and k == 1:
+                    waiting = block
+                    continue
+                block = swap(block, k)
                 for section in range(per) if joined else [s]:
                     arrived[section, k, part] = block
 
-    result = None
+    returned = {}
     for s in range(per):
         blocks = [arrived[s, k, part] for k in range(peers) for part in range(chunks)]
         gradients = fit(mask, section_density, s, blocks, chunks, peers)
-        returned = [swap(gradients[k], k) for k in range(peers)]
-        result = place(slots, returned, result, rows, s, per)
+        for k in range(peers):
+            returned[k, s] = swap(gradients[k], k)
+    last = per - 1
+    early = [key for key in returned if key[1] < last or key[0] < peers // 2]
+    late = [(k, last) for k in range(peers // 2, peers - 1)]
+    result = place(slots, returned, early, None, rows, per)
+    result = place(slots, returned, late, result, rows, per)
+    result = place(slots, returned, [(peers - 1, last)], result, rows, per)
     return jnp.transpose(result, (0, 2, 1, 3))
 
 

time: 94.8 us -> 93.1 us (0.982)
  waiting for transfers between devices: 14.4 us -> 11 us
  Pallas kernels: 59.2 us -> 62.3 us
  starting transfers between devices: 20.6 us -> 18.4 us
    pallas_call x5 -> x9, Pallas kernels: 16.3 us -> 19.2 us  [the longest x2 6.67 us: second_side(): pl.pallas_call(functools.partial(second_kernel, peers, per, joined, width...]
    ppermute x4, waiting for transfers between devices: 3.99 us -> 1.7 us  [the longest x2 1.69 us: body(): one = lax.ppermute(edges[0], 'gz', ones)]
    ppermute x15, starting transfers between devices: 13.9 us -> 11.7 us  [swap(): return lax.ppermute(block, ('gy', 'af'), [(i, i ^ k) for i in range(peers)])]
    ppermute x15, waiting for transfers between devices: 10.5 us -> 9.35 us  [swap(): return lax.ppermute(block, ('gy', 'af'), [(i, i ^ k) for i in range(peers)])]
  transfers between devices with their start and end apart: 19 -> 19, of which waited for: 6 -> 5; matrix products, arithmetic and copies ran while one was open for 0% -> 0% of each run, Pallas kernels for 59% -> 65%
where the time goes in v5:
time: 93.1 us; the launch traced here: 92.3 us
  Pallas kernels  62.3 us (67%)
  starting transfers between devices  18.4 us (20%)
  waiting for transfers between devices  11 us (12%)
    pallas_call x2, Pallas kernels, fit(): pl.pallas_call(functools.partial(fit_kernel, parts, peers), grid=(1,), ou...  39.9 us
    ppermute x15, starting transfers between devices, swap(): return lax.ppermute(block, ('gy', 'af'), [(i, i ^ k) for i in range(peers)])  11.7 us
    ppermute x15, waiting for transfers between devices, swap(): return lax.ppermute(block, ('gy', 'af'), [(i, i ^ k) for i in range(peers)])  9.35 us
    pallas_call x2, Pallas kernels, second_side(): pl.pallas_call(functools.partial(second_kernel, peers, per, joined, width...  6.67 us
    pallas_call x2, Pallas kernels, first_side(): pl.pallas_call(functools.partial(first_kernel, width, start), out_shape=j...  5.66 us
    ppermute x2, starting transfers between devices, body(): two = lax.ppermute(edges[1], 'gz', twos)  5.27 us
    pallas_call x3, Pallas kernels, place(): pl.pallas_call(functools.partial(place_kernel, per, which), out_shape=jax...  4.09 us
    pallas_call x1, Pallas kernels, inner(): pl.pallas_call(inner_kernel, out_shape=[level] * (TSTEPS - 1), in_specs=[...  3.21 us
  transfers between devices with their start and end apart: 19, of which 5 were waited for; matrix products, arithmetic and copies ran while one was open for 0% of the time, Pallas kernels for 65%

profile of v5, /device:TPU:23, one launch (start us, length us, event | category | flops | bytes accessed | tf_op | source)
XLA Modules:
  0.0 92.3 jit_solution(11378099969891444094)
XLA Ops:
  0.0 0.0 copy-start
  0.0 0.0 copy-start.1
  0.0 1.4 %pack_edges.2 = (bf16[12,144,128]{2,1,0:T(8,128)(2,1)S(1)}, bf16[12,144,128]{2,1,0:T(8,128)(2,1)S(1)}) custom-call(bf16[8,12,64,128]{3,2,1,0:T(8,128)(2,1)} %bitcast.3, bf16[3,12,8,128]{3,2,1,0:T(8,128)(2,1)} %bitcast.10), custom_call_target="tpu_custom_call" | custom-call | tf_op jit(solution)/shard_map/pack_edges/pallas_call | solution.py:79
  1.5 1.4 %collective-permute-start.1 = (bf16[12,144,128]{2,1,0:T(8,128)(2,1)S(1)}, bf16[12,144,128]{2,1,0:T(8,128)(2,1)S(1)}, u32[]{:S(2)}, u32[]{:S(2)}) collective-permute-start(bf16[12,144,128]{2,1,0:T(8,128)(2,1)S(1)} %get-tuple-element.44), channel_id=1, source_target_pairs={{0,4},{4,0},{8,12},{12,8},{1,5},{5,1},{9,13},{13,9},{2,6},{6,2},{1... | collective-permute-start | bytes 1327112 | tf_op jit(solution)/shard_map/ppermute | solution.py:481
  2.8 1.9 %collective-permute-start = (bf16[12,144,128]{2,1,0:T(8,128)(2,1)S(1)}, bf16[12,144,128]{2,1,0:T(8,128)(2,1)S(1)}, u32[]{:S(2)}, u32[]{:S(2)}) collective-permute-start(bf16[12,144,128]{2,1,0:T(8,128)(2,1)S(1)} %get-tuple-element.43), channel_id=1, source_target_pairs={{4,8},{8,4},{5,9},{9,5},{6,10},{10,6},{7,11},{11,7},{20,24},{24,20... | collective-permute-start | bytes 1327112 | tf_op jit(solution)/shard_map/ppermute | solution.py:482
  4.7 1.3 %pack_edges.3 = (bf16[12,128,128]{2,1,0:T(8,128)(2,1)S(1)}, bf16[12,128,128]{2,1,0:T(8,128)(2,1)S(1)}) custom-call(bf16[8,12,64,128]{3,2,1,0:T(8,128)(2,1)} %bitcast.4, bf16[3,12,8,128]{3,2,1,0:T(8,128)(2,1)} %bitcast.11), custom_call_target="tpu_custom_call" | custom-call | tf_op jit(solution)/shard_map/pack_edges/pallas_call | solution.py:79
  6.1 0.1 collective-permute-start.3
  6.1 3.4 %collective-permute-start.2 = (bf16[12,128,128]{2,1,0:T(8,128)(2,1)S(1)}, bf16[12,128,128]{2,1,0:T(8,128)(2,1)S(1)}, u32[]{:S(2)}, u32[]{:S(2)}) collective-permute-start(bf16[12,128,128]{2,1,0:T(8,128)(2,1)S(1)} %get-tuple-element.50), channel_id=1, source_target_pairs={{4,8},{8,4},{5,9},{9,5},{6,10},{10,6},{7,11},{11,7},{20,24},{24,20... | collective-permute-start | bytes 1179656 | tf_op jit(solution)/shard_map/ppermute | solution.py:482
  9.5 0.0 copy-done
  9.5 0.0 copy-done.1
  9.5 3.2 %inner_steps.1 = (f32[8,12,64,128]{3,2,1,0:T(8,128)S(1)}, f32[8,12,64,128]{3,2,1,0:T(8,128)S(1)}, f32[8,12,64,128]{3,2,1,0:T(8,128)S(1)}) custom-call(bf16[8,12,64,128]{3,2,1,0:T(8,128)(2,1)S(1)} %bitcast.5, bf16[3,12,8,128]{3,2,1,0:T(8,128)(2,1)S(1)} %bitcast.12), custom_call_target="tpu_custom_call" | custom-call | flops 4000000000 | tf_op jit(solution)/shard_map/inner_steps/pallas_call | solution.py:158
  12.8 0.0 collective-permute-done.1.halo.halo0
  12.8 0.0 copy-start.2
  12.8 2.8 %first_side.2.refs_3_ = bf16[4,12,32,128]{3,2,1,0:T(8,128)(2,1)S(1)} custom-call(bf16[8,12,64,128]{3,2,1,0:T(8,128)(2,1)S(1)} %bitcast.6, bf16[3,12,8,128]{3,2,1,0:T(8,128)(2,1)S(1)} %bitcast.13, bf16[12,144,128]{2,1,0:T(8,128)(2,1)S(1)} %collective-permute-done.1.halo.halo0, bf16[12,144,128]{2,1,0:T(8,128)(2,1)S(1)} %collective-permute-done.1.halo.halo0, ...), custom_call_target="tpu_custom_call" | custom-call | flops 1000000000 | tf_op jit(solution)/shard_map/first_side/pallas_call | solution.py:253
  15.6 0.0 collective-permute-done.halo.halo0
  15.6 0.0 copy-done.2
  15.6 3.3 %second_side.2 = (bf16[2,32,1536]{2,1,0:T(8,128)(2,1)S(1)}, bf16[2,32,1536]{2,1,0:T(8,128)(2,1)S(1)}, bf16[2,32,1536]{2,1,0:T(8,128)(2,1)S(1)}, bf16[2,32,1536]{2,1,0:T(8,128)(2,1)S(1)}) custom-call(s32[8]{0:T(128)S(1)} %copy-done.2, bf16[8,12,64,128]{3,2,1,0:T(8,128)(2,1)S(1)} %bitcast.7, bf16[3,12,8,128]{3,2,1,0:T(8,128)(2,1)S(1)} %bitcast.14, ...), custom_call_target="tpu_custom_call" | custom-call | flops 1000000000 | tf_op jit(solution)/shard_map/second_side/pallas_call | solution.py:269
  19.0 0.3 collective-permute-start.4
  19.3 1.7 %collective-permute-done.3.halo = bf16[12,128,128]{2,1,0:T(8,128)(2,1)S(1)} collective-permute-done((bf16[12,128,128]{2,1,0:T(8,128)(2,1)S(1)}, bf16[12,128,128]{2,1,0:T(8,128)(2,1)S(1)}, u32[]{:S(2)}, u32[]{:S(2)}) %collective-permute-start.3) | collective-permute-done | bytes 393248 | tf_op jit(solution)/shard_map/ppermute | solution.py:481
  21.0 2.8 %collective-permute-start.8 = (bf16[2,32,1536]{2,1,0:T(8,128)(2,1)S(1)}, bf16[2,32,1536]{2,1,0:T(8,128)(2,1)S(1)}, u32[]{:S(2)}, u32[]{:S(2)}) collective-permute-start(bf16[2,32,1536]{2,1,0:T(8,128)(2,1)S(1)} %get-tuple-element.67), channel_id=1, source_target_pairs={{0,3},{1,2},{2,1},{3,0},{4,7},{5,6},{6,5},{7,4},{8,11},{9,10},{10,... | collective-permute-start | bytes 589832 | tf_op jit(solution)/shard_map/ppermute | solution.py:488
  23.8 2.8 %first_side.3.refs_3_ = bf16[4,12,32,128]{3,2,1,0:T(8,128)(2,1)S(1)} custom-call(bf16[8,12,64,128]{3,2,1,0:T(8,128)(2,1)S(1)} %bitcast.8, bf16[3,12,8,128]{3,2,1,0:T(8,128)(2,1)S(1)} %bitcast.15, bf16[12,128,128]{2,1,0:T(8,128)(2,1)S(1)} %collective-permute-done.3.halo, bf16[12,144,128]{2,1,0:T(8,128)(2,1)S(1)} %collective-permute-done.1.halo.halo0, ...), custom_call_target="tpu_custom_call" | custom-call | flops 1000000000 | tf_op jit(solution)/shard_map/first_side/pallas_call | solution.py:253
  26.6 0.0 copy-start.4
  26.6 0.0 copy-start.3
  26.6 0.0 collective-permute-done.2.halo
  26.7 3.3 %second_side.3 = (bf16[1,32,1536]{2,1,0:T(8,128)(2,1)S(1)}, bf16[1,32,1536]{2,1,0:T(8,128)(2,1)S(1)}, bf16[1,32,1536]{2,1,0:T(8,128)(2,1)S(1)}, bf16[1,32,1536]{...) custom-call(s32[8]{0:T(128)S(1)} %copy-done.2, ...), custom_call_target="tpu_custom_call" | custom-call | flops 1000000000 | tf_op jit(solution)/shard_map/second_side/pallas_call | solution.py:269
  30.0 0.0 collective-permute-done.4.refs_4_
  30.0 0.1 collective-permute-start.5
  30.1 0.5 collective-permute-start.12
  30.6 0.3 collective-permute-start.13
  30.9 1.4 %collective-permute-start.14 = (bf16[1,32,1536]{2,1,0:T(8,128)(2,1)S(1)}, bf16[1,32,1536]{2,1,0:T(8,128)(2,1)S(1)}, u32[]{:S(2)}, u32[]{:S(2)}) collective-permute-start(bf16[1,32,1536]{2,1,0:T(8,128)(2,1)S(1)} %get-tuple-element.74), channel_id=1, source_target_pairs={{0,3},{1,2},{2,1},{3,0},{4,7},{5,6},{6,5},{7,4},{8,11},{9,10},{10,... | collective-permute-start | bytes 294920 | tf_op jit(solution)/shard_map/ppermute | solution.py:488
  32.3 0.0 copy-done.4
  32.3 0.0 collective-permute-done.8.refs_6_
  32.3 0.2 collective-permute-start.6
  32.6 0.0 collective-permute-done.12.refs_3_
  32.6 0.3 collective-permute-start.7
  32.8 2.1 %collective-permute-done.13.refs_5_ = bf16[1,32,1536]{2,1,0:T(8,128)(2,1)S(1)} collective-permute-done((bf16[1,32,1536]{2,1,0:T(8,128)(2,1)S(1)}, bf16[1,32,1536]{2,1,0:T(8,128)(2,1)S(1)}, u32[]{:S(2)}, u32[]{:S(2)}) %collective-permute-start.13) | collective-permute-done | bytes 98336 | tf_op jit(solution)/shard_map/ppermute | solution.py:488
  35.0 1.4 %collective-permute-start.9 = (bf16[1,32,1536]{2,1,0:T(8,128)(2,1)S(1)}, bf16[1,32,1536]{2,1,0:T(8,128)(2,1)S(1)}, u32[]{:S(2)}, u32[]{:S(2)}) collective-permute-start(bf16[1,32,1536]{2,1,0:T(8,128)(2,1)S(1)} %get-tuple-element.68), channel_id=1, source_target_pairs={{0,3},{1,2},{2,1},{3,0},{4,7},{5,6},{6,5},{7,4},{8,11},{9,10},{10,... | collective-permute-start | bytes 294920 | tf_op jit(solution)/shard_map/ppermute | solution.py:488
  36.4 1.3 %collective-permute-done.14.refs_7_ = bf16[1,32,1536]{2,1,0:T(8,128)(2,1)S(1)} collective-permute-done((bf16[1,32,1536]{2,1,0:T(8,128)(2,1)S(1)}, bf16[1,32,1536]{2,1,0:T(8,128)(2,1)S(1)}, u32[]{:S(2)}, u32[]{:S(2)}) %collective-permute-start.14) | collective-permute-done | bytes 98336 | tf_op jit(solution)/shard_map/ppermute | solution.py:488
  37.7 0.0 collective-permute-done.5.refs_2_
  37.7 0.0 copy-done.3
  37.7 20.2 %fit.3 = (bf16[12,64,128]{2,1,0:T(8,128)(2,1)S(1)}, bf16[12,64,128]{2,1,0:T(8,128)(2,1)S(1)}, bf16[12,64,128]{2,1,0:T(8,128)(2,1)S(1)}, bf16[12,64,128]{2,1,0:T(8,128)(2,1)S(1)}) custom-call(s32[2,1,1536]{2,1,0:T(1,128)S(1)} %reshape.3.mask, bf16[2,256,1536]{2,1,0:T(8,128)(2,1)S(1)} %copy-done.3, bf16[2,32,1536]{2,1,0:T(8,128)(2,1)S(1)} %get-tuple-element.49.refs_0_, ...), custom_call_target="tpu_custom_call" | custom-call | flops 3000000000 | tf_op jit(solution)/shard_map/fit/pallas_call | solution.py:402
  57.8 0.1 collective-permute-start.15
  57.9 0.1 collective-permute-start.16
  58.0 0.0 collective-permute-done.6.refs_3_
  58.0 2.0 %collective-permute-start.17 = (bf16[12,64,128]{2,1,0:T(8,128)(2,1)S(1)}, bf16[12,64,128]{2,1,0:T(8,128)(2,1)S(1)}, u32[]{:S(2)}, u32[]{:S(2)}) collective-permute-start(bf16[12,64,128]{2,1,0:T(8,128)(2,1)S(1)} %get-tuple-element.78), channel_id=1, source_target_pairs={{0,3},{1,2},{2,1},{3,0},{4,7},{5,6},{6,5},{7,4},{8,11},{9,10},{10,... | collective-permute-start | bytes 589832 | tf_op jit(solution)/shard_map/ppermute | solution.py:488
  60.1 0.0 collective-permute-done.7.refs_5_
  60.1 0.0 collective-permute-done.9.refs_7_
  60.1 19.8 %fit.2 = (bf16[12,64,128]{2,1,0:T(8,128)(2,1)S(1)}, bf16[12,64,128]{2,1,0:T(8,128)(2,1)S(1)}, bf16[12,64,128]{2,1,0:T(8,128)(2,1)S(1)}, bf16[12,64,128]{2,1,0:T(8,128)(2,1)S(1)}) custom-call(s32[2,1,1536]{2,1,0:T(1,128)S(1)} %reshape.3.mask, bf16[2,256,1536]{2,1,0:T(8,128)(2,1)S(1)} %copy-done.3, bf16[2,32,1536]{2,1,0:T(8,128)(2,1)S(1)} %get-tuple-element.49.refs_0_, ...), custom_call_target="tpu_custom_call" | custom-call | flops 3000000000 | tf_op jit(solution)/shard_map/fit/pallas_call | solution.py:402
  79.9 0.1 collective-permute-start.18
  79.9 0.1 collective-permute-start.11
  80.0 0.0 collective-permute-done.15.refs_1_
  80.0 2.0 %collective-permute-start.10 = (bf16[12,64,128]{2,1,0:T(8,128)(2,1)S(1)}, bf16[12,64,128]{2,1,0:T(8,128)(2,1)S(1)}, u32[]{:S(2)}, u32[]{:S(2)}) collective-permute-start(bf16[12,64,128]{2,1,0:T(8,128)(2,1)S(1)} %get-tuple-element.69), channel_id=1, source_target_pairs={{0,3},{1,2},{2,1},{3,0},{4,7},{5,6},{6,5},{7,4},{8,11},{9,10},{10,... | collective-permute-start | bytes 589832 | tf_op jit(solution)/shard_map/ppermute | solution.py:488
  82.1 0.0 collective-permute-done.16.refs_2_
  82.1 0.0 collective-permute-done.17.refs_3_
  82.1 0.0 collective-permute-done.18.refs_5_
  82.1 1.6 %place.3.refs_1_ = bf16[8,12,64,128]{3,2,1,0:T(8,128)(2,1)} custom-call(s32[8]{0:T(128)S(1)} %copy-done.2, bf16[12,64,128]{2,1,0:T(8,128)(2,1)S(1)} %get-tuple-element.75.refs_0_, bf16[12,64,128]{2,1,0:T(8,128)(2,1)S(1)} %collective-permute-done.15.refs_1_, bf16[12,64,128]{2,1,0:T(8,128)(2,1)S(1)} %collective-permute-done.16.refs_2_, ...), custom_call_target="tpu_custom_call" | custom-call | flops 1500000000 | tf_op jit(solution)/shard_map/place/pallas_call | solution.py:442
  83.7 2.3 %collective-permute-done.11.refs_0_ = bf16[12,64,128]{2,1,0:T(8,128)(2,1)S(1)} collective-permute-done((bf16[12,64,128]{2,1,0:T(8,128)(2,1)S(1)}, bf16[12,64,128]{2,1,0:T(8,128)(2,1)S(1)}, u32[]{:S(2)}, u32[]{:S(2)}) %collective-permute-start.11) | collective-permute-done | bytes 196640 | tf_op jit(solution)/shard_map/ppermute | solution.py:488
  86.0 1.2 %place.4.refs_1_ = bf16[8,12,64,128]{3,2,1,0:T(8,128)(2,1)} custom-call(s32[8]{0:T(128)S(1)} %copy-done.2, bf16[12,64,128]{2,1,0:T(8,128)(2,1)S(1)} %collective-permute-done.11.refs_0_, bf16[8,12,64,128]{3,2,1,0:T(8,128)(2,1)} %place.3.refs_1_), custom_call_target="tpu_custom_call", output_to_operand_aliasing={{}: (2, {})} | custom-call | flops 1500000000 | tf_op jit(solution)/shard_map/place/pallas_call | solution.py:442
  87.3 3.5 %collective-permute-done.10.refs_0_ = bf16[12,64,128]{2,1,0:T(8,128)(2,1)S(1)} collective-permute-done((bf16[12,64,128]{2,1,0:T(8,128)(2,1)S(1)}, bf16[12,64,128]{2,1,0:T(8,128)(2,1)S(1)}, u32[]{:S(2)}, u32[]{:S(2)}) %collective-permute-start.10) | collective-permute-done | bytes 196640 | tf_op jit(solution)/shard_map/ppermute | solution.py:488
  90.8 1.2 %place.5 = bf16[8,12,64,128]{3,2,1,0:T(8,128)(2,1)} custom-call(s32[8]{0:T(128)S(1)} %copy-done.2, bf16[12,64,128]{2,1,0:T(8,128)(2,1)S(1)} %collective-permute-done.10.refs_0_, bf16[8,12,64,128]{3,2,1,0:T(8,128)(2,1)} %place.4.refs_1_), custom_call_target="tpu_custom_call", output_to_operand_aliasing={{}: (2, {})} | custom-call | flops 1500000000 | tf_op jit(solution)/shard_map/place/pallas_call | solution.py:442
  (1 shorter events, 0.0 us)
Async XLA Ops:
  0.0 9.5 %copy-start = (bf16[8,64,12,128]{3,1,2,0:T(8,128)(2,1)S(1)}, bf16[8,64,12,128]{3,1,2,0:T(8,128)(2,1)}, u32[]{:S(2)}) copy-start(bf16[8,64,12,128]{3,1,2,0:T(8,128)(2,1)} %param.5) | copy-start | bytes 4718596
  0.0 9.5 %copy-start.1 = (bf16[3,8,12,128]{3,1,2,0:T(8,128)(2,1)S(1)}, bf16[3,8,12,128]{3,1,2,0:T(8,128)(2,1)}, u32[]{:S(2)}) copy-start(bf16[3,8,12,128]{3,1,2,0:T(8,128)(2,1)} %param.6) | copy-start | bytes 221188
  1.5 11.3 %collective-permute-start.1 = (bf16[12,144,128]{2,1,0:T(8,128)(2,1)S(1)}, bf16[12,144,128]{2,1,0:T(8,128)(2,1)S(1)}, u32[]{:S(2)}, u32[]{:S(2)}) collective-permute-start(bf16[12,144,128]{2,1,0:T(8,128)(2,1)S(1)} %get-tuple-element.44), channel_id=1, source_target_pairs={{0,4},{4,0},{8,12},{12,8},{1,5},{5,1},{9,13},{13,9},{2,6},{6,2},{1... | collective-permute-start | bytes 1327112 | tf_op jit(solution)/shard_map/ppermute | solution.py:481
  2.8 12.8 %collective-permute-start = (bf16[12,144,128]{2,1,0:T(8,128)(2,1)S(1)}, bf16[12,144,128]{2,1,0:T(8,128)(2,1)S(1)}, u32[]{:S(2)}, u32[]{:S(2)}) collective-permute-start(bf16[12,144,128]{2,1,0:T(8,128)(2,1)S(1)} %get-tuple-element.43), channel_id=1, source_target_pairs={{4,8},{8,4},{5,9},{9,5},{6,10},{10,6},{7,11},{11,7},{20,24},{24,20... | collective-permute-start | bytes 1327112 | tf_op jit(solution)/shard_map/ppermute | solution.py:482
  6.1 14.9 %collective-permute-start.3 = (bf16[12,128,128]{2,1,0:T(8,128)(2,1)S(1)}, bf16[12,128,128]{2,1,0:T(8,128)(2,1)S(1)}, u32[]{:S(2)}, u32[]{:S(2)}) collective-permute-start(bf16[12,128,128]{2,1,0:T(8,128)(2,1)S(1)} %get-tuple-element.51), channel_id=1, source_target_pairs={{0,4},{4,0},{8,12},{12,8},{1,5},{5,1},{9,13},{13,9},{2,6},{6,2},{1... | collective-permute-start | bytes 1179656 | tf_op jit(solution)/shard_map/ppermute | solution.py:481
  6.1 20.5 %collective-permute-start.2 = (bf16[12,128,128]{2,1,0:T(8,128)(2,1)S(1)}, bf16[12,128,128]{2,1,0:T(8,128)(2,1)S(1)}, u32[]{:S(2)}, u32[]{:S(2)}) collective-permute-start(bf16[12,128,128]{2,1,0:T(8,128)(2,1)S(1)} %get-tuple-element.50), channel_id=1, source_target_pairs={{4,8},{8,4},{5,9},{9,5},{6,10},{10,6},{7,11},{11,7},{20,24},{24,20... | collective-permute-start | bytes 1179656 | tf_op jit(solution)/shard_map/ppermute | solution.py:482
  12.8 2.9 %copy-start.2 = (s32[8]{0:T(128)S(1)}, s32[8]{0:T(128)}, u32[]{:S(2)}) copy-start(s32[8]{0:T(128)} %slots.9) | copy-start | bytes 100
  19.0 11.0 %collective-permute-start.4 = (bf16[2,32,1536]{2,1,0:T(8,128)(2,1)S(1)}, bf16[2,32,1536]{2,1,0:T(8,128)(2,1)S(1)}, u32[]{:S(2)}, u32[]{:S(2)}) collective-permute-start(bf16[2,32,1536]{2,1,0:T(8,128)(2,1)S(1)} %get-tuple-element.62), channel_id=1, source_target_pairs={{0,2},{1,3},{2,0},{3,1},{4,6},{5,7},{6,4},{7,5},{8,10},{9,11},{10,... | collective-permute-start | bytes 589832 | tf_op jit(solution)/shard_map/ppermute | solution.py:488
  21.0 11.3 %collective-permute-start.8 = (bf16[2,32,1536]{2,1,0:T(8,128)(2,1)S(1)}, bf16[2,32,1536]{2,1,0:T(8,128)(2,1)S(1)}, u32[]{:S(2)}, u32[]{:S(2)}) collective-permute-start(bf16[2,32,1536]{2,1,0:T(8,128)(2,1)S(1)} %get-tuple-element.67), channel_id=1, source_target_pairs={{0,3},{1,2},{2,1},{3,0},{4,7},{5,6},{6,5},{7,4},{8,11},{9,10},{10,... | collective-permute-start | bytes 589832 | tf_op jit(solution)/shard_map/ppermute | solution.py:488
  26.6 5.7 %copy-start.4 = (s32[2,1536]{1,0:T(2,128)S(1)}, s32[2,1536]{1,0:T(2,128)}, u32[]{:S(2)}) copy-start(s32[2,1536]{1,0:T(2,128)} %param.8) | copy-start | bytes 36868
  26.6 11.1 %copy-start.3 = (bf16[2,256,1536]{2,1,0:T(8,128)(2,1)S(1)}, bf16[2,256,1536]{2,1,0:T(8,128)(2,1)}, u32[]{:S(2)}) copy-start(bf16[2,256,1536]{2,1,0:T(8,128)(2,1)} %density.3) | copy-start | bytes 4718596
  30.0 7.7 %collective-permute-start.5 = (bf16[2,32,1536]{2,1,0:T(8,128)(2,1)S(1)}, bf16[2,32,1536]{2,1,0:T(8,128)(2,1)S(1)}, u32[]{:S(2)}, u32[]{:S(2)}) collective-permute-start(bf16[2,32,1536]{2,1,0:T(8,128)(2,1)S(1)} %get-tuple-element.64), channel_id=1, source_target_pairs={{0,1},{1,0},{2,3},{3,2},{4,5},{5,4},{6,7},{7,6},{8,9},{9,8},{10,11... | collective-permute-start | bytes 589832 | tf_op jit(solution)/shard_map/ppermute | solution.py:488
  30.1 2.5 %collective-permute-start.12 = (bf16[1,32,1536]{2,1,0:T(8,128)(2,1)S(1)}, bf16[1,32,1536]{2,1,0:T(8,128)(2,1)S(1)}, u32[]{:S(2)}, u32[]{:S(2)}) collective-permute-start(bf16[1,32,1536]{2,1,0:T(8,128)(2,1)S(1)} %get-tuple-element.72), channel_id=1, source_target_pairs={{0,1},{1,0},{2,3},{3,2},{4,5},{5,4},{6,7},{7,6},{8,9},{9,8},{10,11... | collective-permute-start | bytes 294920 | tf_op jit(solution)/shard_map/ppermute | solution.py:488
  30.6 4.4 %collective-permute-start.13 = (bf16[1,32,1536]{2,1,0:T(8,128)(2,1)S(1)}, bf16[1,32,1536]{2,1,0:T(8,128)(2,1)S(1)}, u32[]{:S(2)}, u32[]{:S(2)}) collective-permute-start(bf16[1,32,1536]{2,1,0:T(8,128)(2,1)S(1)} %get-tuple-element.73), channel_id=1, source_target_pairs={{0,2},{1,3},{2,0},{3,1},{4,6},{5,7},{6,4},{7,5},{8,10},{9,11},{10,... | collective-permute-start | bytes 294920 | tf_op jit(solution)/shard_map/ppermute | solution.py:488
  30.9 6.8 %collective-permute-start.14 = (bf16[1,32,1536]{2,1,0:T(8,128)(2,1)S(1)}, bf16[1,32,1536]{2,1,0:T(8,128)(2,1)S(1)}, u32[]{:S(2)}, u32[]{:S(2)}) collective-permute-start(bf16[1,32,1536]{2,1,0:T(8,128)(2,1)S(1)} %get-tuple-element.74), channel_id=1, source_target_pairs={{0,3},{1,2},{2,1},{3,0},{4,7},{5,6},{6,5},{7,4},{8,11},{9,10},{10,... | collective-permute-start | bytes 294920 | tf_op jit(solution)/shard_map/ppermute | solution.py:488
  32.3 25.7 %collective-permute-start.6 = (bf16[1,32,1536]{2,1,0:T(8,128)(2,1)S(1)}, bf16[1,32,1536]{2,1,0:T(8,128)(2,1)S(1)}, u32[]{:S(2)}, u32[]{:S(2)}) collective-permute-start(bf16[1,32,1536]{2,1,0:T(8,128)(2,1)S(1)} %get-tuple-element.65), channel_id=1, source_target_pairs={{0,1},{1,0},{2,3},{3,2},{4,5},{5,4},{6,7},{7,6},{8,9},{9,8},{10,11... | collective-permute-start | bytes 294920 | tf_op jit(solution)/shard_map/ppermute | solution.py:488
  32.6 27.5 %collective-permute-start.7 = (bf16[1,32,1536]{2,1,0:T(8,128)(2,1)S(1)}, bf16[1,32,1536]{2,1,0:T(8,128)(2,1)S(1)}, u32[]{:S(2)}, u32[]{:S(2)}) collective-permute-start(bf16[1,32,1536]{2,1,0:T(8,128)(2,1)S(1)} %get-tuple-element.66), channel_id=1, source_target_pairs={{0,2},{1,3},{2,0},{3,1},{4,6},{5,7},{6,4},{7,5},{8,10},{9,11},{10,... | collective-permute-start | bytes 294920 | tf_op jit(solution)/shard_map/ppermute | solution.py:488
  35.0 25.1 %collective-permute-start.9 = (bf16[1,32,1536]{2,1,0:T(8,128)(2,1)S(1)}, bf16[1,32,1536]{2,1,0:T(8,128)(2,1)S(1)}, u32[]{:S(2)}, u32[]{:S(2)}) collective-permute-start(bf16[1,32,1536]{2,1,0:T(8,128)(2,1)S(1)} %get-tuple-element.68), channel_id=1, source_target_pairs={{0,3},{1,2},{2,1},{3,0},{4,7},{5,6},{6,5},{7,4},{8,11},{9,10},{10,... | collective-permute-start | bytes 294920 | tf_op jit(solution)/shard_map/ppermute | solution.py:488
  57.8 22.2 %collective-permute-start.15 = (bf16[12,64,128]{2,1,0:T(8,128)(2,1)S(1)}, bf16[12,64,128]{2,1,0:T(8,128)(2,1)S(1)}, u32[]{:S(2)}, u32[]{:S(2)}) collective-permute-start(bf16[12,64,128]{2,1,0:T(8,128)(2,1)S(1)} %get-tuple-element.76), channel_id=1, source_target_pairs={{0,1},{1,0},{2,3},{3,2},{4,5},{5,4},{6,7},{7,6},{8,9},{9,8},{10,11... | collective-permute-start | bytes 589832 | tf_op jit(solution)/shard_map/ppermute | solution.py:488
  57.9 24.1 %collective-permute-start.16 = (bf16[12,64,128]{2,1,0:T(8,128)(2,1)S(1)}, bf16[12,64,128]{2,1,0:T(8,128)(2,1)S(1)}, u32[]{:S(2)}, u32[]{:S(2)}) collective-permute-start(bf16[12,64,128]{2,1,0:T(8,128)(2,1)S(1)} %get-tuple-element.77), channel_id=1, source_target_pairs={{0,2},{1,3},{2,0},{3,1},{4,6},{5,7},{6,4},{7,5},{8,10},{9,11},{10,... | collective-permute-start | bytes 589832 | tf_op jit(solution)/shard_map/ppermute | solution.py:488
  58.0 24.1 %collective-permute-start.17 = (bf16[12,64,128]{2,1,0:T(8,128)(2,1)S(1)}, bf16[12,64,128]{2,1,0:T(8,128)(2,1)S(1)}, u32[]{:S(2)}, u32[]{:S(2)}) collective-permute-start(bf16[12,64,128]{2,1,0:T(8,128)(2,1)S(1)} %get-tuple-element.78), channel_id=1, source_target_pairs={{0,3},{1,2},{2,1},{3,0},{4,7},{5,6},{6,5},{7,4},{8,11},{9,10},{10,... | collective-permute-start | bytes 589832 | tf_op jit(solution)/shard_map/ppermute | solution.py:488
  79.9 2.2 %collective-permute-start.18 = (bf16[12,64,128]{2,1,0:T(8,128)(2,1)S(1)}, bf16[12,64,128]{2,1,0:T(8,128)(2,1)S(1)}, u32[]{:S(2)}, u32[]{:S(2)}) collective-permute-start(bf16[12,64,128]{2,1,0:T(8,128)(2,1)S(1)} %get-tuple-element.80), channel_id=1, source_target_pairs={{0,1},{1,0},{2,3},{3,2},{4,5},{5,4},{6,7},{7,6},{8,9},{9,8},{10,11... | collective-permute-start | bytes 589832 | tf_op jit(solution)/shard_map/ppermute | solution.py:488
  79.9 6.1 %collective-permute-start.11 = (bf16[12,64,128]{2,1,0:T(8,128)(2,1)S(1)}, bf16[12,64,128]{2,1,0:T(8,128)(2,1)S(1)}, u32[]{:S(2)}, u32[]{:S(2)}) collective-permute-start(bf16[12,64,128]{2,1,0:T(8,128)(2,1)S(1)} %get-tuple-element.70), channel_id=1, source_target_pairs={{0,2},{1,3},{2,0},{3,1},{4,6},{5,7},{6,4},{7,5},{8,10},{9,11},{10,... | collective-permute-start | bytes 589832 | tf_op jit(solution)/shard_map/ppermute | solution.py:488
  80.0 10.8 %collective-permute-start.10 = (bf16[12,64,128]{2,1,0:T(8,128)(2,1)S(1)}, bf16[12,64,128]{2,1,0:T(8,128)(2,1)S(1)}, u32[]{:S(2)}, u32[]{:S(2)}) collective-permute-start(bf16[12,64,128]{2,1,0:T(8,128)(2,1)S(1)} %get-tuple-element.69), channel_id=1, source_target_pairs={{0,3},{1,2},{2,1},{3,0},{4,7},{5,6},{6,5},{7,4},{8,11},{9,10},{10,... | collective-permute-start | bytes 589832 | tf_op jit(solution)/shard_map/ppermute | solution.py:488

commit v6 on v5

--- a/solution.py
+++ b/solution.py
@@ -171,13 +171,12 @@
     )(atlas, vel)
 
 
-def side_steps(high, width, start, atlas, vel, halo, halo0, levels, state, speed, coef):
-    rows, ny = atlas.shape[:2]
-    deep = rows + 2 * TSTEPS
+def side_weights(high, vel, halo, speed, coef):
+    rows, deep = vel.shape[2], coef.shape[2]
     edge = TSTEPS - 1
     slab, slabs = lax.axis_index("gz"), lax.axis_size("gz")
     has = jnp.where(high, slab < slabs - 1, slab > 0)
-    beyond = halo0[:, halo0.shape[1] - VEL_ROWS :, :].astype(F32)
+    beyond = halo[:, halo.shape[1] - VEL_ROWS :, :].astype(F32)
     for k in range(3):
         lines = beyond[:, edge * k : edge * (k + 1), :]
         speed[k, :, TSTEPS : TSTEPS + rows, :] = vel[k].astype(F32)
@@ -187,47 +186,63 @@
     inside = ((place >= TSTEPS) & (place < TSTEPS + rows)) | has
     set_weights(speed, coef, inside & (place > 0) & (place < deep - 1))
 
+
+def side_steps(high, width, start, atlas, halo, levels, state, coef):
+    rows = atlas.shape[0]
+    deep = rows + 2 * TSTEPS
     channels = slice(start, start + width)
     base = jnp.where(high, TSTEPS + rows, 0)
     for step in range(TSTEPS):
-        state[0, base + step] = halo[:, step * width : (step + 1) * width, :].astype(F32)
+        state[0][base + step] = halo[:, step * width : (step + 1) * width, :].astype(F32)
     for i in range(2):
         z = jnp.where(high, rows - 2, 0) + i
-        state[0, z + TSTEPS] = atlas[z, :, channels, :].astype(F32)
+        state[0][z + TSTEPS] = atlas[z, :, channels, :].astype(F32)
         for level in range(1, TSTEPS):
             z = jnp.where(high, rows - 2 - level, level) + i
-            state[level, z + TSTEPS] = levels[level - 1][z, :, channels, :]
+            state[level][z + TSTEPS] = levels[level - 1][z, :, channels, :]
     for step in range(TSTEPS):
         first = jnp.where(high, deep - 5 - step, step + 1)
-        target = state.at[(step + 1) % TSTEPS]
-        advance_pairs(coef, state.at[step], target, TSTEPS // 2, lambda i: first + 2 * i)
-
-
-def first_kernel(width, start, atlas, vel, halo, halo0, *refs):
-    levels, (done, state, speed, coef) = refs[: TSTEPS - 1], refs[TSTEPS - 1 :]
+        target = state[(step + 1) % TSTEPS]
+        for i in range(TSTEPS):
+            advance(coef, state[step], target, first + i)
+
+
+def first_kernel(width, start, atlas, vel, halo, *refs):
+    levels, refs = refs[: TSTEPS - 1], refs[TSTEPS - 1 :]
+    refs, state = refs[:-TSTEPS], refs[-TSTEPS:]
     high = odd_slab() == 0
-    side_steps(high, width, start, atlas, vel, halo, halo0, levels, state, speed, coef)
+    if start == 0:
+        done, coef, speed = refs
+        side_weights(high, vel, halo, speed, coef)
+    else:
+        coef, done = refs
+    side_steps(high, width, start, atlas, halo, levels, state, coef)
     first = jnp.where(high, atlas.shape[0] - TSTEPS, 0)
     for i in range(TSTEPS):
-        done[i] = state[0, first + TSTEPS + i].astype(BF16)
-
-
-def second_kernel(peers, per, joined, width, start, slots, atlas, vel, halo, halo0, *refs):
-    levels, done, refs = refs[: TSTEPS - 1], refs[TSTEPS - 1], refs[TSTEPS:]
-    outs, (moved, state, speed, coef) = refs[:-4], refs[-4:]
+        done[i] = state[0][first + TSTEPS + i].astype(BF16)
+
+
+def second_kernel(peers, per, joined, width, start, slots, atlas, vel, halo, done, *refs):
+    levels, refs = refs[: TSTEPS - 1], refs[TSTEPS - 1 :]
+    refs, state = refs[:-TSTEPS], refs[-TSTEPS:]
+    high = odd_slab() > 0
+    if start == 0:
+        outs, (coef, moved, speed) = refs[:-3], refs[-3:]
+        side_weights(high, vel, halo, speed, coef)
+    else:
+        coef, outs, moved = refs[0], refs[1:-1], refs[-1]
     rows, ny = atlas.shape[:2]
-    high = odd_slab() > 0
-    side_steps(high, width, start, atlas, vel, halo, halo0, levels, state, speed, coef)
+    side_steps(high, width, start, atlas, halo, levels, state, coef)
     if rows > 2 * TSTEPS:
         source = levels[-1].at[:, :, start : start + width, :]
         pairs = (rows - 2 * TSTEPS) // 2
-        advance_pairs(coef, source, state.at[0], pairs, lambda i: 2 * TSTEPS + 2 * i, TSTEPS)
+        advance_pairs(coef, source, state[0], pairs, lambda i: 2 * TSTEPS + 2 * i, TSTEPS)
         for z in range(TSTEPS, rows - TSTEPS):
-            moved[z] = state[0, z + TSTEPS].astype(BF16)
+            moved[z] = state[0][z + TSTEPS].astype(BF16)
     first = jnp.where(high, rows - TSTEPS, 0)
     other = rows - TSTEPS - first
     for i in range(TSTEPS):
-        moved[first + i] = state[0, first + TSTEPS + i].astype(BF16)
+        moved[first + i] = state[0][first + TSTEPS + i].astype(BF16)
         moved[other + i] = done[i]
     me = lax.axis_index(("gy", "af"))
     slab = lax.axis_index("gz")
@@ -239,43 +254,50 @@
                 out[:, y * LANES : (y + 1) * LANES] = moved[z, y]
 
 
-def side_scratch(atlas, width):
+def side_shapes(atlas, width, start):
     rows, ny = atlas.shape[:2]
     deep = rows + 2 * TSTEPS
-    return [
-        pltpu.VMEM((TSTEPS, deep, ny, width, LANES), F32),
-        pltpu.VMEM((3, ny, deep, LANES), F32),
-        pltpu.VMEM((7, ny, deep, LANES), F32),
-    ]
-
-
-def first_side(atlas, vel, halo, halo0, levels, width, start):
-    return pl.pallas_call(
+    scratch = [pltpu.VMEM((3, ny, deep, LANES), F32)] if start == 0 else []
+    scratch += [pltpu.VMEM((deep, ny, width, LANES), F32)] * TSTEPS
+    return jax.ShapeDtypeStruct((7, ny, deep, LANES), F32), scratch
+
+
+def first_side(atlas, vel, halo, levels, coef, width, start):
+    done = jax.ShapeDtypeStruct((TSTEPS, atlas.shape[1], width, LANES), BF16)
+    weights, scratch = side_shapes(atlas, width, start)
+    outs = [done, weights] if start == 0 else [done]
+    extra = [] if start == 0 else [coef]
+    result = pl.pallas_call(
         functools.partial(first_kernel, width, start),
-        out_shape=jax.ShapeDtypeStruct((TSTEPS, atlas.shape[1], width, LANES), BF16),
-        in_specs=[spec(pltpu.VMEM)] * (4 + len(levels)),
-        out_specs=spec(pltpu.VMEM),
-        scratch_shapes=side_scratch(atlas, width),
+        out_shape=outs,
+        in_specs=[spec(pltpu.VMEM)] * (3 + len(levels) + len(extra)),
+        out_specs=[spec(pltpu.VMEM)] * len(outs),
+        scratch_shapes=scratch,
         compiler_params=params(28),
         cost_estimate=cost(COST_T),
         name="first_side",
-    )(atlas, vel, halo, halo0, *levels)
-
-
-def second_side(slots, atlas, vel, halo, halo0, levels, done, width, start, peers, per, joined):
+    )(atlas, vel, halo, *levels, *extra)
+    return result if start == 0 else (result[0], coef)
+
+
+def second_side(slots, atlas, vel, halo, levels, done, coef, width, start, peers, per, joined):
     rows, ny = atlas.shape[:2]
-    out = (per if joined else 1, width, ny * LANES)
+    out = jax.ShapeDtypeStruct((per if joined else 1, width, ny * LANES), BF16)
     count = peers if joined else peers * per
-    return pl.pallas_call(
+    weights, scratch = side_shapes(atlas, width, start)
+    outs = [out] * count + ([weights] if start == 0 else [])
+    extra = [] if start == 0 else [coef]
+    result = pl.pallas_call(
         functools.partial(second_kernel, peers, per, joined, width, start),
-        out_shape=[jax.ShapeDtypeStruct(out, BF16)] * count,
-        in_specs=[spec(pltpu.SMEM)] + [spec(pltpu.VMEM)] * (5 + len(levels)),
-        out_specs=[spec(pltpu.VMEM)] * count,
-        scratch_shapes=[pltpu.VMEM((rows, ny, width, LANES), BF16)] + side_scratch(atlas, width),
+        out_shape=outs,
+        in_specs=[spec(pltpu.SMEM)] + [spec(pltpu.VMEM)] * (4 + len(levels) + len(extra)),
+        out_specs=[spec(pltpu.VMEM)] * len(outs),
+        scratch_shapes=[pltpu.VMEM((rows, ny, width, LANES), BF16)] + scratch,
         compiler_params=params(28),
         cost_estimate=cost(COST_T),
         name="second_side",
-    )(slots, atlas, vel, halo, halo0, *levels, done)
+    )(slots, atlas, vel, halo, done, *levels, *extra)
+    return (result[:count], result[count]) if start == 0 else (result, coef)
 
 
 def dot(a, b):
@@ -488,15 +510,16 @@
         return lax.ppermute(block, ("gy", "af"), [(i, i ^ k) for i in range(peers)])
 
     arrived = {}
+    coef_one = coef_two = None
     start = 0
     for part, width in enumerate(widths):
         joined = part < chunks - 1
         one, two = halos[part]
         if part > 0:
             one, _ = lax.optimization_barrier((one, moved[0]))
-        done = first_side(atlas, vel, one, halos[0][0], levels, width, start)
-        moved = second_side(
-            slots, atlas, vel, two, halos[0][1], levels, done, width, start, peers, per, joined
+        done, coef_one = first_side(atlas, vel, one, levels, coef_one, width, start)
+        moved, coef_two = second_side(
+            slots, atlas, vel, two, levels, done, coef_two, width, start, peers, per, joined
         )
         start += width
         if part > 0:

time: 93.1 us -> 91.4 us (0.982)
  Pallas kernels: 62.3 us -> 59.2 us
  waiting for transfers between devices: 11 us -> 12.1 us
    pallas_call x2, Pallas kernels: 39.9 us -> 38.6 us  [fit(): pl.pallas_call(functools.partial(fit_kernel, parts, peers), grid=(1,), ou...]
    pallas_call x2, Pallas kernels: 5.66 us -> 4.4 us  [first_side(): pl.pallas_call(functools.partial(first_kernel, width, start), out_shape=o...]
  transfers between devices with their start and end apart: 19 -> 19, of which waited for: 5 -> 6; matrix products, arithmetic and copies ran while one was open for 0% -> 0% of each run, Pallas kernels for 65% -> 62%
where the time goes in v6:
time: 91.4 us; the launch traced here: 90.6 us
  Pallas kernels  59.2 us (65%)
  starting transfers between devices  18.9 us (21%)
  waiting for transfers between devices  12.1 us (13%)
    pallas_call x2, Pallas kernels, fit(): pl.pallas_call(functools.partial(fit_kernel, parts, peers), grid=(1,), ou...  38.6 us
    ppermute x15, starting transfers between devices, swap(): return lax.ppermute(block, ('gy', 'af'), [(i, i ^ k) for i in range(peers)])  12.2 us
    ppermute x15, waiting for transfers between devices, swap(): return lax.ppermute(block, ('gy', 'af'), [(i, i ^ k) for i in range(peers)])  9.69 us
    pallas_call x2, Pallas kernels, second_side(): pl.pallas_call(functools.partial(second_kernel, peers, per, joined, width...  6.07 us
    ppermute x2, starting transfers between devices, body(): two = lax.ppermute(edges[1], 'gz', twos)  5.27 us
    pallas_call x2, Pallas kernels, first_side(): pl.pallas_call(functools.partial(first_kernel, width, start), out_shape=o...  4.4 us
    pallas_call x3, Pallas kernels, place(): pl.pallas_call(functools.partial(place_kernel, per, which), out_shape=jax...  4.09 us
    pallas_call x1, Pallas kernels, inner(): pl.pallas_call(inner_kernel, out_shape=[level] * (TSTEPS - 1), in_specs=[...  3.21 us
  transfers between devices with their start and end apart: 19, of which 6 were waited for; matrix products, arithmetic and copies ran while one was open for 0% of the time, Pallas kernels for 62%

profile of v6, /device:TPU:23, one launch (start us, length us, event | category | flops | bytes accessed | tf_op | source)
XLA Modules:
  0.0 90.6 jit_solution(5845637726275676080)
XLA Ops:
  0.0 0.0 copy-start
  0.0 0.0 copy-start.1
  0.0 1.4 %pack_edges.2 = (bf16[12,144,128]{2,1,0:T(8,128)(2,1)S(1)}, bf16[12,144,128]{2,1,0:T(8,128)(2,1)S(1)}) custom-call(bf16[8,12,64,128]{3,2,1,0:T(8,128)(2,1)} %bitcast.3, bf16[3,12,8,128]{3,2,1,0:T(8,128)(2,1)} %bitcast.10), custom_call_target="tpu_custom_call" | custom-call | tf_op jit(solution)/shard_map/pack_edges/pallas_call | solution.py:79
  1.5 1.4 %collective-permute-start.1 = (bf16[12,144,128]{2,1,0:T(8,128)(2,1)S(1)}, bf16[12,144,128]{2,1,0:T(8,128)(2,1)S(1)}, u32[]{:S(2)}, u32[]{:S(2)}) collective-permute-start(bf16[12,144,128]{2,1,0:T(8,128)(2,1)S(1)} %get-tuple-element.47), channel_id=1, source_target_pairs={{0,4},{4,0},{8,12},{12,8},{1,5},{5,1},{9,13},{13,9},{2,6},{6,2},{1... | collective-permute-start | bytes 1327112 | tf_op jit(solution)/shard_map/ppermute | solution.py:503
  2.8 1.9 %collective-permute-start = (bf16[12,144,128]{2,1,0:T(8,128)(2,1)S(1)}, bf16[12,144,128]{2,1,0:T(8,128)(2,1)S(1)}, u32[]{:S(2)}, u32[]{:S(2)}) collective-permute-start(bf16[12,144,128]{2,1,0:T(8,128)(2,1)S(1)} %get-tuple-element.46), channel_id=1, source_target_pairs={{4,8},{8,4},{5,9},{9,5},{6,10},{10,6},{7,11},{11,7},{20,24},{24,20... | collective-permute-start | bytes 1327112 | tf_op jit(solution)/shard_map/ppermute | solution.py:504
  4.7 1.3 %pack_edges.3 = (bf16[12,128,128]{2,1,0:T(8,128)(2,1)S(1)}, bf16[12,128,128]{2,1,0:T(8,128)(2,1)S(1)}) custom-call(bf16[8,12,64,128]{3,2,1,0:T(8,128)(2,1)} %bitcast.4, bf16[3,12,8,128]{3,2,1,0:T(8,128)(2,1)} %bitcast.11), custom_call_target="tpu_custom_call" | custom-call | tf_op jit(solution)/shard_map/pack_edges/pallas_call | solution.py:79
  6.1 0.1 collective-permute-start.3
  6.1 3.4 %collective-permute-start.2 = (bf16[12,128,128]{2,1,0:T(8,128)(2,1)S(1)}, bf16[12,128,128]{2,1,0:T(8,128)(2,1)S(1)}, u32[]{:S(2)}, u32[]{:S(2)}) collective-permute-start(bf16[12,128,128]{2,1,0:T(8,128)(2,1)S(1)} %get-tuple-element.54), channel_id=1, source_target_pairs={{4,8},{8,4},{5,9},{9,5},{6,10},{10,6},{7,11},{11,7},{20,24},{24,20... | collective-permute-start | bytes 1179656 | tf_op jit(solution)/shard_map/ppermute | solution.py:504
  9.5 0.0 copy-done
  9.5 0.0 copy-done.1
  9.5 3.2 %inner_steps.1 = (f32[8,12,64,128]{3,2,1,0:T(8,128)S(1)}, f32[8,12,64,128]{3,2,1,0:T(8,128)S(1)}, f32[8,12,64,128]{3,2,1,0:T(8,128)S(1)}) custom-call(bf16[8,12,64,128]{3,2,1,0:T(8,128)(2,1)S(1)} %bitcast.5, bf16[3,12,8,128]{3,2,1,0:T(8,128)(2,1)S(1)} %bitcast.12), custom_call_target="tpu_custom_call" | custom-call | flops 4000000000 | tf_op jit(solution)/shard_map/inner_steps/pallas_call | solution.py:158
  12.8 0.0 collective-permute-done.1.halo
  12.8 0.0 copy-start.2
  12.8 2.3 %first_side.2 = (bf16[4,12,32,128]{3,2,1,0:T(8,128)(2,1)S(1)}, f32[7,12,16,128]{3,2,1,0:T(8,128)S(1)}) custom-call(bf16[8,12,64,128]{3,2,1,0:T(8,128)(2,1)S(1)} %bitcast.6, bf16[3,12,8,128]{3,2,1,0:T(8,128)(2,1)S(1)} %bitcast.13, bf16[12,144,128]{2,1,0:T(8,128)(2,1)S(1)} %collective-permute-done.1.halo, f32[8,12,64,128]{3,2,1,0:T(8,128)S(1)} %get-tuple-element.49.refs_0_, ...), custom_call_target="tpu_custom_call" | custom-call | flops 1000000000 | tf_op jit(solution)/shard_map/first_side/pallas_call | solution.py:270
  15.1 0.3 collective-permute-done.halo
  15.4 0.0 copy-done.2
  15.4 3.1 %second_side.2 = (bf16[2,32,1536]{2,1,0:T(8,128)(2,1)S(1)}, bf16[2,32,1536]{2,1,0:T(8,128)(2,1)S(1)}, bf16[2,32,1536]{2,1,0:T(8,128)(2,1)S(1)}, bf16[2,32,1536]{2,1,0:T(8,128)(2,1)S(1)}, f32[7,12,16,128]{3,2,1,0:T(8,128)S(1)}) custom-call(s32[8]{0:T(128)S(1)} %copy-done.2, bf16[8,12,64,128]{3,2,1,0:T(8,128)(2,1)S(1)} %bitcast.7, ...), custom_call_target="tpu_custom_call" | custom-call | flops 1000000000 | tf_op jit(solution)/shard_map/second_side/pallas_call | solution.py:290
  18.6 0.3 collective-permute-start.4
  18.9 2.1 %collective-permute-done.3.halo = bf16[12,128,128]{2,1,0:T(8,128)(2,1)S(1)} collective-permute-done((bf16[12,128,128]{2,1,0:T(8,128)(2,1)S(1)}, bf16[12,128,128]{2,1,0:T(8,128)(2,1)S(1)}, u32[]{:S(2)}, u32[]{:S(2)}) %collective-permute-start.3) | collective-permute-done | bytes 393248 | tf_op jit(solution)/shard_map/ppermute | solution.py:503
  21.0 2.6 %collective-permute-start.8 = (bf16[2,32,1536]{2,1,0:T(8,128)(2,1)S(1)}, bf16[2,32,1536]{2,1,0:T(8,128)(2,1)S(1)}, u32[]{:S(2)}, u32[]{:S(2)}) collective-permute-start(bf16[2,32,1536]{2,1,0:T(8,128)(2,1)S(1)} %get-tuple-element.73), channel_id=1, source_target_pairs={{0,3},{1,2},{2,1},{3,0},{4,7},{5,6},{6,5},{7,4},{8,11},{9,10},{10,... | collective-permute-start | bytes 589832 | tf_op jit(solution)/shard_map/ppermute | solution.py:510
  23.6 2.1 %first_side.3.done = bf16[4,12,32,128]{3,2,1,0:T(8,128)(2,1)S(1)} custom-call(bf16[8,12,64,128]{3,2,1,0:T(8,128)(2,1)S(1)} %bitcast.8, bf16[3,12,8,128]{3,2,1,0:T(8,128)(2,1)S(1)} %bitcast.15, bf16[12,128,128]{2,1,0:T(8,128)(2,1)S(1)} %collective-permute-done.3.halo, f32[8,12,64,128]{3,2,1,0:T(8,128)S(1)} %get-tuple-element.49.refs_0_, ...), custom_call_target="tpu_custom_call" | custom-call | flops 1000000000 | tf_op jit(solution)/shard_map/first_side/pallas_call | solution.py:270
  25.7 0.0 collective-permute-done.2.halo
  25.7 0.0 copy-start.4
  25.7 0.0 copy-start.3
  25.7 2.9 %second_side.3 = (bf16[1,32,1536]{2,1,0:T(8,128)(2,1)S(1)}, bf16[1,32,1536]{2,1,0:T(8,128)(2,1)S(1)}, bf16[1,32,1536]{2,1,0:T(8,128)(2,1)S(1)}, bf16[1,32,1536]{...) custom-call(s32[8]{0:T(128)S(1)} %copy-done.2, ...), custom_call_target="tpu_custom_call" | custom-call | flops 1000000000 | tf_op jit(solution)/shard_map/second_side/pallas_call | solution.py:290
  28.6 0.0 collective-permute-done.4.refs_4_
  28.6 1.1 %collective-permute-start.5 = (bf16[2,32,1536]{2,1,0:T(8,128)(2,1)S(1)}, bf16[2,32,1536]{2,1,0:T(8,128)(2,1)S(1)}, u32[]{:S(2)}, u32[]{:S(2)}) collective-permute-start(bf16[2,32,1536]{2,1,0:T(8,128)(2,1)S(1)} %get-tuple-element.70), channel_id=1, source_target_pairs={{0,1},{1,0},{2,3},{3,2},{4,5},{5,4},{6,7},{7,6},{8,9},{9,8},{10,11... | collective-permute-start | bytes 589832 | tf_op jit(solution)/shard_map/ppermute | solution.py:510
  29.7 0.0 collective-permute-start.12
  29.7 0.0 collective-permute-start.13
  29.7 2.1 %collective-permute-start.14 = (bf16[1,32,1536]{2,1,0:T(8,128)(2,1)S(1)}, bf16[1,32,1536]{2,1,0:T(8,128)(2,1)S(1)}, u32[]{:S(2)}, u32[]{:S(2)}) collective-permute-start(bf16[1,32,1536]{2,1,0:T(8,128)(2,1)S(1)} %get-tuple-element.80), channel_id=1, source_target_pairs={{0,3},{1,2},{2,1},{3,0},{4,7},{5,6},{6,5},{7,4},{8,11},{9,10},{10,... | collective-permute-start | bytes 294920 | tf_op jit(solution)/shard_map/ppermute | solution.py:510
  31.9 0.0 copy-done.4
  31.9 0.0 collective-permute-done.8.refs_6_
  31.9 0.1 collective-permute-start.6
  32.0 0.0 collective-permute-done.12.refs_3_
  32.0 0.1 collective-permute-start.7
  32.1 1.5 %collective-permute-done.13.refs_5_ = bf16[1,32,1536]{2,1,0:T(8,128)(2,1)S(1)} collective-permute-done((bf16[1,32,1536]{2,1,0:T(8,128)(2,1)S(1)}, bf16[1,32,1536]{2,1,0:T(8,128)(2,1)S(1)}, u32[]{:S(2)}, u32[]{:S(2)}) %collective-permute-start.13) | collective-permute-done | bytes 98336 | tf_op jit(solution)/shard_map/ppermute | solution.py:510
  33.6 1.5 %collective-permute-start.9 = (bf16[1,32,1536]{2,1,0:T(8,128)(2,1)S(1)}, bf16[1,32,1536]{2,1,0:T(8,128)(2,1)S(1)}, u32[]{:S(2)}, u32[]{:S(2)}) collective-permute-start(bf16[1,32,1536]{2,1,0:T(8,128)(2,1)S(1)} %get-tuple-element.74), channel_id=1, source_target_pairs={{0,3},{1,2},{2,1},{3,0},{4,7},{5,6},{6,5},{7,4},{8,11},{9,10},{10,... | collective-permute-start | bytes 294920 | tf_op jit(solution)/shard_map/ppermute | solution.py:510
  35.1 2.3 %collective-permute-done.14.refs_7_ = bf16[1,32,1536]{2,1,0:T(8,128)(2,1)S(1)} collective-permute-done((bf16[1,32,1536]{2,1,0:T(8,128)(2,1)S(1)}, bf16[1,32,1536]{2,1,0:T(8,128)(2,1)S(1)}, u32[]{:S(2)}, u32[]{:S(2)}) %collective-permute-start.14) | collective-permute-done | bytes 98336 | tf_op jit(solution)/shard_map/ppermute | solution.py:510
  37.3 0.0 collective-permute-done.5.refs_2_
  37.3 0.0 copy-done.3
  37.3 18.9 %fit.3 = (bf16[12,64,128]{2,1,0:T(8,128)(2,1)S(1)}, bf16[12,64,128]{2,1,0:T(8,128)(2,1)S(1)}, bf16[12,64,128]{2,1,0:T(8,128)(2,1)S(1)}, bf16[12,64,128]{2,1,0:T(8,128)(2,1)S(1)}) custom-call(s32[2,1,1536]{2,1,0:T(1,128)S(1)} %reshape.3.mask, bf16[2,256,1536]{2,1,0:T(8,128)(2,1)S(1)} %copy-done.3, bf16[2,32,1536]{2,1,0:T(8,128)(2,1)S(1)} %get-tuple-element.53.refs_0_, ...), custom_call_target="tpu_custom_call" | custom-call | flops 3000000000 | tf_op jit(solution)/shard_map/fit/pallas_call | solution.py:424
  56.2 0.1 collective-permute-start.15
  56.3 1.0 %collective-permute-start.16 = (bf16[12,64,128]{2,1,0:T(8,128)(2,1)S(1)}, bf16[12,64,128]{2,1,0:T(8,128)(2,1)S(1)}, u32[]{:S(2)}, u32[]{:S(2)}) collective-permute-start(bf16[12,64,128]{2,1,0:T(8,128)(2,1)S(1)} %get-tuple-element.83), channel_id=1, source_target_pairs={{0,2},{1,3},{2,0},{3,1},{4,6},{5,7},{6,4},{7,5},{8,10},{9,11},{10,... | collective-permute-start | bytes 589832 | tf_op jit(solution)/shard_map/ppermute | solution.py:510
  57.3 0.0 collective-permute-done.6.refs_3_
  57.3 1.1 %collective-permute-start.17 = (bf16[12,64,128]{2,1,0:T(8,128)(2,1)S(1)}, bf16[12,64,128]{2,1,0:T(8,128)(2,1)S(1)}, u32[]{:S(2)}, u32[]{:S(2)}) collective-permute-start(bf16[12,64,128]{2,1,0:T(8,128)(2,1)S(1)} %get-tuple-element.84), channel_id=1, source_target_pairs={{0,3},{1,2},{2,1},{3,0},{4,7},{5,6},{6,5},{7,4},{8,11},{9,10},{10,... | collective-permute-start | bytes 589832 | tf_op jit(solution)/shard_map/ppermute | solution.py:510
  58.4 0.0 collective-permute-done.7.refs_5_
  58.4 0.0 collective-permute-done.9.refs_7_
  58.4 19.8 %fit.2 = (bf16[12,64,128]{2,1,0:T(8,128)(2,1)S(1)}, bf16[12,64,128]{2,1,0:T(8,128)(2,1)S(1)}, bf16[12,64,128]{2,1,0:T(8,128)(2,1)S(1)}, bf16[12,64,128]{2,1,0:T(8,128)(2,1)S(1)}) custom-call(s32[2,1,1536]{2,1,0:T(1,128)S(1)} %reshape.3.mask, bf16[2,256,1536]{2,1,0:T(8,128)(2,1)S(1)} %copy-done.3, bf16[2,32,1536]{2,1,0:T(8,128)(2,1)S(1)} %get-tuple-element.53.refs_0_, ...), custom_call_target="tpu_custom_call" | custom-call | flops 3000000000 | tf_op jit(solution)/shard_map/fit/pallas_call | solution.py:424
  78.2 0.1 collective-permute-start.18
  78.3 0.1 collective-permute-start.11
  78.4 0.0 collective-permute-done.15.refs_1_
  78.4 2.0 %collective-permute-start.10 = (bf16[12,64,128]{2,1,0:T(8,128)(2,1)S(1)}, bf16[12,64,128]{2,1,0:T(8,128)(2,1)S(1)}, u32[]{:S(2)}, u32[]{:S(2)}) collective-permute-start(bf16[12,64,128]{2,1,0:T(8,128)(2,1)S(1)} %get-tuple-element.75), channel_id=1, source_target_pairs={{0,3},{1,2},{2,1},{3,0},{4,7},{5,6},{6,5},{7,4},{8,11},{9,10},{10,... | collective-permute-start | bytes 589832 | tf_op jit(solution)/shard_map/ppermute | solution.py:510
  80.4 0.0 collective-permute-done.16.refs_2_
  80.4 0.0 collective-permute-done.17.refs_3_
  80.4 0.0 collective-permute-done.18.refs_5_
  80.4 1.6 %place.3.refs_1_ = bf16[8,12,64,128]{3,2,1,0:T(8,128)(2,1)} custom-call(s32[8]{0:T(128)S(1)} %copy-done.2, bf16[12,64,128]{2,1,0:T(8,128)(2,1)S(1)} %get-tuple-element.81.refs_0_, bf16[12,64,128]{2,1,0:T(8,128)(2,1)S(1)} %collective-permute-done.15.refs_1_, bf16[12,64,128]{2,1,0:T(8,128)(2,1)S(1)} %collective-permute-done.16.refs_2_, ...), custom_call_target="tpu_custom_call" | custom-call | flops 1500000000 | tf_op jit(solution)/shard_map/place/pallas_call | solution.py:464
  82.0 2.3 %collective-permute-done.11.refs_0_ = bf16[12,64,128]{2,1,0:T(8,128)(2,1)S(1)} collective-permute-done((bf16[12,64,128]{2,1,0:T(8,128)(2,1)S(1)}, bf16[12,64,128]{2,1,0:T(8,128)(2,1)S(1)}, u32[]{:S(2)}, u32[]{:S(2)}) %collective-permute-start.11) | collective-permute-done | bytes 196640 | tf_op jit(solution)/shard_map/ppermute | solution.py:510
  84.4 1.2 %place.4.refs_1_ = bf16[8,12,64,128]{3,2,1,0:T(8,128)(2,1)} custom-call(s32[8]{0:T(128)S(1)} %copy-done.2, bf16[12,64,128]{2,1,0:T(8,128)(2,1)S(1)} %collective-permute-done.11.refs_0_, bf16[8,12,64,128]{3,2,1,0:T(8,128)(2,1)} %place.3.refs_1_), custom_call_target="tpu_custom_call", output_to_operand_aliasing={{}: (2, {})} | custom-call | flops 1500000000 | tf_op jit(solution)/shard_map/place/pallas_call | solution.py:464
  85.6 3.5 %collective-permute-done.10.refs_0_ = bf16[12,64,128]{2,1,0:T(8,128)(2,1)S(1)} collective-permute-done((bf16[12,64,128]{2,1,0:T(8,128)(2,1)S(1)}, bf16[12,64,128]{2,1,0:T(8,128)(2,1)S(1)}, u32[]{:S(2)}, u32[]{:S(2)}) %collective-permute-start.10) | collective-permute-done | bytes 196640 | tf_op jit(solution)/shard_map/ppermute | solution.py:510
  89.2 1.2 %place.5 = bf16[8,12,64,128]{3,2,1,0:T(8,128)(2,1)} custom-call(s32[8]{0:T(128)S(1)} %copy-done.2, bf16[12,64,128]{2,1,0:T(8,128)(2,1)S(1)} %collective-permute-done.10.refs_0_, bf16[8,12,64,128]{3,2,1,0:T(8,128)(2,1)} %place.4.refs_1_), custom_call_target="tpu_custom_call", output_to_operand_aliasing={{}: (2, {})} | custom-call | flops 1500000000 | tf_op jit(solution)/shard_map/place/pallas_call | solution.py:464
  (1 shorter events, 0.0 us)
Async XLA Ops:
  0.0 9.5 %copy-start = (bf16[8,64,12,128]{3,1,2,0:T(8,128)(2,1)S(1)}, bf16[8,64,12,128]{3,1,2,0:T(8,128)(2,1)}, u32[]{:S(2)}) copy-start(bf16[8,64,12,128]{3,1,2,0:T(8,128)(2,1)} %param.5) | copy-start | bytes 4718596
  0.0 9.5 %copy-start.1 = (bf16[3,8,12,128]{3,1,2,0:T(8,128)(2,1)S(1)}, bf16[3,8,12,128]{3,1,2,0:T(8,128)(2,1)}, u32[]{:S(2)}) copy-start(bf16[3,8,12,128]{3,1,2,0:T(8,128)(2,1)} %param.6) | copy-start | bytes 221188
  1.5 11.3 %collective-permute-start.1 = (bf16[12,144,128]{2,1,0:T(8,128)(2,1)S(1)}, bf16[12,144,128]{2,1,0:T(8,128)(2,1)S(1)}, u32[]{:S(2)}, u32[]{:S(2)}) collective-permute-start(bf16[12,144,128]{2,1,0:T(8,128)(2,1)S(1)} %get-tuple-element.47), channel_id=1, source_target_pairs={{0,4},{4,0},{8,12},{12,8},{1,5},{5,1},{9,13},{13,9},{2,6},{6,2},{1... | collective-permute-start | bytes 1327112 | tf_op jit(solution)/shard_map/ppermute | solution.py:503
  2.8 12.6 %collective-permute-start = (bf16[12,144,128]{2,1,0:T(8,128)(2,1)S(1)}, bf16[12,144,128]{2,1,0:T(8,128)(2,1)S(1)}, u32[]{:S(2)}, u32[]{:S(2)}) collective-permute-start(bf16[12,144,128]{2,1,0:T(8,128)(2,1)S(1)} %get-tuple-element.46), channel_id=1, source_target_pairs={{4,8},{8,4},{5,9},{9,5},{6,10},{10,6},{7,11},{11,7},{20,24},{24,20... | collective-permute-start | bytes 1327112 | tf_op jit(solution)/shard_map/ppermute | solution.py:504
  6.1 14.9 %collective-permute-start.3 = (bf16[12,128,128]{2,1,0:T(8,128)(2,1)S(1)}, bf16[12,128,128]{2,1,0:T(8,128)(2,1)S(1)}, u32[]{:S(2)}, u32[]{:S(2)}) collective-permute-start(bf16[12,128,128]{2,1,0:T(8,128)(2,1)S(1)} %get-tuple-element.55), channel_id=1, source_target_pairs={{0,4},{4,0},{8,12},{12,8},{1,5},{5,1},{9,13},{13,9},{2,6},{6,2},{1... | collective-permute-start | bytes 1179656 | tf_op jit(solution)/shard_map/ppermute | solution.py:503
  6.1 19.5 %collective-permute-start.2 = (bf16[12,128,128]{2,1,0:T(8,128)(2,1)S(1)}, bf16[12,128,128]{2,1,0:T(8,128)(2,1)S(1)}, u32[]{:S(2)}, u32[]{:S(2)}) collective-permute-start(bf16[12,128,128]{2,1,0:T(8,128)(2,1)S(1)} %get-tuple-element.54), channel_id=1, source_target_pairs={{4,8},{8,4},{5,9},{9,5},{6,10},{10,6},{7,11},{11,7},{20,24},{24,20... | collective-permute-start | bytes 1179656 | tf_op jit(solution)/shard_map/ppermute | solution.py:504
  12.8 2.7 %copy-start.2 = (s32[8]{0:T(128)S(1)}, s32[8]{0:T(128)}, u32[]{:S(2)}) copy-start(s32[8]{0:T(128)} %slots.9) | copy-start | bytes 100
  18.6 10.1 %collective-permute-start.4 = (bf16[2,32,1536]{2,1,0:T(8,128)(2,1)S(1)}, bf16[2,32,1536]{2,1,0:T(8,128)(2,1)S(1)}, u32[]{:S(2)}, u32[]{:S(2)}) collective-permute-start(bf16[2,32,1536]{2,1,0:T(8,128)(2,1)S(1)} %get-tuple-element.68), channel_id=1, source_target_pairs={{0,2},{1,3},{2,0},{3,1},{4,6},{5,7},{6,4},{7,5},{8,10},{9,11},{10,... | collective-permute-start | bytes 589832 | tf_op jit(solution)/shard_map/ppermute | solution.py:510
  21.0 10.9 %collective-permute-start.8 = (bf16[2,32,1536]{2,1,0:T(8,128)(2,1)S(1)}, bf16[2,32,1536]{2,1,0:T(8,128)(2,1)S(1)}, u32[]{:S(2)}, u32[]{:S(2)}) collective-permute-start(bf16[2,32,1536]{2,1,0:T(8,128)(2,1)S(1)} %get-tuple-element.73), channel_id=1, source_target_pairs={{0,3},{1,2},{2,1},{3,0},{4,7},{5,6},{6,5},{7,4},{8,11},{9,10},{10,... | collective-permute-start | bytes 589832 | tf_op jit(solution)/shard_map/ppermute | solution.py:510
  25.7 6.2 %copy-start.4 = (s32[2,1536]{1,0:T(2,128)S(1)}, s32[2,1536]{1,0:T(2,128)}, u32[]{:S(2)}) copy-start(s32[2,1536]{1,0:T(2,128)} %param.8) | copy-start | bytes 36868
  25.7 11.6 %copy-start.3 = (bf16[2,256,1536]{2,1,0:T(8,128)(2,1)S(1)}, bf16[2,256,1536]{2,1,0:T(8,128)(2,1)}, u32[]{:S(2)}) copy-start(bf16[2,256,1536]{2,1,0:T(8,128)(2,1)} %density.3) | copy-start | bytes 4718596
  28.6 8.7 %collective-permute-start.5 = (bf16[2,32,1536]{2,1,0:T(8,128)(2,1)S(1)}, bf16[2,32,1536]{2,1,0:T(8,128)(2,1)S(1)}, u32[]{:S(2)}, u32[]{:S(2)}) collective-permute-start(bf16[2,32,1536]{2,1,0:T(8,128)(2,1)S(1)} %get-tuple-element.70), channel_id=1, source_target_pairs={{0,1},{1,0},{2,3},{3,2},{4,5},{5,4},{6,7},{7,6},{8,9},{9,8},{10,11... | collective-permute-start | bytes 589832 | tf_op jit(solution)/shard_map/ppermute | solution.py:510
  29.7 2.3 %collective-permute-start.12 = (bf16[1,32,1536]{2,1,0:T(8,128)(2,1)S(1)}, bf16[1,32,1536]{2,1,0:T(8,128)(2,1)S(1)}, u32[]{:S(2)}, u32[]{:S(2)}) collective-permute-start(bf16[1,32,1536]{2,1,0:T(8,128)(2,1)S(1)} %get-tuple-element.78), channel_id=1, source_target_pairs={{0,1},{1,0},{2,3},{3,2},{4,5},{5,4},{6,7},{7,6},{8,9},{9,8},{10,11... | collective-permute-start | bytes 294920 | tf_op jit(solution)/shard_map/ppermute | solution.py:510
  29.7 3.9 %collective-permute-start.13 = (bf16[1,32,1536]{2,1,0:T(8,128)(2,1)S(1)}, bf16[1,32,1536]{2,1,0:T(8,128)(2,1)S(1)}, u32[]{:S(2)}, u32[]{:S(2)}) collective-permute-start(bf16[1,32,1536]{2,1,0:T(8,128)(2,1)S(1)} %get-tuple-element.79), channel_id=1, source_target_pairs={{0,2},{1,3},{2,0},{3,1},{4,6},{5,7},{6,4},{7,5},{8,10},{9,11},{10,... | collective-permute-start | bytes 294920 | tf_op jit(solution)/shard_map/ppermute | solution.py:510
  29.7 7.6 %collective-permute-start.14 = (bf16[1,32,1536]{2,1,0:T(8,128)(2,1)S(1)}, bf16[1,32,1536]{2,1,0:T(8,128)(2,1)S(1)}, u32[]{:S(2)}, u32[]{:S(2)}) collective-permute-start(bf16[1,32,1536]{2,1,0:T(8,128)(2,1)S(1)} %get-tuple-element.80), channel_id=1, source_target_pairs={{0,3},{1,2},{2,1},{3,0},{4,7},{5,6},{6,5},{7,4},{8,11},{9,10},{10,... | collective-permute-start | bytes 294920 | tf_op jit(solution)/shard_map/ppermute | solution.py:510
  31.9 25.4 %collective-permute-start.6 = (bf16[1,32,1536]{2,1,0:T(8,128)(2,1)S(1)}, bf16[1,32,1536]{2,1,0:T(8,128)(2,1)S(1)}, u32[]{:S(2)}, u32[]{:S(2)}) collective-permute-start(bf16[1,32,1536]{2,1,0:T(8,128)(2,1)S(1)} %get-tuple-element.71), channel_id=1, source_target_pairs={{0,1},{1,0},{2,3},{3,2},{4,5},{5,4},{6,7},{7,6},{8,9},{9,8},{10,11... | collective-permute-start | bytes 294920 | tf_op jit(solution)/shard_map/ppermute | solution.py:510
  32.0 26.4 %collective-permute-start.7 = (bf16[1,32,1536]{2,1,0:T(8,128)(2,1)S(1)}, bf16[1,32,1536]{2,1,0:T(8,128)(2,1)S(1)}, u32[]{:S(2)}, u32[]{:S(2)}) collective-permute-start(bf16[1,32,1536]{2,1,0:T(8,128)(2,1)S(1)} %get-tuple-element.72), channel_id=1, source_target_pairs={{0,2},{1,3},{2,0},{3,1},{4,6},{5,7},{6,4},{7,5},{8,10},{9,11},{10,... | collective-permute-start | bytes 294920 | tf_op jit(solution)/shard_map/ppermute | solution.py:510
  33.6 24.8 %collective-permute-start.9 = (bf16[1,32,1536]{2,1,0:T(8,128)(2,1)S(1)}, bf16[1,32,1536]{2,1,0:T(8,128)(2,1)S(1)}, u32[]{:S(2)}, u32[]{:S(2)}) collective-permute-start(bf16[1,32,1536]{2,1,0:T(8,128)(2,1)S(1)} %get-tuple-element.74), channel_id=1, source_target_pairs={{0,3},{1,2},{2,1},{3,0},{4,7},{5,6},{6,5},{7,4},{8,11},{9,10},{10,... | collective-permute-start | bytes 294920 | tf_op jit(solution)/shard_map/ppermute | solution.py:510
  56.2 22.2 %collective-permute-start.15 = (bf16[12,64,128]{2,1,0:T(8,128)(2,1)S(1)}, bf16[12,64,128]{2,1,0:T(8,128)(2,1)S(1)}, u32[]{:S(2)}, u32[]{:S(2)}) collective-permute-start(bf16[12,64,128]{2,1,0:T(8,128)(2,1)S(1)} %get-tuple-element.82), channel_id=1, source_target_pairs={{0,1},{1,0},{2,3},{3,2},{4,5},{5,4},{6,7},{7,6},{8,9},{9,8},{10,11... | collective-permute-start | bytes 589832 | tf_op jit(solution)/shard_map/ppermute | solution.py:510
  56.3 24.1 %collective-permute-start.16 = (bf16[12,64,128]{2,1,0:T(8,128)(2,1)S(1)}, bf16[12,64,128]{2,1,0:T(8,128)(2,1)S(1)}, u32[]{:S(2)}, u32[]{:S(2)}) collective-permute-start(bf16[12,64,128]{2,1,0:T(8,128)(2,1)S(1)} %get-tuple-element.83), channel_id=1, source_target_pairs={{0,2},{1,3},{2,0},{3,1},{4,6},{5,7},{6,4},{7,5},{8,10},{9,11},{10,... | collective-permute-start | bytes 589832 | tf_op jit(solution)/shard_map/ppermute | solution.py:510
  57.3 23.1 %collective-permute-start.17 = (bf16[12,64,128]{2,1,0:T(8,128)(2,1)S(1)}, bf16[12,64,128]{2,1,0:T(8,128)(2,1)S(1)}, u32[]{:S(2)}, u32[]{:S(2)}) collective-permute-start(bf16[12,64,128]{2,1,0:T(8,128)(2,1)S(1)} %get-tuple-element.84), channel_id=1, source_target_pairs={{0,3},{1,2},{2,1},{3,0},{4,7},{5,6},{6,5},{7,4},{8,11},{9,10},{10,... | collective-permute-start | bytes 589832 | tf_op jit(solution)/shard_map/ppermute | solution.py:510
  78.2 2.2 %collective-permute-start.18 = (bf16[12,64,128]{2,1,0:T(8,128)(2,1)S(1)}, bf16[12,64,128]{2,1,0:T(8,128)(2,1)S(1)}, u32[]{:S(2)}, u32[]{:S(2)}) collective-permute-start(bf16[12,64,128]{2,1,0:T(8,128)(2,1)S(1)} %get-tuple-element.86), channel_id=1, source_target_pairs={{0,1},{1,0},{2,3},{3,2},{4,5},{5,4},{6,7},{7,6},{8,9},{9,8},{10,11... | collective-permute-start | bytes 589832 | tf_op jit(solution)/shard_map/ppermute | solution.py:510
  78.3 6.1 %collective-permute-start.11 = (bf16[12,64,128]{2,1,0:T(8,128)(2,1)S(1)}, bf16[12,64,128]{2,1,0:T(8,128)(2,1)S(1)}, u32[]{:S(2)}, u32[]{:S(2)}) collective-permute-start(bf16[12,64,128]{2,1,0:T(8,128)(2,1)S(1)} %get-tuple-element.76), channel_id=1, source_target_pairs={{0,2},{1,3},{2,0},{3,1},{4,6},{5,7},{6,4},{7,5},{8,10},{9,11},{10,... | collective-permute-start | bytes 589832 | tf_op jit(solution)/shard_map/ppermute | solution.py:510
  78.4 10.8 %collective-permute-start.10 = (bf16[12,64,128]{2,1,0:T(8,128)(2,1)S(1)}, bf16[12,64,128]{2,1,0:T(8,128)(2,1)S(1)}, u32[]{:S(2)}, u32[]{:S(2)}) collective-permute-start(bf16[12,64,128]{2,1,0:T(8,128)(2,1)S(1)} %get-tuple-element.75), channel_id=1, source_target_pairs={{0,3},{1,2},{2,1},{3,0},{4,7},{5,6},{6,5},{7,4},{8,11},{9,10},{10,... | collective-permute-start | bytes 589832 | tf_op jit(solution)/shard_map/ppermute | solution.py:510

commit v7 on v6

--- a/solution.py
+++ b/solution.py
@@ -223,8 +223,10 @@
 
 
 def second_kernel(peers, per, joined, width, start, slots, atlas, vel, halo, done, *refs):
-    levels, refs = refs[: TSTEPS - 1], refs[TSTEPS - 1 :]
+    levels, refs, (order, sem) = refs[: TSTEPS - 1], refs[TSTEPS - 1 : -2], refs[-2:]
     refs, state = refs[:-TSTEPS], refs[-TSTEPS:]
+    fetch = pltpu.make_async_copy(slots, order, sem)
+    fetch.start()
     high = odd_slab() > 0
     if start == 0:
         outs, (coef, moved, speed) = refs[:-3], refs[-3:]
@@ -246,12 +248,12 @@
         moved[other + i] = done[i]
     me = lax.axis_index(("gy", "af"))
     slab = lax.axis_index("gz")
+    fetch.wait()
     for k in range(peers):
         for s in range(per):
-            z = slots[(me ^ k) * per + s] - slab * rows
+            z = order[(me ^ k) * per + s] - slab * rows
             out = outs[k].at[s] if joined else outs[k * per + s].at[0]
-            for y in range(ny):
-                out[:, y * LANES : (y + 1) * LANES] = moved[z, y]
+            out[...] = moved[z]
 
 
 def side_shapes(atlas, width, start):
@@ -282,7 +284,7 @@
 
 def second_side(slots, atlas, vel, halo, levels, done, coef, width, start, peers, per, joined):
     rows, ny = atlas.shape[:2]
-    out = jax.ShapeDtypeStruct((per if joined else 1, width, ny * LANES), BF16)
+    out = jax.ShapeDtypeStruct((per if joined else 1, ny, width, LANES), BF16)
     count = peers if joined else peers * per
     weights, scratch = side_shapes(atlas, width, start)
     outs = [out] * count + ([weights] if start == 0 else [])
@@ -290,9 +292,11 @@
     result = pl.pallas_call(
         functools.partial(second_kernel, peers, per, joined, width, start),
         out_shape=outs,
-        in_specs=[spec(pltpu.SMEM)] + [spec(pltpu.VMEM)] * (4 + len(levels) + len(extra)),
+        in_specs=[spec(pl.ANY)] + [spec(pltpu.VMEM)] * (4 + len(levels) + len(extra)),
         out_specs=[spec(pltpu.VMEM)] * len(outs),
-        scratch_shapes=[pltpu.VMEM((rows, ny, width, LANES), BF16)] + scratch,
+        scratch_shapes=[pltpu.VMEM((rows, ny, width, LANES), BF16)]
+        + scratch
+        + [pltpu.SMEM((rows,), jnp.int32), pltpu.SemaphoreType.DMA],
         compiler_params=params(28),
         cost_estimate=cost(COST_T),
         name="second_side",
@@ -324,8 +328,10 @@
     for k in range(peers):
         first = k * share
         for block in blocks[k * parts : (k + 1) * parts]:
-            panel[first : first + block.shape[1], :] = block[0]
-            first += block.shape[1]
+            for y in range(ny):
+                rows = slice(first, first + block.shape[2])
+                panel[rows, y * LANES : (y + 1) * LANES] = block[0, y]
+            first += block.shape[2]
     valid = mask[0] > 0
     every = panel[...]
     maps = density[0]
@@ -411,14 +417,14 @@
 
 
 def fit(mask, density, section, blocks, parts, peers):
-    pixels = blocks[0].shape[2]
-    channels = sum(block.shape[1] for block in blocks)
+    ny = blocks[0].shape[1]
+    pixels = ny * LANES
+    channels = sum(block.shape[2] for block in blocks)
     classes = density.shape[1]
-    ny = pixels // LANES
 
     def one(block):
         at = section if block.shape[0] > 1 else 0
-        return pl.BlockSpec((1,) + block.shape[1:], lambda i: (at, 0, 0))
+        return pl.BlockSpec((1,) + block.shape[1:], lambda i: (at, 0, 0, 0))
 
     out = (ny, channels // peers, LANES)
     return pl.pallas_call(
@@ -550,7 +556,10 @@
     late = [(k, last) for k in range(peers // 2, peers - 1)]
     result = place(slots, returned, early, None, rows, per)
     result = place(slots, returned, late, result, rows, per)
-    result = place(slots, returned, [(peers - 1, last)], result, rows, per)
+    far = peers - 1
+    at = (lax.axis_index(("gy", "af")) ^ far) * per + last
+    at = lax.dynamic_index_in_dim(slots, at, keepdims=False) - lax.axis_index("gz") * rows
+    result = lax.dynamic_update_slice(result, returned[far, last][None], (at, 0, 0, 0))
     return jnp.transpose(result, (0, 2, 1, 3))
 
 

time: 91.4 us -> 90 us (0.985)
  Pallas kernels: 59.2 us -> 56 us
  local copies, waits for them, and re-layouts: 0.04 us -> 1.31 us
  waiting for transfers between devices: 12.1 us -> 10.9 us
    ppermute x15, waiting for transfers between devices: 9.69 us -> 7.89 us  [swap(): return lax.ppermute(block, ('gy', 'af'), [(i, i ^ k) for i in range(peers)])]
    pallas_call x3 -> x2, Pallas kernels: 4.09 us -> 2.85 us  [place(): pl.pallas_call(functools.partial(place_kernel, per, which), out_shape=jax...]
    pallas_call x2, Pallas kernels: 38.6 us -> 37.6 us  [fit(): pl.pallas_call(functools.partial(fit_kernel, parts, peers), grid=(1,), ou...]
    pallas_call x2, Pallas kernels: 6.07 us -> 5.15 us  [second_side(): pl.pallas_call(functools.partial(second_kernel, peers, per, joined, width...]
  transfers between devices with their start and end apart: 19 -> 19, of which waited for: 6 -> 6; matrix products, arithmetic and copies ran while one was open for 0% -> 1% of each run, Pallas kernels for 62% -> 62%
where the time goes in v7:
time: 90 us; the launch traced here: 88.6 us
  Pallas kernels  56 us (62%)
  starting transfers between devices  19.6 us (22%)
  waiting for transfers between devices  10.9 us (12%)
  local copies, waits for them, and re-layouts  1.31 us (1%)
    pallas_call x2, Pallas kernels, fit(): pl.pallas_call(functools.partial(fit_kernel, parts, peers), grid=(1,), ou...  37.6 us
    ppermute x15, starting transfers between devices, swap(): return lax.ppermute(block, ('gy', 'af'), [(i, i ^ k) for i in range(peers)])  12.9 us
    ppermute x15, waiting for transfers between devices, swap(): return lax.ppermute(block, ('gy', 'af'), [(i, i ^ k) for i in range(peers)])  7.89 us
    ppermute x2, starting transfers between devices, body(): two = lax.ppermute(edges[1], 'gz', twos)  5.27 us
    pallas_call x2, Pallas kernels, second_side(): pl.pallas_call(functools.partial(second_kernel, peers, per, joined, width...  5.15 us
    pallas_call x2, Pallas kernels, first_side(): pl.pallas_call(functools.partial(first_kernel, width, start), out_shape=o...  4.4 us
    pallas_call x1, Pallas kernels, inner(): pl.pallas_call(inner_kernel, out_shape=[level] * (TSTEPS - 1), in_specs=[...  3.21 us
    pallas_call x2, Pallas kernels, place(): pl.pallas_call(functools.partial(place_kernel, per, which), out_shape=jax...  2.85 us
  transfers between devices with their start and end apart: 19, of which 6 were waited for; matrix products, arithmetic and copies ran while one was open for 1% of the time, Pallas kernels for 62%

profile of v7, /device:TPU:23, one launch (start us, length us, event | category | flops | bytes accessed | tf_op | source)
XLA Modules:
  0.0 88.6 jit_solution(8847773899715607202)
XLA Ops:
  0.0 0.0 copy-start
  0.0 0.0 copy-start.1
  0.0 1.4 %pack_edges.2 = (bf16[12,144,128]{2,1,0:T(8,128)(2,1)S(1)}, bf16[12,144,128]{2,1,0:T(8,128)(2,1)S(1)}) custom-call(bf16[8,12,64,128]{3,2,1,0:T(8,128)(2,1)} %bitcast.6, bf16[3,12,8,128]{3,2,1,0:T(8,128)(2,1)} %bitcast.13), custom_call_target="tpu_custom_call" | custom-call | tf_op jit(solution)/shard_map/pack_edges/pallas_call | solution.py:79
  1.5 1.4 %collective-permute-start.1 = (bf16[12,144,128]{2,1,0:T(8,128)(2,1)S(1)}, bf16[12,144,128]{2,1,0:T(8,128)(2,1)S(1)}, u32[]{:S(2)}, u32[]{:S(2)}) collective-permute-start(bf16[12,144,128]{2,1,0:T(8,128)(2,1)S(1)} %get-tuple-element.47), channel_id=1, source_target_pairs={{0,4},{4,0},{8,12},{12,8},{1,5},{5,1},{9,13},{13,9},{2,6},{6,2},{1... | collective-permute-start | bytes 1327112 | tf_op jit(solution)/shard_map/ppermute | solution.py:509
  2.8 1.9 %collective-permute-start = (bf16[12,144,128]{2,1,0:T(8,128)(2,1)S(1)}, bf16[12,144,128]{2,1,0:T(8,128)(2,1)S(1)}, u32[]{:S(2)}, u32[]{:S(2)}) collective-permute-start(bf16[12,144,128]{2,1,0:T(8,128)(2,1)S(1)} %get-tuple-element.46), channel_id=1, source_target_pairs={{4,8},{8,4},{5,9},{9,5},{6,10},{10,6},{7,11},{11,7},{20,24},{24,20... | collective-permute-start | bytes 1327112 | tf_op jit(solution)/shard_map/ppermute | solution.py:510
  4.7 1.3 %pack_edges.3 = (bf16[12,128,128]{2,1,0:T(8,128)(2,1)S(1)}, bf16[12,128,128]{2,1,0:T(8,128)(2,1)S(1)}) custom-call(bf16[8,12,64,128]{3,2,1,0:T(8,128)(2,1)} %bitcast.7, bf16[3,12,8,128]{3,2,1,0:T(8,128)(2,1)} %bitcast.14), custom_call_target="tpu_custom_call" | custom-call | tf_op jit(solution)/shard_map/pack_edges/pallas_call | solution.py:79
  6.1 0.1 collective-permute-start.3
  6.1 3.4 %collective-permute-start.2 = (bf16[12,128,128]{2,1,0:T(8,128)(2,1)S(1)}, bf16[12,128,128]{2,1,0:T(8,128)(2,1)S(1)}, u32[]{:S(2)}, u32[]{:S(2)}) collective-permute-start(bf16[12,128,128]{2,1,0:T(8,128)(2,1)S(1)} %get-tuple-element.54), channel_id=1, source_target_pairs={{4,8},{8,4},{5,9},{9,5},{6,10},{10,6},{7,11},{11,7},{20,24},{24,20... | collective-permute-start | bytes 1179656 | tf_op jit(solution)/shard_map/ppermute | solution.py:510
  9.5 0.0 copy-done
  9.5 0.0 copy-done.1
  9.5 3.2 %inner_steps.1 = (f32[8,12,64,128]{3,2,1,0:T(8,128)S(1)}, f32[8,12,64,128]{3,2,1,0:T(8,128)S(1)}, f32[8,12,64,128]{3,2,1,0:T(8,128)S(1)}) custom-call(bf16[8,12,64,128]{3,2,1,0:T(8,128)(2,1)S(1)} %bitcast.8, bf16[3,12,8,128]{3,2,1,0:T(8,128)(2,1)S(1)} %bitcast.15), custom_call_target="tpu_custom_call" | custom-call | flops 4000000000 | tf_op jit(solution)/shard_map/inner_steps/pallas_call | solution.py:158
  12.8 0.0 collective-permute-done.1.halo
  12.8 0.0 copy-start.2
  12.8 2.3 %first_side.2 = (bf16[4,12,32,128]{3,2,1,0:T(8,128)(2,1)S(1)}, f32[7,12,16,128]{3,2,1,0:T(8,128)S(1)}) custom-call(bf16[8,12,64,128]{3,2,1,0:T(8,128)(2,1)S(1)} %bitcast.9, bf16[3,12,8,128]{3,2,1,0:T(8,128)(2,1)S(1)} %bitcast.16, bf16[12,144,128]{2,1,0:T(8,128)(2,1)S(1)} %collective-permute-done.1.halo, f32[8,12,64,128]{3,2,1,0:T(8,128)S(1)} %get-tuple-element.49.refs_0_, ...), custom_call_target="tpu_custom_call" | custom-call | flops 1000000000 | tf_op jit(solution)/shard_map/first_side/pallas_call | solution.py:272
  15.1 0.3 collective-permute-done.halo
  15.4 0.0 copy-done.2
  15.4 2.6 %second_side.2 = (bf16[2,12,32,128]{3,2,1,0:T(8,128)(2,1)S(1)}, bf16[2,12,32,128]{3,2,1,0:T(8,128)(2,1)S(1)}, bf16[2,12,32,128]{3,2,1,0:T(8,128)(2,1)S(1)}, bf16...) custom-call(s32[8]{0:T(128)S(1)} %copy-done.2, bf16[8,12,64,128]{3,2,1,0:T(8,128)(2,1)S(1)} %bitcast.10, ...), custom_call_target="tpu_custom_call" | custom-call | flops 1000000000 | tf_op jit(solution)/shard_map/second_side/pallas_call | solution.py:292
  18.0 0.3 collective-permute-start.4
  18.3 2.7 %collective-permute-done.3.halo = bf16[12,128,128]{2,1,0:T(8,128)(2,1)S(1)} collective-permute-done((bf16[12,128,128]{2,1,0:T(8,128)(2,1)S(1)}, bf16[12,128,128]{2,1,0:T(8,128)(2,1)S(1)}, u32[]{:S(2)}, u32[]{:S(2)}) %collective-permute-start.3) | collective-permute-done | bytes 393248 | tf_op jit(solution)/shard_map/ppermute | solution.py:509
  21.0 2.0 %collective-permute-start.8 = (bf16[2,12,32,128]{3,2,1,0:T(8,128)(2,1)S(1)}, bf16[2,12,32,128]{3,2,1,0:T(8,128)(2,1)S(1)}, u32[]{:S(2)}, u32[]{:S(2)}) collective-permute-start(bf16[2,12,32,128]{3,2,1,0:T(8,128)(2,1)S(1)} %get-tuple-element.73), channel_id=1, source_target_pairs={{0,3},{1,2},{2,1},{3,0},{4,7},{5,6},{6,5},{7,4},{8,11},{9,10},{10,... | collective-permute-start | bytes 589832 | tf_op jit(solution)/shard_map/ppermute | solution.py:516
  23.0 2.1 %first_side.3.done = bf16[4,12,32,128]{3,2,1,0:T(8,128)(2,1)S(1)} custom-call(bf16[8,12,64,128]{3,2,1,0:T(8,128)(2,1)S(1)} %bitcast.11, bf16[3,12,8,128]{3,2,1,0:T(8,128)(2,1)S(1)} %bitcast.18, bf16[12,128,128]{2,1,0:T(8,128)(2,1)S(1)} %collective-permute-done.3.halo, f32[8,12,64,128]{3,2,1,0:T(8,128)S(1)} %get-tuple-element.49.refs_0_, ...), custom_call_target="tpu_custom_call" | custom-call | flops 1000000000 | tf_op jit(solution)/shard_map/first_side/pallas_call | solution.py:272
  25.1 0.0 collective-permute-done.2.halo
  25.1 0.0 copy-start.4
  25.1 0.0 copy-start.3
  25.1 2.6 %second_side.3 = (bf16[1,12,32,128]{3,2,1,0:T(8,128)(2,1)S(1)}, bf16[1,12,32,128]{3,2,1,0:T(8,128)(2,1)S(1)}, bf16[1,12,32,128]{3,2,1,0:T(8,128)(2,1)S(1)}, bf16...) custom-call(s32[8]{0:T(128)S(1)} %copy-done.2, ...), custom_call_target="tpu_custom_call" | custom-call | flops 1000000000 | tf_op jit(solution)/shard_map/second_side/pallas_call | solution.py:292
  27.7 0.0 collective-permute-done.4.refs_4_
  27.7 0.9 %collective-permute-start.5 = (bf16[2,12,32,128]{3,2,1,0:T(8,128)(2,1)S(1)}, bf16[2,12,32,128]{3,2,1,0:T(8,128)(2,1)S(1)}, u32[]{:S(2)}, u32[]{:S(2)}) collective-permute-start(bf16[2,12,32,128]{3,2,1,0:T(8,128)(2,1)S(1)} %get-tuple-element.70), channel_id=1, source_target_pairs={{0,1},{1,0},{2,3},{3,2},{4,5},{5,4},{6,7},{7,6},{8,9},{9,8},{10,11... | collective-permute-start | bytes 589832 | tf_op jit(solution)/shard_map/ppermute | solution.py:516
  28.7 0.0 collective-permute-start.11
  28.7 0.5 collective-permute-start.12
  29.2 1.6 %collective-permute-start.13 = (bf16[1,12,32,128]{3,2,1,0:T(8,128)(2,1)S(1)}, bf16[1,12,32,128]{3,2,1,0:T(8,128)(2,1)S(1)}, u32[]{:S(2)}, u32[]{:S(2)}) collective-permute-start(bf16[1,12,32,128]{3,2,1,0:T(8,128)(2,1)S(1)} %get-tuple-element.79), channel_id=1, source_target_pairs={{0,3},{1,2},{2,1},{3,0},{4,7},{5,6},{6,5},{7,4},{8,11},{9,10},{10,... | collective-permute-start | bytes 294920 | tf_op jit(solution)/shard_map/ppermute | solution.py:516
  30.8 0.0 copy-done.4
  30.8 0.0 collective-permute-done.8.refs_6_
  30.8 0.1 collective-permute-start.6
  30.9 0.0 collective-permute-done.11.refs_3_
  30.9 0.2 collective-permute-start.7
  31.1 1.4 %collective-permute-done.12.refs_5_ = bf16[1,12,32,128]{3,2,1,0:T(8,128)(2,1)S(1)} collective-permute-done((bf16[1,12,32,128]{3,2,1,0:T(8,128)(2,1)S(1)}, bf16[1,12,32,128]{3,2,1,0:T(8,128)(2,1)S(1)}, u32[]{:S(2)}, u32[]{:S(2)}) %collective-permute-start.12) | collective-permute-done | bytes 98336 | tf_op jit(solution)/shard_map/ppermute | solution.py:516
  32.5 2.2 %collective-permute-start.9 = (bf16[1,12,32,128]{3,2,1,0:T(8,128)(2,1)S(1)}, bf16[1,12,32,128]{3,2,1,0:T(8,128)(2,1)S(1)}, u32[]{:S(2)}, u32[]{:S(2)}) collective-permute-start(bf16[1,12,32,128]{3,2,1,0:T(8,128)(2,1)S(1)} %get-tuple-element.74), channel_id=1, source_target_pairs={{0,3},{1,2},{2,1},{3,0},{4,7},{5,6},{6,5},{7,4},{8,11},{9,10},{10,... | collective-permute-start | bytes 294920 | tf_op jit(solution)/shard_map/ppermute | solution.py:516
  34.7 1.5 %collective-permute-done.13.refs_7_ = bf16[1,12,32,128]{3,2,1,0:T(8,128)(2,1)S(1)} collective-permute-done((bf16[1,12,32,128]{3,2,1,0:T(8,128)(2,1)S(1)}, bf16[1,12,32,128]{3,2,1,0:T(8,128)(2,1)S(1)}, u32[]{:S(2)}, u32[]{:S(2)}) %collective-permute-start.13) | collective-permute-done | bytes 98336 | tf_op jit(solution)/shard_map/ppermute | solution.py:516
  36.2 0.0 collective-permute-done.5.refs_2_
  36.3 0.0 copy-done.3
  36.3 18.9 %fit.3 = (bf16[12,64,128]{2,1,0:T(8,128)(2,1)S(1)}, bf16[12,64,128]{2,1,0:T(8,128)(2,1)S(1)}, bf16[12,64,128]{2,1,0:T(8,128)(2,1)S(1)}, bf16[12,64,128]{2,1,0:T(8,128)(2,1)S(1)}) custom-call(s32[2,1,1536]{2,1,0:T(1,128)S(1)} %reshape.3.mask, bf16[2,256,1536]{2,1,0:T(8,128)(2,1)S(1)} %copy-done.3, bf16[2,12,32,128]{3,2,1,0:T(8,128)(2,1)S(1)} %get-tuple-element.53.refs_0_, ...), custom_call_target="tpu_custom_call" | custom-call | flops 3000000000 | tf_op jit(solution)/shard_map/fit/pallas_call | solution.py:430
  55.2 0.1 collective-permute-start.14
  55.2 1.1 %collective-permute-start.15 = (bf16[12,64,128]{2,1,0:T(8,128)(2,1)S(1)}, bf16[12,64,128]{2,1,0:T(8,128)(2,1)S(1)}, u32[]{:S(2)}, u32[]{:S(2)}) collective-permute-start(bf16[12,64,128]{2,1,0:T(8,128)(2,1)S(1)} %get-tuple-element.82), channel_id=1, source_target_pairs={{0,2},{1,3},{2,0},{3,1},{4,6},{5,7},{6,4},{7,5},{8,10},{9,11},{10,... | collective-permute-start | bytes 589832 | tf_op jit(solution)/shard_map/ppermute | solution.py:516
  56.4 0.0 collective-permute-done.6.refs_3_
  56.4 1.0 %collective-permute-start.16 = (bf16[12,64,128]{2,1,0:T(8,128)(2,1)S(1)}, bf16[12,64,128]{2,1,0:T(8,128)(2,1)S(1)}, u32[]{:S(2)}, u32[]{:S(2)}) collective-permute-start(bf16[12,64,128]{2,1,0:T(8,128)(2,1)S(1)} %get-tuple-element.83), channel_id=1, source_target_pairs={{0,3},{1,2},{2,1},{3,0},{4,7},{5,6},{6,5},{7,4},{8,11},{9,10},{10,... | collective-permute-start | bytes 589832 | tf_op jit(solution)/shard_map/ppermute | solution.py:516
  57.4 0.0 collective-permute-done.7.refs_5_
  57.4 0.0 collective-permute-done.9.refs_7_
  57.4 18.7 %fit.2 = (bf16[12,64,128]{2,1,0:T(8,128)(2,1)S(1)}, bf16[12,64,128]{2,1,0:T(8,128)(2,1)S(1)}, bf16[12,64,128]{2,1,0:T(8,128)(2,1)S(1)}, bf16[12,64,128]{2,1,0:T(8,128)(2,1)S(1)}) custom-call(s32[2,1,1536]{2,1,0:T(1,128)S(1)} %reshape.3.mask, bf16[2,256,1536]{2,1,0:T(8,128)(2,1)S(1)} %copy-done.3, bf16[2,12,32,128]{3,2,1,0:T(8,128)(2,1)S(1)} %get-tuple-element.53.refs_0_, ...), custom_call_target="tpu_custom_call" | custom-call | flops 3000000000 | tf_op jit(solution)/shard_map/fit/pallas_call | solution.py:430
  76.1 1.0 %collective-permute-start.17 = (bf16[12,64,128]{2,1,0:T(8,128)(2,1)S(1)}, bf16[12,64,128]{2,1,0:T(8,128)(2,1)S(1)}, u32[]{:S(2)}, u32[]{:S(2)}) collective-permute-start(bf16[12,64,128]{2,1,0:T(8,128)(2,1)S(1)} %get-tuple-element.85), channel_id=1, source_target_pairs={{0,1},{1,0},{2,3},{3,2},{4,5},{5,4},{6,7},{7,6},{8,9},{9,8},{10,11... | collective-permute-start | bytes 589832 | tf_op jit(solution)/shard_map/ppermute | solution.py:516
  77.0 1.4 %collective-permute-start.10 = (bf16[12,64,128]{2,1,0:T(8,128)(2,1)S(1)}, bf16[12,64,128]{2,1,0:T(8,128)(2,1)S(1)}, u32[]{:S(2)}, u32[]{:S(2)}) collective-permute-start(bf16[12,64,128]{2,1,0:T(8,128)(2,1)S(1)} %get-tuple-element.75), channel_id=1, source_target_pairs={{0,2},{1,3},{2,0},{3,1},{4,6},{5,7},{6,4},{7,5},{8,10},{9,11},{10,... | collective-permute-start | bytes 589832 | tf_op jit(solution)/shard_map/ppermute | solution.py:516
  78.4 0.6 dynamic_slice.4
  79.7 0.0 collective-permute-done.14.refs_1_
  79.7 0.4 collective-permute-start.18
  80.1 0.0 collective-permute-done.15.refs_2_
  80.1 0.0 collective-permute-done.16.refs_3_
  80.1 0.0 collective-permute-done.17.refs_5_
  80.1 1.6 %place.2.refs_1_ = bf16[8,12,64,128]{3,2,1,0:T(8,128)(2,1)} custom-call(s32[8]{0:T(128)S(1)} %copy-done.2, bf16[12,64,128]{2,1,0:T(8,128)(2,1)S(1)} %get-tuple-element.80.refs_0_, bf16[12,64,128]{2,1,0:T(8,128)(2,1)S(1)} %collective-permute-done.14.refs_1_, bf16[12,64,128]{2,1,0:T(8,128)(2,1)S(1)} %collective-permute-done.15.refs_2_, ...), custom_call_target="tpu_custom_call" | custom-call | flops 1500000000 | tf_op jit(solution)/shard_map/place/pallas_call | solution.py:470
  81.7 1.8 %collective-permute-done.10.refs_0_ = bf16[12,64,128]{2,1,0:T(8,128)(2,1)S(1)} collective-permute-done((bf16[12,64,128]{2,1,0:T(8,128)(2,1)S(1)}, bf16[12,64,128]{2,1,0:T(8,128)(2,1)S(1)}, u32[]{:S(2)}, u32[]{:S(2)}) %collective-permute-start.10) | collective-permute-done | bytes 196640 | tf_op jit(solution)/shard_map/ppermute | solution.py:516
  83.5 1.2 %place.3 = bf16[8,12,64,128]{3,2,1,0:T(8,128)(2,1)} custom-call(s32[8]{0:T(128)S(1)} %copy-done.2, bf16[12,64,128]{2,1,0:T(8,128)(2,1)S(1)} %collective-permute-done.10.refs_0_, bf16[8,12,64,128]{3,2,1,0:T(8,128)(2,1)} %place.2.refs_1_), custom_call_target="tpu_custom_call", output_to_operand_aliasing={{}: (2, {})} | custom-call | flops 1500000000 | tf_op jit(solution)/shard_map/place/pallas_call | solution.py:470
  84.8 3.1 %collective-permute-done.18 = bf16[12,64,128]{2,1,0:T(8,128)(2,1)S(1)} collective-permute-done((bf16[12,64,128]{2,1,0:T(8,128)(2,1)S(1)}, bf16[12,64,128]{2,1,0:T(8,128)(2,1)S(1)}, u32[]{:S(2)}, u32[]{:S(2)}) %collective-permute-start.18) | collective-permute-done | bytes 196640 | tf_op jit(solution)/shard_map/ppermute | solution.py:516
  87.9 0.7 bitcast_dynamic-update-slice_fusion
  (1 shorter events, 0.0 us)
Async XLA Ops:
  0.0 9.5 %copy-start = (bf16[8,64,12,128]{3,1,2,0:T(8,128)(2,1)S(1)}, bf16[8,64,12,128]{3,1,2,0:T(8,128)(2,1)}, u32[]{:S(2)}) copy-start(bf16[8,64,12,128]{3,1,2,0:T(8,128)(2,1)} %param.5) | copy-start | bytes 4718596
  0.0 9.5 %copy-start.1 = (bf16[3,8,12,128]{3,1,2,0:T(8,128)(2,1)S(1)}, bf16[3,8,12,128]{3,1,2,0:T(8,128)(2,1)}, u32[]{:S(2)}) copy-start(bf16[3,8,12,128]{3,1,2,0:T(8,128)(2,1)} %param.6) | copy-start | bytes 221188
  1.5 11.3 %collective-permute-start.1 = (bf16[12,144,128]{2,1,0:T(8,128)(2,1)S(1)}, bf16[12,144,128]{2,1,0:T(8,128)(2,1)S(1)}, u32[]{:S(2)}, u32[]{:S(2)}) collective-permute-start(bf16[12,144,128]{2,1,0:T(8,128)(2,1)S(1)} %get-tuple-element.47), channel_id=1, source_target_pairs={{0,4},{4,0},{8,12},{12,8},{1,5},{5,1},{9,13},{13,9},{2,6},{6,2},{1... | collective-permute-start | bytes 1327112 | tf_op jit(solution)/shard_map/ppermute | solution.py:509
  2.8 12.6 %collective-permute-start = (bf16[12,144,128]{2,1,0:T(8,128)(2,1)S(1)}, bf16[12,144,128]{2,1,0:T(8,128)(2,1)S(1)}, u32[]{:S(2)}, u32[]{:S(2)}) collective-permute-start(bf16[12,144,128]{2,1,0:T(8,128)(2,1)S(1)} %get-tuple-element.46), channel_id=1, source_target_pairs={{4,8},{8,4},{5,9},{9,5},{6,10},{10,6},{7,11},{11,7},{20,24},{24,20... | collective-permute-start | bytes 1327112 | tf_op jit(solution)/shard_map/ppermute | solution.py:510
  6.1 14.9 %collective-permute-start.3 = (bf16[12,128,128]{2,1,0:T(8,128)(2,1)S(1)}, bf16[12,128,128]{2,1,0:T(8,128)(2,1)S(1)}, u32[]{:S(2)}, u32[]{:S(2)}) collective-permute-start(bf16[12,128,128]{2,1,0:T(8,128)(2,1)S(1)} %get-tuple-element.55), channel_id=1, source_target_pairs={{0,4},{4,0},{8,12},{12,8},{1,5},{5,1},{9,13},{13,9},{2,6},{6,2},{1... | collective-permute-start | bytes 1179656 | tf_op jit(solution)/shard_map/ppermute | solution.py:509
  6.1 18.9 %collective-permute-start.2 = (bf16[12,128,128]{2,1,0:T(8,128)(2,1)S(1)}, bf16[12,128,128]{2,1,0:T(8,128)(2,1)S(1)}, u32[]{:S(2)}, u32[]{:S(2)}) collective-permute-start(bf16[12,128,128]{2,1,0:T(8,128)(2,1)S(1)} %get-tuple-element.54), channel_id=1, source_target_pairs={{4,8},{8,4},{5,9},{9,5},{6,10},{10,6},{7,11},{11,7},{20,24},{24,20... | collective-permute-start | bytes 1179656 | tf_op jit(solution)/shard_map/ppermute | solution.py:510
  12.8 2.7 %copy-start.2 = (s32[8]{0:T(128)S(1)}, s32[8]{0:T(128)}, u32[]{:S(2)}) copy-start(s32[8]{0:T(128)} %slots.7) | copy-start | bytes 100
  18.0 9.7 %collective-permute-start.4 = (bf16[2,12,32,128]{3,2,1,0:T(8,128)(2,1)S(1)}, bf16[2,12,32,128]{3,2,1,0:T(8,128)(2,1)S(1)}, u32[]{:S(2)}, u32[]{:S(2)}) collective-permute-start(bf16[2,12,32,128]{3,2,1,0:T(8,128)(2,1)S(1)} %get-tuple-element.68), channel_id=1, source_target_pairs={{0,2},{1,3},{2,0},{3,1},{4,6},{5,7},{6,4},{7,5},{8,10},{9,11},{10,... | collective-permute-start | bytes 589832 | tf_op jit(solution)/shard_map/ppermute | solution.py:516
  21.0 9.8 %collective-permute-start.8 = (bf16[2,12,32,128]{3,2,1,0:T(8,128)(2,1)S(1)}, bf16[2,12,32,128]{3,2,1,0:T(8,128)(2,1)S(1)}, u32[]{:S(2)}, u32[]{:S(2)}) collective-permute-start(bf16[2,12,32,128]{3,2,1,0:T(8,128)(2,1)S(1)} %get-tuple-element.73), channel_id=1, source_target_pairs={{0,3},{1,2},{2,1},{3,0},{4,7},{5,6},{6,5},{7,4},{8,11},{9,10},{10,... | collective-permute-start | bytes 589832 | tf_op jit(solution)/shard_map/ppermute | solution.py:516
  25.1 5.7 %copy-start.4 = (s32[2,1536]{1,0:T(2,128)S(1)}, s32[2,1536]{1,0:T(2,128)}, u32[]{:S(2)}) copy-start(s32[2,1536]{1,0:T(2,128)} %param.8) | copy-start | bytes 36868
  25.1 11.1 %copy-start.3 = (bf16[2,256,1536]{2,1,0:T(8,128)(2,1)S(1)}, bf16[2,256,1536]{2,1,0:T(8,128)(2,1)}, u32[]{:S(2)}) copy-start(bf16[2,256,1536]{2,1,0:T(8,128)(2,1)} %density.3) | copy-start | bytes 4718596
  27.7 8.5 %collective-permute-start.5 = (bf16[2,12,32,128]{3,2,1,0:T(8,128)(2,1)S(1)}, bf16[2,12,32,128]{3,2,1,0:T(8,128)(2,1)S(1)}, u32[]{:S(2)}, u32[]{:S(2)}) collective-permute-start(bf16[2,12,32,128]{3,2,1,0:T(8,128)(2,1)S(1)} %get-tuple-element.70), channel_id=1, source_target_pairs={{0,1},{1,0},{2,3},{3,2},{4,5},{5,4},{6,7},{7,6},{8,9},{9,8},{10,11... | collective-permute-start | bytes 589832 | tf_op jit(solution)/shard_map/ppermute | solution.py:516
  28.7 2.3 %collective-permute-start.11 = (bf16[1,12,32,128]{3,2,1,0:T(8,128)(2,1)S(1)}, bf16[1,12,32,128]{3,2,1,0:T(8,128)(2,1)S(1)}, u32[]{:S(2)}, u32[]{:S(2)}) collective-permute-start(bf16[1,12,32,128]{3,2,1,0:T(8,128)(2,1)S(1)} %get-tuple-element.77), channel_id=1, source_target_pairs={{0,1},{1,0},{2,3},{3,2},{4,5},{5,4},{6,7},{7,6},{8,9},{9,8},{10,11... | collective-permute-start | bytes 294920 | tf_op jit(solution)/shard_map/ppermute | solution.py:516
  28.7 3.9 %collective-permute-start.12 = (bf16[1,12,32,128]{3,2,1,0:T(8,128)(2,1)S(1)}, bf16[1,12,32,128]{3,2,1,0:T(8,128)(2,1)S(1)}, u32[]{:S(2)}, u32[]{:S(2)}) collective-permute-start(bf16[1,12,32,128]{3,2,1,0:T(8,128)(2,1)S(1)} %get-tuple-element.78), channel_id=1, source_target_pairs={{0,2},{1,3},{2,0},{3,1},{4,6},{5,7},{6,4},{7,5},{8,10},{9,11},{10,... | collective-permute-start | bytes 294920 | tf_op jit(solution)/shard_map/ppermute | solution.py:516
  29.2 7.1 %collective-permute-start.13 = (bf16[1,12,32,128]{3,2,1,0:T(8,128)(2,1)S(1)}, bf16[1,12,32,128]{3,2,1,0:T(8,128)(2,1)S(1)}, u32[]{:S(2)}, u32[]{:S(2)}) collective-permute-start(bf16[1,12,32,128]{3,2,1,0:T(8,128)(2,1)S(1)} %get-tuple-element.79), channel_id=1, source_target_pairs={{0,3},{1,2},{2,1},{3,0},{4,7},{5,6},{6,5},{7,4},{8,11},{9,10},{10,... | collective-permute-start | bytes 294920 | tf_op jit(solution)/shard_map/ppermute | solution.py:516
  30.8 25.5 %collective-permute-start.6 = (bf16[1,12,32,128]{3,2,1,0:T(8,128)(2,1)S(1)}, bf16[1,12,32,128]{3,2,1,0:T(8,128)(2,1)S(1)}, u32[]{:S(2)}, u32[]{:S(2)}) collective-permute-start(bf16[1,12,32,128]{3,2,1,0:T(8,128)(2,1)S(1)} %get-tuple-element.71), channel_id=1, source_target_pairs={{0,1},{1,0},{2,3},{3,2},{4,5},{5,4},{6,7},{7,6},{8,9},{9,8},{10,11... | collective-permute-start | bytes 294920 | tf_op jit(solution)/shard_map/ppermute | solution.py:516
  30.9 26.5 %collective-permute-start.7 = (bf16[1,12,32,128]{3,2,1,0:T(8,128)(2,1)S(1)}, bf16[1,12,32,128]{3,2,1,0:T(8,128)(2,1)S(1)}, u32[]{:S(2)}, u32[]{:S(2)}) collective-permute-start(bf16[1,12,32,128]{3,2,1,0:T(8,128)(2,1)S(1)} %get-tuple-element.72), channel_id=1, source_target_pairs={{0,2},{1,3},{2,0},{3,1},{4,6},{5,7},{6,4},{7,5},{8,10},{9,11},{10,... | collective-permute-start | bytes 294920 | tf_op jit(solution)/shard_map/ppermute | solution.py:516
  32.5 24.9 %collective-permute-start.9 = (bf16[1,12,32,128]{3,2,1,0:T(8,128)(2,1)S(1)}, bf16[1,12,32,128]{3,2,1,0:T(8,128)(2,1)S(1)}, u32[]{:S(2)}, u32[]{:S(2)}) collective-permute-start(bf16[1,12,32,128]{3,2,1,0:T(8,128)(2,1)S(1)} %get-tuple-element.74), channel_id=1, source_target_pairs={{0,3},{1,2},{2,1},{3,0},{4,7},{5,6},{6,5},{7,4},{8,11},{9,10},{10,... | collective-permute-start | bytes 294920 | tf_op jit(solution)/shard_map/ppermute | solution.py:516
  55.2 24.5 %collective-permute-start.14 = (bf16[12,64,128]{2,1,0:T(8,128)(2,1)S(1)}, bf16[12,64,128]{2,1,0:T(8,128)(2,1)S(1)}, u32[]{:S(2)}, u32[]{:S(2)}) collective-permute-start(bf16[12,64,128]{2,1,0:T(8,128)(2,1)S(1)} %get-tuple-element.81), channel_id=1, source_target_pairs={{0,1},{1,0},{2,3},{3,2},{4,5},{5,4},{6,7},{7,6},{8,9},{9,8},{10,11... | collective-permute-start | bytes 589832 | tf_op jit(solution)/shard_map/ppermute | solution.py:516
  55.2 24.8 %collective-permute-start.15 = (bf16[12,64,128]{2,1,0:T(8,128)(2,1)S(1)}, bf16[12,64,128]{2,1,0:T(8,128)(2,1)S(1)}, u32[]{:S(2)}, u32[]{:S(2)}) collective-permute-start(bf16[12,64,128]{2,1,0:T(8,128)(2,1)S(1)} %get-tuple-element.82), channel_id=1, source_target_pairs={{0,2},{1,3},{2,0},{3,1},{4,6},{5,7},{6,4},{7,5},{8,10},{9,11},{10,... | collective-permute-start | bytes 589832 | tf_op jit(solution)/shard_map/ppermute | solution.py:516
  56.4 23.7 %collective-permute-start.16 = (bf16[12,64,128]{2,1,0:T(8,128)(2,1)S(1)}, bf16[12,64,128]{2,1,0:T(8,128)(2,1)S(1)}, u32[]{:S(2)}, u32[]{:S(2)}) collective-permute-start(bf16[12,64,128]{2,1,0:T(8,128)(2,1)S(1)} %get-tuple-element.83), channel_id=1, source_target_pairs={{0,3},{1,2},{2,1},{3,0},{4,7},{5,6},{6,5},{7,4},{8,11},{9,10},{10,... | collective-permute-start | bytes 589832 | tf_op jit(solution)/shard_map/ppermute | solution.py:516
  76.1 4.0 %collective-permute-start.17 = (bf16[12,64,128]{2,1,0:T(8,128)(2,1)S(1)}, bf16[12,64,128]{2,1,0:T(8,128)(2,1)S(1)}, u32[]{:S(2)}, u32[]{:S(2)}) collective-permute-start(bf16[12,64,128]{2,1,0:T(8,128)(2,1)S(1)} %get-tuple-element.85), channel_id=1, source_target_pairs={{0,1},{1,0},{2,3},{3,2},{4,5},{5,4},{6,7},{7,6},{8,9},{9,8},{10,11... | collective-permute-start | bytes 589832 | tf_op jit(solution)/shard_map/ppermute | solution.py:516
  77.0 6.5 %collective-permute-start.10 = (bf16[12,64,128]{2,1,0:T(8,128)(2,1)S(1)}, bf16[12,64,128]{2,1,0:T(8,128)(2,1)S(1)}, u32[]{:S(2)}, u32[]{:S(2)}) collective-permute-start(bf16[12,64,128]{2,1,0:T(8,128)(2,1)S(1)} %get-tuple-element.75), channel_id=1, source_target_pairs={{0,2},{1,3},{2,0},{3,1},{4,6},{5,7},{6,4},{7,5},{8,10},{9,11},{10,... | collective-permute-start | bytes 589832 | tf_op jit(solution)/shard_map/ppermute | solution.py:516
  79.7 8.2 %collective-permute-start.18 = (bf16[12,64,128]{2,1,0:T(8,128)(2,1)S(1)}, bf16[12,64,128]{2,1,0:T(8,128)(2,1)S(1)}, u32[]{:S(2)}, u32[]{:S(2)}) collective-permute-start(bf16[12,64,128]{2,1,0:T(8,128)(2,1)S(1)} %get-tuple-element.86), channel_id=1, source_target_pairs={{0,3},{1,2},{2,1},{3,0},{4,7},{5,6},{6,5},{7,4},{8,11},{9,10},{10,... | collective-permute-start | bytes 589832 | tf_op jit(solution)/shard_map/ppermute | solution.py:516

commit v8 on v7

--- a/solution.py
+++ b/solution.py
@@ -16,7 +16,7 @@
 BF16 = jnp.bfloat16
 VEL_ROWS = 16
 WIDTHS = (32, 32)
-COST_I, COST_T, COST_F, COST_P = 4 * 10**9, 10**9, 3 * 10**9, 15 * 10**8
+COST_I, COST_T, COST_F, COST_P = 4 * 10**9, 10**8, 10 * 10**9, 10**8
 EASY = 1.08
 FAIR = 3.8
 
@@ -343,9 +343,11 @@
     gram[...] = lax.dot_general(every, masked, contract, preferred_element_type=F32) * (
         1.0 / pixels
     ) + jnp.where(same, RIDGE, 0.0)
-    right[...] = lax.dot_general(maps, masked, contract, preferred_element_type=F32) * (
-        1.0 / pixels
-    )
+
+    def set_right():
+        product = lax.dot_general(maps, masked, contract, preferred_element_type=F32)
+        right[...] = product * (1.0 / pixels)
+
     sums = jnp.sum(jnp.abs(gram[...]), axis=0, keepdims=True)
     bound_row = jnp.max(sums, axis=1, keepdims=True)
     bound = jnp.max(sums)
@@ -368,30 +370,33 @@
         left = (right[...] - product).astype(BF16)
         answer[...] = answer[...] + dot(left, inverse[...].astype(BF16))
 
-    @pl.when(bound <= FAIR)
-    def _():
-        spread1, scale1 = narrowed(spread)
-        spread2, scale2 = narrowed(spread1)
-        _, scale3 = narrowed(spread2)
-        inverse[...] = scale1 * (
+    def solve(doublings):
+        scales = []
+        rest = spread
+        for _ in range(doublings + 1):
+            rest, scale = narrowed(rest)
+            scales.append(scale)
+        set_right()
+        inverse[...] = scales[0] * (
             jnp.where(same, 2.0 * start, 0.0) - (start * start) * gram[...]
         )
-        doubled(scale2)
-
-        @pl.when(bound > EASY)
-        def _():
-            doubled(scale3)
-
+        for scale in scales[1:]:
+            doubled(scale)
         answer[...] = dot(right[...].astype(BF16), inverse[...].astype(BF16))
-        refined()
-        refined()
-
-        @pl.when(bound > EASY)
-        def _():
+        for _ in range(doublings + 1):
             refined()
+
+    @pl.when(bound <= EASY)
+    def _():
+        solve(1)
+
+    @pl.when((bound > EASY) & (bound <= FAIR))
+    def _():
+        solve(2)
 
     @pl.when(bound > FAIR)
     def _():
+        set_right()
         inverse[...] = jnp.where(same, start, 0.0)
 
         def step(spread):

time: 90 us -> 90.8 us (level)
  no operation moved by 1% of the time
where the time goes in v8:
time: 90.8 us; the launch traced here: 89.1 us
  Pallas kernels  56.4 us (62%)
  starting transfers between devices  19.5 us (21%)
  waiting for transfers between devices  10.9 us (12%)
  local copies, waits for them, and re-layouts  1.31 us (1%)
    pallas_call x2, Pallas kernels, fit(): pl.pallas_call(functools.partial(fit_kernel, parts, peers), grid=(1,), ou...  38.1 us
    ppermute x15, starting transfers between devices, swap(): return lax.ppermute(block, ('gy', 'af'), [(i, i ^ k) for i in range(peers)])  12.8 us
    ppermute x15, waiting for transfers between devices, swap(): return lax.ppermute(block, ('gy', 'af'), [(i, i ^ k) for i in range(peers)])  7.93 us
    ppermute x2, starting transfers between devices, body(): two = lax.ppermute(edges[1], 'gz', twos)  5.27 us
    pallas_call x2, Pallas kernels, second_side(): pl.pallas_call(functools.partial(second_kernel, peers, per, joined, width...  5.15 us
    pallas_call x2, Pallas kernels, first_side(): pl.pallas_call(functools.partial(first_kernel, width, start), out_shape=o...  4.4 us
    pallas_call x1, Pallas kernels, inner(): pl.pallas_call(inner_kernel, out_shape=[level] * (TSTEPS - 1), in_specs=[...  3.21 us
    pallas_call x2, Pallas kernels, place(): pl.pallas_call(functools.partial(place_kernel, per, which), out_shape=jax...  2.85 us
  transfers between devices with their start and end apart: 19, of which 6 were waited for; matrix products, arithmetic and copies ran while one was open for 1% of the time, Pallas kernels for 62%

profile of v8, /device:TPU:23, one launch (start us, length us, event | category | flops | bytes accessed | tf_op | source)
XLA Modules:
  0.0 89.1 jit_solution(17466296707328048791)
XLA Ops:
  0.0 0.0 copy-start
  0.0 0.0 copy-start.1
  0.0 1.4 %pack_edges.2 = (bf16[12,144,128]{2,1,0:T(8,128)(2,1)S(1)}, bf16[12,144,128]{2,1,0:T(8,128)(2,1)S(1)}) custom-call(bf16[8,12,64,128]{3,2,1,0:T(8,128)(2,1)} %bitcast.6, bf16[3,12,8,128]{3,2,1,0:T(8,128)(2,1)} %bitcast.13), custom_call_target="tpu_custom_call" | custom-call | tf_op jit(solution)/shard_map/pack_edges/pallas_call | solution.py:79
  1.5 1.4 %collective-permute-start.1 = (bf16[12,144,128]{2,1,0:T(8,128)(2,1)S(1)}, bf16[12,144,128]{2,1,0:T(8,128)(2,1)S(1)}, u32[]{:S(2)}, u32[]{:S(2)}) collective-permute-start(bf16[12,144,128]{2,1,0:T(8,128)(2,1)S(1)} %get-tuple-element.47), channel_id=1, source_target_pairs={{0,4},{4,0},{8,12},{12,8},{1,5},{5,1},{9,13},{13,9},{2,6},{6,2},{1... | collective-permute-start | bytes 1327112 | tf_op jit(solution)/shard_map/ppermute | solution.py:514
  2.8 1.9 %collective-permute-start = (bf16[12,144,128]{2,1,0:T(8,128)(2,1)S(1)}, bf16[12,144,128]{2,1,0:T(8,128)(2,1)S(1)}, u32[]{:S(2)}, u32[]{:S(2)}) collective-permute-start(bf16[12,144,128]{2,1,0:T(8,128)(2,1)S(1)} %get-tuple-element.46), channel_id=1, source_target_pairs={{4,8},{8,4},{5,9},{9,5},{6,10},{10,6},{7,11},{11,7},{20,24},{24,20... | collective-permute-start | bytes 1327112 | tf_op jit(solution)/shard_map/ppermute | solution.py:515
  4.7 1.3 %pack_edges.3 = (bf16[12,128,128]{2,1,0:T(8,128)(2,1)S(1)}, bf16[12,128,128]{2,1,0:T(8,128)(2,1)S(1)}) custom-call(bf16[8,12,64,128]{3,2,1,0:T(8,128)(2,1)} %bitcast.7, bf16[3,12,8,128]{3,2,1,0:T(8,128)(2,1)} %bitcast.14), custom_call_target="tpu_custom_call" | custom-call | tf_op jit(solution)/shard_map/pack_edges/pallas_call | solution.py:79
  6.1 0.1 collective-permute-start.3
  6.1 3.4 %collective-permute-start.2 = (bf16[12,128,128]{2,1,0:T(8,128)(2,1)S(1)}, bf16[12,128,128]{2,1,0:T(8,128)(2,1)S(1)}, u32[]{:S(2)}, u32[]{:S(2)}) collective-permute-start(bf16[12,128,128]{2,1,0:T(8,128)(2,1)S(1)} %get-tuple-element.54), channel_id=1, source_target_pairs={{4,8},{8,4},{5,9},{9,5},{6,10},{10,6},{7,11},{11,7},{20,24},{24,20... | collective-permute-start | bytes 1179656 | tf_op jit(solution)/shard_map/ppermute | solution.py:515
  9.5 0.0 copy-done
  9.5 0.0 copy-done.1
  9.5 3.2 %inner_steps.1 = (f32[8,12,64,128]{3,2,1,0:T(8,128)S(1)}, f32[8,12,64,128]{3,2,1,0:T(8,128)S(1)}, f32[8,12,64,128]{3,2,1,0:T(8,128)S(1)}) custom-call(bf16[8,12,64,128]{3,2,1,0:T(8,128)(2,1)S(1)} %bitcast.8, bf16[3,12,8,128]{3,2,1,0:T(8,128)(2,1)S(1)} %bitcast.15), custom_call_target="tpu_custom_call" | custom-call | flops 4000000000 | tf_op jit(solution)/shard_map/inner_steps/pallas_call | solution.py:158
  12.8 0.0 collective-permute-done.1.halo
  12.8 0.0 copy-start.2
  12.8 2.3 %first_side.2 = (bf16[4,12,32,128]{3,2,1,0:T(8,128)(2,1)S(1)}, f32[7,12,16,128]{3,2,1,0:T(8,128)S(1)}) custom-call(bf16[8,12,64,128]{3,2,1,0:T(8,128)(2,1)S(1)} %bitcast.9, bf16[3,12,8,128]{3,2,1,0:T(8,128)(2,1)S(1)} %bitcast.16, bf16[12,144,128]{2,1,0:T(8,128)(2,1)S(1)} %collective-permute-done.1.halo, f32[8,12,64,128]{3,2,1,0:T(8,128)S(1)} %get-tuple-element.49.refs_0_, ...), custom_call_target="tpu_custom_call" | custom-call | flops 100000000 | tf_op jit(solution)/shard_map/first_side/pallas_call | solution.py:272
  15.1 0.3 collective-permute-done.halo
  15.4 0.0 copy-done.2
  15.4 2.6 %second_side.2 = (bf16[2,12,32,128]{3,2,1,0:T(8,128)(2,1)S(1)}, bf16[2,12,32,128]{3,2,1,0:T(8,128)(2,1)S(1)}, bf16[2,12,32,128]{3,2,1,0:T(8,128)(2,1)S(1)}, bf16...) custom-call(s32[8]{0:T(128)S(1)} %copy-done.2, bf16[8,12,64,128]{3,2,1,0:T(8,128)(2,1)S(1)} %bitcast.10, ...), custom_call_target="tpu_custom_call" | custom-call | flops 100000000 | tf_op jit(solution)/shard_map/second_side/pallas_call | solution.py:292
  18.0 0.3 collective-permute-start.4
  18.3 2.7 %collective-permute-done.3.halo = bf16[12,128,128]{2,1,0:T(8,128)(2,1)S(1)} collective-permute-done((bf16[12,128,128]{2,1,0:T(8,128)(2,1)S(1)}, bf16[12,128,128]{2,1,0:T(8,128)(2,1)S(1)}, u32[]{:S(2)}, u32[]{:S(2)}) %collective-permute-start.3) | collective-permute-done | bytes 393248 | tf_op jit(solution)/shard_map/ppermute | solution.py:514
  21.0 2.0 %collective-permute-start.8 = (bf16[2,12,32,128]{3,2,1,0:T(8,128)(2,1)S(1)}, bf16[2,12,32,128]{3,2,1,0:T(8,128)(2,1)S(1)}, u32[]{:S(2)}, u32[]{:S(2)}) collective-permute-start(bf16[2,12,32,128]{3,2,1,0:T(8,128)(2,1)S(1)} %get-tuple-element.73), channel_id=1, source_target_pairs={{0,3},{1,2},{2,1},{3,0},{4,7},{5,6},{6,5},{7,4},{8,11},{9,10},{10,... | collective-permute-start | bytes 589832 | tf_op jit(solution)/shard_map/ppermute | solution.py:521
  23.0 2.1 %first_side.3.done = bf16[4,12,32,128]{3,2,1,0:T(8,128)(2,1)S(1)} custom-call(bf16[8,12,64,128]{3,2,1,0:T(8,128)(2,1)S(1)} %bitcast.11, bf16[3,12,8,128]{3,2,1,0:T(8,128)(2,1)S(1)} %bitcast.18, bf16[12,128,128]{2,1,0:T(8,128)(2,1)S(1)} %collective-permute-done.3.halo, f32[8,12,64,128]{3,2,1,0:T(8,128)S(1)} %get-tuple-element.49.refs_0_, ...), custom_call_target="tpu_custom_call" | custom-call | flops 100000000 | tf_op jit(solution)/shard_map/first_side/pallas_call | solution.py:272
  25.1 0.0 collective-permute-done.2.halo
  25.1 0.0 copy-start.4
  25.1 0.0 copy-start.3
  25.1 2.6 %second_side.3 = (bf16[1,12,32,128]{3,2,1,0:T(8,128)(2,1)S(1)}, bf16[1,12,32,128]{3,2,1,0:T(8,128)(2,1)S(1)}, bf16[1,12,32,128]{3,2,1,0:T(8,128)(2,1)S(1)}, bf16...) custom-call(s32[8]{0:T(128)S(1)} %copy-done.2, ...), custom_call_target="tpu_custom_call" | custom-call | flops 100000000 | tf_op jit(solution)/shard_map/second_side/pallas_call | solution.py:292
  27.7 0.0 collective-permute-done.4.refs_4_
  27.7 0.9 %collective-permute-start.5 = (bf16[2,12,32,128]{3,2,1,0:T(8,128)(2,1)S(1)}, bf16[2,12,32,128]{3,2,1,0:T(8,128)(2,1)S(1)}, u32[]{:S(2)}, u32[]{:S(2)}) collective-permute-start(bf16[2,12,32,128]{3,2,1,0:T(8,128)(2,1)S(1)} %get-tuple-element.70), channel_id=1, source_target_pairs={{0,1},{1,0},{2,3},{3,2},{4,5},{5,4},{6,7},{7,6},{8,9},{9,8},{10,11... | collective-permute-start | bytes 589832 | tf_op jit(solution)/shard_map/ppermute | solution.py:521
  28.7 0.0 collective-permute-start.11
  28.7 0.5 collective-permute-start.12
  29.2 1.6 %collective-permute-start.13 = (bf16[1,12,32,128]{3,2,1,0:T(8,128)(2,1)S(1)}, bf16[1,12,32,128]{3,2,1,0:T(8,128)(2,1)S(1)}, u32[]{:S(2)}, u32[]{:S(2)}) collective-permute-start(bf16[1,12,32,128]{3,2,1,0:T(8,128)(2,1)S(1)} %get-tuple-element.79), channel_id=1, source_target_pairs={{0,3},{1,2},{2,1},{3,0},{4,7},{5,6},{6,5},{7,4},{8,11},{9,10},{10,... | collective-permute-start | bytes 294920 | tf_op jit(solution)/shard_map/ppermute | solution.py:521
  30.8 0.0 copy-done.4
  30.8 0.0 collective-permute-done.8.refs_6_
  30.8 0.1 collective-permute-start.6
  30.9 0.0 collective-permute-done.11.refs_3_
  30.9 0.2 collective-permute-start.7
  31.1 1.4 %collective-permute-done.12.refs_5_ = bf16[1,12,32,128]{3,2,1,0:T(8,128)(2,1)S(1)} collective-permute-done((bf16[1,12,32,128]{3,2,1,0:T(8,128)(2,1)S(1)}, bf16[1,12,32,128]{3,2,1,0:T(8,128)(2,1)S(1)}, u32[]{:S(2)}, u32[]{:S(2)}) %collective-permute-start.12) | collective-permute-done | bytes 98336 | tf_op jit(solution)/shard_map/ppermute | solution.py:521
  32.5 2.2 %collective-permute-start.9 = (bf16[1,12,32,128]{3,2,1,0:T(8,128)(2,1)S(1)}, bf16[1,12,32,128]{3,2,1,0:T(8,128)(2,1)S(1)}, u32[]{:S(2)}, u32[]{:S(2)}) collective-permute-start(bf16[1,12,32,128]{3,2,1,0:T(8,128)(2,1)S(1)} %get-tuple-element.74), channel_id=1, source_target_pairs={{0,3},{1,2},{2,1},{3,0},{4,7},{5,6},{6,5},{7,4},{8,11},{9,10},{10,... | collective-permute-start | bytes 294920 | tf_op jit(solution)/shard_map/ppermute | solution.py:521
  34.7 1.5 %collective-permute-done.13.refs_7_ = bf16[1,12,32,128]{3,2,1,0:T(8,128)(2,1)S(1)} collective-permute-done((bf16[1,12,32,128]{3,2,1,0:T(8,128)(2,1)S(1)}, bf16[1,12,32,128]{3,2,1,0:T(8,128)(2,1)S(1)}, u32[]{:S(2)}, u32[]{:S(2)}) %collective-permute-start.13) | collective-permute-done | bytes 98336 | tf_op jit(solution)/shard_map/ppermute | solution.py:521
  36.2 0.0 collective-permute-done.5.refs_2_
  36.3 0.0 copy-done.3
  36.3 19.1 %fit.3 = (bf16[12,64,128]{2,1,0:T(8,128)(2,1)S(1)}, bf16[12,64,128]{2,1,0:T(8,128)(2,1)S(1)}, bf16[12,64,128]{2,1,0:T(8,128)(2,1)S(1)}, bf16[12,64,128]{2,1,0:T(8,128)(2,1)S(1)}) custom-call(s32[2,1,1536]{2,1,0:T(1,128)S(1)} %reshape.3.mask, bf16[2,256,1536]{2,1,0:T(8,128)(2,1)S(1)} %copy-done.3, bf16[2,12,32,128]{3,2,1,0:T(8,128)(2,1)S(1)} %get-tuple-element.53.refs_0_, ...), custom_call_target="tpu_custom_call" | custom-call | flops 10000000000 | tf_op jit(solution)/shard_map/fit/pallas_call | solution.py:435
  55.4 0.1 collective-permute-start.14
  55.5 1.2 %collective-permute-start.15 = (bf16[12,64,128]{2,1,0:T(8,128)(2,1)S(1)}, bf16[12,64,128]{2,1,0:T(8,128)(2,1)S(1)}, u32[]{:S(2)}, u32[]{:S(2)}) collective-permute-start(bf16[12,64,128]{2,1,0:T(8,128)(2,1)S(1)} %get-tuple-element.82), channel_id=1, source_target_pairs={{0,2},{1,3},{2,0},{3,1},{4,6},{5,7},{6,4},{7,5},{8,10},{9,11},{10,... | collective-permute-start | bytes 589832 | tf_op jit(solution)/shard_map/ppermute | solution.py:521
  56.6 0.0 collective-permute-done.6.refs_3_
  56.6 1.0 %collective-permute-start.16 = (bf16[12,64,128]{2,1,0:T(8,128)(2,1)S(1)}, bf16[12,64,128]{2,1,0:T(8,128)(2,1)S(1)}, u32[]{:S(2)}, u32[]{:S(2)}) collective-permute-start(bf16[12,64,128]{2,1,0:T(8,128)(2,1)S(1)} %get-tuple-element.83), channel_id=1, source_target_pairs={{0,3},{1,2},{2,1},{3,0},{4,7},{5,6},{6,5},{7,4},{8,11},{9,10},{10,... | collective-permute-start | bytes 589832 | tf_op jit(solution)/shard_map/ppermute | solution.py:521
  57.6 0.0 collective-permute-done.7.refs_5_
  57.6 0.0 collective-permute-done.9.refs_7_
  57.6 18.9 %fit.2 = (bf16[12,64,128]{2,1,0:T(8,128)(2,1)S(1)}, bf16[12,64,128]{2,1,0:T(8,128)(2,1)S(1)}, bf16[12,64,128]{2,1,0:T(8,128)(2,1)S(1)}, bf16[12,64,128]{2,1,0:T(8,128)(2,1)S(1)}) custom-call(s32[2,1,1536]{2,1,0:T(1,128)S(1)} %reshape.3.mask, bf16[2,256,1536]{2,1,0:T(8,128)(2,1)S(1)} %copy-done.3, bf16[2,12,32,128]{3,2,1,0:T(8,128)(2,1)S(1)} %get-tuple-element.53.refs_0_, ...), custom_call_target="tpu_custom_call" | custom-call | flops 10000000000 | tf_op jit(solution)/shard_map/fit/pallas_call | solution.py:435
  76.6 1.0 %collective-permute-start.17 = (bf16[12,64,128]{2,1,0:T(8,128)(2,1)S(1)}, bf16[12,64,128]{2,1,0:T(8,128)(2,1)S(1)}, u32[]{:S(2)}, u32[]{:S(2)}) collective-permute-start(bf16[12,64,128]{2,1,0:T(8,128)(2,1)S(1)} %get-tuple-element.85), channel_id=1, source_target_pairs={{0,1},{1,0},{2,3},{3,2},{4,5},{5,4},{6,7},{7,6},{8,9},{9,8},{10,11... | collective-permute-start | bytes 589832 | tf_op jit(solution)/shard_map/ppermute | solution.py:521
  77.5 1.4 %collective-permute-start.10 = (bf16[12,64,128]{2,1,0:T(8,128)(2,1)S(1)}, bf16[12,64,128]{2,1,0:T(8,128)(2,1)S(1)}, u32[]{:S(2)}, u32[]{:S(2)}) collective-permute-start(bf16[12,64,128]{2,1,0:T(8,128)(2,1)S(1)} %get-tuple-element.75), channel_id=1, source_target_pairs={{0,2},{1,3},{2,0},{3,1},{4,6},{5,7},{6,4},{7,5},{8,10},{9,11},{10,... | collective-permute-start | bytes 589832 | tf_op jit(solution)/shard_map/ppermute | solution.py:521
  78.9 0.0 collective-permute-done.14.refs_1_
  78.9 0.3 collective-permute-start.18
  79.2 0.6 dynamic_slice.4
  80.5 0.0 collective-permute-done.15.refs_2_
  80.5 0.0 collective-permute-done.16.refs_3_
  80.5 0.0 collective-permute-done.17.refs_5_
  80.5 1.6 %place.2.refs_1_ = bf16[8,12,64,128]{3,2,1,0:T(8,128)(2,1)} custom-call(s32[8]{0:T(128)S(1)} %copy-done.2, bf16[12,64,128]{2,1,0:T(8,128)(2,1)S(1)} %get-tuple-element.80.refs_0_, bf16[12,64,128]{2,1,0:T(8,128)(2,1)S(1)} %collective-permute-done.14.refs_1_, bf16[12,64,128]{2,1,0:T(8,128)(2,1)S(1)} %collective-permute-done.15.refs_2_, ...), custom_call_target="tpu_custom_call" | custom-call | flops 100000000 | tf_op jit(solution)/shard_map/place/pallas_call | solution.py:475
  82.1 1.9 %collective-permute-done.10.refs_0_ = bf16[12,64,128]{2,1,0:T(8,128)(2,1)S(1)} collective-permute-done((bf16[12,64,128]{2,1,0:T(8,128)(2,1)S(1)}, bf16[12,64,128]{2,1,0:T(8,128)(2,1)S(1)}, u32[]{:S(2)}, u32[]{:S(2)}) %collective-permute-start.10) | collective-permute-done | bytes 196640 | tf_op jit(solution)/shard_map/ppermute | solution.py:521
  84.0 1.2 %place.3 = bf16[8,12,64,128]{3,2,1,0:T(8,128)(2,1)} custom-call(s32[8]{0:T(128)S(1)} %copy-done.2, bf16[12,64,128]{2,1,0:T(8,128)(2,1)S(1)} %collective-permute-done.10.refs_0_, bf16[8,12,64,128]{3,2,1,0:T(8,128)(2,1)} %place.2.refs_1_), custom_call_target="tpu_custom_call", output_to_operand_aliasing={{}: (2, {})} | custom-call | flops 100000000 | tf_op jit(solution)/shard_map/place/pallas_call | solution.py:475
  85.2 3.1 %collective-permute-done.18 = bf16[12,64,128]{2,1,0:T(8,128)(2,1)S(1)} collective-permute-done((bf16[12,64,128]{2,1,0:T(8,128)(2,1)S(1)}, bf16[12,64,128]{2,1,0:T(8,128)(2,1)S(1)}, u32[]{:S(2)}, u32[]{:S(2)}) %collective-permute-start.18) | collective-permute-done | bytes 196640 | tf_op jit(solution)/shard_map/ppermute | solution.py:521
  88.4 0.7 bitcast_dynamic-update-slice_fusion
  (1 shorter events, 0.0 us)
Async XLA Ops:
  0.0 9.5 %copy-start = (bf16[8,64,12,128]{3,1,2,0:T(8,128)(2,1)S(1)}, bf16[8,64,12,128]{3,1,2,0:T(8,128)(2,1)}, u32[]{:S(2)}) copy-start(bf16[8,64,12,128]{3,1,2,0:T(8,128)(2,1)} %param.5) | copy-start | bytes 4718596
  0.0 9.5 %copy-start.1 = (bf16[3,8,12,128]{3,1,2,0:T(8,128)(2,1)S(1)}, bf16[3,8,12,128]{3,1,2,0:T(8,128)(2,1)}, u32[]{:S(2)}) copy-start(bf16[3,8,12,128]{3,1,2,0:T(8,128)(2,1)} %param.6) | copy-start | bytes 221188
  1.5 11.3 %collective-permute-start.1 = (bf16[12,144,128]{2,1,0:T(8,128)(2,1)S(1)}, bf16[12,144,128]{2,1,0:T(8,128)(2,1)S(1)}, u32[]{:S(2)}, u32[]{:S(2)}) collective-permute-start(bf16[12,144,128]{2,1,0:T(8,128)(2,1)S(1)} %get-tuple-element.47), channel_id=1, source_target_pairs={{0,4},{4,0},{8,12},{12,8},{1,5},{5,1},{9,13},{13,9},{2,6},{6,2},{1... | collective-permute-start | bytes 1327112 | tf_op jit(solution)/shard_map/ppermute | solution.py:514
  2.8 12.6 %collective-permute-start = (bf16[12,144,128]{2,1,0:T(8,128)(2,1)S(1)}, bf16[12,144,128]{2,1,0:T(8,128)(2,1)S(1)}, u32[]{:S(2)}, u32[]{:S(2)}) collective-permute-start(bf16[12,144,128]{2,1,0:T(8,128)(2,1)S(1)} %get-tuple-element.46), channel_id=1, source_target_pairs={{4,8},{8,4},{5,9},{9,5},{6,10},{10,6},{7,11},{11,7},{20,24},{24,20... | collective-permute-start | bytes 1327112 | tf_op jit(solution)/shard_map/ppermute | solution.py:515
  6.1 14.9 %collective-permute-start.3 = (bf16[12,128,128]{2,1,0:T(8,128)(2,1)S(1)}, bf16[12,128,128]{2,1,0:T(8,128)(2,1)S(1)}, u32[]{:S(2)}, u32[]{:S(2)}) collective-permute-start(bf16[12,128,128]{2,1,0:T(8,128)(2,1)S(1)} %get-tuple-element.55), channel_id=1, source_target_pairs={{0,4},{4,0},{8,12},{12,8},{1,5},{5,1},{9,13},{13,9},{2,6},{6,2},{1... | collective-permute-start | bytes 1179656 | tf_op jit(solution)/shard_map/ppermute | solution.py:514
  6.1 18.9 %collective-permute-start.2 = (bf16[12,128,128]{2,1,0:T(8,128)(2,1)S(1)}, bf16[12,128,128]{2,1,0:T(8,128)(2,1)S(1)}, u32[]{:S(2)}, u32[]{:S(2)}) collective-permute-start(bf16[12,128,128]{2,1,0:T(8,128)(2,1)S(1)} %get-tuple-element.54), channel_id=1, source_target_pairs={{4,8},{8,4},{5,9},{9,5},{6,10},{10,6},{7,11},{11,7},{20,24},{24,20... | collective-permute-start | bytes 1179656 | tf_op jit(solution)/shard_map/ppermute | solution.py:515
  12.8 2.7 %copy-start.2 = (s32[8]{0:T(128)S(1)}, s32[8]{0:T(128)}, u32[]{:S(2)}) copy-start(s32[8]{0:T(128)} %slots.7) | copy-start | bytes 100
  18.0 9.7 %collective-permute-start.4 = (bf16[2,12,32,128]{3,2,1,0:T(8,128)(2,1)S(1)}, bf16[2,12,32,128]{3,2,1,0:T(8,128)(2,1)S(1)}, u32[]{:S(2)}, u32[]{:S(2)}) collective-permute-start(bf16[2,12,32,128]{3,2,1,0:T(8,128)(2,1)S(1)} %get-tuple-element.68), channel_id=1, source_target_pairs={{0,2},{1,3},{2,0},{3,1},{4,6},{5,7},{6,4},{7,5},{8,10},{9,11},{10,... | collective-permute-start | bytes 589832 | tf_op jit(solution)/shard_map/ppermute | solution.py:521
  21.0 9.8 %collective-permute-start.8 = (bf16[2,12,32,128]{3,2,1,0:T(8,128)(2,1)S(1)}, bf16[2,12,32,128]{3,2,1,0:T(8,128)(2,1)S(1)}, u32[]{:S(2)}, u32[]{:S(2)}) collective-permute-start(bf16[2,12,32,128]{3,2,1,0:T(8,128)(2,1)S(1)} %get-tuple-element.73), channel_id=1, source_target_pairs={{0,3},{1,2},{2,1},{3,0},{4,7},{5,6},{6,5},{7,4},{8,11},{9,10},{10,... | collective-permute-start | bytes 589832 | tf_op jit(solution)/shard_map/ppermute | solution.py:521
  25.1 5.7 %copy-start.4 = (s32[2,1536]{1,0:T(2,128)S(1)}, s32[2,1536]{1,0:T(2,128)}, u32[]{:S(2)}) copy-start(s32[2,1536]{1,0:T(2,128)} %param.8) | copy-start | bytes 36868
  25.1 11.1 %copy-start.3 = (bf16[2,256,1536]{2,1,0:T(8,128)(2,1)S(1)}, bf16[2,256,1536]{2,1,0:T(8,128)(2,1)}, u32[]{:S(2)}) copy-start(bf16[2,256,1536]{2,1,0:T(8,128)(2,1)} %density.3) | copy-start | bytes 4718596
  27.7 8.5 %collective-permute-start.5 = (bf16[2,12,32,128]{3,2,1,0:T(8,128)(2,1)S(1)}, bf16[2,12,32,128]{3,2,1,0:T(8,128)(2,1)S(1)}, u32[]{:S(2)}, u32[]{:S(2)}) collective-permute-start(bf16[2,12,32,128]{3,2,1,0:T(8,128)(2,1)S(1)} %get-tuple-element.70), channel_id=1, source_target_pairs={{0,1},{1,0},{2,3},{3,2},{4,5},{5,4},{6,7},{7,6},{8,9},{9,8},{10,11... | collective-permute-start | bytes 589832 | tf_op jit(solution)/shard_map/ppermute | solution.py:521
  28.7 2.3 %collective-permute-start.11 = (bf16[1,12,32,128]{3,2,1,0:T(8,128)(2,1)S(1)}, bf16[1,12,32,128]{3,2,1,0:T(8,128)(2,1)S(1)}, u32[]{:S(2)}, u32[]{:S(2)}) collective-permute-start(bf16[1,12,32,128]{3,2,1,0:T(8,128)(2,1)S(1)} %get-tuple-element.77), channel_id=1, source_target_pairs={{0,1},{1,0},{2,3},{3,2},{4,5},{5,4},{6,7},{7,6},{8,9},{9,8},{10,11... | collective-permute-start | bytes 294920 | tf_op jit(solution)/shard_map/ppermute | solution.py:521
  28.7 3.9 %collective-permute-start.12 = (bf16[1,12,32,128]{3,2,1,0:T(8,128)(2,1)S(1)}, bf16[1,12,32,128]{3,2,1,0:T(8,128)(2,1)S(1)}, u32[]{:S(2)}, u32[]{:S(2)}) collective-permute-start(bf16[1,12,32,128]{3,2,1,0:T(8,128)(2,1)S(1)} %get-tuple-element.78), channel_id=1, source_target_pairs={{0,2},{1,3},{2,0},{3,1},{4,6},{5,7},{6,4},{7,5},{8,10},{9,11},{10,... | collective-permute-start | bytes 294920 | tf_op jit(solution)/shard_map/ppermute | solution.py:521
  29.2 7.1 %collective-permute-start.13 = (bf16[1,12,32,128]{3,2,1,0:T(8,128)(2,1)S(1)}, bf16[1,12,32,128]{3,2,1,0:T(8,128)(2,1)S(1)}, u32[]{:S(2)}, u32[]{:S(2)}) collective-permute-start(bf16[1,12,32,128]{3,2,1,0:T(8,128)(2,1)S(1)} %get-tuple-element.79), channel_id=1, source_target_pairs={{0,3},{1,2},{2,1},{3,0},{4,7},{5,6},{6,5},{7,4},{8,11},{9,10},{10,... | collective-permute-start | bytes 294920 | tf_op jit(solution)/shard_map/ppermute | solution.py:521
  30.8 25.8 %collective-permute-start.6 = (bf16[1,12,32,128]{3,2,1,0:T(8,128)(2,1)S(1)}, bf16[1,12,32,128]{3,2,1,0:T(8,128)(2,1)S(1)}, u32[]{:S(2)}, u32[]{:S(2)}) collective-permute-start(bf16[1,12,32,128]{3,2,1,0:T(8,128)(2,1)S(1)} %get-tuple-element.71), channel_id=1, source_target_pairs={{0,1},{1,0},{2,3},{3,2},{4,5},{5,4},{6,7},{7,6},{8,9},{9,8},{10,11... | collective-permute-start | bytes 294920 | tf_op jit(solution)/shard_map/ppermute | solution.py:521
  30.9 26.7 %collective-permute-start.7 = (bf16[1,12,32,128]{3,2,1,0:T(8,128)(2,1)S(1)}, bf16[1,12,32,128]{3,2,1,0:T(8,128)(2,1)S(1)}, u32[]{:S(2)}, u32[]{:S(2)}) collective-permute-start(bf16[1,12,32,128]{3,2,1,0:T(8,128)(2,1)S(1)} %get-tuple-element.72), channel_id=1, source_target_pairs={{0,2},{1,3},{2,0},{3,1},{4,6},{5,7},{6,4},{7,5},{8,10},{9,11},{10,... | collective-permute-start | bytes 294920 | tf_op jit(solution)/shard_map/ppermute | solution.py:521
  32.5 25.1 %collective-permute-start.9 = (bf16[1,12,32,128]{3,2,1,0:T(8,128)(2,1)S(1)}, bf16[1,12,32,128]{3,2,1,0:T(8,128)(2,1)S(1)}, u32[]{:S(2)}, u32[]{:S(2)}) collective-permute-start(bf16[1,12,32,128]{3,2,1,0:T(8,128)(2,1)S(1)} %get-tuple-element.74), channel_id=1, source_target_pairs={{0,3},{1,2},{2,1},{3,0},{4,7},{5,6},{6,5},{7,4},{8,11},{9,10},{10,... | collective-permute-start | bytes 294920 | tf_op jit(solution)/shard_map/ppermute | solution.py:521
  55.4 23.5 %collective-permute-start.14 = (bf16[12,64,128]{2,1,0:T(8,128)(2,1)S(1)}, bf16[12,64,128]{2,1,0:T(8,128)(2,1)S(1)}, u32[]{:S(2)}, u32[]{:S(2)}) collective-permute-start(bf16[12,64,128]{2,1,0:T(8,128)(2,1)S(1)} %get-tuple-element.81), channel_id=1, source_target_pairs={{0,1},{1,0},{2,3},{3,2},{4,5},{5,4},{6,7},{7,6},{8,9},{9,8},{10,11... | collective-permute-start | bytes 589832 | tf_op jit(solution)/shard_map/ppermute | solution.py:521
  55.5 25.0 %collective-permute-start.15 = (bf16[12,64,128]{2,1,0:T(8,128)(2,1)S(1)}, bf16[12,64,128]{2,1,0:T(8,128)(2,1)S(1)}, u32[]{:S(2)}, u32[]{:S(2)}) collective-permute-start(bf16[12,64,128]{2,1,0:T(8,128)(2,1)S(1)} %get-tuple-element.82), channel_id=1, source_target_pairs={{0,2},{1,3},{2,0},{3,1},{4,6},{5,7},{6,4},{7,5},{8,10},{9,11},{10,... | collective-permute-start | bytes 589832 | tf_op jit(solution)/shard_map/ppermute | solution.py:521
  56.6 23.9 %collective-permute-start.16 = (bf16[12,64,128]{2,1,0:T(8,128)(2,1)S(1)}, bf16[12,64,128]{2,1,0:T(8,128)(2,1)S(1)}, u32[]{:S(2)}, u32[]{:S(2)}) collective-permute-start(bf16[12,64,128]{2,1,0:T(8,128)(2,1)S(1)} %get-tuple-element.83), channel_id=1, source_target_pairs={{0,3},{1,2},{2,1},{3,0},{4,7},{5,6},{6,5},{7,4},{8,11},{9,10},{10,... | collective-permute-start | bytes 589832 | tf_op jit(solution)/shard_map/ppermute | solution.py:521
  76.6 3.9 %collective-permute-start.17 = (bf16[12,64,128]{2,1,0:T(8,128)(2,1)S(1)}, bf16[12,64,128]{2,1,0:T(8,128)(2,1)S(1)}, u32[]{:S(2)}, u32[]{:S(2)}) collective-permute-start(bf16[12,64,128]{2,1,0:T(8,128)(2,1)S(1)} %get-tuple-element.85), channel_id=1, source_target_pairs={{0,1},{1,0},{2,3},{3,2},{4,5},{5,4},{6,7},{7,6},{8,9},{9,8},{10,11... | collective-permute-start | bytes 589832 | tf_op jit(solution)/shard_map/ppermute | solution.py:521
  77.5 6.5 %collective-permute-start.10 = (bf16[12,64,128]{2,1,0:T(8,128)(2,1)S(1)}, bf16[12,64,128]{2,1,0:T(8,128)(2,1)S(1)}, u32[]{:S(2)}, u32[]{:S(2)}) collective-permute-start(bf16[12,64,128]{2,1,0:T(8,128)(2,1)S(1)} %get-tuple-element.75), channel_id=1, source_target_pairs={{0,2},{1,3},{2,0},{3,1},{4,6},{5,7},{6,4},{7,5},{8,10},{9,11},{10,... | collective-permute-start | bytes 589832 | tf_op jit(solution)/shard_map/ppermute | solution.py:521
  78.9 9.5 %collective-permute-start.18 = (bf16[12,64,128]{2,1,0:T(8,128)(2,1)S(1)}, bf16[12,64,128]{2,1,0:T(8,128)(2,1)S(1)}, u32[]{:S(2)}, u32[]{:S(2)}) collective-permute-start(bf16[12,64,128]{2,1,0:T(8,128)(2,1)S(1)} %get-tuple-element.86), channel_id=1, source_target_pairs={{0,3},{1,2},{2,1},{3,0},{4,7},{5,6},{6,5},{7,4},{8,11},{9,10},{10,... | collective-permute-start | bytes 589832 | tf_op jit(solution)/shard_map/ppermute | solution.py:521

commit v9 on v8

--- a/solution.py
+++ b/solution.py
@@ -534,18 +534,10 @@
         )
         start += width
         if part > 0:
-            moved, waiting, _ = lax.optimization_barrier(
-                (moved, waiting, arrived[0, peers // 2, part - 1])
-            )
-            waiting = swap(waiting, 1)
-            for section in range(per):
-                arrived[section, 1, part - 1] = waiting
+            moved, _ = lax.optimization_barrier((moved, arrived[0, peers // 2, part - 1]))
         for s in range(1 if joined else per):
             for k in reversed(range(peers)):
                 block = moved[k if joined else k * per + s]
-                if joined and k == 1:
-                    waiting = block
-                    continue
                 block = swap(block, k)
                 for section in range(per) if joined else [s]:
                     arrived[section, k, part] = block

time: 90.8 us -> 90.5 us (level); the launches traced: 89.1 us -> 90.3 us
  waiting for transfers between devices: 10.9 us -> 8.11 us
  Pallas kernels: 56.4 us -> 58.6 us
  starting transfers between devices: 19.5 us -> 21.3 us
    ppermute x2, waiting for transfers between devices: 2.67 us -> 0.01 us  [body(): one = lax.ppermute(edges[0], 'gz', ones)]
    pallas_call x2, Pallas kernels: 38.1 us -> 40.3 us  [fit(): pl.pallas_call(functools.partial(fit_kernel, parts, peers), grid=(1,), ou...]
    ppermute x15, starting transfers between devices: 12.8 us -> 14.6 us  [swap(): return lax.ppermute(block, ('gy', 'af'), [(i, i ^ k) for i in range(peers)])]
  transfers between devices with their start and end apart: 19 -> 19, of which waited for: 6 -> 5; matrix products, arithmetic and copies ran while one was open for 1% -> 1% of each run, Pallas kernels for 62% -> 63%
where the time goes in v9:
time: 90.5 us; the launch traced here: 90.3 us
  Pallas kernels  58.6 us (65%)
  starting transfers between devices  21.3 us (24%)
  waiting for transfers between devices  8.11 us (9%)
  local copies, waits for them, and re-layouts  1.31 us (1%)
  between operations  0.91 us (1%)
    pallas_call x2, Pallas kernels, fit(): pl.pallas_call(functools.partial(fit_kernel, parts, peers), grid=(1,), ou...  40.3 us
    ppermute x15, starting transfers between devices, swap(): return lax.ppermute(block, ('gy', 'af'), [(i, i ^ k) for i in range(peers)])  14.6 us
    ppermute x15, waiting for transfers between devices, swap(): return lax.ppermute(block, ('gy', 'af'), [(i, i ^ k) for i in range(peers)])  7.8 us
    ppermute x2, starting transfers between devices, body(): two = lax.ppermute(edges[1], 'gz', twos)  5.27 us
    pallas_call x2, Pallas kernels, second_side(): pl.pallas_call(functools.partial(second_kernel, peers, per, joined, width...  5.15 us
    pallas_call x2, Pallas kernels, first_side(): pl.pallas_call(functools.partial(first_kernel, width, start), out_shape=o...  4.4 us
    pallas_call x1, Pallas kernels, inner(): pl.pallas_call(inner_kernel, out_shape=[level] * (TSTEPS - 1), in_specs=[...  3.21 us
    pallas_call x2, Pallas kernels, place(): pl.pallas_call(functools.partial(place_kernel, per, which), out_shape=jax...  2.85 us
  transfers between devices with their start and end apart: 19, of which 5 were waited for; matrix products, arithmetic and copies ran while one was open for 1% of the time, Pallas kernels for 63%

profile of v9, /device:TPU:23, one launch (start us, length us, event | category | flops | bytes accessed | tf_op | source)
XLA Modules:
  0.0 90.3 jit_solution(1094569136727953166)
XLA Ops:
  0.0 0.0 copy-start
  0.0 0.0 copy-start.1
  0.0 1.4 %pack_edges.2 = (bf16[12,144,128]{2,1,0:T(8,128)(2,1)S(1)}, bf16[12,144,128]{2,1,0:T(8,128)(2,1)S(1)}) custom-call(bf16[8,12,64,128]{3,2,1,0:T(8,128)(2,1)} %bitcast.6, bf16[3,12,8,128]{3,2,1,0:T(8,128)(2,1)} %bitcast.13), custom_call_target="tpu_custom_call" | custom-call | tf_op jit(solution)/shard_map/pack_edges/pallas_call | solution.py:79
  1.5 1.4 %collective-permute-start.1 = (bf16[12,144,128]{2,1,0:T(8,128)(2,1)S(1)}, bf16[12,144,128]{2,1,0:T(8,128)(2,1)S(1)}, u32[]{:S(2)}, u32[]{:S(2)}) collective-permute-start(bf16[12,144,128]{2,1,0:T(8,128)(2,1)S(1)} %get-tuple-element.46), channel_id=1, source_target_pairs={{0,4},{4,0},{8,12},{12,8},{1,5},{5,1},{9,13},{13,9},{2,6},{6,2},{1... | collective-permute-start | bytes 1327112 | tf_op jit(solution)/shard_map/ppermute | solution.py:514
  2.8 1.9 %collective-permute-start = (bf16[12,144,128]{2,1,0:T(8,128)(2,1)S(1)}, bf16[12,144,128]{2,1,0:T(8,128)(2,1)S(1)}, u32[]{:S(2)}, u32[]{:S(2)}) collective-permute-start(bf16[12,144,128]{2,1,0:T(8,128)(2,1)S(1)} %get-tuple-element.45), channel_id=1, source_target_pairs={{4,8},{8,4},{5,9},{9,5},{6,10},{10,6},{7,11},{11,7},{20,24},{24,20... | collective-permute-start | bytes 1327112 | tf_op jit(solution)/shard_map/ppermute | solution.py:515
  4.7 1.3 %pack_edges.3 = (bf16[12,128,128]{2,1,0:T(8,128)(2,1)S(1)}, bf16[12,128,128]{2,1,0:T(8,128)(2,1)S(1)}) custom-call(bf16[8,12,64,128]{3,2,1,0:T(8,128)(2,1)} %bitcast.7, bf16[3,12,8,128]{3,2,1,0:T(8,128)(2,1)} %bitcast.14), custom_call_target="tpu_custom_call" | custom-call | tf_op jit(solution)/shard_map/pack_edges/pallas_call | solution.py:79
  6.1 0.1 collective-permute-start.3
  6.1 3.4 %collective-permute-start.2 = (bf16[12,128,128]{2,1,0:T(8,128)(2,1)S(1)}, bf16[12,128,128]{2,1,0:T(8,128)(2,1)S(1)}, u32[]{:S(2)}, u32[]{:S(2)}) collective-permute-start(bf16[12,128,128]{2,1,0:T(8,128)(2,1)S(1)} %get-tuple-element.53), channel_id=1, source_target_pairs={{4,8},{8,4},{5,9},{9,5},{6,10},{10,6},{7,11},{11,7},{20,24},{24,20... | collective-permute-start | bytes 1179656 | tf_op jit(solution)/shard_map/ppermute | solution.py:515
  9.5 0.0 copy-done
  9.5 0.0 copy-done.1
  9.5 3.2 %inner_steps.1 = (f32[8,12,64,128]{3,2,1,0:T(8,128)S(1)}, f32[8,12,64,128]{3,2,1,0:T(8,128)S(1)}, f32[8,12,64,128]{3,2,1,0:T(8,128)S(1)}) custom-call(bf16[8,12,64,128]{3,2,1,0:T(8,128)(2,1)S(1)} %bitcast.8, bf16[3,12,8,128]{3,2,1,0:T(8,128)(2,1)S(1)} %bitcast.15), custom_call_target="tpu_custom_call" | custom-call | flops 4000000000 | tf_op jit(solution)/shard_map/inner_steps/pallas_call | solution.py:158
  12.8 0.0 collective-permute-done.1.halo
  12.8 0.0 copy-start.2
  12.8 2.3 %first_side.2 = (bf16[4,12,32,128]{3,2,1,0:T(8,128)(2,1)S(1)}, f32[7,12,16,128]{3,2,1,0:T(8,128)S(1)}) custom-call(bf16[8,12,64,128]{3,2,1,0:T(8,128)(2,1)S(1)} %bitcast.9, bf16[3,12,8,128]{3,2,1,0:T(8,128)(2,1)S(1)} %bitcast.16, bf16[12,144,128]{2,1,0:T(8,128)(2,1)S(1)} %collective-permute-done.1.halo, f32[8,12,64,128]{3,2,1,0:T(8,128)S(1)} %get-tuple-element.48.refs_0_, ...), custom_call_target="tpu_custom_call" | custom-call | flops 100000000 | tf_op jit(solution)/shard_map/first_side/pallas_call | solution.py:272
  15.1 0.3 collective-permute-done.halo
  15.4 0.0 copy-done.2
  15.4 2.6 %second_side.2 = (bf16[2,12,32,128]{3,2,1,0:T(8,128)(2,1)S(1)}, bf16[2,12,32,128]{3,2,1,0:T(8,128)(2,1)S(1)}, bf16[2,12,32,128]{3,2,1,0:T(8,128)(2,1)S(1)}, bf16...) custom-call(s32[8]{0:T(128)S(1)} %copy-done.2, bf16[8,12,64,128]{3,2,1,0:T(8,128)(2,1)S(1)} %bitcast.10, ...), custom_call_target="tpu_custom_call" | custom-call | flops 100000000 | tf_op jit(solution)/shard_map/second_side/pallas_call | solution.py:292
  18.0 0.3 collective-permute-start.4
  18.3 3.6 %collective-permute-start.5 = (bf16[2,12,32,128]{3,2,1,0:T(8,128)(2,1)S(1)}, bf16[2,12,32,128]{3,2,1,0:T(8,128)(2,1)S(1)}, u32[]{:S(2)}, u32[]{:S(2)}) collective-permute-start(bf16[2,12,32,128]{3,2,1,0:T(8,128)(2,1)S(1)} %get-tuple-element.68), channel_id=1, source_target_pairs={{0,1},{1,0},{2,3},{3,2},{4,5},{5,4},{6,7},{7,6},{8,9},{9,8},{10,11... | collective-permute-start | bytes 589832 | tf_op jit(solution)/shard_map/ppermute | solution.py:521
  21.9 1.1 %collective-permute-start.8 = (bf16[2,12,32,128]{3,2,1,0:T(8,128)(2,1)S(1)}, bf16[2,12,32,128]{3,2,1,0:T(8,128)(2,1)S(1)}, u32[]{:S(2)}, u32[]{:S(2)}) collective-permute-start(bf16[2,12,32,128]{3,2,1,0:T(8,128)(2,1)S(1)} %get-tuple-element.71), channel_id=1, source_target_pairs={{0,3},{1,2},{2,1},{3,0},{4,7},{5,6},{6,5},{7,4},{8,11},{9,10},{10,... | collective-permute-start | bytes 589832 | tf_op jit(solution)/shard_map/ppermute | solution.py:521
  23.0 0.0 collective-permute-done.3.halo
  23.0 2.1 %first_side.3.done = bf16[4,12,32,128]{3,2,1,0:T(8,128)(2,1)S(1)} custom-call(bf16[8,12,64,128]{3,2,1,0:T(8,128)(2,1)S(1)} %bitcast.11, bf16[3,12,8,128]{3,2,1,0:T(8,128)(2,1)S(1)} %bitcast.18, bf16[12,128,128]{2,1,0:T(8,128)(2,1)S(1)} %collective-permute-done.3.halo, f32[8,12,64,128]{3,2,1,0:T(8,128)S(1)} %get-tuple-element.48.refs_0_, ...), custom_call_target="tpu_custom_call" | custom-call | flops 100000000 | tf_op jit(solution)/shard_map/first_side/pallas_call | solution.py:272
  25.1 0.0 collective-permute-done.2.halo
  25.1 0.0 copy-start.4
  25.1 0.0 copy-start.3
  25.1 2.6 %second_side.3 = (bf16[1,12,32,128]{3,2,1,0:T(8,128)(2,1)S(1)}, bf16[1,12,32,128]{3,2,1,0:T(8,128)(2,1)S(1)}, bf16[1,12,32,128]{3,2,1,0:T(8,128)(2,1)S(1)}, bf16...) custom-call(s32[8]{0:T(128)S(1)} %copy-done.2, ...), custom_call_target="tpu_custom_call" | custom-call | flops 100000000 | tf_op jit(solution)/shard_map/second_side/pallas_call | solution.py:292
  27.7 0.0 collective-permute-done.4.refs_4_
  27.7 1.4 %collective-permute-start.11 = (bf16[1,12,32,128]{3,2,1,0:T(8,128)(2,1)S(1)}, bf16[1,12,32,128]{3,2,1,0:T(8,128)(2,1)S(1)}, u32[]{:S(2)}, u32[]{:S(2)}) collective-permute-start(bf16[1,12,32,128]{3,2,1,0:T(8,128)(2,1)S(1)} %get-tuple-element.75), channel_id=1, source_target_pairs={{0,1},{1,0},{2,3},{3,2},{4,5},{5,4},{6,7},{7,6},{8,9},{9,8},{10,11... | collective-permute-start | bytes 294920 | tf_op jit(solution)/shard_map/ppermute | solution.py:521
  29.1 0.0 collective-permute-start.12
  29.1 1.6 %collective-permute-start.13 = (bf16[1,12,32,128]{3,2,1,0:T(8,128)(2,1)S(1)}, bf16[1,12,32,128]{3,2,1,0:T(8,128)(2,1)S(1)}, u32[]{:S(2)}, u32[]{:S(2)}) collective-permute-start(bf16[1,12,32,128]{3,2,1,0:T(8,128)(2,1)S(1)} %get-tuple-element.77), channel_id=1, source_target_pairs={{0,3},{1,2},{2,1},{3,0},{4,7},{5,6},{6,5},{7,4},{8,11},{9,10},{10,... | collective-permute-start | bytes 294920 | tf_op jit(solution)/shard_map/ppermute | solution.py:521
  30.8 0.0 copy-done.4
  30.8 0.0 collective-permute-done.5.refs_2_
  30.8 0.3 collective-permute-start.6
  31.1 0.0 collective-permute-done.8.refs_6_
  31.1 0.0 collective-permute-start.7
  31.1 0.0 collective-permute-done.11.refs_3_
  31.1 1.9 %collective-permute-start.9 = (bf16[1,12,32,128]{3,2,1,0:T(8,128)(2,1)S(1)}, bf16[1,12,32,128]{3,2,1,0:T(8,128)(2,1)S(1)}, u32[]{:S(2)}, u32[]{:S(2)}) collective-permute-start(bf16[1,12,32,128]{3,2,1,0:T(8,128)(2,1)S(1)} %get-tuple-element.72), channel_id=1, source_target_pairs={{0,3},{1,2},{2,1},{3,0},{4,7},{5,6},{6,5},{7,4},{8,11},{9,10},{10,... | collective-permute-start | bytes 294920 | tf_op jit(solution)/shard_map/ppermute | solution.py:521
  33.0 0.5 collective-permute-done.12.refs_5_
  33.6 2.6 %collective-permute-done.13.refs_7_ = bf16[1,12,32,128]{3,2,1,0:T(8,128)(2,1)S(1)} collective-permute-done((bf16[1,12,32,128]{3,2,1,0:T(8,128)(2,1)S(1)}, bf16[1,12,32,128]{3,2,1,0:T(8,128)(2,1)S(1)}, u32[]{:S(2)}, u32[]{:S(2)}) %collective-permute-start.13) | collective-permute-done | bytes 98336 | tf_op jit(solution)/shard_map/ppermute | solution.py:521
  36.1 0.0 copy-done.3
  36.1 20.2 %fit.3 = (bf16[12,64,128]{2,1,0:T(8,128)(2,1)S(1)}, bf16[12,64,128]{2,1,0:T(8,128)(2,1)S(1)}, bf16[12,64,128]{2,1,0:T(8,128)(2,1)S(1)}, bf16[12,64,128]{2,1,0:T(8,128)(2,1)S(1)}) custom-call(s32[2,1,1536]{2,1,0:T(1,128)S(1)} %reshape.3.mask, bf16[2,256,1536]{2,1,0:T(8,128)(2,1)S(1)} %copy-done.3, bf16[2,12,32,128]{3,2,1,0:T(8,128)(2,1)S(1)} %get-tuple-element.52.refs_0_, ...), custom_call_target="tpu_custom_call" | custom-call | flops 10000000000 | tf_op jit(solution)/shard_map/fit/pallas_call | solution.py:435
  56.4 0.1 collective-permute-start.14
  56.4 0.1 collective-permute-start.15
  56.5 0.0 collective-permute-done.6.refs_3_
  56.5 2.0 %collective-permute-start.16 = (bf16[12,64,128]{2,1,0:T(8,128)(2,1)S(1)}, bf16[12,64,128]{2,1,0:T(8,128)(2,1)S(1)}, u32[]{:S(2)}, u32[]{:S(2)}) collective-permute-start(bf16[12,64,128]{2,1,0:T(8,128)(2,1)S(1)} %get-tuple-element.81), channel_id=1, source_target_pairs={{0,3},{1,2},{2,1},{3,0},{4,7},{5,6},{6,5},{7,4},{8,11},{9,10},{10,... | collective-permute-start | bytes 589832 | tf_op jit(solution)/shard_map/ppermute | solution.py:521
  58.6 0.0 collective-permute-done.7.refs_5_
  58.6 0.0 collective-permute-done.9.refs_7_
  58.6 20.0 %fit.2 = (bf16[12,64,128]{2,1,0:T(8,128)(2,1)S(1)}, bf16[12,64,128]{2,1,0:T(8,128)(2,1)S(1)}, bf16[12,64,128]{2,1,0:T(8,128)(2,1)S(1)}, bf16[12,64,128]{2,1,0:T(8,128)(2,1)S(1)}) custom-call(s32[2,1,1536]{2,1,0:T(1,128)S(1)} %reshape.3.mask, bf16[2,256,1536]{2,1,0:T(8,128)(2,1)S(1)} %copy-done.3, bf16[2,12,32,128]{3,2,1,0:T(8,128)(2,1)S(1)} %get-tuple-element.52.refs_0_, ...), custom_call_target="tpu_custom_call" | custom-call | flops 10000000000 | tf_op jit(solution)/shard_map/fit/pallas_call | solution.py:435
  78.6 0.1 collective-permute-start.17
  78.7 0.1 collective-permute-start.10
  78.8 0.0 collective-permute-done.14.refs_1_
  78.8 2.0 %collective-permute-start.18 = (bf16[12,64,128]{2,1,0:T(8,128)(2,1)S(1)}, bf16[12,64,128]{2,1,0:T(8,128)(2,1)S(1)}, u32[]{:S(2)}, u32[]{:S(2)}) collective-permute-start(bf16[12,64,128]{2,1,0:T(8,128)(2,1)S(1)} %get-tuple-element.84), channel_id=1, source_target_pairs={{0,3},{1,2},{2,1},{3,0},{4,7},{5,6},{6,5},{7,4},{8,11},{9,10},{10,... | collective-permute-start | bytes 589832 | tf_op jit(solution)/shard_map/ppermute | solution.py:521
  80.8 0.6 dynamic_slice.4
  82.1 0.0 collective-permute-done.15.refs_2_
  82.1 0.0 collective-permute-done.16.refs_3_
  82.1 0.0 collective-permute-done.17.refs_5_
  82.1 1.6 %place.2.refs_1_ = bf16[8,12,64,128]{3,2,1,0:T(8,128)(2,1)} custom-call(s32[8]{0:T(128)S(1)} %copy-done.2, bf16[12,64,128]{2,1,0:T(8,128)(2,1)S(1)} %get-tuple-element.78.refs_0_, bf16[12,64,128]{2,1,0:T(8,128)(2,1)S(1)} %collective-permute-done.14.refs_1_, bf16[12,64,128]{2,1,0:T(8,128)(2,1)S(1)} %collective-permute-done.15.refs_2_, ...), custom_call_target="tpu_custom_call" | custom-call | flops 100000000 | tf_op jit(solution)/shard_map/place/pallas_call | solution.py:475
  83.7 1.1 %collective-permute-done.10.refs_0_ = bf16[12,64,128]{2,1,0:T(8,128)(2,1)S(1)} collective-permute-done((bf16[12,64,128]{2,1,0:T(8,128)(2,1)S(1)}, bf16[12,64,128]{2,1,0:T(8,128)(2,1)S(1)}, u32[]{:S(2)}, u32[]{:S(2)}) %collective-permute-start.10) | collective-permute-done | bytes 196640 | tf_op jit(solution)/shard_map/ppermute | solution.py:521
  84.8 1.2 %place.3 = bf16[8,12,64,128]{3,2,1,0:T(8,128)(2,1)} custom-call(s32[8]{0:T(128)S(1)} %copy-done.2, bf16[12,64,128]{2,1,0:T(8,128)(2,1)S(1)} %collective-permute-done.10.refs_0_, bf16[8,12,64,128]{3,2,1,0:T(8,128)(2,1)} %place.2.refs_1_), custom_call_target="tpu_custom_call", output_to_operand_aliasing={{}: (2, {})} | custom-call | flops 100000000 | tf_op jit(solution)/shard_map/place/pallas_call | solution.py:475
  86.1 3.5 %collective-permute-done.18 = bf16[12,64,128]{2,1,0:T(8,128)(2,1)S(1)} collective-permute-done((bf16[12,64,128]{2,1,0:T(8,128)(2,1)S(1)}, bf16[12,64,128]{2,1,0:T(8,128)(2,1)S(1)}, u32[]{:S(2)}, u32[]{:S(2)}) %collective-permute-start.18) | collective-permute-done | bytes 196640 | tf_op jit(solution)/shard_map/ppermute | solution.py:521
  89.6 0.7 bitcast_dynamic-update-slice_fusion
  (1 shorter events, 0.0 us)
Async XLA Ops:
  0.0 9.5 %copy-start = (bf16[8,64,12,128]{3,1,2,0:T(8,128)(2,1)S(1)}, bf16[8,64,12,128]{3,1,2,0:T(8,128)(2,1)}, u32[]{:S(2)}) copy-start(bf16[8,64,12,128]{3,1,2,0:T(8,128)(2,1)} %param.5) | copy-start | bytes 4718596
  0.0 9.5 %copy-start.1 = (bf16[3,8,12,128]{3,1,2,0:T(8,128)(2,1)S(1)}, bf16[3,8,12,128]{3,1,2,0:T(8,128)(2,1)}, u32[]{:S(2)}) copy-start(bf16[3,8,12,128]{3,1,2,0:T(8,128)(2,1)} %param.6) | copy-start | bytes 221188
  1.5 11.3 %collective-permute-start.1 = (bf16[12,144,128]{2,1,0:T(8,128)(2,1)S(1)}, bf16[12,144,128]{2,1,0:T(8,128)(2,1)S(1)}, u32[]{:S(2)}, u32[]{:S(2)}) collective-permute-start(bf16[12,144,128]{2,1,0:T(8,128)(2,1)S(1)} %get-tuple-element.46), channel_id=1, source_target_pairs={{0,4},{4,0},{8,12},{12,8},{1,5},{5,1},{9,13},{13,9},{2,6},{6,2},{1... | collective-permute-start | bytes 1327112 | tf_op jit(solution)/shard_map/ppermute | solution.py:514
  2.8 12.6 %collective-permute-start = (bf16[12,144,128]{2,1,0:T(8,128)(2,1)S(1)}, bf16[12,144,128]{2,1,0:T(8,128)(2,1)S(1)}, u32[]{:S(2)}, u32[]{:S(2)}) collective-permute-start(bf16[12,144,128]{2,1,0:T(8,128)(2,1)S(1)} %get-tuple-element.45), channel_id=1, source_target_pairs={{4,8},{8,4},{5,9},{9,5},{6,10},{10,6},{7,11},{11,7},{20,24},{24,20... | collective-permute-start | bytes 1327112 | tf_op jit(solution)/shard_map/ppermute | solution.py:515
  6.1 17.0 %collective-permute-start.3 = (bf16[12,128,128]{2,1,0:T(8,128)(2,1)S(1)}, bf16[12,128,128]{2,1,0:T(8,128)(2,1)S(1)}, u32[]{:S(2)}, u32[]{:S(2)}) collective-permute-start(bf16[12,128,128]{2,1,0:T(8,128)(2,1)S(1)} %get-tuple-element.54), channel_id=1, source_target_pairs={{0,4},{4,0},{8,12},{12,8},{1,5},{5,1},{9,13},{13,9},{2,6},{6,2},{1... | collective-permute-start | bytes 1179656 | tf_op jit(solution)/shard_map/ppermute | solution.py:514
  6.1 19.0 %collective-permute-start.2 = (bf16[12,128,128]{2,1,0:T(8,128)(2,1)S(1)}, bf16[12,128,128]{2,1,0:T(8,128)(2,1)S(1)}, u32[]{:S(2)}, u32[]{:S(2)}) collective-permute-start(bf16[12,128,128]{2,1,0:T(8,128)(2,1)S(1)} %get-tuple-element.53), channel_id=1, source_target_pairs={{4,8},{8,4},{5,9},{9,5},{6,10},{10,6},{7,11},{11,7},{20,24},{24,20... | collective-permute-start | bytes 1179656 | tf_op jit(solution)/shard_map/ppermute | solution.py:515
  12.8 2.7 %copy-start.2 = (s32[8]{0:T(128)S(1)}, s32[8]{0:T(128)}, u32[]{:S(2)}) copy-start(s32[8]{0:T(128)} %slots.7) | copy-start | bytes 100
  18.0 9.7 %collective-permute-start.4 = (bf16[2,12,32,128]{3,2,1,0:T(8,128)(2,1)S(1)}, bf16[2,12,32,128]{3,2,1,0:T(8,128)(2,1)S(1)}, u32[]{:S(2)}, u32[]{:S(2)}) collective-permute-start(bf16[2,12,32,128]{3,2,1,0:T(8,128)(2,1)S(1)} %get-tuple-element.66), channel_id=1, source_target_pairs={{0,2},{1,3},{2,0},{3,1},{4,6},{5,7},{6,4},{7,5},{8,10},{9,11},{10,... | collective-permute-start | bytes 589832 | tf_op jit(solution)/shard_map/ppermute | solution.py:521
  18.3 12.5 %collective-permute-start.5 = (bf16[2,12,32,128]{3,2,1,0:T(8,128)(2,1)S(1)}, bf16[2,12,32,128]{3,2,1,0:T(8,128)(2,1)S(1)}, u32[]{:S(2)}, u32[]{:S(2)}) collective-permute-start(bf16[2,12,32,128]{3,2,1,0:T(8,128)(2,1)S(1)} %get-tuple-element.68), channel_id=1, source_target_pairs={{0,1},{1,0},{2,3},{3,2},{4,5},{5,4},{6,7},{7,6},{8,9},{9,8},{10,11... | collective-permute-start | bytes 589832 | tf_op jit(solution)/shard_map/ppermute | solution.py:521
  21.9 9.2 %collective-permute-start.8 = (bf16[2,12,32,128]{3,2,1,0:T(8,128)(2,1)S(1)}, bf16[2,12,32,128]{3,2,1,0:T(8,128)(2,1)S(1)}, u32[]{:S(2)}, u32[]{:S(2)}) collective-permute-start(bf16[2,12,32,128]{3,2,1,0:T(8,128)(2,1)S(1)} %get-tuple-element.71), channel_id=1, source_target_pairs={{0,3},{1,2},{2,1},{3,0},{4,7},{5,6},{6,5},{7,4},{8,11},{9,10},{10,... | collective-permute-start | bytes 589832 | tf_op jit(solution)/shard_map/ppermute | solution.py:521
  25.1 5.7 %copy-start.4 = (s32[2,1536]{1,0:T(2,128)S(1)}, s32[2,1536]{1,0:T(2,128)}, u32[]{:S(2)}) copy-start(s32[2,1536]{1,0:T(2,128)} %param.8) | copy-start | bytes 36868
  25.1 11.0 %copy-start.3 = (bf16[2,256,1536]{2,1,0:T(8,128)(2,1)S(1)}, bf16[2,256,1536]{2,1,0:T(8,128)(2,1)}, u32[]{:S(2)}) copy-start(bf16[2,256,1536]{2,1,0:T(8,128)(2,1)} %density.3) | copy-start | bytes 4718596
  27.7 3.4 %collective-permute-start.11 = (bf16[1,12,32,128]{3,2,1,0:T(8,128)(2,1)S(1)}, bf16[1,12,32,128]{3,2,1,0:T(8,128)(2,1)S(1)}, u32[]{:S(2)}, u32[]{:S(2)}) collective-permute-start(bf16[1,12,32,128]{3,2,1,0:T(8,128)(2,1)S(1)} %get-tuple-element.75), channel_id=1, source_target_pairs={{0,1},{1,0},{2,3},{3,2},{4,5},{5,4},{6,7},{7,6},{8,9},{9,8},{10,11... | collective-permute-start | bytes 294920 | tf_op jit(solution)/shard_map/ppermute | solution.py:521
  29.1 4.4 %collective-permute-start.12 = (bf16[1,12,32,128]{3,2,1,0:T(8,128)(2,1)S(1)}, bf16[1,12,32,128]{3,2,1,0:T(8,128)(2,1)S(1)}, u32[]{:S(2)}, u32[]{:S(2)}) collective-permute-start(bf16[1,12,32,128]{3,2,1,0:T(8,128)(2,1)S(1)} %get-tuple-element.76), channel_id=1, source_target_pairs={{0,2},{1,3},{2,0},{3,1},{4,6},{5,7},{6,4},{7,5},{8,10},{9,11},{10,... | collective-permute-start | bytes 294920 | tf_op jit(solution)/shard_map/ppermute | solution.py:521
  29.1 7.0 %collective-permute-start.13 = (bf16[1,12,32,128]{3,2,1,0:T(8,128)(2,1)S(1)}, bf16[1,12,32,128]{3,2,1,0:T(8,128)(2,1)S(1)}, u32[]{:S(2)}, u32[]{:S(2)}) collective-permute-start(bf16[1,12,32,128]{3,2,1,0:T(8,128)(2,1)S(1)} %get-tuple-element.77), channel_id=1, source_target_pairs={{0,3},{1,2},{2,1},{3,0},{4,7},{5,6},{6,5},{7,4},{8,11},{9,10},{10,... | collective-permute-start | bytes 294920 | tf_op jit(solution)/shard_map/ppermute | solution.py:521
  30.8 25.7 %collective-permute-start.6 = (bf16[1,12,32,128]{3,2,1,0:T(8,128)(2,1)S(1)}, bf16[1,12,32,128]{3,2,1,0:T(8,128)(2,1)S(1)}, u32[]{:S(2)}, u32[]{:S(2)}) collective-permute-start(bf16[1,12,32,128]{3,2,1,0:T(8,128)(2,1)S(1)} %get-tuple-element.69), channel_id=1, source_target_pairs={{0,1},{1,0},{2,3},{3,2},{4,5},{5,4},{6,7},{7,6},{8,9},{9,8},{10,11... | collective-permute-start | bytes 294920 | tf_op jit(solution)/shard_map/ppermute | solution.py:521
  31.1 27.5 %collective-permute-start.7 = (bf16[1,12,32,128]{3,2,1,0:T(8,128)(2,1)S(1)}, bf16[1,12,32,128]{3,2,1,0:T(8,128)(2,1)S(1)}, u32[]{:S(2)}, u32[]{:S(2)}) collective-permute-start(bf16[1,12,32,128]{3,2,1,0:T(8,128)(2,1)S(1)} %get-tuple-element.70), channel_id=1, source_target_pairs={{0,2},{1,3},{2,0},{3,1},{4,6},{5,7},{6,4},{7,5},{8,10},{9,11},{10,... | collective-permute-start | bytes 294920 | tf_op jit(solution)/shard_map/ppermute | solution.py:521
  31.1 27.4 %collective-permute-start.9 = (bf16[1,12,32,128]{3,2,1,0:T(8,128)(2,1)S(1)}, bf16[1,12,32,128]{3,2,1,0:T(8,128)(2,1)S(1)}, u32[]{:S(2)}, u32[]{:S(2)}) collective-permute-start(bf16[1,12,32,128]{3,2,1,0:T(8,128)(2,1)S(1)} %get-tuple-element.72), channel_id=1, source_target_pairs={{0,3},{1,2},{2,1},{3,0},{4,7},{5,6},{6,5},{7,4},{8,11},{9,10},{10,... | collective-permute-start | bytes 294920 | tf_op jit(solution)/shard_map/ppermute | solution.py:521
  56.4 22.4 %collective-permute-start.14 = (bf16[12,64,128]{2,1,0:T(8,128)(2,1)S(1)}, bf16[12,64,128]{2,1,0:T(8,128)(2,1)S(1)}, u32[]{:S(2)}, u32[]{:S(2)}) collective-permute-start(bf16[12,64,128]{2,1,0:T(8,128)(2,1)S(1)} %get-tuple-element.79), channel_id=1, source_target_pairs={{0,1},{1,0},{2,3},{3,2},{4,5},{5,4},{6,7},{7,6},{8,9},{9,8},{10,11... | collective-permute-start | bytes 589832 | tf_op jit(solution)/shard_map/ppermute | solution.py:521
  56.4 25.6 %collective-permute-start.15 = (bf16[12,64,128]{2,1,0:T(8,128)(2,1)S(1)}, bf16[12,64,128]{2,1,0:T(8,128)(2,1)S(1)}, u32[]{:S(2)}, u32[]{:S(2)}) collective-permute-start(bf16[12,64,128]{2,1,0:T(8,128)(2,1)S(1)} %get-tuple-element.80), channel_id=1, source_target_pairs={{0,2},{1,3},{2,0},{3,1},{4,6},{5,7},{6,4},{7,5},{8,10},{9,11},{10,... | collective-permute-start | bytes 589832 | tf_op jit(solution)/shard_map/ppermute | solution.py:521
  56.5 25.6 %collective-permute-start.16 = (bf16[12,64,128]{2,1,0:T(8,128)(2,1)S(1)}, bf16[12,64,128]{2,1,0:T(8,128)(2,1)S(1)}, u32[]{:S(2)}, u32[]{:S(2)}) collective-permute-start(bf16[12,64,128]{2,1,0:T(8,128)(2,1)S(1)} %get-tuple-element.81), channel_id=1, source_target_pairs={{0,3},{1,2},{2,1},{3,0},{4,7},{5,6},{6,5},{7,4},{8,11},{9,10},{10,... | collective-permute-start | bytes 589832 | tf_op jit(solution)/shard_map/ppermute | solution.py:521
  78.6 3.5 %collective-permute-start.17 = (bf16[12,64,128]{2,1,0:T(8,128)(2,1)S(1)}, bf16[12,64,128]{2,1,0:T(8,128)(2,1)S(1)}, u32[]{:S(2)}, u32[]{:S(2)}) collective-permute-start(bf16[12,64,128]{2,1,0:T(8,128)(2,1)S(1)} %get-tuple-element.83), channel_id=1, source_target_pairs={{0,1},{1,0},{2,3},{3,2},{4,5},{5,4},{6,7},{7,6},{8,9},{9,8},{10,11... | collective-permute-start | bytes 589832 | tf_op jit(solution)/shard_map/ppermute | solution.py:521
  78.7 6.1 %collective-permute-start.10 = (bf16[12,64,128]{2,1,0:T(8,128)(2,1)S(1)}, bf16[12,64,128]{2,1,0:T(8,128)(2,1)S(1)}, u32[]{:S(2)}, u32[]{:S(2)}) collective-permute-start(bf16[12,64,128]{2,1,0:T(8,128)(2,1)S(1)} %get-tuple-element.73), channel_id=1, source_target_pairs={{0,2},{1,3},{2,0},{3,1},{4,6},{5,7},{6,4},{7,5},{8,10},{9,11},{10,... | collective-permute-start | bytes 589832 | tf_op jit(solution)/shard_map/ppermute | solution.py:521
  78.8 10.8 %collective-permute-start.18 = (bf16[12,64,128]{2,1,0:T(8,128)(2,1)S(1)}, bf16[12,64,128]{2,1,0:T(8,128)(2,1)S(1)}, u32[]{:S(2)}, u32[]{:S(2)}) collective-permute-start(bf16[12,64,128]{2,1,0:T(8,128)(2,1)S(1)} %get-tuple-element.84), channel_id=1, source_target_pairs={{0,3},{1,2},{2,1},{3,0},{4,7},{5,6},{6,5},{7,4},{8,11},{9,10},{10,... | collective-permute-start | bytes 589832 | tf_op jit(solution)/shard_map/ppermute | solution.py:521
